TPU v7x, 32 devices: a whole 2x2x4 slice. The times are simulated.
32 devices in a mesh: groups: 2 (over x), wide: 16 (over z, y, core).
Axes of the slice: x: 2, y: 2, z: 4, core: 2. Of those that a mesh axis runs over, the one named last changes fastest.
Arguments:
- tokens: bfloat16 [4096, 5120], P(('groups', 'wide')), parts along dimension 0, may hold values from -6 to 6
- query_output_gradient: bfloat16 [4096, 4096], P(('groups', 'wide')), parts along dimension 0, may hold values from -6 to 6
- down_factors: bfloat16 [5120, 4096], P('wide', 'groups'), parts along dimension 1, may hold values from -0.078125 to 0.078125
- up_factors_transposed: bfloat16 [4096, 4096], P('wide', 'groups'), parts along dimension 1, may hold values from -0.09375 to 0.09375
- tenant_of_block: int32 [32], P('groups'), parts along dimension 0, may hold values from 0 to 63
- device_tenant_list: int32 [32, 4], P(('groups', 'wide')), parts along dimension 0, may hold values from 0 to 63
- row_list_entry: int32 [128], P(('groups', 'wide')), parts along dimension 0, may hold values from 0 to 3
- hidden: bfloat16 [128, 5120], P(('groups', 'wide')), parts along dimension 0, may hold values from -6 to 6
- base_query_rows: bfloat16 [128, 4096], P(('groups', 'wide')), parts along dimension 0, may hold values from -6 to 6
- cached_key_rows: bfloat16 [128, 256, 512], P(('groups', 'wide')), parts along dimension 0, may hold values from -6 to 6
- cached_value_rows: bfloat16 [128, 256, 512], P(('groups', 'wide')), parts along dimension 0, may hold values from -6 to 6
- live_cache_length: int32 [128], P(('groups', 'wide')), parts along dimension 0, may hold values from 1 to 256, 10240 in all
Outputs:
- down_gradient: float32 [5120, 4096], P('wide', 'groups'), parts along dimension 1
- up_gradient: float32 [4096, 4096], P('wide', 'groups'), parts along dimension 1
- attended: bfloat16 [128, 4096], P(('groups', 'wide')), parts along dimension 0
There are 2 independent parts, one for each index of `groups`. A program takes and returns all parts, laid end to end along the dimension named above; each array names one. Nothing has to cross between parts.
All inputs are finite; a program needn't handle non-finite values. No bound on the sum of `live_cache_length` on one device may be relied on, other than what follows from the above.
Results may differ from a plain program's by a relative error of at most 0.0056.
Values may be sent and summed in bfloat16 or wider, within the bound.
No kernel may reach another device: no remote copies, remote signals or barrier semaphores. Data moves between devices by JAX's collectives and lax.ppermute only.
A program may use at most 64 MiB of HBM per device.

v0:
```python
import jax
import jax.numpy as jnp
from jax import lax
from jax.sharding import PartitionSpec as P

HEAD_DIM = 128
HEADS = 32
KV_HEADS = 4
RANK = 32
TENANTS = 64
BLOCK = 128
ROWS_DEV = 4


adapter_scale = 2.0
learning_rate = 0.0002


def pick_tenant_columns(table, tenants):
    grouped = table.reshape(table.shape[0], TENANTS, RANK)
    return jnp.take(grouped, tenants, axis=1)


def per_device(
    tokens,
    query_output_gradient,
    down_factors,
    up_factors_transposed,
    tenant_of_block,
    device_tenant_list,
    row_list_entry,
    hidden,
    base_query_rows,
    cached_key_rows,
    cached_value_rows,
    live_cache_length,
):
    tenant_indicator = (
        tenant_of_block[:, None] == jnp.arange(TENANTS, dtype=jnp.int32)[None, :]
    ).astype(jnp.float32)
    x_cols, g_cols, h_cols = (
        lax.all_to_all(tokens, "wide", split_axis=1, concat_axis=0, tiled=True),
        lax.all_to_all(query_output_gradient, "wide", split_axis=1, concat_axis=0, tiled=True),
        lax.all_to_all(hidden, "wide", split_axis=1, concat_axis=0, tiled=True),
    )
    total_tokens = x_cols.shape[0]
    local_tokens = tokens.shape[0]
    block_count = total_tokens // BLOCK
    token_partial = x_cols.reshape(
        local_tokens * lax.axis_size("wide") // BLOCK, BLOCK, x_cols.shape[1]
    )
    grad_part = g_cols.reshape(
        local_tokens * lax.axis_size("wide") // BLOCK, BLOCK, g_cols.shape[1]
    )
    selected_down = pick_tenant_columns(down_factors, tenant_of_block)
    selected_up = pick_tenant_columns(up_factors_transposed, tenant_of_block)
    down_partial = jnp.einsum(
        "jwt,tjo->jwo", token_partial, selected_down, preferred_element_type=jnp.float32
    )
    back_part = jnp.einsum(
        "bkq,qbr->bkr", grad_part, selected_up, preferred_element_type=jnp.float32
    )
    shares = lax.psum_scatter(
        jnp.concatenate([down_partial, back_part], axis=2).reshape(
            local_tokens * lax.axis_size("wide"), 2 * RANK
        ),
        "wide",
        scatter_dimension=0,
        tiled=True,
    ).astype(jnp.bfloat16)
    ranks = lax.all_gather(shares, "wide", axis=0, tiled=True)
    down_projected = ranks[:, :RANK].reshape(block_count, BLOCK, RANK)
    backward_input = ranks[:, RANK:].reshape(block_count, BLOCK, RANK)
    input_block = x_cols.reshape(block_count, BLOCK, x_cols.shape[1])
    gb = g_cols.reshape(block_count, BLOCK, g_cols.shape[1])
    tenant_up_gradient = jnp.einsum(
        "bkq,bkr->bqr", gb, down_projected, preferred_element_type=jnp.float32
    )
    tenant_down_gradient = jnp.einsum(
        "vzu,vzh->vuh", input_block, backward_input, preferred_element_type=jnp.float32
    )
    up_gradient = adapter_scale * jnp.einsum(
        "pfx,pw->fwx", tenant_up_gradient, tenant_indicator, precision=lax.Precision.HIGHEST
    ).reshape(tenant_up_gradient.shape[1], TENANTS * RANK)
    down_gradient = adapter_scale * jnp.einsum(
        "xai,xk->aki", tenant_down_gradient, tenant_indicator, precision=lax.Precision.HIGHEST
    ).reshape(tenant_down_gradient.shape[1], TENANTS * RANK)
    updated_down = (down_factors.astype(jnp.float32) - learning_rate * down_gradient).astype(
        jnp.bfloat16
    )
    updated_up = (up_factors_transposed.astype(jnp.float32) - learning_rate * up_gradient).astype(
        jnp.bfloat16
    )
    lists, slots = (
        lax.all_gather(device_tenant_list, "wide", axis=0, tiled=True),
        lax.all_gather(row_list_entry, "wide", axis=0, tiled=True),
    )
    total_rows = slots.shape[0]
    owner = jnp.arange(total_rows, dtype=jnp.int32) // ROWS_DEV
    row_tenant = lists[owner, slots]
    a_rows = pick_tenant_columns(updated_down, row_tenant)
    partial_rank = jnp.einsum("rd,drk->rk", h_cols, a_rows, preferred_element_type=jnp.float32)
    adapted_query = lax.psum(partial_rank, "wide").astype(jnp.bfloat16)
    b_rows = pick_tenant_columns(updated_up, row_tenant)
    query_change = adapter_scale * jnp.einsum(
        "ez,jez->ej", adapted_query, b_rows, preferred_element_type=jnp.float32
    )
    delta_rows = lax.all_to_all(query_change, "wide", split_axis=0, concat_axis=1, tiled=True)
    query = (base_query_rows.astype(jnp.float32) + delta_rows).astype(jnp.bfloat16)
    local_rows = query.shape[0]
    cache_size = cached_key_rows.shape[1]
    group = HEADS // KV_HEADS
    q_heads = query.reshape(local_rows, KV_HEADS, group, HEAD_DIM)
    keys = cached_key_rows.reshape(local_rows, cache_size, KV_HEADS, HEAD_DIM)
    values = cached_value_rows.reshape(local_rows, cache_size, KV_HEADS, HEAD_DIM)
    scores = jnp.einsum(
        "rhgd,rphd->rhgp", q_heads, keys, preferred_element_type=jnp.float32
    ) / jnp.sqrt(jnp.float32(HEAD_DIM))
    live = jnp.arange(cache_size, dtype=jnp.int32)[None, :] < live_cache_length[:, None]
    scores = jnp.where(live[:, None, None, :], scores, jnp.float32(-1e30))
    top = jnp.max(scores, axis=-1, keepdims=True)
    expo = jnp.where(live[:, None, None, :], jnp.exp(scores - top), jnp.float32(0.0))
    weights = (expo / jnp.sum(expo, axis=-1, keepdims=True)).astype(jnp.bfloat16)
    attended = jnp.einsum("rhgp,rphd->rhgd", weights, values, preferred_element_type=jnp.float32)
    return (
        down_gradient,
        up_gradient,
        attended.reshape(local_rows, HEADS * HEAD_DIM).astype(jnp.bfloat16),
    )


def solution(mesh):
    placed = (
        P(("groups", "wide"), None),
        P(("groups", "wide"), None),
        P("wide", "groups"),
        P("wide", "groups"),
        P("groups"),
        P(("groups", "wide"), None),
        P(("groups", "wide")),
        P(("groups", "wide"), None),
        P(("groups", "wide"), None),
        P(("groups", "wide"), None, None),
        P(("groups", "wide"), None, None),
        P(("groups", "wide")),
    )
    return jax.shard_map(
        per_device,
        mesh=mesh,
        in_specs=placed,
        out_specs=(P("wide", "groups"), P("wide", "groups"), P(("groups", "wide"), None)),
        check_vma=False,
    )
```

profile of v0, /device:TPU:0, one launch (start us, length us, event | category | flops | bytes accessed | tf_op | source)
XLA Modules:
  0.0 259.6 jit_solution(9210505050922150425)
XLA Ops:
  10.2 7.4 %all-to-all-start.1 = ((bf16[128,16,256]{2,0,1:T(8,128)(2,1)}), bf16[128,16,256]{2,0,1:T(8,128)(2,1)S(1)}, u32[]{:S(2)}, u32[]{:S(2)}) async-start(bf16[128,16,256]{2,0,1:T(8,128)(2,1)} %copy.61), calls=%async_computation.1 | async-start | bytes 2097152 | tf_op jit(solution)/shard_map/all_to_all | solution.py:43
  19.1 21.5 %all-to-all-done.1 = bf16[128,16,256]{2,0,1:T(8,128)(2,1)S(1)} async-done(((bf16[128,16,256]{2,0,1:T(8,128)(2,1)}), bf16[128,16,256]{2,0,1:T(8,128)(2,1)S(1)}, u32[]{:S(2)}, u32[]{:S(2)}) %all-to-all-start.1) | async-done | bytes 1048608 | tf_op jit(solution)/shard_map/all_to_all | solution.py:43
  40.6 6.9 %all-to-all-start = ((bf16[128,16,320]{0,2,1:T(8,128)(2,1)}), bf16[128,16,320]{0,2,1:T(8,128)(2,1)}, u32[]{:S(2)}, u32[]{:S(2)}) async-start(bf16[128,16,320]{0,2,1:T(8,128)(2,1)} %bitcast.3), calls=%async_computation | async-start | bytes 2621440 | tf_op jit(solution)/shard_map/all_to_all | solution.py:42
  48.9 1.8 copy.57
  50.7 2.3 gather_fusion.1
  53.7 1.7 convolution_bitcast_fusion.1
  55.5 19.4 %all-to-all-done = bf16[128,16,320]{0,2,1:T(8,128)(2,1)} async-done(((bf16[128,16,320]{0,2,1:T(8,128)(2,1)}), bf16[128,16,320]{0,2,1:T(8,128)(2,1)}, u32[]{:S(2)}, u32[]{:S(2)}) %all-to-all-start) | async-done | bytes 1310752 | tf_op jit(solution)/shard_map/all_to_all | solution.py:42
  78.3 8.0 %all-to-all-start.2 = ((bf16[4,16,320]{2,0,1:T(4,128)(2,1)}), bf16[4,16,320]{2,0,1:T(4,128)(2,1)S(1)}, u32[]{:S(2)}, u32[]{:S(2)}) async-start(bf16[4,16,320]{2,0,1:T(4,128)(2,1)} %copy.72), calls=%async_computation.3 | async-start | bytes 98304 | tf_op jit(solution)/shard_map/all_to_all | solution.py:44
  86.3 21.6 %all-gather = s32[16,1,4]{2,1,0:T(1,128)S(1)} all-gather(s32[1,1,4]{2,1,0:T(1,128)S(1)} %bitcast.147), channel_id=1, replica_groups=mesh['groups'=2,'wide'=16] {'wide'}, dimensions={0}, use_global_device_ids=true | all-gather | bytes 272 | tf_op jit(solution)/shard_map/all_gather | solution.py:95
  109.5 7.2 %all-reduce = s32[64]{0:T(128)S(1)} all-reduce(s32[64]{0:T(128)S(1)} %dynamic-update-slice), channel_id=1, replica_groups=mesh['groups'=2,'wide'=16] {'wide'}, use_global_device_ids=true, to_apply=%add | all-reduce | flops 64 | bytes 512
  117.7 19.1 %reduce-scatter.2.cloned.1.call-done = f32[128,64]{0,1:T(8,128)} async-done(((f32[2048,64]{0,1:T(8,128)}), f32[128,64]{0,1:T(8,128)}) %reduce-scatter.2.cloned.1.call-update) | async-done | bytes 32784 | tf_op jit(solution)/shard_map/reduce_scatter | solution.py:63
  137.5 20.1 %all_gather.9 = bf16[2048,64]{0,1:T(8,128)(2,1)S(1)} all-gather(bf16[128,64]{0,1:T(8,128)(2,1)S(1)} %convert_element_type.34), channel_id=1, replica_groups=mesh['groups'=2,'wide'=16] {'wide'}, dimensions={0}, use_global_device_ids=true | all-gather | bytes 278528 | tf_op jit(solution)/shard_map/all_gather | solution.py:71
  157.7 1.8 fusion.11
  159.5 3.5 %multiply_bitcast_fusion = (f32[320,64,32]{0,1,2:T(8,128)S(1)}, f32[320,64,32]{0,1,2:T(8,128)}) fusion(f32[16,320,32]{1,2,0:T(8,128)S(1)} %fusion.11, s32[16]{0:T(128)S(1)} %copy-done.11), kind=kOutput, calls=%fused_computation.8 | convolution fusion | flops 127140864 | bytes 5898304 | tf_op jit(solution)/shard_map/xai,xk->aki/dot_general | solution.py:85
  163.0 1.8 copy.71
  165.2 1.9 gather_fusion.3
  167.1 2.2 fusion.3
  169.3 57.8 %psum.7 = bf16[64,32]{1,0:T(8,128)(2,1)S(1)} all-reduce(f32[64,32]{1,0:T(8,128)S(1)} %bitcast.144), channel_id=1, replica_groups=mesh['groups'=2,'wide'=16] {'wide'}, use_global_device_ids=true, to_apply=%region_1.2 | all-reduce | flops 2048 | bytes 12288 | tf_op jit(solution)/shard_map/psum | solution.py:103
  227.4 2.6 multiply_bitcast_fusion.2
  233.1 3.5 %all-to-all-start.3 = ((f32[16,4,256]{2,1,0:T(4,128)}), f32[16,4,256]{2,1,0:T(4,128)S(1)}, u32[]{:S(2)}, u32[]{:S(2)}) async-start(f32[16,4,256]{2,1,0:T(4,128)} %all_to_all.62), calls=%async_computation.4 | async-start | bytes 131072 | tf_op jit(solution)/shard_map/all_to_all | solution.py:108
  236.7 5.4 %copy.65 = f32[320,64,32]{0,2,1:T(8,128)} copy(f32[320,64,32]{0,1,2:T(8,128)} %get-tuple-element.13) | data formatting | bytes 5242880 | tf_op jit(solution)/shard_map/mul | solution.py:85
  242.1 3.5 %copy.77 = f32[320,2048]{1,0:T(8,128)} copy(f32[320,2048]{0,1:T(8,128)} %bitcast.138) | data formatting | bytes 5242880
  245.6 2.5 copy.68
  248.2 3.0 %copy.78 = f32[256,2048]{1,0:T(8,128)} copy(f32[256,2048]{0,1:T(8,128)} %bitcast.140) | data formatting | bytes 4194304
  (76 shorter events, 17.8 us)
Async XLA Ops:
  7.2 244.0 %copy-start = (bf16[4,256,512]{2,1,0:T(8,128)(2,1)S(1)}, bf16[4,256,512]{2,1,0:T(8,128)(2,1)}, u32[]{:S(2)}) copy-start(bf16[4,256,512]{2,1,0:T(8,128)(2,1)} %param.21) | copy-start | bytes 3145732
  8.9 8.7 %copy-start.7 = (bf16[128,5120]{1,0:T(8,128)(2,1)S(1)}, bf16[128,5120]{1,0:T(8,128)(2,1)}, u32[]{:S(2)}) copy-start(bf16[128,5120]{1,0:T(8,128)(2,1)} %param.12) | copy-start | bytes 3932164
  10.2 30.3 %all-to-all-start.1 = ((bf16[128,16,256]{2,0,1:T(8,128)(2,1)}), bf16[128,16,256]{2,0,1:T(8,128)(2,1)S(1)}, u32[]{:S(2)}, u32[]{:S(2)}) async-start(bf16[128,16,256]{2,0,1:T(8,128)(2,1)} %copy.61), calls=%async_computation.1 | async-start | bytes 2097152 | tf_op jit(solution)/shard_map/all_to_all | solution.py:43
  19.1 28.5 %copy-start.8 = (bf16[256,2048]{1,0:T(8,128)(2,1)S(1)}, bf16[256,2048]{1,0:T(8,128)(2,1)}, u32[]{:S(2)}) copy-start(bf16[256,2048]{1,0:T(8,128)(2,1)} %param.15) | copy-start | bytes 3145732
  40.6 7.0 %copy-start.3 = (bf16[128,16,256]{2,0,1:T(8,128)(2,1)}, bf16[128,16,256]{2,0,1:T(8,128)(2,1)S(1)}, u32[]{:S(2)}) copy-start(bf16[128,16,256]{2,0,1:T(8,128)(2,1)S(1)} %all-to-all-done.1) | copy-start | bytes 3145732
  40.6 34.4 %all-to-all-start = ((bf16[128,16,320]{0,2,1:T(8,128)(2,1)}), bf16[128,16,320]{0,2,1:T(8,128)(2,1)}, u32[]{:S(2)}, u32[]{:S(2)}) async-start(bf16[128,16,320]{0,2,1:T(8,128)(2,1)} %bitcast.3), calls=%async_computation | async-start | bytes 2621440 | tf_op jit(solution)/shard_map/all_to_all | solution.py:42
  47.5 3.2 %copy-start.11 = (s32[16]{0:T(128)S(1)}, s32[16]{0:T(128)}, u32[]{:S(2)}) copy-start(s32[16]{0:T(128)} %param.16) | copy-start | bytes 196
  47.5 89.3 %reduce-scatter.2.cloned.1.call-start = ((), (), s32[]{:S(2)}) async-start(), calls=%async_computation.5 | async-start | bytes 557056 | tf_op jit(solution)/shard_map/reduce_scatter | solution.py:63
  50.7 3.0 %copy-start.1 = (bf16[320,2048]{0,1:T(8,128)(2,1)}, bf16[320,2048]{0,1:T(8,128)(2,1)S(1)}, u32[]{:S(2)}) copy-start(bf16[320,2048]{0,1:T(8,128)(2,1)S(1)} %copy.57) | copy-start | bytes 3932164
  55.5 22.1 %copy-start.9 = (bf16[4,5120]{1,0:T(4,128)(2,1)S(1)}, bf16[4,5120]{1,0:T(4,128)(2,1)}, u32[]{:S(2)}) copy-start(bf16[4,5120]{1,0:T(4,128)(2,1)} %param.19) | copy-start | bytes 122884
  55.5 30.8 %copy-start.12 = (s32[1,4]{1,0:T(1,128)S(1)}, s32[1,4]{1,0:T(1,128)}, u32[]{:S(2)}) copy-start(s32[1,4]{1,0:T(1,128)} %param.17) | copy-start | bytes 52
  55.5 52.5 %copy-start.16 = (u32[32]{0:T(128)S(1)}, u32[32]{0:T(128)}, u32[]{:S(2)}) copy-start(u32[32]{0:T(128)} %constant.114) | copy-start | bytes 388
  55.5 53.7 %copy-start.14 = (s32[4]{0:T(128)S(1)}, s32[4]{0:T(128)}, u32[]{:S(2)}) copy-start(s32[4]{0:T(128)} %param.18) | copy-start | bytes 52
  78.3 39.4 %all-to-all-start.2 = ((bf16[4,16,320]{2,0,1:T(4,128)(2,1)}), bf16[4,16,320]{2,0,1:T(4,128)(2,1)S(1)}, u32[]{:S(2)}, u32[]{:S(2)}) async-start(bf16[4,16,320]{2,0,1:T(4,128)(2,1)} %copy.72), calls=%async_computation.3 | async-start | bytes 98304 | tf_op jit(solution)/shard_map/all_to_all | solution.py:44
  163.0 1.8 copy-start.2
  167.1 60.1 %copy-start.4 = (bf16[128,16,256]{2,0,1:T(8,128)(2,1)S(1)}, bf16[128,16,256]{2,0,1:T(8,128)(2,1)}, u32[]{:S(2)}) copy-start(bf16[128,16,256]{2,0,1:T(8,128)(2,1)} %copy-done.3) | copy-start | bytes 3145732
  230.0 1.2 copy-start.5
  231.5 5.1 %copy-start.15 = (s32[4]{0:T(128)S(1)}, s32[4]{0:T(128)}, u32[]{:S(2)}) copy-start(s32[4]{0:T(128)} %param.23) | copy-start | bytes 52
  233.1 18.0 %all-to-all-start.3 = ((f32[16,4,256]{2,1,0:T(4,128)}), f32[16,4,256]{2,1,0:T(4,128)S(1)}, u32[]{:S(2)}, u32[]{:S(2)}) async-start(f32[16,4,256]{2,1,0:T(4,128)} %all_to_all.62), calls=%async_computation.4 | async-start | bytes 131072 | tf_op jit(solution)/shard_map/all_to_all | solution.py:108
  242.1 3.5 %copy-start.6 = (f32[256,64,32]{0,1,2:T(8,128)S(1)}, f32[256,64,32]{0,1,2:T(8,128)}, u32[]{:S(2)}) copy-start(f32[256,64,32]{0,1,2:T(8,128)} %get-tuple-element.15) | copy-start | bytes 6291460
  248.2 3.0 %copy-start.10 = (bf16[4,4096]{1,0:T(4,128)(2,1)S(1)}, bf16[4,4096]{1,0:T(4,128)(2,1)}, u32[]{:S(2)}) copy-start(bf16[4,4096]{1,0:T(4,128)(2,1)} %param.20) | copy-start | bytes 98308
  248.2 3.6 %copy-start.13 = (bf16[4,256,512]{2,1,0:T(8,128)(2,1)S(1)}, bf16[4,256,512]{2,1,0:T(8,128)(2,1)}, u32[]{:S(2)}) copy-start(bf16[4,256,512]{2,1,0:T(8,128)(2,1)} %param.22) | copy-start | bytes 3145732
Sparse Core Ops, SparseCore 0:
  77.6 59.0 reduce-scatter.1
where the time goes:
time: 260 us
  blocking collectives  107 us (41%)
  waiting for transfers between devices  60 us (23%)
  local copies, waits for them, and re-layouts  34.5 us (13%)
  starting transfers between devices  25.8 us (10%)
  between operations  15 us (6%)
  matrix products  14.8 us (6%)
    psum x1, blocking collectives, per_device(): adapted_query = lax.psum(partial_rank, 'wide').astype(jnp.bfloat16)  57.8 us
    all_gather x1, blocking collectives, per_device(): lax.all_gather(device_tenant_list, 'wide', axis=0, tiled=True)  21.6 us
    all_to_all x1, waiting for transfers between devices, per_device(): lax.all_to_all(query_output_gradient, 'wide', split_axis=1, concat_axis=0...  21.5 us
    all_gather x1, blocking collectives, per_device(): ranks = lax.all_gather(shares, 'wide', axis=0, tiled=True)  20.1 us
    all_to_all x1, waiting for transfers between devices, per_device(): lax.all_to_all(tokens, 'wide', split_axis=1, concat_axis=0, tiled=True)  19.4 us
    reduce_scatter x1, waiting for transfers between devices, per_device(): lax.psum_scatter(jnp.concatenate([down_partial, back_part], axis=2).resha...  19.1 us
    unnamed x44, local copies, waits for them, and re-layouts  14.4 us
    all_to_all x1, starting transfers between devices, per_device(): lax.all_to_all(hidden, 'wide', split_axis=1, concat_axis=0, tiled=True)  8.01 us
  transfers between devices with their start and end apart: 5, of which 3 were waited for; matrix products, arithmetic and copies ran while one was open for 10% of the time, Pallas kernels for 0%

commit v1 on v0

v1 whole, which is shorter than its diff:
```python
import functools

import jax
import jax.numpy as jnp
from jax import lax
from jax.experimental import pallas as pl
from jax.experimental.pallas import tpu as pltpu
from jax.sharding import PartitionSpec as P

HEAD_DIM = 128
HEADS = 32
KV_HEADS = 4
RANK = 32
TENANTS = 64
BLOCK = 128
ROWS_DEV = 4
LANES = 128
PER_TILE = LANES // RANK

adapter_scale = 2.0
learning_rate = 0.0002

F32 = jnp.float32
BF16 = jnp.bfloat16
VMEM_LIMIT = 40 * 1024 * 1024


def vmem():
    return pl.BlockSpec(memory_space=pltpu.VMEM)


def smem():
    return pl.BlockSpec(memory_space=pltpu.SMEM)


def call(kernel, out_shape, in_specs, scratch=(), flops=0, nbytes=0):
    single = not isinstance(out_shape, (list, tuple))
    return pl.pallas_call(
        kernel,
        out_shape=out_shape,
        in_specs=in_specs,
        out_specs=vmem() if single else [vmem()] * len(out_shape),
        scratch_shapes=list(scratch),
        compiler_params=pltpu.CompilerParams(vmem_limit_bytes=VMEM_LIMIT),
        cost_estimate=pl.CostEstimate(flops=flops, bytes_accessed=nbytes, transcendentals=0),
    )


def each(count, body):
    if count <= 16:
        for j in range(count):
            body(j)
    else:
        pl.loop(0, count)(body)


def dot(a, b, ca, cb):
    return lax.dot_general(a, b, (((ca,), (cb,)), ((), ())), preferred_element_type=F32)


def quarter_indicator(quarter, value):
    lane = lax.broadcasted_iota(jnp.int32, (RANK, LANES), 1)
    row = lax.broadcasted_iota(jnp.int32, (RANK, LANES), 0)
    return jnp.where(lane - row == quarter * RANK, value, 0.0).astype(BF16)


def tile_of(tenant):
    return pl.ds(pl.multiple_of((tenant // PER_TILE) * LANES, LANES), LANES)


def pick_kernel(t_ref, a_ref, b_ref, extra_ref, o_ref):
    fa, fb, w = a_ref.shape[0], b_ref.shape[0], extra_ref.shape[2]
    o_ref[...] = jnp.zeros_like(o_ref)

    def body(j):
        t = t_ref[j]
        pick = quarter_indicator(t % PER_TILE, 1.0)
        o_ref[j, :, :fb] = dot(pick, b_ref[:, tile_of(t)], 1, 1).astype(BF16)
        o_ref[j, :, fb : fb + fa] = dot(pick, a_ref[:, tile_of(t)], 1, 1).astype(BF16)
        o_ref[j, :, fb + fa : fb + fa + w] = extra_ref[j]

    each(t_ref.shape[0], body)


def block_kernel(x_ref, g_ref, r_ref, o_ref, wa_ref, wb_ref):
    n = r_ref.shape[0]
    fa, fb = x_ref.shape[1] // n, g_ref.shape[1] // n
    for d in range(n):
        wb_ref[:, d * fb : (d + 1) * fb] = r_ref[d, :, :fb]
        wa_ref[:, d * fa : (d + 1) * fa] = r_ref[d, :, fb : fb + fa]
    down = dot(wa_ref[...], x_ref[...], 1, 1).astype(BF16)
    back = dot(wb_ref[...], g_ref[...], 1, 1).astype(BF16)
    up_part = dot(down, g_ref[...], 1, 0).astype(BF16)
    down_part = dot(back, x_ref[...], 1, 0).astype(BF16)
    o_ref[...] = jnp.zeros_like(o_ref)
    for d in range(n):
        o_ref[d, :, :fb] = up_part[:, d * fb : (d + 1) * fb]
        o_ref[d, :, fb : fb + fa] = down_part[:, d * fa : (d + 1) * fa]


def sum_by_tenant(t_ref, part_ref, low, high, grad_ref):
    grad_ref[...] = jnp.zeros_like(grad_ref)

    def body(j):
        t = t_ref[j]
        place = quarter_indicator(t % PER_TILE, adapter_scale)
        grad_ref[:, tile_of(t)] += dot(part_ref[j, :, low:high], place, 0, 0)

    each(t_ref.shape[0], body)


def down_kernel(fb, t_ref, part_ref, a_ref, h_ref, u_ref, grad_ref, o_ref):
    fa = a_ref.shape[0]
    rows = h_ref.shape[0]
    sum_by_tenant(t_ref, part_ref, fb, fb + fa, grad_ref)
    new_a = (a_ref[...].astype(F32) - learning_rate * grad_ref[...]).astype(BF16)
    product = dot(h_ref[...], new_a, 1, 0)
    lane = lax.broadcasted_iota(jnp.int32, (rows, LANES), 1)
    tenant = u_ref[...]
    total = jnp.zeros((rows, LANES), F32)
    for c in range(TENANTS // PER_TILE):
        mine = tenant == c * PER_TILE + lane // RANK
        total = total + jnp.where(mine, product[:, c * LANES : (c + 1) * LANES], 0.0)
    half = total + pltpu.roll(total, 2 * RANK, 1)
    full = half + pltpu.roll(half, RANK, 1)
    quarter = rows // PER_TILE
    packed = jnp.zeros((quarter, LANES), F32)
    spot = lax.broadcasted_iota(jnp.int32, (quarter, LANES), 1) // RANK
    for q in range(PER_TILE):
        packed = packed + jnp.where(spot == q, full[q * quarter : (q + 1) * quarter], 0.0)
    for d in range(o_ref.shape[0]):
        o_ref[d] = packed


def up_kernel(t_ref, part_ref, b_ref, grad_ref, new_ref):
    sum_by_tenant(t_ref, part_ref, 0, b_ref.shape[0], grad_ref)
    new_ref[...] = (b_ref[...].astype(F32) - learning_rate * grad_ref[...]).astype(BF16)


def delta_kernel(p_ref, u_ref, new_ref, o_ref):
    n, quarter = p_ref.shape[0], p_ref.shape[1]
    total = p_ref[0]
    for d in range(1, n):
        total = total + p_ref[d]
    spot = lax.broadcasted_iota(jnp.int32, (quarter, LANES), 1) // RANK
    pieces = []
    for q in range(PER_TILE):
        one = jnp.where(spot == q, total, 0.0)
        half = one + pltpu.roll(one, 2 * RANK, 1)
        pieces.append(half + pltpu.roll(half, RANK, 1))
    adapted = jnp.concatenate(pieces, axis=0)
    rows = adapted.shape[0]
    lane = lax.broadcasted_iota(jnp.int32, (rows, LANES), 1)
    tenant = u_ref[...]
    spread = jnp.concatenate(
        [
            jnp.where(tenant == c * PER_TILE + lane // RANK, adapted, 0.0).astype(BF16)
            for c in range(TENANTS // PER_TILE)
        ],
        axis=1,
    )
    delta = adapter_scale * dot(spread, new_ref[...], 1, 1)
    for d in range(n):
        o_ref[d] = delta[d * ROWS_DEV : (d + 1) * ROWS_DEV]


def attention_kernel(len_ref, delta_ref, base_ref, k_ref, v_ref, o_ref):
    n = delta_ref.shape[0]
    delta = jnp.concatenate([delta_ref[d] for d in range(n)], axis=1)
    query = (base_ref[...] + delta).astype(BF16).astype(F32)
    group = HEADS // KV_HEADS
    cache = k_ref.shape[1]
    many = group * ROWS_DEV
    row_p = lax.broadcasted_iota(jnp.int32, (many, cache), 0) % ROWS_DEV
    row_d = lax.broadcasted_iota(jnp.int32, (many, HEAD_DIM), 0) % ROWS_DEV
    position = lax.broadcasted_iota(jnp.int32, (many, cache), 1)
    length = jnp.zeros((many, cache), jnp.int32)
    for r in range(ROWS_DEV):
        length = jnp.where(row_p == r, len_ref[r], length)
    live = position < length
    outs = []
    for g in range(KV_HEADS):
        cols = slice(g * HEAD_DIM, (g + 1) * HEAD_DIM)
        heads = jnp.concatenate(
            [query[:, (g * group + i) * HEAD_DIM : (g * group + i + 1) * HEAD_DIM] for i in range(group)],
            axis=0,
        ).astype(BF16)
        scores = jnp.zeros((many, cache), F32)
        for r in range(ROWS_DEV):
            scores = jnp.where(row_p == r, dot(heads, k_ref[r, :, cols], 1, 1), scores)
        scores = scores / jnp.sqrt(F32(HEAD_DIM))
        scores = jnp.where(live, scores, F32(-1e30))
        top = jnp.max(scores, axis=-1, keepdims=True)
        expo = jnp.where(live, jnp.exp(scores - top), 0.0)
        weights = (expo / jnp.sum(expo, axis=-1, keepdims=True)).astype(BF16)
        mixed = jnp.zeros((many, HEAD_DIM), F32)
        for r in range(ROWS_DEV):
            mixed = jnp.where(row_d == r, dot(weights, v_ref[r, :, cols], 1, 0), mixed)
        outs.extend(mixed[i * ROWS_DEV : (i + 1) * ROWS_DEV] for i in range(group))
    o_ref[...] = jnp.concatenate(outs, axis=1).astype(BF16)


def exchange(x):
    return lax.all_to_all(x, "wide", split_axis=0, concat_axis=0, tiled=True)


def per_device(
    tokens,
    query_output_gradient,
    down_factors,
    up_factors_transposed,
    tenant_of_block,
    device_tenant_list,
    row_list_entry,
    hidden,
    base_query_rows,
    cached_key_rows,
    cached_value_rows,
    live_cache_length,
):
    n = lax.axis_size("wide")
    fa, cols = down_factors.shape
    fb = up_factors_transposed.shape[0]
    local_rows = hidden.shape[0]
    rows = local_rows * n
    assert tokens.shape[0] == BLOCK and tenant_of_block.shape[0] == n
    wide = -(-(fa + fb + 1) // LANES) * LANES
    room = wide - fa - fb
    w = max(k for k in range(1, room + 1) if fa % k == 0)
    pieces = fa // w
    assert local_rows * (pieces + 1) <= RANK

    slot = row_list_entry[:, None] == jnp.arange(device_tenant_list.shape[1], dtype=jnp.int32)[None, :]
    row_tenant = jnp.sum(jnp.where(slot, device_tenant_list, 0), axis=1)
    slices = hidden.reshape(local_rows, n, pieces, w).transpose(1, 2, 0, 3).reshape(n, pieces * local_rows, w)
    marks = jnp.broadcast_to(row_tenant.astype(BF16)[None, :, None], (n, local_rows, w))
    extra = jnp.concatenate([slices, marks], axis=1)
    extra = jnp.pad(extra, ((0, 0), (0, RANK - extra.shape[1]), (0, 0)))

    packed = call(
        pick_kernel,
        jax.ShapeDtypeStruct((n, RANK, wide), BF16),
        [smem(), vmem(), vmem(), vmem()],
        flops=2 * RANK * LANES * n * (fa + fb),
        nbytes=2 * cols * (fa + fb),
    )(tenant_of_block, down_factors, up_factors_transposed, extra)
    got = exchange(packed)

    parts = call(
        block_kernel,
        jax.ShapeDtypeStruct((n, RANK, wide), BF16),
        [vmem(), vmem(), vmem()],
        scratch=[
            pltpu.VMEM((RANK, tokens.shape[1]), BF16),
            pltpu.VMEM((RANK, query_output_gradient.shape[1]), BF16),
        ],
        flops=4 * RANK * BLOCK * n * (fa + fb),
        nbytes=2 * BLOCK * n * (fa + fb),
    )(tokens, query_output_gradient, got)
    shares = exchange(parts)

    tail = got[:, :, fa + fb : fa + fb + w]
    h_cols = (
        tail[:, : pieces * local_rows]
        .reshape(n, pieces, local_rows, w)
        .transpose(0, 2, 1, 3)
        .reshape(rows, fa)
    )
    tenants = tail[:, pieces * local_rows : (pieces + 1) * local_rows, 0].reshape(rows, 1)
    tenants = jnp.broadcast_to(tenants.astype(jnp.int32), (rows, LANES))

    down_gradient, low_rank = call(
        functools.partial(down_kernel, fb),
        [
            jax.ShapeDtypeStruct((fa, cols), F32),
            jax.ShapeDtypeStruct((n, rows // PER_TILE, LANES), F32),
        ],
        [smem(), vmem(), vmem(), vmem(), vmem()],
        flops=2 * rows * fa * cols,
        nbytes=6 * cols * fa,
    )(tenant_of_block, shares, down_factors, h_cols, tenants)
    low_rank = exchange(low_rank)
    up_gradient, new_up = call(
        up_kernel,
        [jax.ShapeDtypeStruct((fb, cols), F32), jax.ShapeDtypeStruct((fb, cols), BF16)],
        [smem(), vmem(), vmem()],
        flops=2 * n * RANK * fb * LANES,
        nbytes=8 * cols * fb,
    )(tenant_of_block, shares, up_factors_transposed)
    delta = call(
        delta_kernel,
        jax.ShapeDtypeStruct((n, local_rows, fb), F32),
        [vmem(), vmem(), vmem()],
        flops=2 * rows * cols * fb,
        nbytes=2 * cols * fb,
    )(low_rank, tenants, new_up)
    delta = exchange(delta)
    attended = call(
        attention_kernel,
        jax.ShapeDtypeStruct((local_rows, HEADS * HEAD_DIM), BF16),
        [smem(), vmem(), vmem(), vmem(), vmem()],
        flops=4 * HEADS * local_rows * cached_key_rows.shape[1] * HEAD_DIM,
        nbytes=4 * cached_key_rows.size,
    )(live_cache_length, delta, base_query_rows.astype(F32), cached_key_rows, cached_value_rows)
    return down_gradient, up_gradient, attended


def solution(mesh):
    placed = (
        P(("groups", "wide"), None),
        P(("groups", "wide"), None),
        P("wide", "groups"),
        P("wide", "groups"),
        P("groups"),
        P(("groups", "wide"), None),
        P(("groups", "wide")),
        P(("groups", "wide"), None),
        P(("groups", "wide"), None),
        P(("groups", "wide"), None, None),
        P(("groups", "wide"), None, None),
        P(("groups", "wide")),
    )
    return jax.shard_map(
        per_device,
        mesh=mesh,
        in_specs=placed,
        out_specs=(P("wide", "groups"), P("wide", "groups"), P(("groups", "wide"), None)),
        check_vma=False,
    )
```

time: 260 us -> 88.4 us (0.34)
  blocking collectives: 107 us -> 25.4 us
  waiting for transfers between devices: 60 us -> 25.1 us
  local copies, waits for them, and re-layouts: 34.5 us -> 9.54 us
  matrix products: 14.8 us -> 0 us
  between operations: 15 us -> 0.8 us
  starting transfers between devices: 25.8 us -> 12.1 us
  Pallas kernels: 0 us -> 12.6 us
    psum x1 -> x0, blocking collectives: 57.8 us -> none  [per_device(): adapted_query = lax.psum(partial_rank, 'wide').astype(jnp.bfloat16)]
    all_gather x2 -> x0, blocking collectives: 41.7 us -> none  [the longest x1 21.6 us: per_device(): lax.all_gather(device_tenant_list, 'wide', axis=0, tiled=True)]
    all_to_all x0 -> x1, blocking collectives: none -> 25.4 us  [exchange(): return lax.all_to_all(x, 'wide', split_axis=0, concat_axis=0, tiled=True)]
    reduce_scatter x1 -> x0, waiting for transfers between devices: 19.1 us -> none  [per_device(): lax.psum_scatter(jnp.concatenate([down_partial, back_part], axis=2).resha...]
    all_to_all x4 -> x3, waiting for transfers between devices: 40.9 us -> 25.1 us  [exchange(): return lax.all_to_all(x, 'wide', split_axis=0, concat_axis=0, tiled=True)]
    dot_general x10 -> x0, matrix products: 14.8 us -> none  [the longest x1 3.49 us: per_device(): jnp.einsum('xai,xk->aki', tenant_down_gradient, tenant_indicator, precisi...]
    all_to_all x4 -> x3, starting transfers between devices: 25.8 us -> 12.1 us  [exchange(): return lax.all_to_all(x, 'wide', split_axis=0, concat_axis=0, tiled=True)]
    pallas_call x0 -> x6, Pallas kernels: none -> 12.6 us  [the longest x1 3.03 us: per_device(): call(functools.partial(down_kernel, fb), [jax.ShapeDtypeStruct((fa, cols)...]
  transfers between devices with their start and end apart: 5 -> 3, of which waited for: 3 -> 3; matrix products, arithmetic and copies ran while one was open for 10% -> 3% of each run, Pallas kernels for 0% -> 3%
where the time goes in v1:
time: 88.4 us; the launch traced here: 87.7 us
  blocking collectives  25.4 us (29%)
  waiting for transfers between devices  25.1 us (28%)
  Pallas kernels  12.6 us (14%)
  starting transfers between devices  12.1 us (14%)
  local copies, waits for them, and re-layouts  9.54 us (11%)
  other arithmetic  2.14 us (2%)
    all_to_all x1, blocking collectives, exchange(): return lax.all_to_all(x, 'wide', split_axis=0, concat_axis=0, tiled=True)  25.4 us
    all_to_all x3, waiting for transfers between devices, exchange(): return lax.all_to_all(x, 'wide', split_axis=0, concat_axis=0, tiled=True)  25.1 us
    all_to_all x3, starting transfers between devices, exchange(): return lax.all_to_all(x, 'wide', split_axis=0, concat_axis=0, tiled=True)  12.1 us
    unnamed x32, local copies, waits for them, and re-layouts  7.1 us
    pallas_call x1, Pallas kernels, per_device(): call(functools.partial(down_kernel, fb), [jax.ShapeDtypeStruct((fa, cols)...  3.03 us
    pallas_call x1, Pallas kernels, per_device(): call(attention_kernel, jax.ShapeDtypeStruct((local_rows, HEADS * HEAD_DIM...  2.86 us
    pallas_call x1, Pallas kernels, per_device(): call(up_kernel, [jax.ShapeDtypeStruct((fb, cols), F32), jax.ShapeDtypeStr...  2.71 us
  transfers between devices with their start and end apart: 3, of which 3 were waited for; matrix products, arithmetic and copies ran while one was open for 3% of the time, Pallas kernels for 3%

profile of v1, /device:TPU:0, one launch (start us, length us, event | category | flops | bytes accessed | tf_op | source)
XLA Modules:
  0.0 87.7 jit_solution(3830641584911229909)
XLA Ops:
  0.6 0.9 %reshape.31 = bf16[4,16,5,64]{3,2,1,0:T(8,128)(2,1)S(1)} reshape(bf16[4,5120]{1,0:T(4,128)(2,1)} %param.19) | data formatting | bytes 81920 | tf_op jit(solution)/shard_map/reshape | solution.py:235
  1.6 0.9 select_reduce_fusion
  2.7 1.3 %copy-done = bf16[320,2048]{1,0:T(8,128)(2,1)S(1)} copy-done((bf16[320,2048]{1,0:T(8,128)(2,1)S(1)}, bf16[320,2048]{1,0:T(8,128)(2,1)}, u32[]{:S(2)}) %copy-start) | copy-done | bytes 1310744
  4.0 1.2 %copy-done.2 = bf16[256,2048]{1,0:T(8,128)(2,1)S(1)} copy-done((bf16[256,2048]{1,0:T(8,128)(2,1)S(1)}, bf16[256,2048]{1,0:T(8,128)(2,1)}, u32[]{:S(2)}) %copy-start.2) | copy-done | bytes 1048600
  5.2 0.7 copy-done.12
  5.9 1.4 %shard_map.139 = bf16[16,32,640]{2,1,0:T(8,128)(2,1)S(1)} custom-call(s32[16]{0:T(128)S(1)} %copy-done.12, bf16[320,2048]{1,0:T(8,128)(2,1)S(1)} %copy-done, bf16[256,2048]{1,0:T(8,128)(2,1)S(1)} %copy-done.2, bf16[16,32,64]{2,1,0:T(8,128)(2,1)S(1)} %pad.4.extra_ref), custom_call_target="tpu_custom_call" | custom-call | flops 75497472 | bytes 2359296 | tf_op jit(solution)/shard_map/pallas_call | solution.py:240
  7.3 25.4 %all_to_all.20.r_ref = bf16[16,32,640]{2,1,0:T(8,128)(2,1)S(1)} all-to-all(bf16[16,32,640]{2,1,0:T(8,128)(2,1)S(1)} %shard_map.139), channel_id=1, replica_groups=mesh['groups'=2,'wide'=16] {'wide'}, dimensions={0} | all-to-all | bytes 1310720 | tf_op jit(solution)/shard_map/all_to_all | solution.py:204
  32.8 1.4 %shard_map.140 = bf16[16,32,640]{2,1,0:T(8,128)(2,1)S(1)} custom-call(bf16[128,5120]{1,0:T(8,128)(2,1)S(1)} %copy-done.6, bf16[128,4096]{1,0:T(8,128)(2,1)S(1)} %copy-done.7, bf16[16,32,640]{2,1,0:T(8,128)(2,1)S(1)} %all_to_all.20.r_ref), custom_call_target="tpu_custom_call" | custom-call | flops 150994944 | bytes 2359296 | tf_op jit(solution)/shard_map/pallas_call | solution.py:249
  34.2 0.8 copy-done.4
  35.0 0.8 copy-done.5
  35.9 3.7 %all-to-all-start.1 = ((bf16[16,32,640]{2,1,0:T(8,128)(2,1)}), bf16[16,32,640]{2,1,0:T(8,128)(2,1)S(1)}, u32[]{:S(2)}, u32[]{:S(2)}) async-start(bf16[16,32,640]{2,1,0:T(8,128)(2,1)} %copy-done.5), calls=%async_computation.1 | async-start | bytes 1310720 | tf_op jit(solution)/shard_map/all_to_all | solution.py:204
  39.6 1.2 %convert_reduce_fusion = s32[16,4]{1,0:T(8,128)S(1)} fusion(bf16[16,32,640]{2,1,0:T(8,128)(2,1)} %copy-done.4), kind=kLoop, calls=%fused_computation.1 | loop fusion | flops 64 | bytes 384 | tf_op jit(solution)/shard_map/convert_element_type | solution.py:270
  40.9 1.0 %slice.11 = bf16[16,20,64]{2,1,0:T(8,128)(2,1)S(1)} slice(bf16[16,32,640]{2,1,0:T(8,128)(2,1)} %copy-done.4), slice={[0:16], [0:20], [576:640]} | slice | bytes 81920 | tf_op jit(solution)/shard_map/slice | solution.py:264
  42.1 14.0 %all-to-all-done.1.part_ref = bf16[16,32,640]{2,1,0:T(8,128)(2,1)S(1)} async-done(((bf16[16,32,640]{2,1,0:T(8,128)(2,1)}), bf16[16,32,640]{2,1,0:T(8,128)(2,1)S(1)}, u32[]{:S(2)}, u32[]{:S(2)}) %all-to-all-start.1) | async-done | bytes 655392 | tf_op jit(solution)/shard_map/all_to_all | solution.py:204
  56.2 3.0 %shard_map.141 = (f32[320,2048]{1,0:T(8,128)}, f32[16,16,128]{2,1,0:T(8,128)}) custom-call(s32[16]{0:T(128)S(1)} %copy-done.13, bf16[16,32,640]{2,1,0:T(8,128)(2,1)S(1)} %all-to-all-done.1.part_ref, bf16[320,2048]{1,0:T(8,128)(2,1)S(1)} %copy-done.1, bf16[64,320]{1,0:T(8,128)(2,1)S(1)} %reshape.34.h_ref, s32[64,128]{1,0:T(8,128)S(1)} %broadcast_in_dim.31.u_ref), custom_call_target="tpu_custom_call" | custom-call | flops 83886080 | bytes 3932160 | tf_op jit(solution)/shard_map/pallas_call | solution.py:272
  59.3 4.9 %all-to-all-start.2 = ((f32[16,16,128]{2,1,0:T(8,128)}), f32[16,16,128]{2,1,0:T(8,128)S(1)}, u32[]{:S(2)}, u32[]{:S(2)}) async-start(f32[16,16,128]{2,1,0:T(8,128)} %get-tuple-element.9), calls=%async_computation.2 | async-start | bytes 262144 | tf_op jit(solution)/shard_map/all_to_all | solution.py:204
  64.1 2.7 %shard_map.142 = (f32[256,2048]{1,0:T(8,128)}, bf16[256,2048]{1,0:T(8,128)(2,1)S(1)}) custom-call(s32[16]{0:T(128)S(1)} %copy-done.13, bf16[16,32,640]{2,1,0:T(8,128)(2,1)S(1)} %all-to-all-done.1.part_ref, bf16[256,2048]{1,0:T(8,128)(2,1)S(1)} %copy-done.3), custom_call_target="tpu_custom_call" | custom-call | flops 33554432 | bytes 4194304 | tf_op jit(solution)/shard_map/pallas_call | solution.py:283
  66.8 1.0 %copy-done.10 = bf16[256,2048]{1,0:T(8,128)(2,1)} copy-done((bf16[256,2048]{1,0:T(8,128)(2,1)}, bf16[256,2048]{1,0:T(8,128)(2,1)S(1)}, u32[]{:S(2)}) %copy-start.10) | copy-done | bytes 1048600
  67.8 4.2 %all-to-all-done.2.p_ref = f32[16,16,128]{2,1,0:T(8,128)S(1)} async-done(((f32[16,16,128]{2,1,0:T(8,128)}), f32[16,16,128]{2,1,0:T(8,128)S(1)}, u32[]{:S(2)}, u32[]{:S(2)}) %all-to-all-start.2) | async-done | bytes 131104 | tf_op jit(solution)/shard_map/all_to_all | solution.py:204
  72.1 1.2 %copy-done.11 = bf16[256,2048]{1,0:T(8,128)(2,1)S(1)} copy-done((bf16[256,2048]{1,0:T(8,128)(2,1)S(1)}, bf16[256,2048]{1,0:T(8,128)(2,1)}, u32[]{:S(2)}) %copy-start.11) | copy-done | bytes 1048600
  73.3 1.2 %shard_map.143 = f32[16,4,256]{2,1,0:T(4,128)} custom-call(f32[16,16,128]{2,1,0:T(8,128)S(1)} %all-to-all-done.2.p_ref, s32[64,128]{1,0:T(8,128)S(1)} %broadcast_in_dim.31.u_ref, bf16[256,2048]{1,0:T(8,128)(2,1)S(1)} %copy-done.11), custom_call_target="tpu_custom_call" | custom-call | flops 67108864 | bytes 1048576 | tf_op jit(solution)/shard_map/pallas_call | solution.py:290
  74.5 3.5 %all-to-all-start.3 = ((f32[16,4,256]{2,1,0:T(4,128)}), f32[16,4,256]{2,1,0:T(4,128)S(1)}, u32[]{:S(2)}, u32[]{:S(2)}) async-start(f32[16,4,256]{2,1,0:T(4,128)} %shard_map.143), calls=%async_computation.3 | async-start | bytes 131072 | tf_op jit(solution)/shard_map/all_to_all | solution.py:204
  78.0 6.8 %all-to-all-done.3.delta_ref = f32[16,4,256]{2,1,0:T(4,128)S(1)} async-done(((f32[16,4,256]{2,1,0:T(4,128)}), f32[16,4,256]{2,1,0:T(4,128)S(1)}, u32[]{:S(2)}, u32[]{:S(2)}) %all-to-all-start.3) | async-done | bytes 65568 | tf_op jit(solution)/shard_map/all_to_all | solution.py:204
  84.8 2.9 %shard_map.144 = bf16[4,4096]{1,0:T(4,128)(2,1)} custom-call(s32[4]{0:T(128)S(1)} %copy-done.14, f32[16,4,256]{2,1,0:T(4,128)S(1)} %all-to-all-done.3.delta_ref, f32[4,4096]{1,0:T(4,128)S(1)} %convert_element_type.26.base_ref, bf16[4,256,512]{2,1,0:T(8,128)(2,1)S(1)} %copy-done.8, bf16[4,256,512]{2,1,0:T(8,128)(2,1)S(1)} %copy-done.9), custom_call_target="tpu_custom_call" | custom-call | flops 16777216 | bytes 2097152 | tf_op jit(solution)/shard_map/pallas_call | solution.py:298
  (37 shorter events, 0.7 us)
Async XLA Ops:
  2.7 1.3 %copy-start = (bf16[320,2048]{1,0:T(8,128)(2,1)S(1)}, bf16[320,2048]{1,0:T(8,128)(2,1)}, u32[]{:S(2)}) copy-start(bf16[320,2048]{1,0:T(8,128)(2,1)} %a_ref.3) | copy-start | bytes 3932164
  4.0 1.2 %copy-start.2 = (bf16[256,2048]{1,0:T(8,128)(2,1)S(1)}, bf16[256,2048]{1,0:T(8,128)(2,1)}, u32[]{:S(2)}) copy-start(bf16[256,2048]{1,0:T(8,128)(2,1)} %b_ref.3) | copy-start | bytes 3145732
  5.2 0.7 copy-start.12
  5.9 26.9 %copy-start.6 = (bf16[128,5120]{1,0:T(8,128)(2,1)S(1)}, bf16[128,5120]{1,0:T(8,128)(2,1)}, u32[]{:S(2)}) copy-start(bf16[128,5120]{1,0:T(8,128)(2,1)} %x_ref.1) | copy-start | bytes 3932164
  5.9 26.9 %copy-start.7 = (bf16[128,4096]{1,0:T(8,128)(2,1)S(1)}, bf16[128,4096]{1,0:T(8,128)(2,1)}, u32[]{:S(2)}) copy-start(bf16[128,4096]{1,0:T(8,128)(2,1)} %g_ref.1) | copy-start | bytes 3145732
  32.7 23.5 %copy-start.1 = (bf16[320,2048]{1,0:T(8,128)(2,1)S(1)}, bf16[320,2048]{1,0:T(8,128)(2,1)}, u32[]{:S(2)}) copy-start(bf16[320,2048]{1,0:T(8,128)(2,1)} %a_ref.3) | copy-start | bytes 3932164
  32.8 23.5 %copy-start.13 = (s32[16]{0:T(128)S(1)}, s32[16]{0:T(128)}, u32[]{:S(2)}) copy-start(s32[16]{0:T(128)} %t_ref.5) | copy-start | bytes 196
  34.2 0.8 copy-start.4
  35.0 0.8 copy-start.5
  35.9 28.3 %copy-start.3 = (bf16[256,2048]{1,0:T(8,128)(2,1)S(1)}, bf16[256,2048]{1,0:T(8,128)(2,1)}, u32[]{:S(2)}) copy-start(bf16[256,2048]{1,0:T(8,128)(2,1)} %b_ref.3) | copy-start | bytes 3145732
  35.9 20.3 %all-to-all-start.1 = ((bf16[16,32,640]{2,1,0:T(8,128)(2,1)}), bf16[16,32,640]{2,1,0:T(8,128)(2,1)S(1)}, u32[]{:S(2)}, u32[]{:S(2)}) async-start(bf16[16,32,640]{2,1,0:T(8,128)(2,1)} %copy-done.5), calls=%async_computation.1 | async-start | bytes 1310720 | tf_op jit(solution)/shard_map/all_to_all | solution.py:204
  59.2 18.7 %copy-start.15 = (bf16[4,4096]{1,0:T(4,128)(2,1)S(1)}, bf16[4,4096]{1,0:T(4,128)(2,1)}, u32[]{:S(2)}) copy-start(bf16[4,4096]{1,0:T(4,128)(2,1)} %param.20) | copy-start | bytes 98308
  59.3 25.6 %copy-start.8 = (bf16[4,256,512]{2,1,0:T(8,128)(2,1)S(1)}, bf16[4,256,512]{2,1,0:T(8,128)(2,1)}, u32[]{:S(2)}) copy-start(bf16[4,256,512]{2,1,0:T(8,128)(2,1)} %k_ref.1) | copy-start | bytes 3145732
  59.3 25.6 %copy-start.14 = (s32[4]{0:T(128)S(1)}, s32[4]{0:T(128)}, u32[]{:S(2)}) copy-start(s32[4]{0:T(128)} %len_ref.1) | copy-start | bytes 52
  59.3 12.8 %all-to-all-start.2 = ((f32[16,16,128]{2,1,0:T(8,128)}), f32[16,16,128]{2,1,0:T(8,128)S(1)}, u32[]{:S(2)}, u32[]{:S(2)}) async-start(f32[16,16,128]{2,1,0:T(8,128)} %get-tuple-element.9), calls=%async_computation.2 | async-start | bytes 262144 | tf_op jit(solution)/shard_map/all_to_all | solution.py:204
  66.8 1.0 %copy-start.10 = (bf16[256,2048]{1,0:T(8,128)(2,1)}, bf16[256,2048]{1,0:T(8,128)(2,1)S(1)}, u32[]{:S(2)}) copy-start(bf16[256,2048]{1,0:T(8,128)(2,1)S(1)} %get-tuple-element.10.new_ref) | copy-start | bytes 3145732
  67.8 17.0 %copy-start.9 = (bf16[4,256,512]{2,1,0:T(8,128)(2,1)S(1)}, bf16[4,256,512]{2,1,0:T(8,128)(2,1)}, u32[]{:S(2)}) copy-start(bf16[4,256,512]{2,1,0:T(8,128)(2,1)} %v_ref.1) | copy-start | bytes 3145732
  72.1 1.2 %copy-start.11 = (bf16[256,2048]{1,0:T(8,128)(2,1)S(1)}, bf16[256,2048]{1,0:T(8,128)(2,1)}, u32[]{:S(2)}) copy-start(bf16[256,2048]{1,0:T(8,128)(2,1)} %copy-done.10) | copy-start | bytes 3145732
  74.5 10.4 %all-to-all-start.3 = ((f32[16,4,256]{2,1,0:T(4,128)}), f32[16,4,256]{2,1,0:T(4,128)S(1)}, u32[]{:S(2)}, u32[]{:S(2)}) async-start(f32[16,4,256]{2,1,0:T(4,128)} %shard_map.143), calls=%async_computation.3 | async-start | bytes 131072 | tf_op jit(solution)/shard_map/all_to_all | solution.py:204

commit v2 on v1

v2 whole, which is shorter than its diff:
```python
import functools

import jax
import jax.numpy as jnp
from jax import lax
from jax.experimental import pallas as pl
from jax.experimental.pallas import tpu as pltpu
from jax.sharding import PartitionSpec as P

HEAD_DIM = 128
HEADS = 32
KV_HEADS = 4
RANK = 32
TENANTS = 64
BLOCK = 128
ROWS_DEV = 4
LANES = 128
PER_TILE = LANES // RANK

adapter_scale = 2.0
learning_rate = 0.0002

F32 = jnp.float32
BF16 = jnp.bfloat16
VMEM_LIMIT = 40 * 1024 * 1024


def vmem():
    return pl.BlockSpec(memory_space=pltpu.VMEM)


def smem():
    return pl.BlockSpec(memory_space=pltpu.SMEM)


def hbm():
    return pl.BlockSpec(memory_space=pltpu.HBM)


def call(kernel, out_shape, in_specs, out_specs, scratch=(), flops=0, nbytes=0):
    return pl.pallas_call(
        kernel,
        out_shape=out_shape,
        in_specs=in_specs,
        out_specs=out_specs,
        scratch_shapes=list(scratch),
        compiler_params=pltpu.CompilerParams(vmem_limit_bytes=VMEM_LIMIT),
        cost_estimate=pl.CostEstimate(flops=flops, bytes_accessed=nbytes, transcendentals=0),
    )


def each(count, body):
    if count <= 16:
        for j in range(count):
            body(j)
    else:
        pl.loop(0, count)(body)


def dot(a, b, ca, cb):
    return lax.dot_general(a, b, (((ca,), (cb,)), ((), ())), preferred_element_type=F32)


def quarter_indicator(quarter, value):
    lane = lax.broadcasted_iota(jnp.int32, (RANK, LANES), 1)
    row = lax.broadcasted_iota(jnp.int32, (RANK, LANES), 0)
    return jnp.where(lane - row == quarter * RANK, value, 0.0).astype(BF16)


def tile_of(tenant):
    return pl.ds(pl.multiple_of((tenant // PER_TILE) * LANES, LANES), LANES)


HALF = RANK // 2


def up_half(h, fa, fb):
    return slice(h * fb, (h + 1) * fb)


def down_half(h, fa, fb):
    return slice(2 * fb + h * fa, 2 * fb + (h + 1) * fa)


def halves(part, cut, fa, fb):
    return jnp.concatenate([part[:, cut(h, fa, fb)] for h in range(2)], axis=0)


def pick_kernel(t_ref, a_ref, b_ref, o_ref, a_buf, b_buf, o_buf, sem_a, sem_b, sem_o):
    n = t_ref.shape[0]
    fa, fb = a_ref.shape[0], b_ref.shape[0]

    def copies(j):
        cols = tile_of(t_ref[j])
        return (
            pltpu.make_async_copy(b_ref.at[:, cols], b_buf.at[j], sem_b.at[j]),
            pltpu.make_async_copy(a_ref.at[:, cols], a_buf.at[j], sem_a.at[j]),
        )

    def start(j):
        for copy in copies(j):
            copy.start()

    def body(j):
        for copy in copies(j):
            copy.wait()
        pick = quarter_indicator(t_ref[j] % PER_TILE, 1.0)
        up = dot(pick, b_buf[j], 1, 1).astype(BF16)
        down = dot(pick, a_buf[j], 1, 1).astype(BF16)
        for h in range(2):
            o_buf[j, :, up_half(h, fa, fb)] = up[h * HALF : (h + 1) * HALF]
            o_buf[j, :, down_half(h, fa, fb)] = down[h * HALF : (h + 1) * HALF]
        pltpu.make_async_copy(o_buf.at[j], o_ref.at[j], sem_o.at[j]).start()

    def finish(j):
        pltpu.make_async_copy(o_buf.at[j], o_ref.at[j], sem_o.at[j]).wait()

    each(n, start)
    each(n, body)
    each(n, finish)


def fold_rows(product, tenant):
    rows = product.shape[0]
    lane = lax.broadcasted_iota(jnp.int32, (rows, LANES), 1)
    total = jnp.zeros((rows, LANES), F32)
    for c in range(TENANTS // PER_TILE):
        mine = tenant == c * PER_TILE + lane // RANK
        total = total + jnp.where(mine, product[:, c * LANES : (c + 1) * LANES], 0.0)
    half = total + pltpu.roll(total, 2 * RANK, 1)
    return half + pltpu.roll(half, RANK, 1)


def rows_kernel(h_ref, x_ref, a_ref, hc_ref, u_ref, hx_ref, base_ref):
    hx_ref[...] = dot(h_ref[:, : x_ref.shape[1]], x_ref[...], 1, 1)
    base_ref[...] = fold_rows(dot(hc_ref[...], a_ref[...], 1, 0), u_ref[...])


def block_kernel(x_ref, g_ref, r_ref, o_ref, back_ref, wa_ref, wb_ref, o_buf, sem):
    n = r_ref.shape[0]
    fa, fb = x_ref.shape[1] // n, g_ref.shape[1] // n
    for d in range(n):
        for h in range(2):
            rank = slice(h * HALF, (h + 1) * HALF)
            wb_ref[rank, d * fb : (d + 1) * fb] = r_ref[d, :, up_half(h, fa, fb)]
            wa_ref[rank, d * fa : (d + 1) * fa] = r_ref[d, :, down_half(h, fa, fb)]
    down = dot(wa_ref[...], x_ref[...], 1, 1).astype(BF16)
    back = dot(wb_ref[...], g_ref[...], 1, 1).astype(BF16)
    back_ref[...] = back
    up_part = dot(down, g_ref[...], 1, 0).astype(BF16)
    down_part = dot(back, x_ref[...], 1, 0).astype(BF16)
    copies = []
    for d in range(n):
        for h in range(2):
            rank = slice(h * HALF, (h + 1) * HALF)
            o_buf[d, :, up_half(h, fa, fb)] = up_part[rank, d * fb : (d + 1) * fb]
            o_buf[d, :, down_half(h, fa, fb)] = down_part[rank, d * fa : (d + 1) * fa]
        copy = pltpu.make_async_copy(o_buf.at[d], o_ref.at[d], sem.at[d])
        copy.start()
        copies.append(copy)
    for copy in copies:
        copy.wait()


def share_kernel(t_ref, hx_ref, back_ref, base_ref, u_ref, o_ref):
    hx = hx_ref[...]
    high = hx.astype(BF16)
    low = (hx - high.astype(F32)).astype(BF16)
    back = jnp.concatenate([back_ref[...]] * PER_TILE, axis=0)
    change = dot(high, back, 1, 1) + dot(low, back, 1, 1)
    mine = u_ref[...] == t_ref[0]
    full = base_ref[...] - jnp.where(mine, learning_rate * (adapter_scale * change), 0.0)
    quarter = full.shape[0] // PER_TILE
    spot = lax.broadcasted_iota(jnp.int32, (quarter, LANES), 1) // RANK
    packed = jnp.zeros((quarter, LANES), F32)
    for q in range(PER_TILE):
        packed = packed + jnp.where(spot == q, full[q * quarter : (q + 1) * quarter], 0.0)
    o_ref[...] = packed


def sum_by_tenant(t_ref, part_ref, cut, fa, fb, grad_ref):
    grad_ref[...] = jnp.zeros_like(grad_ref)

    def body(j):
        t = t_ref[j]
        place = quarter_indicator(t % PER_TILE, adapter_scale)
        grad_ref[:, tile_of(t)] += dot(halves(part_ref.at[j], cut, fa, fb), place, 0, 0)

    each(t_ref.shape[0], body)


def delta_kernel(fa, t_ref, part_ref, b_ref, p_ref, u_ref, o_ref, grad_ref):
    n, fb = part_ref.shape[0], b_ref.shape[0]
    sum_by_tenant(t_ref, part_ref, up_half, fa, fb, grad_ref)
    new_b = (b_ref[...].astype(F32) - learning_rate * grad_ref[...]).astype(BF16)
    total = p_ref[...]
    spot = lax.broadcasted_iota(jnp.int32, total.shape, 1) // RANK
    pieces = []
    for q in range(PER_TILE):
        one = jnp.where(spot == q, total, 0.0)
        half = one + pltpu.roll(one, 2 * RANK, 1)
        pieces.append(half + pltpu.roll(half, RANK, 1))
    adapted = jnp.concatenate(pieces, axis=0)
    lane = lax.broadcasted_iota(jnp.int32, adapted.shape, 1)
    tenant = u_ref[...]
    spread = jnp.concatenate(
        [
            jnp.where(tenant == c * PER_TILE + lane // RANK, adapted, 0.0).astype(BF16)
            for c in range(TENANTS // PER_TILE)
        ],
        axis=1,
    )
    delta = adapter_scale * dot(spread, new_b, 1, 1)
    for d in range(n):
        o_ref[d] = delta[d * ROWS_DEV : (d + 1) * ROWS_DEV]


def gradient_kernel(t_ref, part_ref, down_ref, up_ref):
    fa, fb = down_ref.shape[0], up_ref.shape[0]
    sum_by_tenant(t_ref, part_ref, down_half, fa, fb, down_ref)
    sum_by_tenant(t_ref, part_ref, up_half, fa, fb, up_ref)


def attention_kernel(len_ref, delta_ref, base_ref, k_ref, v_ref, o_ref):
    n = delta_ref.shape[0]
    delta = jnp.concatenate([delta_ref[d] for d in range(n)], axis=1)
    query = (base_ref[...] + delta).astype(BF16).astype(F32)
    group = HEADS // KV_HEADS
    cache = k_ref.shape[1]
    many = group * ROWS_DEV
    row_p = lax.broadcasted_iota(jnp.int32, (many, cache), 0) % ROWS_DEV
    row_d = lax.broadcasted_iota(jnp.int32, (many, HEAD_DIM), 0) % ROWS_DEV
    position = lax.broadcasted_iota(jnp.int32, (many, cache), 1)
    length = jnp.zeros((many, cache), jnp.int32)
    for r in range(ROWS_DEV):
        length = jnp.where(row_p == r, len_ref[r], length)
    live = position < length
    outs = []
    for g in range(KV_HEADS):
        cols = slice(g * HEAD_DIM, (g + 1) * HEAD_DIM)
        heads = jnp.concatenate(
            [query[:, (g * group + i) * HEAD_DIM : (g * group + i + 1) * HEAD_DIM] for i in range(group)],
            axis=0,
        ).astype(BF16)
        scores = jnp.zeros((many, cache), F32)
        for r in range(ROWS_DEV):
            scores = jnp.where(row_p == r, dot(heads, k_ref[r, :, cols], 1, 1), scores)
        scores = scores / jnp.sqrt(F32(HEAD_DIM))
        scores = jnp.where(live, scores, F32(-1e30))
        top = jnp.max(scores, axis=-1, keepdims=True)
        expo = jnp.where(live, jnp.exp(scores - top), 0.0)
        weights = (expo / jnp.sum(expo, axis=-1, keepdims=True)).astype(BF16)
        mixed = jnp.zeros((many, HEAD_DIM), F32)
        for r in range(ROWS_DEV):
            mixed = jnp.where(row_d == r, dot(weights, v_ref[r, :, cols], 1, 0), mixed)
        outs.extend(mixed[i * ROWS_DEV : (i + 1) * ROWS_DEV] for i in range(group))
    o_ref[...] = jnp.concatenate(outs, axis=1).astype(BF16)


def exchange(x):
    return lax.all_to_all(x, "wide", split_axis=0, concat_axis=0, tiled=True)


def partner(x, bit):
    n = lax.axis_size("wide")
    return lax.ppermute(x, "wide", [(i, i ^ bit) for i in range(n)])


def gather_rows(x):
    n = lax.axis_size("wide")
    me = lax.axis_index("wide")
    held = x[None]
    bit = n // 2
    while bit:
        other = partner(held, bit)
        second = (me & bit) != 0
        pair = [jnp.where(second, other, held), jnp.where(second, held, other)]
        held = jnp.stack(pair, axis=1).reshape((2 * held.shape[0],) + x.shape)
        bit //= 2
    return held.reshape((n * x.shape[0],) + x.shape[1:])


def sum_all(x):
    bit = lax.axis_size("wide") // 2
    while bit:
        x = x + partner(x, bit)
        bit //= 2
    return x


def per_device(
    tokens,
    query_output_gradient,
    down_factors,
    up_factors_transposed,
    tenant_of_block,
    device_tenant_list,
    row_list_entry,
    hidden,
    base_query_rows,
    cached_key_rows,
    cached_value_rows,
    live_cache_length,
):
    n = lax.axis_size("wide")
    me = lax.axis_index("wide")
    fa, cols = down_factors.shape
    fb = up_factors_transposed.shape[0]
    local_rows = hidden.shape[0]
    rows = local_rows * n
    width = tokens.shape[1]
    assert tokens.shape[0] == BLOCK and tenant_of_block.shape[0] == n and n & (n - 1) == 0
    block_shape = (n, HALF, 2 * (fa + fb))

    packed = call(
        pick_kernel,
        jax.ShapeDtypeStruct(block_shape, BF16),
        [smem(), hbm(), hbm()],
        hbm(),
        scratch=[
            pltpu.VMEM((n, fa, LANES), BF16),
            pltpu.VMEM((n, fb, LANES), BF16),
            pltpu.VMEM(block_shape, BF16),
            pltpu.SemaphoreType.DMA((n,)),
            pltpu.SemaphoreType.DMA((n,)),
            pltpu.SemaphoreType.DMA((n,)),
        ],
        flops=2 * RANK * LANES * n * (fa + fb),
        nbytes=2 * cols * (fa + fb),
    )(tenant_of_block, down_factors, up_factors_transposed)
    got = exchange(packed)

    slot = row_list_entry[:, None] == jnp.arange(device_tenant_list.shape[1], dtype=jnp.int32)[None, :]
    row_tenant = jnp.sum(jnp.where(slot, device_tenant_list, 0), axis=1)
    marks = jnp.broadcast_to(row_tenant.astype(BF16)[:, None], (local_rows, LANES))
    everyone = gather_rows(jnp.concatenate([hidden, marks], axis=1))
    tenants = everyone[:, width:].astype(jnp.int32)
    h_cols = lax.dynamic_slice(everyone, (0, me * fa), (rows, fa))
    hx, base_low_rank = call(
        rows_kernel,
        [jax.ShapeDtypeStruct((rows, BLOCK), F32), jax.ShapeDtypeStruct((rows, LANES), F32)],
        [vmem()] * 5,
        [vmem()] * 2,
        flops=2 * rows * BLOCK * width + 2 * rows * fa * cols,
        nbytes=2 * BLOCK * width + 2 * fa * cols,
    )(everyone, tokens, down_factors, h_cols, tenants)

    parts, back = call(
        block_kernel,
        [jax.ShapeDtypeStruct(block_shape, BF16), jax.ShapeDtypeStruct((RANK, BLOCK), BF16)],
        [vmem(), vmem(), vmem()],
        [hbm(), vmem()],
        scratch=[
            pltpu.VMEM((RANK, width), BF16),
            pltpu.VMEM((RANK, query_output_gradient.shape[1]), BF16),
            pltpu.VMEM(block_shape, BF16),
            pltpu.SemaphoreType.DMA((n,)),
        ],
        flops=4 * RANK * BLOCK * n * (fa + fb),
        nbytes=2 * BLOCK * n * (fa + fb),
    )(tokens, query_output_gradient, got)
    shares = exchange(parts)

    my_tenant = lax.dynamic_slice(tenant_of_block, (me,), (1,))
    low_rank = call(
        share_kernel,
        jax.ShapeDtypeStruct((rows // PER_TILE, LANES), F32),
        [smem(), vmem(), vmem(), vmem(), vmem()],
        vmem(),
        flops=4 * rows * BLOCK * LANES,
        nbytes=12 * rows * LANES,
    )(my_tenant, hx, back, base_low_rank, tenants)
    low_rank = sum_all(low_rank)

    delta = call(
        functools.partial(delta_kernel, fa),
        jax.ShapeDtypeStruct((n, local_rows, fb), F32),
        [smem(), vmem(), vmem(), vmem(), vmem()],
        vmem(),
        scratch=[pltpu.VMEM((fb, cols), F32)],
        flops=2 * rows * cols * fb,
        nbytes=2 * cols * fb,
    )(tenant_of_block, shares, up_factors_transposed, low_rank, tenants)
    delta = exchange(delta)

    down_gradient, up_gradient = call(
        gradient_kernel,
        [jax.ShapeDtypeStruct((fa, cols), F32), jax.ShapeDtypeStruct((fb, cols), F32)],
        [smem(), vmem()],
        [vmem(), vmem()],
        flops=2 * n * RANK * (fa + fb) * LANES,
        nbytes=4 * cols * (fa + fb),
    )(tenant_of_block, shares)
    attended = call(
        attention_kernel,
        jax.ShapeDtypeStruct((local_rows, HEADS * HEAD_DIM), BF16),
        [smem(), vmem(), vmem(), vmem(), vmem()],
        vmem(),
        flops=4 * HEADS * local_rows * cached_key_rows.shape[1] * HEAD_DIM,
        nbytes=4 * cached_key_rows.size,
    )(live_cache_length, delta, base_query_rows.astype(F32), cached_key_rows, cached_value_rows)
    return down_gradient, up_gradient, attended


def solution(mesh):
    placed = (
        P(("groups", "wide"), None),
        P(("groups", "wide"), None),
        P("wide", "groups"),
        P("wide", "groups"),
        P("groups"),
        P(("groups", "wide"), None),
        P(("groups", "wide")),
        P(("groups", "wide"), None),
        P(("groups", "wide"), None),
        P(("groups", "wide"), None, None),
        P(("groups", "wide"), None, None),
        P(("groups", "wide")),
    )
    return jax.shard_map(
        per_device,
        mesh=mesh,
        in_specs=placed,
        out_specs=(P("wide", "groups"), P("wide", "groups"), P(("groups", "wide"), None)),
        check_vma=False,
    )
```

time: 88.4 us -> 101 us (1.14)
  blocking collectives: 25.4 us -> 0 us
  starting transfers between devices: 12.1 us -> 25.4 us
  waiting for transfers between devices: 25.1 us -> 32.9 us
  Pallas kernels: 12.6 us -> 20 us
  local copies, waits for them, and re-layouts: 9.54 us -> 15.3 us
  other arithmetic: 2.14 us -> 5.87 us
    all_to_all x1 -> x0, blocking collectives: 25.4 us -> none  [exchange(): return lax.all_to_all(x, 'wide', split_axis=0, concat_axis=0, tiled=True)]
    ppermute x0 -> x8, waiting for transfers between devices: none -> 16.9 us  [partner(): return lax.ppermute(x, 'wide', [(i, i ^ bit) for i in range(n)])]
    ppermute x0 -> x8, starting transfers between devices: none -> 12.2 us  [partner(): return lax.ppermute(x, 'wide', [(i, i ^ bit) for i in range(n)])]
    all_to_all x3, waiting for transfers between devices: 25.1 us -> 16 us  [exchange(): return lax.all_to_all(x, 'wide', split_axis=0, concat_axis=0, tiled=True)]
    pallas_call x5 -> x6, Pallas kernels: 9.76 us -> 17.1 us  [the longest x1 5.98 us: per_device(): call(pick_kernel, jax.ShapeDtypeStruct(block_shape, BF16), [smem(), hbm()...]
    another operation x0 -> x4, local copies, waits for them, and re-layouts: none -> 4.23 us  [the longest x1 2.25 us: gather_rows(): return held.reshape((n * x.shape[0],) + x.shape[1:])]
    another operation x0 -> x7, other arithmetic: none -> 3.27 us  [gather_rows(): held = jnp.stack(pair, axis=1).reshape((2 * held.shape[0],) + x.shape)]
    unnamed x32 -> x28, local copies, waits for them, and re-layouts: 7.1 us -> 9.52 us
  transfers between devices with their start and end apart: 3 -> 11, of which waited for: 3 -> 8; matrix products, arithmetic and copies ran while one was open for 3% -> 9% of each run, Pallas kernels for 3% -> 15%
where the time goes in v2:
time: 101 us; the launch traced here: 100 us
  waiting for transfers between devices  32.9 us (33%)
  starting transfers between devices  25.4 us (25%)
  Pallas kernels  20 us (20%)
  local copies, waits for them, and re-layouts  15.3 us (15%)
  other arithmetic  5.87 us (6%)
    ppermute x8, waiting for transfers between devices, partner(): return lax.ppermute(x, 'wide', [(i, i ^ bit) for i in range(n)])  16.9 us
    all_to_all x3, waiting for transfers between devices, exchange(): return lax.all_to_all(x, 'wide', split_axis=0, concat_axis=0, tiled=True)  16 us
    all_to_all x3, starting transfers between devices, exchange(): return lax.all_to_all(x, 'wide', split_axis=0, concat_axis=0, tiled=True)  13.2 us
    ppermute x8, starting transfers between devices, partner(): return lax.ppermute(x, 'wide', [(i, i ^ bit) for i in range(n)])  12.2 us
    unnamed x28, local copies, waits for them, and re-layouts  9.52 us
    pallas_call x1, Pallas kernels, per_device(): call(pick_kernel, jax.ShapeDtypeStruct(block_shape, BF16), [smem(), hbm()...  5.98 us
    pallas_call x1, Pallas kernels, per_device(): call(gradient_kernel, [jax.ShapeDtypeStruct((fa, cols), F32), jax.ShapeDt...  4.2 us
    another operation x7, other arithmetic, gather_rows(): held = jnp.stack(pair, axis=1).reshape((2 * held.shape[0],) + x.shape)  3.27 us
  transfers between devices with their start and end apart: 11, of which 8 were waited for; matrix products, arithmetic and copies ran while one was open for 9% of the time, Pallas kernels for 15%

profile of v2, /device:TPU:0, one launch (start us, length us, event | category | flops | bytes accessed | tf_op | source)
XLA Modules:
  0.0 100.3 jit_solution(4324076306748712474)
XLA Ops:
  2.5 4.1 %collective-permute-start = (bf16[1,4,5248]{2,1,0:T(4,128)(2,1)S(1)}, bf16[1,4,5248]{2,1,0:T(4,128)(2,1)S(1)}, u32[]{:S(2)}, u32[]{:S(2)}) collective-permute-start(bf16[1,4,5248]{2,1,0:T(4,128)(2,1)S(1)} %maximum_bitcast_fusion.1), channel_id=1, source_target_pairs={{0,8},{1,9},{2,10},{3,11},{4,12},{5,13},{6,14},{7,15},{8,0},{9,1},... | collective-permute-start | bytes 125960 | tf_op jit(solution)/shard_map/ppermute | solution.py:266
  6.6 2.4 %collective-permute-done = bf16[1,4,5248]{2,1,0:T(4,128)(2,1)S(1)} collective-permute-done((bf16[1,4,5248]{2,1,0:T(4,128)(2,1)S(1)}, bf16[1,4,5248]{2,1,0:T(4,128)(2,1)S(1)}, u32[]{:S(2)}, u32[]{:S(2)}) %collective-permute-start) | collective-permute-done | bytes 42016 | tf_op jit(solution)/shard_map/ppermute | solution.py:266
  9.9 1.5 %collective-permute-start.1 = (bf16[2,4,5248]{2,1,0:T(4,128)(2,1)S(1)}, bf16[2,4,5248]{2,1,0:T(4,128)(2,1)S(1)}, u32[]{:S(2)}, u32[]{:S(2)}) collective-permute-start(bf16[2,4,5248]{2,1,0:T(4,128)(2,1)S(1)} %maximum_bitcast_fusion), channel_id=1, source_target_pairs={{0,4},{1,5},{2,6},{3,7},{4,0},{5,1},{6,2},{7,3},{8,12},{9,13},{10,... | collective-permute-start | bytes 251912 | tf_op jit(solution)/shard_map/ppermute | solution.py:266
  11.4 3.0 %collective-permute-done.1 = bf16[2,4,5248]{2,1,0:T(4,128)(2,1)S(1)} collective-permute-done((bf16[2,4,5248]{2,1,0:T(4,128)(2,1)S(1)}, bf16[2,4,5248]{2,1,0:T(4,128)(2,1)S(1)}, u32[]{:S(2)}, u32[]{:S(2)}) %collective-permute-start.1) | collective-permute-done | bytes 84000 | tf_op jit(solution)/shard_map/ppermute | solution.py:266
  14.7 1.8 %collective-permute-start.2 = (bf16[4,4,5248]{2,1,0:T(4,128)(2,1)S(1)}, bf16[4,4,5248]{2,1,0:T(4,128)(2,1)S(1)}, u32[]{:S(2)}, u32[]{:S(2)}) collective-permute-start(bf16[4,4,5248]{2,1,0:T(4,128)(2,1)S(1)} %bitcast.35), channel_id=1, source_target_pairs={{0,2},{1,3},{2,0},{3,1},{4,6},{5,7},{6,4},{7,5},{8,10},{9,11},{10,... | collective-permute-start | bytes 503816 | tf_op jit(solution)/shard_map/ppermute | solution.py:266
  18.4 6.0 %shard_map.139 = bf16[16,16,1152]{2,1,0:T(8,128)(2,1)S(1)} custom-call(s32[16]{0:T(128)S(1)} %copy-done.10, bf16[320,2048]{1,0:T(8,128)(2,1)S(1)} %copy-done.1, bf16[256,2048]{1,0:T(8,128)(2,1)S(1)} %copy-done.2), custom_call_target="tpu_custom_call" | custom-call | flops 75497472 | bytes 2359296 | tf_op jit(solution)/shard_map/pallas_call | solution.py:315
  25.2 5.1 %all-to-all-start = ((bf16[16,16,1152]{2,1,0:T(8,128)(2,1)}), bf16[16,16,1152]{2,1,0:T(8,128)(2,1)S(1)}, u32[]{:S(2)}, u32[]{:S(2)}) async-start(bf16[16,16,1152]{2,1,0:T(8,128)(2,1)} %copy-done.5), calls=%async_computation | async-start | bytes 1179648 | tf_op jit(solution)/shard_map/all_to_all | solution.py:261
  32.6 13.3 %all-to-all-done.r_ref = bf16[16,16,1152]{2,1,0:T(8,128)(2,1)S(1)} async-done(((bf16[16,16,1152]{2,1,0:T(8,128)(2,1)}), bf16[16,16,1152]{2,1,0:T(8,128)(2,1)S(1)}, u32[]{:S(2)}, u32[]{:S(2)}) %all-to-all-start) | async-done | bytes 589856 | tf_op jit(solution)/shard_map/all_to_all | solution.py:261
  45.9 1.2 %copy-done.6 = bf16[128,4096]{1,0:T(8,128)(2,1)S(1)} copy-done((bf16[128,4096]{1,0:T(8,128)(2,1)S(1)}, bf16[128,4096]{1,0:T(8,128)(2,1)}, u32[]{:S(2)}) %copy-start.6) | copy-done | bytes 1048600
  47.1 2.9 %shard_map.140 = (bf16[16,16,1152]{2,1,0:T(8,128)(2,1)S(1)}, bf16[32,128]{1,0:T(8,128)(2,1)S(1)}) custom-call(bf16[128,5120]{1,0:T(8,128)(2,1)S(1)} %copy-done, bf16[128,4096]{1,0:T(8,128)(2,1)S(1)} %copy-done.6, bf16[16,16,1152]{2,1,0:T(8,128)(2,1)S(1)} %all-to-all-done.r_ref), custom_call_target="tpu_custom_call" | custom-call | flops 150994944 | bytes 2359296 | tf_op jit(solution)/shard_map/pallas_call | solution.py:348
  50.8 4.4 %all-to-all-start.1 = ((bf16[16,16,1152]{2,1,0:T(8,128)(2,1)}), bf16[16,16,1152]{2,1,0:T(8,128)(2,1)S(1)}, u32[]{:S(2)}, u32[]{:S(2)}) async-start(bf16[16,16,1152]{2,1,0:T(8,128)(2,1)} %copy-done.9), calls=%async_computation.1 | async-start | bytes 1179648 | tf_op jit(solution)/shard_map/all_to_all | solution.py:261
  55.3 1.4 %select_bitcast_fusion.1 = (bf16[8,1,4,5248]{3,2,0,1:T(4,128)(2,1)S(1)}, bf16[8,1,4,5248]{3,2,0,1:T(4,128)(2,1)S(1)}) fusion(bf16[8,4,5248]{2,1,0:T(4,128)(2,1)} %collective-permute-done.3, pred[]{:T(512)S(6)} %ne.12, bf16[4,2,4,5248]{3,2,1,0:T(4,128)(2,1)} %copy.23), kind=kLoop, calls=%fused_computation.3 | loop fusion | flops 335872 | bytes 1343489 | tf_op jit(solution)/shard_map/stack | solution.py:278
  58.2 2.3 %reshape_reshape.3.h_ref = bf16[64,5248]{1,0:T(8,128)(2,1)} reshape(bf16[8,2,4,5248]{3,2,1,0:T(4,128)(2,1)} %copy.24) | data formatting | bytes 1343488 | tf_op jit(solution)/shard_map/reshape;reshape | solution.py:280
  65.0 2.9 %collective-permute-start.4 = (f32[16,128]{1,0:T(8,128)S(1)}, f32[16,128]{1,0:T(8,128)S(1)}, u32[]{:S(2)}, u32[]{:S(2)}) collective-permute-start(f32[16,128]{1,0:T(8,128)S(1)} %shard_map.143), channel_id=1, source_target_pairs={{0,8},{1,9},{2,10},{3,11},{4,12},{5,13},{6,14},{7,15},{8,0},{9,1},... | collective-permute-start | bytes 24584 | tf_op jit(solution)/shard_map/ppermute | solution.py:266
  67.9 4.5 %collective-permute-done.4 = f32[16,128]{1,0:T(8,128)S(1)} collective-permute-done((f32[16,128]{1,0:T(8,128)S(1)}, f32[16,128]{1,0:T(8,128)S(1)}, u32[]{:S(2)}, u32[]{:S(2)}) %collective-permute-start.4) | collective-permute-done | bytes 8224 | tf_op jit(solution)/shard_map/ppermute | solution.py:266
  72.3 3.6 %collective-permute-done.5 = f32[16,128]{1,0:T(8,128)S(1)} collective-permute-done((f32[16,128]{1,0:T(8,128)S(1)}, f32[16,128]{1,0:T(8,128)S(1)}, u32[]{:S(2)}, u32[]{:S(2)}) %collective-permute-start.5) | collective-permute-done | bytes 8224 | tf_op jit(solution)/shard_map/ppermute | solution.py:266
  76.0 1.5 %collective-permute-start.6 = (f32[16,128]{1,0:T(8,128)S(1)}, f32[16,128]{1,0:T(8,128)S(1)}, u32[]{:S(2)}, u32[]{:S(2)}) collective-permute-start(f32[16,128]{1,0:T(8,128)S(1)} %add.21), channel_id=1, source_target_pairs={{0,2},{1,3},{2,0},{3,1},{4,6},{5,7},{6,4},{7,5},{8,10},{9,11},{10,... | collective-permute-start | bytes 24584 | tf_op jit(solution)/shard_map/ppermute | solution.py:266
  77.4 2.2 %collective-permute-done.6 = f32[16,128]{1,0:T(8,128)S(1)} collective-permute-done((f32[16,128]{1,0:T(8,128)S(1)}, f32[16,128]{1,0:T(8,128)S(1)}, u32[]{:S(2)}, u32[]{:S(2)}) %collective-permute-start.6) | collective-permute-done | bytes 8224 | tf_op jit(solution)/shard_map/ppermute | solution.py:266
  82.0 2.4 %shard_map.144 = f32[16,4,256]{2,1,0:T(4,128)} custom-call(s32[16]{0:T(128)S(1)} %copy-done.11, bf16[16,16,1152]{2,1,0:T(8,128)(2,1)S(1)} %all-to-all-done.1.part_ref, bf16[256,2048]{1,0:T(8,128)(2,1)S(1)} %copy-done.3, f32[16,128]{1,0:T(8,128)S(1)} %add.23.p_ref, s32[64,128]{1,0:T(8,128)S(1)} %slice_convert_fusion.u_ref), custom_call_target="tpu_custom_call" | custom-call | flops 67108864 | bytes 1048576 | tf_op jit(solution)/shard_map/pallas_call | solution.py:375
  84.4 3.7 %all-to-all-start.2 = ((f32[16,4,256]{2,1,0:T(4,128)}), f32[16,4,256]{2,1,0:T(4,128)S(1)}, u32[]{:S(2)}, u32[]{:S(2)}) async-start(f32[16,4,256]{2,1,0:T(4,128)} %shard_map.144), calls=%async_computation.2 | async-start | bytes 131072 | tf_op jit(solution)/shard_map/all_to_all | solution.py:261
  88.1 4.2 %shard_map.141 = (f32[320,2048]{1,0:T(8,128)}, f32[256,2048]{1,0:T(8,128)}) custom-call(s32[16]{0:T(128)S(1)} %copy-done.11, bf16[16,16,1152]{2,1,0:T(8,128)(2,1)S(1)} %all-to-all-done.1.part_ref), custom_call_target="tpu_custom_call" | custom-call | flops 75497472 | bytes 4718592 | tf_op jit(solution)/shard_map/pallas_call | solution.py:386
  92.3 2.7 %all-to-all-done.2.delta_ref = f32[16,4,256]{2,1,0:T(4,128)S(1)} async-done(((f32[16,4,256]{2,1,0:T(4,128)}), f32[16,4,256]{2,1,0:T(4,128)S(1)}, u32[]{:S(2)}, u32[]{:S(2)}) %all-to-all-start.2) | async-done | bytes 65568 | tf_op jit(solution)/shard_map/all_to_all | solution.py:261
  95.0 1.2 %copy-done.7 = bf16[4,256,512]{2,1,0:T(8,128)(2,1)S(1)} copy-done((bf16[4,256,512]{2,1,0:T(8,128)(2,1)S(1)}, bf16[4,256,512]{2,1,0:T(8,128)(2,1)}, u32[]{:S(2)}) %copy-start.7) | copy-done | bytes 1048600
  97.5 2.9 %shard_map.145 = bf16[4,4096]{1,0:T(4,128)(2,1)} custom-call(s32[4]{0:T(128)S(1)} %copy-done.12, f32[16,4,256]{2,1,0:T(4,128)S(1)} %all-to-all-done.2.delta_ref, f32[4,4096]{1,0:T(4,128)S(1)} %convert_element_type.15.base_ref, bf16[4,256,512]{2,1,0:T(8,128)(2,1)S(1)} %copy-done.7, bf16[4,256,512]{2,1,0:T(8,128)(2,1)S(1)} %copy-done.8), custom_call_target="tpu_custom_call" | custom-call | flops 16777216 | bytes 2097152 | tf_op jit(solution)/shard_map/pallas_call | solution.py:394
  (57 shorter events, 18.4 us)
Async XLA Ops:
  0.6 15.9 %copy-start.1 = (bf16[320,2048]{1,0:T(8,128)(2,1)S(1)}, bf16[320,2048]{1,0:T(8,128)(2,1)}, u32[]{:S(2)}) copy-start(bf16[320,2048]{1,0:T(8,128)(2,1)} %a_ref.3) | copy-start | bytes 3932164
  2.5 6.5 %collective-permute-start = (bf16[1,4,5248]{2,1,0:T(4,128)(2,1)S(1)}, bf16[1,4,5248]{2,1,0:T(4,128)(2,1)S(1)}, u32[]{:S(2)}, u32[]{:S(2)}) collective-permute-start(bf16[1,4,5248]{2,1,0:T(4,128)(2,1)S(1)} %maximum_bitcast_fusion.1), channel_id=1, source_target_pairs={{0,8},{1,9},{2,10},{3,11},{4,12},{5,13},{6,14},{7,15},{8,0},{9,1},... | collective-permute-start | bytes 125960 | tf_op jit(solution)/shard_map/ppermute | solution.py:266
  9.9 4.5 %collective-permute-start.1 = (bf16[2,4,5248]{2,1,0:T(4,128)(2,1)S(1)}, bf16[2,4,5248]{2,1,0:T(4,128)(2,1)S(1)}, u32[]{:S(2)}, u32[]{:S(2)}) collective-permute-start(bf16[2,4,5248]{2,1,0:T(4,128)(2,1)S(1)} %maximum_bitcast_fusion), channel_id=1, source_target_pairs={{0,4},{1,5},{2,6},{3,7},{4,0},{5,1},{6,2},{7,3},{8,12},{9,13},{10,... | collective-permute-start | bytes 251912 | tf_op jit(solution)/shard_map/ppermute | solution.py:266
  14.7 15.6 %collective-permute-start.2 = (bf16[4,4,5248]{2,1,0:T(4,128)(2,1)S(1)}, bf16[4,4,5248]{2,1,0:T(4,128)(2,1)S(1)}, u32[]{:S(2)}, u32[]{:S(2)}) collective-permute-start(bf16[4,4,5248]{2,1,0:T(4,128)(2,1)S(1)} %bitcast.35), channel_id=1, source_target_pairs={{0,2},{1,3},{2,0},{3,1},{4,6},{5,7},{6,4},{7,5},{8,10},{9,11},{10,... | collective-permute-start | bytes 503816 | tf_op jit(solution)/shard_map/ppermute | solution.py:266
  16.5 1.2 %copy-start.2 = (bf16[256,2048]{1,0:T(8,128)(2,1)S(1)}, bf16[256,2048]{1,0:T(8,128)(2,1)}, u32[]{:S(2)}) copy-start(bf16[256,2048]{1,0:T(8,128)(2,1)} %b_ref.3) | copy-start | bytes 3145732
  24.4 0.8 copy-start.5
  25.2 6.8 %copy-start.11 = (s32[16]{0:T(128)S(1)}, s32[16]{0:T(128)}, u32[]{:S(2)}) copy-start(s32[16]{0:T(128)} %t_ref.5) | copy-start | bytes 196
  25.2 20.7 %copy-start = (bf16[128,5120]{1,0:T(8,128)(2,1)S(1)}, bf16[128,5120]{1,0:T(8,128)(2,1)}, u32[]{:S(2)}) copy-start(bf16[128,5120]{1,0:T(8,128)(2,1)} %x_ref.3) | copy-start | bytes 3932164
  25.2 20.7 %all-to-all-start = ((bf16[16,16,1152]{2,1,0:T(8,128)(2,1)}), bf16[16,16,1152]{2,1,0:T(8,128)(2,1)S(1)}, u32[]{:S(2)}, u32[]{:S(2)}) async-start(bf16[16,16,1152]{2,1,0:T(8,128)(2,1)} %copy-done.5), calls=%async_computation | async-start | bytes 1179648 | tf_op jit(solution)/shard_map/all_to_all | solution.py:261
  31.6 23.6 %collective-permute-start.3 = (bf16[8,4,5248]{2,1,0:T(4,128)(2,1)}, bf16[8,4,5248]{2,1,0:T(4,128)(2,1)}, u32[]{:S(2)}, u32[]{:S(2)}) collective-permute-start(bf16[8,4,5248]{2,1,0:T(4,128)(2,1)} %bitcast.10), channel_id=1, source_target_pairs={{0,1},{1,0},{2,3},{3,2},{4,5},{5,4},{6,7},{7,6},{8,9},{9,8},{10,11... | collective-permute-start | bytes 1007624 | tf_op jit(solution)/shard_map/ppermute | solution.py:266
  45.9 1.2 %copy-start.6 = (bf16[128,4096]{1,0:T(8,128)(2,1)S(1)}, bf16[128,4096]{1,0:T(8,128)(2,1)}, u32[]{:S(2)}) copy-start(bf16[128,4096]{1,0:T(8,128)(2,1)} %g_ref.1) | copy-start | bytes 3145732
  50.0 0.8 copy-start.9
  50.8 30.0 %all-to-all-start.1 = ((bf16[16,16,1152]{2,1,0:T(8,128)(2,1)}), bf16[16,16,1152]{2,1,0:T(8,128)(2,1)S(1)}, u32[]{:S(2)}, u32[]{:S(2)}) async-start(bf16[16,16,1152]{2,1,0:T(8,128)(2,1)} %copy-done.9), calls=%async_computation.1 | async-start | bytes 1179648 | tf_op jit(solution)/shard_map/all_to_all | solution.py:261
  62.1 1.1 %copy-start.4 = (bf16[64,5248]{1,0:T(8,128)(2,1)S(1)}, bf16[64,5248]{1,0:T(8,128)(2,1)}, u32[]{:S(2)}) copy-start(bf16[64,5248]{1,0:T(8,128)(2,1)} %reshape_reshape.3.h_ref) | copy-start | bytes 2015236
  63.2 24.9 %copy-start.13 = (bf16[4,4096]{1,0:T(4,128)(2,1)S(1)}, bf16[4,4096]{1,0:T(4,128)(2,1)}, u32[]{:S(2)}) copy-start(bf16[4,4096]{1,0:T(4,128)(2,1)} %param.20) | copy-start | bytes 98308
  64.2 30.9 %copy-start.12 = (s32[4]{0:T(128)S(1)}, s32[4]{0:T(128)}, u32[]{:S(2)}) copy-start(s32[4]{0:T(128)} %len_ref.1) | copy-start | bytes 52
  65.0 7.3 %collective-permute-start.4 = (f32[16,128]{1,0:T(8,128)S(1)}, f32[16,128]{1,0:T(8,128)S(1)}, u32[]{:S(2)}, u32[]{:S(2)}) collective-permute-start(f32[16,128]{1,0:T(8,128)S(1)} %shard_map.143), channel_id=1, source_target_pairs={{0,8},{1,9},{2,10},{3,11},{4,12},{5,13},{6,14},{7,15},{8,0},{9,1},... | collective-permute-start | bytes 24584 | tf_op jit(solution)/shard_map/ppermute | solution.py:266
  72.3 3.7 %collective-permute-start.5 = (f32[16,128]{1,0:T(8,128)S(1)}, f32[16,128]{1,0:T(8,128)S(1)}, u32[]{:S(2)}, u32[]{:S(2)}) collective-permute-start(f32[16,128]{1,0:T(8,128)S(1)} %add.20), channel_id=1, source_target_pairs={{0,4},{1,5},{2,6},{3,7},{4,0},{5,1},{6,2},{7,3},{8,12},{9,13},{10,... | collective-permute-start | bytes 24584 | tf_op jit(solution)/shard_map/ppermute | solution.py:266
  76.0 3.7 %collective-permute-start.6 = (f32[16,128]{1,0:T(8,128)S(1)}, f32[16,128]{1,0:T(8,128)S(1)}, u32[]{:S(2)}, u32[]{:S(2)}) collective-permute-start(f32[16,128]{1,0:T(8,128)S(1)} %add.21), channel_id=1, source_target_pairs={{0,2},{1,3},{2,0},{3,1},{4,6},{5,7},{6,4},{7,5},{8,10},{9,11},{10,... | collective-permute-start | bytes 24584 | tf_op jit(solution)/shard_map/ppermute | solution.py:266
  79.6 1.2 %collective-permute-start.7 = (f32[16,128]{1,0:T(8,128)S(1)}, f32[16,128]{1,0:T(8,128)S(1)}, u32[]{:S(2)}, u32[]{:S(2)}) collective-permute-start(f32[16,128]{1,0:T(8,128)S(1)} %add.22), channel_id=1, source_target_pairs={{0,1},{1,0},{2,3},{3,2},{4,5},{5,4},{6,7},{7,6},{8,9},{9,8},{10,11... | collective-permute-start | bytes 24584 | tf_op jit(solution)/shard_map/ppermute | solution.py:266
  80.8 1.2 %copy-start.3 = (bf16[256,2048]{1,0:T(8,128)(2,1)S(1)}, bf16[256,2048]{1,0:T(8,128)(2,1)}, u32[]{:S(2)}) copy-start(bf16[256,2048]{1,0:T(8,128)(2,1)} %b_ref.3) | copy-start | bytes 3145732
  84.4 10.6 %all-to-all-start.2 = ((f32[16,4,256]{2,1,0:T(4,128)}), f32[16,4,256]{2,1,0:T(4,128)S(1)}, u32[]{:S(2)}, u32[]{:S(2)}) async-start(f32[16,4,256]{2,1,0:T(4,128)} %shard_map.144), calls=%async_computation.2 | async-start | bytes 131072 | tf_op jit(solution)/shard_map/all_to_all | solution.py:261
  95.0 1.2 %copy-start.7 = (bf16[4,256,512]{2,1,0:T(8,128)(2,1)S(1)}, bf16[4,256,512]{2,1,0:T(8,128)(2,1)}, u32[]{:S(2)}) copy-start(bf16[4,256,512]{2,1,0:T(8,128)(2,1)} %k_ref.1) | copy-start | bytes 3145732
  96.2 1.2 %copy-start.8 = (bf16[4,256,512]{2,1,0:T(8,128)(2,1)S(1)}, bf16[4,256,512]{2,1,0:T(8,128)(2,1)}, u32[]{:S(2)}) copy-start(bf16[4,256,512]{2,1,0:T(8,128)(2,1)} %v_ref.1) | copy-start | bytes 3145732
  (1 other events, 0.7 us)

commit v3 on v1

v3 whole, which is shorter than its diff:
```python
import functools

import jax
import jax.numpy as jnp
from jax import lax
from jax.experimental import pallas as pl
from jax.experimental.pallas import tpu as pltpu
from jax.sharding import PartitionSpec as P

HEAD_DIM = 128
HEADS = 32
KV_HEADS = 4
RANK = 32
TENANTS = 64
BLOCK = 128
ROWS_DEV = 4
LANES = 128
PER_TILE = LANES // RANK

adapter_scale = 2.0
learning_rate = 0.0002

F32 = jnp.float32
BF16 = jnp.bfloat16
VMEM_LIMIT = 40 * 1024 * 1024
ALL_VMEM = 60 * 1024 * 1024


def vmem():
    return pl.BlockSpec(memory_space=pltpu.VMEM)


def smem():
    return pl.BlockSpec(memory_space=pltpu.SMEM)


def hbm():
    return pl.BlockSpec(memory_space=pltpu.HBM)


def call(kernel, out_shape, in_specs, out_specs, scratch=(), flops=0, nbytes=0, limit=VMEM_LIMIT):
    return pl.pallas_call(
        kernel,
        out_shape=out_shape,
        in_specs=in_specs,
        out_specs=out_specs,
        scratch_shapes=list(scratch),
        compiler_params=pltpu.CompilerParams(vmem_limit_bytes=limit),
        cost_estimate=pl.CostEstimate(flops=flops, bytes_accessed=nbytes, transcendentals=0),
    )


def each(count, body):
    if count <= 16:
        for j in range(count):
            body(j)
    else:
        pl.loop(0, count)(body)


def dot(a, b, ca, cb):
    return lax.dot_general(a, b, (((ca,), (cb,)), ((), ())), preferred_element_type=F32)


def quarter_indicator(quarter, value):
    lane = lax.broadcasted_iota(jnp.int32, (RANK, LANES), 1)
    row = lax.broadcasted_iota(jnp.int32, (RANK, LANES), 0)
    return jnp.where(lane - row == quarter * RANK, value, 0.0).astype(BF16)


def tile_of(tenant):
    return pl.ds(pl.multiple_of((tenant // PER_TILE) * LANES, LANES), LANES)


HALF = RANK // 2


def pick_kernel(t_ref, table_ref, *refs):
    extra_ref = refs[0] if len(refs) == 6 else None
    o_ref, table, o_buf, sem_in, sem_out = refs[-5:]
    n, f = t_ref.shape[0], table_ref.shape[0]
    chunks = sem_in.shape[0]
    step = f // chunks
    loads = []
    for c in range(chunks):
        rows = slice(c * step, (c + 1) * step)
        load = pltpu.make_async_copy(table_ref.at[rows], table.at[rows], sem_in.at[c])
        load.start()
        loads.append(load)
    for load in loads:
        load.wait()

    def body(j):
        t = t_ref[j]
        got = dot(quarter_indicator(t % PER_TILE, 1.0), table[:, tile_of(t)], 1, 1).astype(BF16)
        if extra_ref is None:
            o_buf[j] = got
        else:
            o_buf[j, :, :f] = got[:HALF]
            o_buf[j, :, f : 2 * f] = got[HALF:]
            o_buf[j, :, o_buf.shape[2] - LANES :] = extra_ref[j]
        pltpu.make_async_copy(o_buf.at[j], o_ref.at[j], sem_out.at[j]).start()

    def finish(j):
        pltpu.make_async_copy(o_buf.at[j], o_ref.at[j], sem_out.at[j]).wait()

    each(n, body)
    each(n, finish)


def back_kernel(g_ref, x_ref, r_ref, o_ref, w_ref):
    n, fb = r_ref.shape[0], r_ref.shape[2]
    fa = x_ref.shape[1] // n
    for d in range(n):
        w_ref[:, d * fb : (d + 1) * fb] = r_ref[d]
    back = dot(w_ref[...], g_ref[...], 1, 1).astype(BF16)
    part = dot(back, x_ref[...], 1, 0).astype(BF16)
    for d in range(n):
        for h in range(2):
            o_ref[d, :, h * fa : (h + 1) * fa] = part[h * HALF : (h + 1) * HALF, d * fa : (d + 1) * fa]


def down_kernel(x_ref, g_ref, r_ref, o_ref, w_ref):
    n, fb = o_ref.shape[0], o_ref.shape[2]
    fa = x_ref.shape[1] // n
    for d in range(n):
        for h in range(2):
            w_ref[h * HALF : (h + 1) * HALF, d * fa : (d + 1) * fa] = r_ref[d, :, h * fa : (h + 1) * fa]
    down = dot(w_ref[...], x_ref[...], 1, 1).astype(BF16)
    part = dot(down, g_ref[...], 1, 0).astype(BF16)
    for d in range(n):
        o_ref[d] = part[:, d * fb : (d + 1) * fb]


def sum_by_tenant(t_ref, part_ref, grad_ref):
    f = grad_ref.shape[0]
    grad_ref[...] = jnp.zeros_like(grad_ref)

    def body(j):
        t = t_ref[j]
        part = part_ref[j]
        if part.shape[0] == HALF:
            part = jnp.concatenate([part[:, :f], part[:, f:]], axis=0)
        place = quarter_indicator(t % PER_TILE, adapter_scale)
        grad_ref[:, tile_of(t)] += dot(part, place, 0, 0)

    each(t_ref.shape[0], body)


def updated(table_ref, grad_ref):
    return (table_ref[...].astype(F32) - learning_rate * grad_ref[...]).astype(BF16)


def fold_rows(product, tenant):
    rows = product.shape[0]
    lane = lax.broadcasted_iota(jnp.int32, (rows, LANES), 1)
    total = jnp.zeros((rows, LANES), F32)
    for c in range(TENANTS // PER_TILE):
        mine = tenant == c * PER_TILE + lane // RANK
        total = total + jnp.where(mine, product[:, c * LANES : (c + 1) * LANES], 0.0)
    half = total + pltpu.roll(total, 2 * RANK, 1)
    return half + pltpu.roll(half, RANK, 1)


def share_kernel(t_ref, part_ref, a_ref, h_ref, u_ref, o_ref, grad_ref):
    sum_by_tenant(t_ref, part_ref, grad_ref)
    full = fold_rows(dot(h_ref[...], updated(a_ref, grad_ref), 1, 0), u_ref[...])
    quarter = full.shape[0] // PER_TILE
    spot = lax.broadcasted_iota(jnp.int32, (quarter, LANES), 1) // RANK
    packed = jnp.zeros((quarter, LANES), F32)
    for q in range(PER_TILE):
        packed = packed + jnp.where(spot == q, full[q * quarter : (q + 1) * quarter], 0.0)
    for d in range(o_ref.shape[0]):
        o_ref[d] = packed


def up_kernel(t_ref, part_ref, b_ref, grad_ref, new_ref):
    sum_by_tenant(t_ref, part_ref, grad_ref)
    new_ref[...] = updated(b_ref, grad_ref)


def delta_kernel(p_ref, u_ref, new_ref, o_ref):
    n, quarter = p_ref.shape[0], p_ref.shape[1]
    total = p_ref[0]
    for d in range(1, n):
        total = total + p_ref[d]
    spot = lax.broadcasted_iota(jnp.int32, (quarter, LANES), 1) // RANK
    pieces = []
    for q in range(PER_TILE):
        one = jnp.where(spot == q, total, 0.0)
        half = one + pltpu.roll(one, 2 * RANK, 1)
        pieces.append(half + pltpu.roll(half, RANK, 1))
    adapted = jnp.concatenate(pieces, axis=0)
    lane = lax.broadcasted_iota(jnp.int32, adapted.shape, 1)
    tenant = u_ref[...]
    spread = jnp.concatenate(
        [
            jnp.where(tenant == c * PER_TILE + lane // RANK, adapted, 0.0).astype(BF16)
            for c in range(TENANTS // PER_TILE)
        ],
        axis=1,
    )
    delta = adapter_scale * dot(spread, new_ref[...], 1, 1)
    for d in range(n):
        o_ref[d] = delta[d * ROWS_DEV : (d + 1) * ROWS_DEV]


def attention_kernel(len_ref, delta_ref, base_ref, k_ref, v_ref, o_ref):
    n = delta_ref.shape[0]
    delta = jnp.concatenate([delta_ref[d] for d in range(n)], axis=1)
    query = (base_ref[...] + delta).astype(BF16).astype(F32)
    group = HEADS // KV_HEADS
    cache = k_ref.shape[1]
    many = group * ROWS_DEV
    row_p = lax.broadcasted_iota(jnp.int32, (many, cache), 0) % ROWS_DEV
    row_d = lax.broadcasted_iota(jnp.int32, (many, HEAD_DIM), 0) % ROWS_DEV
    position = lax.broadcasted_iota(jnp.int32, (many, cache), 1)
    length = jnp.zeros((many, cache), jnp.int32)
    for r in range(ROWS_DEV):
        length = jnp.where(row_p == r, len_ref[r], length)
    live = position < length
    outs = []
    for g in range(KV_HEADS):
        cols = slice(g * HEAD_DIM, (g + 1) * HEAD_DIM)
        heads = jnp.concatenate(
            [query[:, (g * group + i) * HEAD_DIM : (g * group + i + 1) * HEAD_DIM] for i in range(group)],
            axis=0,
        ).astype(BF16)
        scores = jnp.zeros((many, cache), F32)
        for r in range(ROWS_DEV):
            scores = jnp.where(row_p == r, dot(heads, k_ref[r, :, cols], 1, 1), scores)
        scores = scores / jnp.sqrt(F32(HEAD_DIM))
        scores = jnp.where(live, scores, F32(-1e30))
        top = jnp.max(scores, axis=-1, keepdims=True)
        expo = jnp.where(live, jnp.exp(scores - top), 0.0)
        weights = (expo / jnp.sum(expo, axis=-1, keepdims=True)).astype(BF16)
        mixed = jnp.zeros((many, HEAD_DIM), F32)
        for r in range(ROWS_DEV):
            mixed = jnp.where(row_d == r, dot(weights, v_ref[r, :, cols], 1, 0), mixed)
        outs.extend(mixed[i * ROWS_DEV : (i + 1) * ROWS_DEV] for i in range(group))
    o_ref[...] = jnp.concatenate(outs, axis=1).astype(BF16)


def exchange(x):
    return lax.all_to_all(x, "wide", split_axis=0, concat_axis=0, tiled=True)


def per_device(
    tokens,
    query_output_gradient,
    down_factors,
    up_factors_transposed,
    tenant_of_block,
    device_tenant_list,
    row_list_entry,
    hidden,
    base_query_rows,
    cached_key_rows,
    cached_value_rows,
    live_cache_length,
):
    n = lax.axis_size("wide")
    fa, cols = down_factors.shape
    fb = up_factors_transposed.shape[0]
    local_rows = hidden.shape[0]
    rows = local_rows * n
    width = tokens.shape[1]
    features = query_output_gradient.shape[1]
    pieces = -(-fa // LANES)
    assert tokens.shape[0] == BLOCK and tenant_of_block.shape[0] == n and local_rows * (pieces + 1) <= HALF

    def pick(table, extra):
        f = table.shape[0]
        chunks = 4 if f % 64 == 0 else 1
        lanes = -(-2 * f // LANES) * LANES + LANES
        shape = (n, RANK, f) if extra is None else (n, HALF, lanes)
        return call(
            pick_kernel,
            jax.ShapeDtypeStruct(shape, BF16),
            [smem(), hbm()] + ([] if extra is None else [vmem()]),
            hbm(),
            scratch=[
                pltpu.VMEM(table.shape, BF16),
                pltpu.VMEM(shape, BF16),
                pltpu.SemaphoreType.DMA((chunks,)),
                pltpu.SemaphoreType.DMA((n,)),
            ],
            flops=2 * RANK * LANES * n * f,
            nbytes=2 * cols * f,
            limit=ALL_VMEM,
        )(tenant_of_block, table, *([] if extra is None else [extra]))

    got_up = exchange(pick(up_factors_transposed, None))

    slot = row_list_entry[:, None] == jnp.arange(device_tenant_list.shape[1], dtype=jnp.int32)[None, :]
    row_tenant = jnp.sum(jnp.where(slot, device_tenant_list, 0), axis=1)
    slices = jnp.pad(hidden.reshape(local_rows, n, fa), ((0, 0), (0, 0), (0, pieces * LANES - fa)))
    slices = slices.reshape(local_rows, n, pieces, LANES).transpose(1, 2, 0, 3).reshape(n, pieces * local_rows, LANES)
    marks = jnp.broadcast_to(row_tenant.astype(BF16)[None, :, None], (n, local_rows, LANES))
    extra = jnp.concatenate([slices, marks], axis=1)
    extra = jnp.pad(extra, ((0, 0), (0, HALF - extra.shape[1]), (0, 0)))
    got_down = exchange(pick(down_factors, extra))

    down_parts = call(
        back_kernel,
        jax.ShapeDtypeStruct((n, HALF, 2 * fa), BF16),
        [vmem()] * 3,
        vmem(),
        scratch=[pltpu.VMEM((RANK, features), BF16)],
        flops=2 * RANK * BLOCK * (width + features),
        nbytes=2 * BLOCK * (width + features),
    )(query_output_gradient, tokens, got_up)
    down_parts = exchange(down_parts)

    up_parts = call(
        down_kernel,
        jax.ShapeDtypeStruct((n, RANK, fb), BF16),
        [vmem()] * 3,
        vmem(),
        scratch=[pltpu.VMEM((RANK, width), BF16)],
        flops=2 * RANK * BLOCK * (width + features),
        nbytes=2 * BLOCK * (width + features),
    )(tokens, query_output_gradient, got_down)
    up_parts = exchange(up_parts)

    tail = got_down[:, :, got_down.shape[2] - LANES :]
    h_cols = tail[:, : pieces * local_rows].reshape(n, pieces, local_rows, LANES).transpose(0, 2, 1, 3)
    h_cols = h_cols.reshape(rows, pieces * LANES)[:, :fa]
    tenants = tail[:, pieces * local_rows : (pieces + 1) * local_rows].astype(jnp.int32).reshape(rows, LANES)
    low_rank = call(
        share_kernel,
        jax.ShapeDtypeStruct((n, rows // PER_TILE, LANES), F32),
        [smem(), vmem(), vmem(), vmem(), vmem()],
        vmem(),
        scratch=[pltpu.VMEM((fa, cols), F32)],
        flops=2 * rows * fa * cols,
        nbytes=2 * cols * fa,
    )(tenant_of_block, down_parts, down_factors, h_cols, tenants)
    low_rank = exchange(low_rank)

    up_gradient, new_up = call(
        up_kernel,
        [jax.ShapeDtypeStruct((fb, cols), F32), jax.ShapeDtypeStruct((fb, cols), BF16)],
        [smem(), vmem(), vmem()],
        [vmem()] * 2,
        flops=2 * n * RANK * fb * LANES,
        nbytes=8 * cols * fb,
    )(tenant_of_block, up_parts, up_factors_transposed)
    delta = call(
        delta_kernel,
        jax.ShapeDtypeStruct((n, local_rows, fb), F32),
        [vmem()] * 3,
        vmem(),
        flops=2 * rows * cols * fb,
        nbytes=2 * cols * fb,
    )(low_rank, tenants, new_up)
    delta = exchange(delta)

    down_gradient = call(
        sum_by_tenant,
        jax.ShapeDtypeStruct((fa, cols), F32),
        [smem(), vmem()],
        vmem(),
        flops=2 * n * RANK * fa * LANES,
        nbytes=4 * cols * fa,
    )(tenant_of_block, down_parts)
    attended = call(
        attention_kernel,
        jax.ShapeDtypeStruct((local_rows, HEADS * HEAD_DIM), BF16),
        [smem(), vmem(), vmem(), vmem(), vmem()],
        vmem(),
        flops=4 * HEADS * local_rows * cached_key_rows.shape[1] * HEAD_DIM,
        nbytes=4 * cached_key_rows.size,
    )(live_cache_length, delta, base_query_rows.astype(F32), cached_key_rows, cached_value_rows)
    return down_gradient, up_gradient, attended


def solution(mesh):
    placed = (
        P(("groups", "wide"), None),
        P(("groups", "wide"), None),
        P("wide", "groups"),
        P("wide", "groups"),
        P("groups"),
        P(("groups", "wide"), None),
        P(("groups", "wide")),
        P(("groups", "wide"), None),
        P(("groups", "wide"), None),
        P(("groups", "wide"), None, None),
        P(("groups", "wide"), None, None),
        P(("groups", "wide")),
    )
    return jax.shard_map(
        per_device,
        mesh=mesh,
        in_specs=placed,
        out_specs=(P("wide", "groups"), P("wide", "groups"), P(("groups", "wide"), None)),
        check_vma=False,
    )
```

time: 88.4 us -> 94.4 us (1.068)
  blocking collectives: 25.4 us -> 0 us
  starting transfers between devices: 12.1 us -> 25.8 us
  waiting for transfers between devices: 25.1 us -> 38.4 us
  Pallas kernels: 12.6 us -> 21.4 us
  local copies, waits for them, and re-layouts: 9.54 us -> 5.98 us
  other arithmetic: 2.14 us -> 0.91 us
    all_to_all x1 -> x0, blocking collectives: 25.4 us -> none  [exchange(): return lax.all_to_all(x, 'wide', split_axis=0, concat_axis=0, tiled=True)]
    all_to_all x3 -> x6, starting transfers between devices: 12.1 us -> 25.8 us  [exchange(): return lax.all_to_all(x, 'wide', split_axis=0, concat_axis=0, tiled=True)]
    all_to_all x3 -> x6, waiting for transfers between devices: 25.1 us -> 38.4 us  [exchange(): return lax.all_to_all(x, 'wide', split_axis=0, concat_axis=0, tiled=True)]
    pallas_call x3 -> x6, Pallas kernels: 5.87 us -> 14.9 us  [the longest x2 6.72 us: pick(): call(pick_kernel, jax.ShapeDtypeStruct(shape, BF16), [smem(), hbm()] + ([...]
    unnamed x32 -> x35, local copies, waits for them, and re-layouts: 7.1 us -> 4.88 us
    convert_element_type x1 -> x0, other arithmetic: 1.18 us -> none  [per_device(): tenants = jnp.broadcast_to(tenants.astype(jnp.int32), (rows, LANES))]
    slice x2 -> x3, local copies, waits for them, and re-layouts: 1.01 us -> 0.04 us  [the longest x2 0.03 us: per_device(): tail[:, :pieces * local_rows].reshape(n, pieces, local_rows, LANES)]
  transfers between devices with their start and end apart: 3 -> 6, of which waited for: 3 -> 6; matrix products, arithmetic and copies ran while one was open for 3% -> 2% of each run, Pallas kernels for 3% -> 16%
where the time goes in v3:
time: 94.4 us; the launch traced here: 93.4 us
  waiting for transfers between devices  38.4 us (41%)
  starting transfers between devices  25.8 us (27%)
  Pallas kernels  21.4 us (23%)
  local copies, waits for them, and re-layouts  5.98 us (6%)
  between operations  0.95 us (1%)
    all_to_all x6, waiting for transfers between devices, exchange(): return lax.all_to_all(x, 'wide', split_axis=0, concat_axis=0, tiled=True)  38.4 us
    all_to_all x6, starting transfers between devices, exchange(): return lax.all_to_all(x, 'wide', split_axis=0, concat_axis=0, tiled=True)  25.8 us
    pallas_call x2, Pallas kernels, pick(): call(pick_kernel, jax.ShapeDtypeStruct(shape, BF16), [smem(), hbm()] + ([...  6.72 us
    unnamed x35, local copies, waits for them, and re-layouts  4.88 us
    pallas_call x1, Pallas kernels, per_device(): call(up_kernel, [jax.ShapeDtypeStruct((fb, cols), F32), jax.ShapeDtypeStr...  3.14 us
    pallas_call x1, Pallas kernels, per_device(): call(sum_by_tenant, jax.ShapeDtypeStruct((fa, cols), F32), [smem(), vmem(...  3.06 us
    pallas_call x1, Pallas kernels, per_device(): call(share_kernel, jax.ShapeDtypeStruct((n, rows // PER_TILE, LANES), F32...  2.98 us
    pallas_call x1, Pallas kernels, per_device(): call(attention_kernel, jax.ShapeDtypeStruct((local_rows, HEADS * HEAD_DIM...  2.87 us
  transfers between devices with their start and end apart: 6, of which 6 were waited for; matrix products, arithmetic and copies ran while one was open for 2% of the time, Pallas kernels for 16%

profile of v3, /device:TPU:0, one launch (start us, length us, event | category | flops | bytes accessed | tf_op | source)
XLA Modules:
  0.0 93.4 jit_solution(10934893314620162773)
XLA Ops:
  0.7 3.2 %shard_map.139 = bf16[16,32,256]{2,1,0:T(8,128)(2,1)} custom-call(s32[16]{0:T(128)} %t_ref.9, bf16[256,2048]{1,0:T(8,128)(2,1)} %b_ref.1), custom_call_target="tpu_custom_call" | custom-call | flops 33554432 | bytes 1048576 | tf_op jit(solution)/shard_map/pallas_call | solution.py:277
  3.9 7.5 %all-to-all-start = ((bf16[16,32,256]{2,1,0:T(8,128)(2,1)}), bf16[16,32,256]{2,1,0:T(8,128)(2,1)S(1)}, u32[]{:S(2)}, u32[]{:S(2)}) async-start(bf16[16,32,256]{2,1,0:T(8,128)(2,1)} %shard_map.139), calls=%async_computation | async-start | bytes 524288 | tf_op jit(solution)/shard_map/all_to_all | solution.py:245
  11.4 0.9 reshape.30
  13.4 3.5 %shard_map.142 = bf16[16,16,768]{2,1,0:T(8,128)(2,1)} custom-call(s32[16]{0:T(128)} %t_ref.9, bf16[320,2048]{1,0:T(8,128)(2,1)} %a_ref.1, bf16[16,16,128]{2,1,0:T(8,128)(2,1)} %pad_maximum_fusion.refs_0_), custom_call_target="tpu_custom_call" | custom-call | flops 41943040 | bytes 1310720 | tf_op jit(solution)/shard_map/pallas_call | solution.py:277
  16.9 4.6 %all-to-all-done.r_ref = bf16[16,32,256]{2,1,0:T(8,128)(2,1)S(1)} async-done(((bf16[16,32,256]{2,1,0:T(8,128)(2,1)}), bf16[16,32,256]{2,1,0:T(8,128)(2,1)S(1)}, u32[]{:S(2)}, u32[]{:S(2)}) %all-to-all-start) | async-done | bytes 262176 | tf_op jit(solution)/shard_map/all_to_all | solution.py:245
  21.5 3.6 %all-to-all-start.2 = ((bf16[16,16,768]{2,1,0:T(8,128)(2,1)}), bf16[16,16,768]{2,1,0:T(8,128)(2,1)S(1)}, u32[]{:S(2)}, u32[]{:S(2)}) async-start(bf16[16,16,768]{2,1,0:T(8,128)(2,1)} %shard_map.142), calls=%async_computation.2 | async-start | bytes 786432 | tf_op jit(solution)/shard_map/all_to_all | solution.py:245
  25.1 1.1 %shard_map.140 = bf16[16,16,640]{2,1,0:T(8,128)(2,1)S(1)} custom-call(bf16[128,4096]{1,0:T(8,128)(2,1)S(1)} %copy-done.2, bf16[128,5120]{1,0:T(8,128)(2,1)S(1)} %copy-done, bf16[16,32,256]{2,1,0:T(8,128)(2,1)S(1)} %all-to-all-done.r_ref), custom_call_target="tpu_custom_call" | custom-call | flops 75497472 | bytes 2359296 | tf_op jit(solution)/shard_map/pallas_call | solution.py:304
  26.2 0.7 copy-done.5
  26.9 10.3 %all-to-all-done.2.r_ref = bf16[16,16,768]{2,1,0:T(8,128)(2,1)S(1)} async-done(((bf16[16,16,768]{2,1,0:T(8,128)(2,1)}), bf16[16,16,768]{2,1,0:T(8,128)(2,1)S(1)}, u32[]{:S(2)}, u32[]{:S(2)}) %all-to-all-start.2) | async-done | bytes 393248 | tf_op jit(solution)/shard_map/all_to_all | solution.py:245
  37.2 3.5 %all-to-all-start.1 = ((bf16[16,16,640]{2,1,0:T(8,128)(2,1)}), bf16[16,16,640]{2,1,0:T(8,128)(2,1)S(1)}, u32[]{:S(2)}, u32[]{:S(2)}) async-start(bf16[16,16,640]{2,1,0:T(8,128)(2,1)} %copy-done.5), calls=%async_computation.1 | async-start | bytes 655360 | tf_op jit(solution)/shard_map/all_to_all | solution.py:245
  40.8 1.2 %copy-done.3 = bf16[128,4096]{1,0:T(8,128)(2,1)S(1)} copy-done((bf16[128,4096]{1,0:T(8,128)(2,1)S(1)}, bf16[128,4096]{1,0:T(8,128)(2,1)}, u32[]{:S(2)}) %copy-start.3) | copy-done | bytes 1048600
  42.0 1.0 %shard_map.143 = bf16[16,32,256]{2,1,0:T(8,128)(2,1)S(1)} custom-call(bf16[128,5120]{1,0:T(8,128)(2,1)S(1)} %copy-done, bf16[128,4096]{1,0:T(8,128)(2,1)S(1)} %copy-done.3, bf16[16,16,768]{2,1,0:T(8,128)(2,1)S(1)} %all-to-all-done.2.r_ref), custom_call_target="tpu_custom_call" | custom-call | flops 75497472 | bytes 2359296 | tf_op jit(solution)/shard_map/pallas_call | solution.py:315
  43.7 8.1 %all-to-all-done.1.part_ref = bf16[16,16,640]{2,1,0:T(8,128)(2,1)S(1)} async-done(((bf16[16,16,640]{2,1,0:T(8,128)(2,1)}), bf16[16,16,640]{2,1,0:T(8,128)(2,1)S(1)}, u32[]{:S(2)}, u32[]{:S(2)}) %all-to-all-start.1) | async-done | bytes 327712 | tf_op jit(solution)/shard_map/all_to_all | solution.py:245
  51.8 4.2 %all-to-all-start.3 = ((bf16[16,32,256]{2,1,0:T(8,128)(2,1)}), bf16[16,32,256]{2,1,0:T(8,128)(2,1)}, u32[]{:S(2)}, u32[]{:S(2)}) async-start(bf16[16,32,256]{2,1,0:T(8,128)(2,1)} %copy-done.8), calls=%async_computation.3 | async-start | bytes 524288 | tf_op jit(solution)/shard_map/all_to_all | solution.py:245
  56.2 3.0 %shard_map.145 = f32[16,16,128]{2,1,0:T(8,128)} custom-call(s32[16]{0:T(128)S(1)} %copy-done.12, bf16[16,16,640]{2,1,0:T(8,128)(2,1)S(1)} %all-to-all-done.1.part_ref, bf16[320,2048]{1,0:T(8,128)(2,1)S(1)} %copy-done.1, bf16[64,320]{1,0:T(8,128)(2,1)S(1)} %bitcast.14, s32[64,128]{1,0:T(8,128)S(1)} %convert.1.u_ref), custom_call_target="tpu_custom_call" | custom-call | flops 83886080 | bytes 1310720 | tf_op jit(solution)/shard_map/pallas_call | solution.py:330
  59.2 6.9 %all-to-all-done.3.part_ref = bf16[16,32,256]{2,1,0:T(8,128)(2,1)} async-done(((bf16[16,32,256]{2,1,0:T(8,128)(2,1)}), bf16[16,32,256]{2,1,0:T(8,128)(2,1)}, u32[]{:S(2)}, u32[]{:S(2)}) %all-to-all-start.3) | async-done | bytes 262176 | tf_op jit(solution)/shard_map/all_to_all | solution.py:245
  66.1 3.5 %all-to-all-start.4 = ((f32[16,16,128]{2,1,0:T(8,128)}), f32[16,16,128]{2,1,0:T(8,128)S(1)}, u32[]{:S(2)}, u32[]{:S(2)}) async-start(f32[16,16,128]{2,1,0:T(8,128)} %shard_map.145), calls=%async_computation.4 | async-start | bytes 262144 | tf_op jit(solution)/shard_map/all_to_all | solution.py:245
  69.6 3.1 %shard_map.144 = (f32[256,2048]{1,0:T(8,128)}, bf16[256,2048]{1,0:T(8,128)(2,1)S(1)}) custom-call(s32[16]{0:T(128)S(1)} %copy-done.12, bf16[16,32,256]{2,1,0:T(8,128)(2,1)} %all-to-all-done.3.part_ref, bf16[256,2048]{1,0:T(8,128)(2,1)S(1)} %copy-done.4), custom_call_target="tpu_custom_call" | custom-call | flops 33554432 | bytes 4194304 | tf_op jit(solution)/shard_map/pallas_call | solution.py:341
  72.7 4.8 %all-to-all-done.4.p_ref = f32[16,16,128]{2,1,0:T(8,128)S(1)} async-done(((f32[16,16,128]{2,1,0:T(8,128)}), f32[16,16,128]{2,1,0:T(8,128)S(1)}, u32[]{:S(2)}, u32[]{:S(2)}) %all-to-all-start.4) | async-done | bytes 131104 | tf_op jit(solution)/shard_map/all_to_all | solution.py:245
  78.1 0.9 copy-done.10
  80.2 3.5 %all-to-all-start.5 = ((f32[16,4,256]{2,1,0:T(4,128)}), f32[16,4,256]{2,1,0:T(4,128)S(1)}, u32[]{:S(2)}, u32[]{:S(2)}) async-start(f32[16,4,256]{2,1,0:T(4,128)} %copy-done.11), calls=%async_computation.5 | async-start | bytes 131072 | tf_op jit(solution)/shard_map/all_to_all | solution.py:245
  83.7 3.1 %shard_map.141 = f32[320,2048]{1,0:T(8,128)} custom-call(s32[16]{0:T(128)S(1)} %copy-done.12, bf16[16,16,640]{2,1,0:T(8,128)(2,1)S(1)} %all-to-all-done.1.part_ref), custom_call_target="tpu_custom_call" | custom-call | flops 41943040 | bytes 2621440 | tf_op jit(solution)/shard_map/pallas_call | solution.py:359
  86.8 3.8 %all-to-all-done.5.delta_ref = f32[16,4,256]{2,1,0:T(4,128)S(1)} async-done(((f32[16,4,256]{2,1,0:T(4,128)}), f32[16,4,256]{2,1,0:T(4,128)S(1)}, u32[]{:S(2)}, u32[]{:S(2)}) %all-to-all-start.5) | async-done | bytes 65568 | tf_op jit(solution)/shard_map/all_to_all | solution.py:245
  90.6 2.9 %shard_map.147 = bf16[4,4096]{1,0:T(4,128)(2,1)} custom-call(s32[4]{0:T(128)S(1)} %copy-done.13, f32[16,4,256]{2,1,0:T(4,128)S(1)} %all-to-all-done.5.delta_ref, f32[4,4096]{1,0:T(4,128)S(1)} %convert_element_type.14.base_ref, bf16[4,256,512]{2,1,0:T(8,128)(2,1)S(1)} %copy-done.6, bf16[4,256,512]{2,1,0:T(8,128)(2,1)S(1)} %copy-done.7), custom_call_target="tpu_custom_call" | custom-call | flops 16777216 | bytes 2097152 | tf_op jit(solution)/shard_map/pallas_call | solution.py:367
  (47 shorter events, 3.7 us)
Async XLA Ops:
  0.6 11.8 %copy-start.15 = (s32[1,4]{1,0:T(1,128)S(1)}, s32[1,4]{1,0:T(1,128)}, u32[]{:S(2)}) copy-start(s32[1,4]{1,0:T(1,128)} %param.17) | copy-start | bytes 52
  0.6 11.8 %copy-start.16 = (s32[4]{0:T(128)S(1)}, s32[4]{0:T(128)}, u32[]{:S(2)}) copy-start(s32[4]{0:T(128)} %param.18) | copy-start | bytes 52
  3.9 21.2 %copy-start = (bf16[128,5120]{1,0:T(8,128)(2,1)S(1)}, bf16[128,5120]{1,0:T(8,128)(2,1)}, u32[]{:S(2)}) copy-start(bf16[128,5120]{1,0:T(8,128)(2,1)} %x_ref.3) | copy-start | bytes 3932164
  3.9 21.2 %copy-start.2 = (bf16[128,4096]{1,0:T(8,128)(2,1)S(1)}, bf16[128,4096]{1,0:T(8,128)(2,1)}, u32[]{:S(2)}) copy-start(bf16[128,4096]{1,0:T(8,128)(2,1)} %g_ref.3) | copy-start | bytes 3145732
  3.9 17.6 %all-to-all-start = ((bf16[16,32,256]{2,1,0:T(8,128)(2,1)}), bf16[16,32,256]{2,1,0:T(8,128)(2,1)S(1)}, u32[]{:S(2)}, u32[]{:S(2)}) async-start(bf16[16,32,256]{2,1,0:T(8,128)(2,1)} %shard_map.139), calls=%async_computation | async-start | bytes 524288 | tf_op jit(solution)/shard_map/all_to_all | solution.py:245
  21.5 15.7 %all-to-all-start.2 = ((bf16[16,16,768]{2,1,0:T(8,128)(2,1)}), bf16[16,16,768]{2,1,0:T(8,128)(2,1)S(1)}, u32[]{:S(2)}, u32[]{:S(2)}) async-start(bf16[16,16,768]{2,1,0:T(8,128)(2,1)} %shard_map.142), calls=%async_computation.2 | async-start | bytes 786432 | tf_op jit(solution)/shard_map/all_to_all | solution.py:245
  26.1 0.7 copy-start.5
  37.2 14.6 %all-to-all-start.1 = ((bf16[16,16,640]{2,1,0:T(8,128)(2,1)}), bf16[16,16,640]{2,1,0:T(8,128)(2,1)S(1)}, u32[]{:S(2)}, u32[]{:S(2)}) async-start(bf16[16,16,640]{2,1,0:T(8,128)(2,1)} %copy-done.5), calls=%async_computation.1 | async-start | bytes 655360 | tf_op jit(solution)/shard_map/all_to_all | solution.py:245
  40.8 1.2 %copy-start.3 = (bf16[128,4096]{1,0:T(8,128)(2,1)S(1)}, bf16[128,4096]{1,0:T(8,128)(2,1)}, u32[]{:S(2)}) copy-start(bf16[128,4096]{1,0:T(8,128)(2,1)} %g_ref.3) | copy-start | bytes 3145732
  42.0 14.2 %copy-start.1 = (bf16[320,2048]{1,0:T(8,128)(2,1)S(1)}, bf16[320,2048]{1,0:T(8,128)(2,1)}, u32[]{:S(2)}) copy-start(bf16[320,2048]{1,0:T(8,128)(2,1)} %a_ref.1) | copy-start | bytes 3932164
  42.0 14.2 %copy-start.12 = (s32[16]{0:T(128)S(1)}, s32[16]{0:T(128)}, u32[]{:S(2)}) copy-start(s32[16]{0:T(128)} %t_ref.9) | copy-start | bytes 196
  43.0 0.7 copy-start.8
  43.7 25.8 %copy-start.4 = (bf16[256,2048]{1,0:T(8,128)(2,1)S(1)}, bf16[256,2048]{1,0:T(8,128)(2,1)}, u32[]{:S(2)}) copy-start(bf16[256,2048]{1,0:T(8,128)(2,1)} %b_ref.1) | copy-start | bytes 3145732
  51.8 14.3 %all-to-all-start.3 = ((bf16[16,32,256]{2,1,0:T(8,128)(2,1)}), bf16[16,32,256]{2,1,0:T(8,128)(2,1)}, u32[]{:S(2)}, u32[]{:S(2)}) async-start(bf16[16,32,256]{2,1,0:T(8,128)(2,1)} %copy-done.8), calls=%async_computation.3 | async-start | bytes 524288 | tf_op jit(solution)/shard_map/all_to_all | solution.py:245
  56.2 27.5 %copy-start.14 = (bf16[4,4096]{1,0:T(4,128)(2,1)S(1)}, bf16[4,4096]{1,0:T(4,128)(2,1)}, u32[]{:S(2)}) copy-start(bf16[4,4096]{1,0:T(4,128)(2,1)} %param.20) | copy-start | bytes 98308
  66.1 11.4 %all-to-all-start.4 = ((f32[16,16,128]{2,1,0:T(8,128)}), f32[16,16,128]{2,1,0:T(8,128)S(1)}, u32[]{:S(2)}, u32[]{:S(2)}) async-start(f32[16,16,128]{2,1,0:T(8,128)} %shard_map.145), calls=%async_computation.4 | async-start | bytes 262144 | tf_op jit(solution)/shard_map/all_to_all | solution.py:245
  77.5 0.7 copy-start.9
  78.1 0.9 copy-start.10
  79.0 11.5 %copy-start.6 = (bf16[4,256,512]{2,1,0:T(8,128)(2,1)S(1)}, bf16[4,256,512]{2,1,0:T(8,128)(2,1)}, u32[]{:S(2)}) copy-start(bf16[4,256,512]{2,1,0:T(8,128)(2,1)} %k_ref.1) | copy-start | bytes 3145732
  79.0 11.5 %copy-start.7 = (bf16[4,256,512]{2,1,0:T(8,128)(2,1)S(1)}, bf16[4,256,512]{2,1,0:T(8,128)(2,1)}, u32[]{:S(2)}) copy-start(bf16[4,256,512]{2,1,0:T(8,128)(2,1)} %v_ref.1) | copy-start | bytes 3145732
  79.0 11.5 %copy-start.13 = (s32[4]{0:T(128)S(1)}, s32[4]{0:T(128)}, u32[]{:S(2)}) copy-start(s32[4]{0:T(128)} %len_ref.1) | copy-start | bytes 52
  79.6 0.6 copy-start.11
  80.2 10.4 %all-to-all-start.5 = ((f32[16,4,256]{2,1,0:T(4,128)}), f32[16,4,256]{2,1,0:T(4,128)S(1)}, u32[]{:S(2)}, u32[]{:S(2)}) async-start(f32[16,4,256]{2,1,0:T(4,128)} %copy-done.11), calls=%async_computation.5 | async-start | bytes 131072 | tf_op jit(solution)/shard_map/all_to_all | solution.py:245

commit v4 on v3

v4 whole, which is shorter than its diff:
```python
import functools

import jax
import jax.numpy as jnp
from jax import lax
from jax.experimental import pallas as pl
from jax.experimental.pallas import tpu as pltpu
from jax.sharding import PartitionSpec as P

HEAD_DIM = 128
HEADS = 32
KV_HEADS = 4
RANK = 32
TENANTS = 64
BLOCK = 128
ROWS_DEV = 4
LANES = 128
PER_TILE = LANES // RANK

adapter_scale = 2.0
learning_rate = 0.0002

F32 = jnp.float32
BF16 = jnp.bfloat16
VMEM_LIMIT = 40 * 1024 * 1024
ALL_VMEM = 60 * 1024 * 1024


def vmem():
    return pl.BlockSpec(memory_space=pltpu.VMEM)


def smem():
    return pl.BlockSpec(memory_space=pltpu.SMEM)


def hbm():
    return pl.BlockSpec(memory_space=pltpu.HBM)


def call(kernel, out_shape, in_specs, out_specs, scratch=(), flops=0, nbytes=0, limit=VMEM_LIMIT):
    return pl.pallas_call(
        kernel,
        out_shape=out_shape,
        in_specs=in_specs,
        out_specs=out_specs,
        scratch_shapes=list(scratch),
        compiler_params=pltpu.CompilerParams(vmem_limit_bytes=limit),
        cost_estimate=pl.CostEstimate(flops=flops, bytes_accessed=nbytes, transcendentals=0),
    )


def each(count, body):
    if count <= 16:
        for j in range(count):
            body(j)
    else:
        pl.loop(0, count)(body)


def dot(a, b, ca, cb):
    return lax.dot_general(a, b, (((ca,), (cb,)), ((), ())), preferred_element_type=F32)


def quarter_indicator(quarter, value):
    lane = lax.broadcasted_iota(jnp.int32, (RANK, LANES), 1)
    row = lax.broadcasted_iota(jnp.int32, (RANK, LANES), 0)
    return jnp.where(lane - row == quarter * RANK, value, 0.0).astype(BF16)


def tile_of(tenant):
    return pl.ds(pl.multiple_of((tenant // PER_TILE) * LANES, LANES), LANES)


HALF = RANK // 2


def up_half(h, fa, fb):
    return slice(h * fb, (h + 1) * fb)


def down_half(h, fa, fb):
    return slice(2 * fb + h * fa, 2 * fb + (h + 1) * fa)


def pick_kernel(t_ref, b_ref, a_ref, o_ref, b_tab, a_tab, o_buf, sem_b, sem_a, sem_o):
    n = t_ref.shape[0]
    fa, fb = a_ref.shape[0], b_ref.shape[0]

    def loads(src, dst, sem):
        step = src.shape[0] // sem.shape[0]
        parts = [slice(c * step, (c + 1) * step) for c in range(sem.shape[0])]
        return [pltpu.make_async_copy(src.at[r], dst.at[r], sem.at[c]) for c, r in enumerate(parts)]

    first, second = loads(b_ref, b_tab, sem_b), loads(a_ref, a_tab, sem_a)
    for load in first + second:
        load.start()

    def picked(j, table):
        t = t_ref[j]
        return dot(quarter_indicator(t % PER_TILE, 1.0), table[:, tile_of(t)], 1, 1).astype(BF16)

    def up_body(j):
        up = picked(j, b_tab)
        for h in range(2):
            o_buf[j, :, up_half(h, fa, fb)] = up[h * HALF : (h + 1) * HALF]

    def down_body(j):
        down = picked(j, a_tab)
        for h in range(2):
            o_buf[j, :, down_half(h, fa, fb)] = down[h * HALF : (h + 1) * HALF]
        pltpu.make_async_copy(o_buf.at[j], o_ref.at[j], sem_o.at[j]).start()

    def finish(j):
        pltpu.make_async_copy(o_buf.at[j], o_ref.at[j], sem_o.at[j]).wait()

    for load in first:
        load.wait()
    each(n, up_body)
    for load in second:
        load.wait()
    each(n, down_body)
    each(n, finish)


def block_kernel(x_ref, g_ref, extra_ref, r_ref, o_ref, wa_ref, wb_ref):
    n = r_ref.shape[0]
    fa, fb = x_ref.shape[1] // n, g_ref.shape[1] // n
    for d in range(n):
        for h in range(2):
            rank = slice(h * HALF, (h + 1) * HALF)
            wb_ref[rank, d * fb : (d + 1) * fb] = r_ref[d, :, up_half(h, fa, fb)]
            wa_ref[rank, d * fa : (d + 1) * fa] = r_ref[d, :, down_half(h, fa, fb)]
    down = dot(wa_ref[...], x_ref[...], 1, 1).astype(BF16)
    back = dot(wb_ref[...], g_ref[...], 1, 1).astype(BF16)
    up_part = dot(down, g_ref[...], 1, 0).astype(BF16)
    down_part = dot(back, x_ref[...], 1, 0).astype(BF16)
    for d in range(n):
        for h in range(2):
            rank = slice(h * HALF, (h + 1) * HALF)
            o_ref[d, :, up_half(h, fa, fb)] = up_part[rank, d * fb : (d + 1) * fb]
            o_ref[d, :, down_half(h, fa, fb)] = down_part[rank, d * fa : (d + 1) * fa]
        o_ref[d, :, o_ref.shape[2] - LANES :] = extra_ref[d]


def sum_by_tenant(t_ref, part_ref, cut, fa, fb, grad_ref):
    grad_ref[...] = jnp.zeros_like(grad_ref)

    def body(j):
        t = t_ref[j]
        part = jnp.concatenate([part_ref[j, :, cut(h, fa, fb)] for h in range(2)], axis=0)
        place = quarter_indicator(t % PER_TILE, adapter_scale)
        grad_ref[:, tile_of(t)] += dot(part, place, 0, 0)

    each(t_ref.shape[0], body)


def updated(table_ref, grad_ref):
    return (table_ref[...].astype(F32) - learning_rate * grad_ref[...]).astype(BF16)


def fold_rows(product, tenant):
    rows = product.shape[0]
    lane = lax.broadcasted_iota(jnp.int32, (rows, LANES), 1)
    total = jnp.zeros((rows, LANES), F32)
    for c in range(TENANTS // PER_TILE):
        mine = tenant == c * PER_TILE + lane // RANK
        total = total + jnp.where(mine, product[:, c * LANES : (c + 1) * LANES], 0.0)
    half = total + pltpu.roll(total, 2 * RANK, 1)
    return half + pltpu.roll(half, RANK, 1)


def share_kernel(fb, t_ref, part_ref, a_ref, o_ref, u_ref, grad_ref):
    n, fa = part_ref.shape[0], a_ref.shape[0]
    pieces = -(-fa // LANES)
    sum_by_tenant(t_ref, part_ref, down_half, fa, fb, grad_ref)
    ride = [part_ref[d, :, part_ref.shape[2] - LANES :].astype(F32) for d in range(n)]

    def gathered(p):
        return jnp.concatenate([e[p * ROWS_DEV : (p + 1) * ROWS_DEV] for e in ride], axis=0)

    h_cols = jnp.concatenate([gathered(p) for p in range(pieces)], axis=1)[:, :fa].astype(BF16)
    tenant = gathered(pieces).astype(jnp.int32)
    u_ref[...] = tenant
    full = fold_rows(dot(h_cols, updated(a_ref, grad_ref), 1, 0), tenant)
    quarter = full.shape[0] // PER_TILE
    spot = lax.broadcasted_iota(jnp.int32, (quarter, LANES), 1) // RANK
    packed = jnp.zeros((quarter, LANES), F32)
    for q in range(PER_TILE):
        packed = packed + jnp.where(spot == q, full[q * quarter : (q + 1) * quarter], 0.0)
    o_ref[...] = packed


def up_kernel(fa, t_ref, part_ref, b_ref, grad_ref, new_ref):
    sum_by_tenant(t_ref, part_ref, up_half, fa, b_ref.shape[0], grad_ref)
    new_ref[...] = updated(b_ref, grad_ref)


def down_kernel(fb, t_ref, part_ref, grad_ref):
    sum_by_tenant(t_ref, part_ref, down_half, grad_ref.shape[0], fb, grad_ref)


def delta_kernel(shares, me_ref, u_ref, new_ref, *refs):
    p_refs, o_refs, term = refs[:shares], refs[shares:-1], refs[-1]
    total = p_refs[0][...]
    for p_ref in p_refs[1:]:
        total = total + p_ref[...]
    spot = lax.broadcasted_iota(jnp.int32, total.shape, 1) // RANK
    pieces = []
    for q in range(PER_TILE):
        one = jnp.where(spot == q, total, 0.0)
        half = one + pltpu.roll(one, 2 * RANK, 1)
        pieces.append(half + pltpu.roll(half, RANK, 1))
    adapted = jnp.concatenate(pieces, axis=0)
    lane = lax.broadcasted_iota(jnp.int32, adapted.shape, 1)
    tenant = u_ref[...]
    spread = jnp.concatenate(
        [
            jnp.where(tenant == c * PER_TILE + lane // RANK, adapted, 0.0).astype(BF16)
            for c in range(TENANTS // PER_TILE)
        ],
        axis=1,
    )
    delta = adapter_scale * dot(spread, new_ref[...], 1, 1)
    dest = o_refs[0] if len(o_refs) == 1 else term
    for d in range(dest.shape[0]):
        dest[d] = delta[d * ROWS_DEV : (d + 1) * ROWS_DEV]
    if len(o_refs) > 1:
        for s, o_ref in enumerate(o_refs):
            o_ref[...] = term[me_ref[0] ^ s]


def attention_kernel(len_ref, me_ref, base_ref, k_ref, v_ref, *refs):
    delta_refs, o_ref, term = refs[:-2], refs[-2], refs[-1]
    n = term.shape[0]
    if len(delta_refs) == 1:
        term[...] = delta_refs[0][...]
    else:
        for s in range(n):
            term[me_ref[0] ^ s] = delta_refs[s][...]
    delta = jnp.concatenate([term[d] for d in range(n)], axis=1)
    query = (base_ref[...] + delta).astype(BF16).astype(F32)
    group = HEADS // KV_HEADS
    cache = k_ref.shape[1]
    many = group * ROWS_DEV
    row_p = lax.broadcasted_iota(jnp.int32, (many, cache), 0) % ROWS_DEV
    row_d = lax.broadcasted_iota(jnp.int32, (many, HEAD_DIM), 0) % ROWS_DEV
    position = lax.broadcasted_iota(jnp.int32, (many, cache), 1)
    length = jnp.zeros((many, cache), jnp.int32)
    for r in range(ROWS_DEV):
        length = jnp.where(row_p == r, len_ref[r], length)
    live = position < length
    outs = []
    for g in range(KV_HEADS):
        cols = slice(g * HEAD_DIM, (g + 1) * HEAD_DIM)
        heads = jnp.concatenate(
            [query[:, (g * group + i) * HEAD_DIM : (g * group + i + 1) * HEAD_DIM] for i in range(group)],
            axis=0,
        ).astype(BF16)
        scores = jnp.zeros((many, cache), F32)
        for r in range(ROWS_DEV):
            scores = jnp.where(row_p == r, dot(heads, k_ref[r, :, cols], 1, 1), scores)
        scores = scores / jnp.sqrt(F32(HEAD_DIM))
        scores = jnp.where(live, scores, F32(-1e30))
        top = jnp.max(scores, axis=-1, keepdims=True)
        expo = jnp.where(live, jnp.exp(scores - top), 0.0)
        weights = (expo / jnp.sum(expo, axis=-1, keepdims=True)).astype(BF16)
        mixed = jnp.zeros((many, HEAD_DIM), F32)
        for r in range(ROWS_DEV):
            mixed = jnp.where(row_d == r, dot(weights, v_ref[r, :, cols], 1, 0), mixed)
        outs.extend(mixed[i * ROWS_DEV : (i + 1) * ROWS_DEV] for i in range(group))
    o_ref[...] = jnp.concatenate(outs, axis=1).astype(BF16)


def exchange(x):
    return lax.all_to_all(x, "wide", split_axis=0, concat_axis=0, tiled=True)


def partner(x, mask):
    return lax.ppermute(x, "wide", [(i, i ^ mask) for i in range(lax.axis_size("wide"))])


def per_device(
    tokens,
    query_output_gradient,
    down_factors,
    up_factors_transposed,
    tenant_of_block,
    device_tenant_list,
    row_list_entry,
    hidden,
    base_query_rows,
    cached_key_rows,
    cached_value_rows,
    live_cache_length,
):
    n = lax.axis_size("wide")
    me = lax.axis_index("wide").astype(jnp.int32)[None]
    direct = n == 16
    fa, cols = down_factors.shape
    fb = up_factors_transposed.shape[0]
    local_rows = hidden.shape[0]
    rows = local_rows * n
    width = tokens.shape[1]
    features = query_output_gradient.shape[1]
    pieces = -(-fa // LANES)
    assert tokens.shape[0] == BLOCK and tenant_of_block.shape[0] == n and local_rows * (pieces + 1) <= HALF

    shape = (n, HALF, 2 * (fa + fb))
    chunks = 4 if fa % 64 == 0 and fb % 64 == 0 else 1
    packed = call(
        pick_kernel,
        jax.ShapeDtypeStruct(shape, BF16),
        [smem(), hbm(), hbm()],
        hbm(),
        scratch=[
            pltpu.VMEM(up_factors_transposed.shape, BF16),
            pltpu.VMEM(down_factors.shape, BF16),
            pltpu.VMEM(shape, BF16),
            pltpu.SemaphoreType.DMA((chunks,)),
            pltpu.SemaphoreType.DMA((chunks,)),
            pltpu.SemaphoreType.DMA((n,)),
        ],
        flops=2 * RANK * LANES * n * (fa + fb),
        nbytes=2 * cols * (fa + fb),
        limit=ALL_VMEM,
    )(tenant_of_block, up_factors_transposed, down_factors)
    got = exchange(packed)

    slot = row_list_entry[:, None] == jnp.arange(device_tenant_list.shape[1], dtype=jnp.int32)[None, :]
    row_tenant = jnp.sum(jnp.where(slot, device_tenant_list, 0), axis=1)
    slices = jnp.pad(hidden.reshape(local_rows, n, fa), ((0, 0), (0, 0), (0, pieces * LANES - fa)))
    slices = slices.reshape(local_rows, n, pieces, LANES).transpose(1, 2, 0, 3).reshape(n, pieces * local_rows, LANES)
    marks = jnp.broadcast_to(row_tenant.astype(BF16)[None, :, None], (n, local_rows, LANES))
    extra = jnp.concatenate([slices, marks], axis=1)
    extra = jnp.pad(extra, ((0, 0), (0, HALF - extra.shape[1]), (0, 0)))

    parts = call(
        block_kernel,
        jax.ShapeDtypeStruct((n, HALF, -(-2 * (fa + fb) // LANES) * LANES + LANES), BF16),
        [vmem()] * 4,
        vmem(),
        scratch=[pltpu.VMEM((RANK, width), BF16), pltpu.VMEM((RANK, features), BF16)],
        flops=4 * RANK * BLOCK * n * (fa + fb),
        nbytes=2 * BLOCK * n * (fa + fb),
    )(tokens, query_output_gradient, extra, got)
    parts = exchange(parts)

    low_rank, tenants = call(
        functools.partial(share_kernel, fb),
        [
            jax.ShapeDtypeStruct((rows // PER_TILE, LANES), F32),
            jax.ShapeDtypeStruct((rows, LANES), jnp.int32),
        ],
        [smem(), vmem(), vmem()],
        [vmem()] * 2,
        scratch=[pltpu.VMEM((fa, cols), F32)],
        flops=2 * rows * fa * cols,
        nbytes=2 * cols * fa,
    )(tenant_of_block, parts, down_factors)
    if direct:
        low_rank = low_rank + partner(low_rank, 1)
        low_rank = [low_rank] + [partner(low_rank, 2 * s) for s in range(1, n // 2)]
    else:
        low_rank = [lax.psum(low_rank, "wide")]

    up_gradient, new_up = call(
        functools.partial(up_kernel, fa),
        [jax.ShapeDtypeStruct((fb, cols), F32), jax.ShapeDtypeStruct((fb, cols), BF16)],
        [smem(), vmem(), vmem()],
        [vmem()] * 2,
        flops=2 * n * RANK * fb * LANES,
        nbytes=8 * cols * fb,
    )(tenant_of_block, parts, up_factors_transposed)
    if direct:
        shapes = [jax.ShapeDtypeStruct((local_rows, fb), F32)] * n
    else:
        shapes = [jax.ShapeDtypeStruct((n, local_rows, fb), F32)]
    delta = call(
        functools.partial(delta_kernel, len(low_rank)),
        shapes,
        [smem()] + [vmem()] * (2 + len(low_rank)),
        [vmem()] * len(shapes),
        scratch=[pltpu.VMEM((n, local_rows, fb), F32)],
        flops=2 * rows * cols * fb,
        nbytes=2 * cols * fb,
    )(me, tenants, new_up, *low_rank)
    if direct:
        delta = [partner(d, s) if s else d for s, d in enumerate(delta)]
    else:
        delta = [exchange(delta[0])]

    down_gradient = call(
        functools.partial(down_kernel, fb),
        jax.ShapeDtypeStruct((fa, cols), F32),
        [smem(), vmem()],
        vmem(),
        flops=2 * n * RANK * fa * LANES,
        nbytes=4 * cols * fa,
    )(tenant_of_block, parts)
    attended = call(
        attention_kernel,
        jax.ShapeDtypeStruct((local_rows, HEADS * HEAD_DIM), BF16),
        [smem(), smem()] + [vmem()] * (3 + len(delta)),
        vmem(),
        scratch=[pltpu.VMEM((n, local_rows, fb), F32)],
        flops=4 * HEADS * local_rows * cached_key_rows.shape[1] * HEAD_DIM,
        nbytes=4 * cached_key_rows.size,
    )(live_cache_length, me, base_query_rows.astype(F32), cached_key_rows, cached_value_rows, *delta)
    return down_gradient, up_gradient, attended


def solution(mesh):
    placed = (
        P(("groups", "wide"), None),
        P(("groups", "wide"), None),
        P("wide", "groups"),
        P("wide", "groups"),
        P("groups"),
        P(("groups", "wide"), None),
        P(("groups", "wide")),
        P(("groups", "wide"), None),
        P(("groups", "wide"), None),
        P(("groups", "wide"), None, None),
        P(("groups", "wide"), None, None),
        P(("groups", "wide")),
    )
    return jax.shard_map(
        per_device,
        mesh=mesh,
        in_specs=placed,
        out_specs=(P("wide", "groups"), P("wide", "groups"), P(("groups", "wide"), None)),
        check_vma=False,
    )
```

time: 94.4 us -> 99.1 us (1.050)
  blocking collectives: 0 us -> 22.6 us
  waiting for transfers between devices: 38.4 us -> 16.6 us
  starting transfers between devices: 25.8 us -> 39.7 us
  local copies, waits for them, and re-layouts: 5.98 us -> 1.51 us
  Pallas kernels: 21.4 us -> 17.1 us
    ppermute x0 -> x23, starting transfers between devices: none -> 32.3 us  [partner(): lax.ppermute(x, 'wide', [(i, i ^ mask) for i in range(lax.axis_size('wide...]
    all_to_all x6 -> x1, waiting for transfers between devices: 38.4 us -> 15 us  [exchange(): return lax.all_to_all(x, 'wide', split_axis=0, concat_axis=0, tiled=True)]
    all_to_all x0 -> x1, blocking collectives: none -> 22.6 us  [exchange(): return lax.all_to_all(x, 'wide', split_axis=0, concat_axis=0, tiled=True)]
    all_to_all x6 -> x1, starting transfers between devices: 25.8 us -> 7.4 us  [exchange(): return lax.all_to_all(x, 'wide', split_axis=0, concat_axis=0, tiled=True)]
    pallas_call x8 -> x6, Pallas kernels: 18.6 us -> 14.2 us  [the longest x1 4.17 us: per_device(): call(pick_kernel, jax.ShapeDtypeStruct(shape, BF16), [smem(), hbm(), hbm(...]
    unnamed x35 -> x24, local copies, waits for them, and re-layouts: 4.88 us -> 1.27 us
    ppermute x0 -> x23, waiting for transfers between devices: none -> 1.66 us  [partner(): lax.ppermute(x, 'wide', [(i, i ^ mask) for i in range(lax.axis_size('wide...]
  transfers between devices with their start and end apart: 6 -> 24, of which waited for: 6 -> 3; matrix products, arithmetic and copies ran while one was open for 2% -> 1% of each run, Pallas kernels for 16% -> 6%
where the time goes in v4:
time: 99.1 us; the launch traced here: 98.7 us
  starting transfers between devices  39.7 us (40%)
  blocking collectives  22.6 us (23%)
  Pallas kernels  17.1 us (17%)
  waiting for transfers between devices  16.6 us (17%)
  local copies, waits for them, and re-layouts  1.51 us (2%)
    ppermute x23, starting transfers between devices, partner(): lax.ppermute(x, 'wide', [(i, i ^ mask) for i in range(lax.axis_size('wide...  32.3 us
    all_to_all x1, blocking collectives, exchange(): return lax.all_to_all(x, 'wide', split_axis=0, concat_axis=0, tiled=True)  22.6 us
    all_to_all x1, waiting for transfers between devices, exchange(): return lax.all_to_all(x, 'wide', split_axis=0, concat_axis=0, tiled=True)  15 us
    all_to_all x1, starting transfers between devices, exchange(): return lax.all_to_all(x, 'wide', split_axis=0, concat_axis=0, tiled=True)  7.4 us
    pallas_call x1, Pallas kernels, per_device(): call(pick_kernel, jax.ShapeDtypeStruct(shape, BF16), [smem(), hbm(), hbm(...  4.17 us
    pallas_call x1, Pallas kernels, per_device(): call(functools.partial(down_kernel, fb), jax.ShapeDtypeStruct((fa, cols),...  3.05 us
    pallas_call x1, Pallas kernels, per_device(): call(attention_kernel, jax.ShapeDtypeStruct((local_rows, HEADS * HEAD_DIM...  2.88 us
    pallas_call x1, Pallas kernels, per_device(): call(functools.partial(up_kernel, fa), [jax.ShapeDtypeStruct((fb, cols),...  2.73 us
  transfers between devices with their start and end apart: 24, of which 3 were waited for; matrix products, arithmetic and copies ran while one was open for 1% of the time, Pallas kernels for 6%

profile of v4, /device:TPU:0, one launch (start us, length us, event | category | flops | bytes accessed | tf_op | source)
XLA Modules:
  0.0 98.7 jit_solution(12283203167677316349)
XLA Ops:
  0.7 4.2 %shard_map.139 = bf16[16,16,1152]{2,1,0:T(8,128)(2,1)} custom-call(s32[16]{0:T(128)} %t_ref.7, bf16[256,2048]{1,0:T(8,128)(2,1)} %b_ref.3, bf16[320,2048]{1,0:T(8,128)(2,1)} %a_ref.3), custom_call_target="tpu_custom_call" | custom-call | flops 75497472 | bytes 2359296 | tf_op jit(solution)/shard_map/pallas_call | solution.py:311
  4.8 7.4 %all-to-all-start = ((bf16[16,16,1152]{2,1,0:T(8,128)(2,1)}), bf16[16,16,1152]{2,1,0:T(8,128)(2,1)S(1)}, u32[]{:S(2)}, u32[]{:S(2)}) async-start(bf16[16,16,1152]{2,1,0:T(8,128)(2,1)} %shard_map.139), calls=%async_computation | async-start | bytes 1179648 | tf_op jit(solution)/shard_map/all_to_all | solution.py:276
  12.8 15.0 %all-to-all-done.r_ref = bf16[16,16,1152]{2,1,0:T(8,128)(2,1)S(1)} async-done(((bf16[16,16,1152]{2,1,0:T(8,128)(2,1)}), bf16[16,16,1152]{2,1,0:T(8,128)(2,1)S(1)}, u32[]{:S(2)}, u32[]{:S(2)}) %all-to-all-start) | async-done | bytes 589856 | tf_op jit(solution)/shard_map/all_to_all | solution.py:276
  27.8 1.2 %copy-done.3 = bf16[128,4096]{1,0:T(8,128)(2,1)S(1)} copy-done((bf16[128,4096]{1,0:T(8,128)(2,1)S(1)}, bf16[128,4096]{1,0:T(8,128)(2,1)}, u32[]{:S(2)}) %copy-start.3) | copy-done | bytes 1048600
  29.0 1.4 %shard_map.140 = bf16[16,16,1280]{2,1,0:T(8,128)(2,1)S(1)} custom-call(bf16[128,5120]{1,0:T(8,128)(2,1)S(1)} %copy-done.2, bf16[128,4096]{1,0:T(8,128)(2,1)S(1)} %copy-done.3, bf16[16,16,128]{2,1,0:T(8,128)(2,1)S(1)} %pad_maximum_fusion.extra_ref, bf16[16,16,1152]{2,1,0:T(8,128)(2,1)S(1)} %all-to-all-done.r_ref), custom_call_target="tpu_custom_call" | custom-call | flops 150994944 | bytes 2359296 | tf_op jit(solution)/shard_map/pallas_call | solution.py:338
  30.4 22.6 %all_to_all.10.part_ref = bf16[16,16,1280]{2,1,0:T(8,128)(2,1)S(1)} all-to-all(bf16[16,16,1280]{2,1,0:T(8,128)(2,1)S(1)} %shard_map.140), channel_id=1, replica_groups=mesh['groups'=2,'wide'=16] {'wide'}, dimensions={0} | all-to-all | bytes 1310720 | tf_op jit(solution)/shard_map/all_to_all | solution.py:276
  53.0 2.3 %shard_map.143 = (f32[16,128]{1,0:T(8,128)S(1)}, s32[64,128]{1,0:T(8,128)S(1)}) custom-call(s32[16]{0:T(128)S(1)} %copy-done.6, bf16[16,16,1280]{2,1,0:T(8,128)(2,1)S(1)} %all_to_all.10.part_ref, bf16[320,2048]{1,0:T(8,128)(2,1)S(1)} %copy-done), custom_call_target="tpu_custom_call" | custom-call | flops 83886080 | bytes 1310720 | tf_op jit(solution)/shard_map/pallas_call | solution.py:349
  58.1 2.0 %collective-permute-start.3 = (f32[16,128]{1,0:T(8,128)S(1)}, f32[16,128]{1,0:T(8,128)S(1)}, u32[]{:S(2)}, u32[]{:S(2)}) collective-permute-start(f32[16,128]{1,0:T(8,128)S(1)} %add.5.refs_0_), channel_id=1, source_target_pairs={{0,6},{1,7},{2,4},{3,5},{4,2},{5,3},{6,0},{7,1},{8,14},{9,15},{10,... | collective-permute-start | bytes 24584 | tf_op jit(solution)/shard_map/ppermute | solution.py:280
  60.1 1.3 %collective-permute-start.4 = (f32[16,128]{1,0:T(8,128)S(1)}, f32[16,128]{1,0:T(8,128)S(1)}, u32[]{:S(2)}, u32[]{:S(2)}) collective-permute-start(f32[16,128]{1,0:T(8,128)S(1)} %add.5.refs_0_), channel_id=1, source_target_pairs={{0,8},{1,9},{2,10},{3,11},{4,12},{5,13},{6,14},{7,15},{8,0},{9,1},... | collective-permute-start | bytes 24584 | tf_op jit(solution)/shard_map/ppermute | solution.py:280
  61.4 1.8 %collective-permute-start.5 = (f32[16,128]{1,0:T(8,128)S(1)}, f32[16,128]{1,0:T(8,128)S(1)}, u32[]{:S(2)}, u32[]{:S(2)}) collective-permute-start(f32[16,128]{1,0:T(8,128)S(1)} %add.5.refs_0_), channel_id=1, source_target_pairs={{0,10},{1,11},{2,8},{3,9},{4,14},{5,15},{6,12},{7,13},{8,2},{9,3},... | collective-permute-start | bytes 24584 | tf_op jit(solution)/shard_map/ppermute | solution.py:280
  63.2 1.7 %collective-permute-start.6 = (f32[16,128]{1,0:T(8,128)S(1)}, f32[16,128]{1,0:T(8,128)S(1)}, u32[]{:S(2)}, u32[]{:S(2)}) collective-permute-start(f32[16,128]{1,0:T(8,128)S(1)} %add.5.refs_0_), channel_id=1, source_target_pairs={{0,12},{1,13},{2,14},{3,15},{4,8},{5,9},{6,10},{7,11},{8,4},{9,5},... | collective-permute-start | bytes 24584 | tf_op jit(solution)/shard_map/ppermute | solution.py:280
  64.9 2.8 %collective-permute-start.7 = (f32[16,128]{1,0:T(8,128)S(1)}, f32[16,128]{1,0:T(8,128)S(1)}, u32[]{:S(2)}, u32[]{:S(2)}) collective-permute-start(f32[16,128]{1,0:T(8,128)S(1)} %add.5.refs_0_), channel_id=1, source_target_pairs={{0,14},{1,15},{2,12},{3,13},{4,10},{5,11},{6,8},{7,9},{8,6},{9,7},... | collective-permute-start | bytes 24584 | tf_op jit(solution)/shard_map/ppermute | solution.py:280
  67.8 2.7 %shard_map.142 = (f32[256,2048]{1,0:T(8,128)}, bf16[256,2048]{1,0:T(8,128)(2,1)S(1)}) custom-call(s32[16]{0:T(128)S(1)} %copy-done.6, bf16[16,16,1280]{2,1,0:T(8,128)(2,1)S(1)} %all_to_all.10.part_ref, bf16[256,2048]{1,0:T(8,128)(2,1)S(1)} %copy-done.1), custom_call_target="tpu_custom_call" | custom-call | flops 33554432 | bytes 4194304 | tf_op jit(solution)/shard_map/pallas_call | solution.py:367
  72.0 2.5 %collective-permute-start.12 = (f32[4,256]{1,0:T(4,128)S(1)}, f32[4,256]{1,0:T(4,128)S(1)}, u32[]{:S(2)}, u32[]{:S(2)}) collective-permute-start(f32[4,256]{1,0:T(4,128)S(1)} %get-tuple-element.32), channel_id=1, source_target_pairs={{0,5},{1,4},{2,7},{3,6},{4,1},{5,0},{6,3},{7,2},{8,13},{9,12},{10,... | collective-permute-start | bytes 12296 | tf_op jit(solution)/shard_map/ppermute | solution.py:280
  75.1 1.2 %collective-permute-start.14 = (f32[4,256]{1,0:T(4,128)S(1)}, f32[4,256]{1,0:T(4,128)S(1)}, u32[]{:S(2)}, u32[]{:S(2)}) collective-permute-start(f32[4,256]{1,0:T(4,128)S(1)} %get-tuple-element.34), channel_id=1, source_target_pairs={{0,7},{1,6},{2,5},{3,4},{4,3},{5,2},{6,1},{7,0},{8,15},{9,14},{10,... | collective-permute-start | bytes 12296 | tf_op jit(solution)/shard_map/ppermute | solution.py:280
  76.4 1.6 %collective-permute-start.15 = (f32[4,256]{1,0:T(4,128)S(1)}, f32[4,256]{1,0:T(4,128)S(1)}, u32[]{:S(2)}, u32[]{:S(2)}) collective-permute-start(f32[4,256]{1,0:T(4,128)S(1)} %get-tuple-element.35), channel_id=1, source_target_pairs={{0,8},{1,9},{2,10},{3,11},{4,12},{5,13},{6,14},{7,15},{8,0},{9,1},... | collective-permute-start | bytes 12296 | tf_op jit(solution)/shard_map/ppermute | solution.py:280
  78.0 1.8 %collective-permute-start.16 = (f32[4,256]{1,0:T(4,128)S(1)}, f32[4,256]{1,0:T(4,128)S(1)}, u32[]{:S(2)}, u32[]{:S(2)}) collective-permute-start(f32[4,256]{1,0:T(4,128)S(1)} %get-tuple-element.36), channel_id=1, source_target_pairs={{0,9},{1,8},{2,11},{3,10},{4,13},{5,12},{6,15},{7,14},{8,1},{9,0},... | collective-permute-start | bytes 12296 | tf_op jit(solution)/shard_map/ppermute | solution.py:280
  79.8 1.3 %collective-permute-start.17 = (f32[4,256]{1,0:T(4,128)S(1)}, f32[4,256]{1,0:T(4,128)S(1)}, u32[]{:S(2)}, u32[]{:S(2)}) collective-permute-start(f32[4,256]{1,0:T(4,128)S(1)} %get-tuple-element.37), channel_id=1, source_target_pairs={{0,10},{1,11},{2,8},{3,9},{4,14},{5,15},{6,12},{7,13},{8,2},{9,3},... | collective-permute-start | bytes 12296 | tf_op jit(solution)/shard_map/ppermute | solution.py:280
  81.1 1.5 %collective-permute-start.18 = (f32[4,256]{1,0:T(4,128)S(1)}, f32[4,256]{1,0:T(4,128)S(1)}, u32[]{:S(2)}, u32[]{:S(2)}) collective-permute-start(f32[4,256]{1,0:T(4,128)S(1)} %get-tuple-element.38), channel_id=1, source_target_pairs={{0,11},{1,10},{2,9},{3,8},{4,15},{5,14},{6,13},{7,12},{8,3},{9,2},... | collective-permute-start | bytes 12296 | tf_op jit(solution)/shard_map/ppermute | solution.py:280
  82.6 2.1 %collective-permute-start.19 = (f32[4,256]{1,0:T(4,128)S(1)}, f32[4,256]{1,0:T(4,128)S(1)}, u32[]{:S(2)}, u32[]{:S(2)}) collective-permute-start(f32[4,256]{1,0:T(4,128)S(1)} %get-tuple-element.39), channel_id=1, source_target_pairs={{0,12},{1,13},{2,14},{3,15},{4,8},{5,9},{6,10},{7,11},{8,4},{9,5},... | collective-permute-start | bytes 12296 | tf_op jit(solution)/shard_map/ppermute | solution.py:280
  84.7 2.2 %collective-permute-start.20 = (f32[4,256]{1,0:T(4,128)S(1)}, f32[4,256]{1,0:T(4,128)S(1)}, u32[]{:S(2)}, u32[]{:S(2)}) collective-permute-start(f32[4,256]{1,0:T(4,128)S(1)} %get-tuple-element.40), channel_id=1, source_target_pairs={{0,13},{1,12},{2,15},{3,14},{4,9},{5,8},{6,11},{7,10},{8,5},{9,4},... | collective-permute-start | bytes 12296 | tf_op jit(solution)/shard_map/ppermute | solution.py:280
  87.0 2.5 %collective-permute-start.21 = (f32[4,256]{1,0:T(4,128)S(1)}, f32[4,256]{1,0:T(4,128)S(1)}, u32[]{:S(2)}, u32[]{:S(2)}) collective-permute-start(f32[4,256]{1,0:T(4,128)S(1)} %get-tuple-element.41), channel_id=1, source_target_pairs={{0,14},{1,15},{2,12},{3,13},{4,10},{5,11},{6,8},{7,9},{8,6},{9,7},... | collective-permute-start | bytes 12296 | tf_op jit(solution)/shard_map/ppermute | solution.py:280
  92.7 3.0 %shard_map.141 = f32[320,2048]{1,0:T(8,128)} custom-call(s32[16]{0:T(128)S(1)} %copy-done.6, bf16[16,16,1280]{2,1,0:T(8,128)(2,1)S(1)} %all_to_all.10.part_ref), custom_call_target="tpu_custom_call" | custom-call | flops 41943040 | bytes 2621440 | tf_op jit(solution)/shard_map/pallas_call | solution.py:393
  95.8 2.9 %shard_map.145 = bf16[4,4096]{1,0:T(4,128)(2,1)} custom-call(s32[4]{0:T(128)S(1)} %copy-done.7, s32[1]{0:T(128)} %bitcast.3.me_ref, f32[4,4096]{1,0:T(4,128)S(1)} %convert_element_type.13.base_ref, bf16[4,256,512]{2,1,0:T(8,128)(2,1)S(1)} %copy-done.4, bf16[4,256,512]{2,1,0:T(8,128)(2,1)S(1)} %copy-done.5, f32[4,256]{1,0:T(4,128)S(1)} %get-tuple-element.27.refs_0_, ...), custom_call_target="tpu_custom_call" | custom-call | flops 16777216 | bytes 2097152 | tf_op jit(solution)/shard_map/pallas_call | solution.py:401
  (67 shorter events, 8.8 us)
Async XLA Ops:
  4.8 23.0 %all-to-all-start = ((bf16[16,16,1152]{2,1,0:T(8,128)(2,1)}), bf16[16,16,1152]{2,1,0:T(8,128)(2,1)S(1)}, u32[]{:S(2)}, u32[]{:S(2)}) async-start(bf16[16,16,1152]{2,1,0:T(8,128)(2,1)} %shard_map.139), calls=%async_computation | async-start | bytes 1179648 | tf_op jit(solution)/shard_map/all_to_all | solution.py:276
  55.4 1.2 %collective-permute-start = (f32[16,128]{1,0:T(8,128)S(1)}, f32[16,128]{1,0:T(8,128)S(1)}, u32[]{:S(2)}, u32[]{:S(2)}) collective-permute-start(f32[16,128]{1,0:T(8,128)S(1)} %get-tuple-element.26), channel_id=1, source_target_pairs={{0,1},{1,0},{2,3},{3,2},{4,5},{5,4},{6,7},{7,6},{8,9},{9,8},{10,11... | collective-permute-start | bytes 24584 | tf_op jit(solution)/shard_map/ppermute | solution.py:280
  56.6 6.6 %collective-permute-start.1 = (f32[16,128]{1,0:T(8,128)S(1)}, f32[16,128]{1,0:T(8,128)S(1)}, u32[]{:S(2)}, u32[]{:S(2)}) collective-permute-start(f32[16,128]{1,0:T(8,128)S(1)} %add.5.refs_0_), channel_id=1, source_target_pairs={{0,2},{1,3},{2,0},{3,1},{4,6},{5,7},{6,4},{7,5},{8,10},{9,11},{10,... | collective-permute-start | bytes 24584 | tf_op jit(solution)/shard_map/ppermute | solution.py:280
  57.4 7.6 %collective-permute-start.2 = (f32[16,128]{1,0:T(8,128)S(1)}, f32[16,128]{1,0:T(8,128)S(1)}, u32[]{:S(2)}, u32[]{:S(2)}) collective-permute-start(f32[16,128]{1,0:T(8,128)S(1)} %add.5.refs_0_), channel_id=1, source_target_pairs={{0,4},{1,5},{2,6},{3,7},{4,0},{5,1},{6,2},{7,3},{8,12},{9,13},{10,... | collective-permute-start | bytes 24584 | tf_op jit(solution)/shard_map/ppermute | solution.py:280
  58.1 12.3 %collective-permute-start.3 = (f32[16,128]{1,0:T(8,128)S(1)}, f32[16,128]{1,0:T(8,128)S(1)}, u32[]{:S(2)}, u32[]{:S(2)}) collective-permute-start(f32[16,128]{1,0:T(8,128)S(1)} %add.5.refs_0_), channel_id=1, source_target_pairs={{0,6},{1,7},{2,4},{3,5},{4,2},{5,3},{6,0},{7,1},{8,14},{9,15},{10,... | collective-permute-start | bytes 24584 | tf_op jit(solution)/shard_map/ppermute | solution.py:280
  60.1 10.4 %collective-permute-start.4 = (f32[16,128]{1,0:T(8,128)S(1)}, f32[16,128]{1,0:T(8,128)S(1)}, u32[]{:S(2)}, u32[]{:S(2)}) collective-permute-start(f32[16,128]{1,0:T(8,128)S(1)} %add.5.refs_0_), channel_id=1, source_target_pairs={{0,8},{1,9},{2,10},{3,11},{4,12},{5,13},{6,14},{7,15},{8,0},{9,1},... | collective-permute-start | bytes 24584 | tf_op jit(solution)/shard_map/ppermute | solution.py:280
  61.4 9.1 %collective-permute-start.5 = (f32[16,128]{1,0:T(8,128)S(1)}, f32[16,128]{1,0:T(8,128)S(1)}, u32[]{:S(2)}, u32[]{:S(2)}) collective-permute-start(f32[16,128]{1,0:T(8,128)S(1)} %add.5.refs_0_), channel_id=1, source_target_pairs={{0,10},{1,11},{2,8},{3,9},{4,14},{5,15},{6,12},{7,13},{8,2},{9,3},... | collective-permute-start | bytes 24584 | tf_op jit(solution)/shard_map/ppermute | solution.py:280
  63.2 7.3 %collective-permute-start.6 = (f32[16,128]{1,0:T(8,128)S(1)}, f32[16,128]{1,0:T(8,128)S(1)}, u32[]{:S(2)}, u32[]{:S(2)}) collective-permute-start(f32[16,128]{1,0:T(8,128)S(1)} %add.5.refs_0_), channel_id=1, source_target_pairs={{0,12},{1,13},{2,14},{3,15},{4,8},{5,9},{6,10},{7,11},{8,4},{9,5},... | collective-permute-start | bytes 24584 | tf_op jit(solution)/shard_map/ppermute | solution.py:280
  64.9 6.3 %collective-permute-start.7 = (f32[16,128]{1,0:T(8,128)S(1)}, f32[16,128]{1,0:T(8,128)S(1)}, u32[]{:S(2)}, u32[]{:S(2)}) collective-permute-start(f32[16,128]{1,0:T(8,128)S(1)} %add.5.refs_0_), channel_id=1, source_target_pairs={{0,14},{1,15},{2,12},{3,13},{4,10},{5,11},{6,8},{7,9},{8,6},{9,7},... | collective-permute-start | bytes 24584 | tf_op jit(solution)/shard_map/ppermute | solution.py:280
  71.8 4.5 %collective-permute-start.10 = (f32[4,256]{1,0:T(4,128)S(1)}, f32[4,256]{1,0:T(4,128)S(1)}, u32[]{:S(2)}, u32[]{:S(2)}) collective-permute-start(f32[4,256]{1,0:T(4,128)S(1)} %get-tuple-element.30), channel_id=1, source_target_pairs={{0,3},{1,2},{2,1},{3,0},{4,7},{5,6},{6,5},{7,4},{8,11},{9,10},{10,... | collective-permute-start | bytes 12296 | tf_op jit(solution)/shard_map/ppermute | solution.py:280
  71.9 6.1 %collective-permute-start.11 = (f32[4,256]{1,0:T(4,128)S(1)}, f32[4,256]{1,0:T(4,128)S(1)}, u32[]{:S(2)}, u32[]{:S(2)}) collective-permute-start(f32[4,256]{1,0:T(4,128)S(1)} %get-tuple-element.31), channel_id=1, source_target_pairs={{0,4},{1,5},{2,6},{3,7},{4,0},{5,1},{6,2},{7,3},{8,12},{9,13},{10,... | collective-permute-start | bytes 12296 | tf_op jit(solution)/shard_map/ppermute | solution.py:280
  72.0 7.8 %collective-permute-start.12 = (f32[4,256]{1,0:T(4,128)S(1)}, f32[4,256]{1,0:T(4,128)S(1)}, u32[]{:S(2)}, u32[]{:S(2)}) collective-permute-start(f32[4,256]{1,0:T(4,128)S(1)} %get-tuple-element.32), channel_id=1, source_target_pairs={{0,5},{1,4},{2,7},{3,6},{4,1},{5,0},{6,3},{7,2},{8,13},{9,12},{10,... | collective-permute-start | bytes 12296 | tf_op jit(solution)/shard_map/ppermute | solution.py:280
  74.5 6.6 %collective-permute-start.13 = (f32[4,256]{1,0:T(4,128)S(1)}, f32[4,256]{1,0:T(4,128)S(1)}, u32[]{:S(2)}, u32[]{:S(2)}) collective-permute-start(f32[4,256]{1,0:T(4,128)S(1)} %get-tuple-element.33), channel_id=1, source_target_pairs={{0,6},{1,7},{2,4},{3,5},{4,2},{5,3},{6,0},{7,1},{8,14},{9,15},{10,... | collective-permute-start | bytes 12296 | tf_op jit(solution)/shard_map/ppermute | solution.py:280
  75.1 7.4 %collective-permute-start.14 = (f32[4,256]{1,0:T(4,128)S(1)}, f32[4,256]{1,0:T(4,128)S(1)}, u32[]{:S(2)}, u32[]{:S(2)}) collective-permute-start(f32[4,256]{1,0:T(4,128)S(1)} %get-tuple-element.34), channel_id=1, source_target_pairs={{0,7},{1,6},{2,5},{3,4},{4,3},{5,2},{6,1},{7,0},{8,15},{9,14},{10,... | collective-permute-start | bytes 12296 | tf_op jit(solution)/shard_map/ppermute | solution.py:280
  76.4 8.3 %collective-permute-start.15 = (f32[4,256]{1,0:T(4,128)S(1)}, f32[4,256]{1,0:T(4,128)S(1)}, u32[]{:S(2)}, u32[]{:S(2)}) collective-permute-start(f32[4,256]{1,0:T(4,128)S(1)} %get-tuple-element.35), channel_id=1, source_target_pairs={{0,8},{1,9},{2,10},{3,11},{4,12},{5,13},{6,14},{7,15},{8,0},{9,1},... | collective-permute-start | bytes 12296 | tf_op jit(solution)/shard_map/ppermute | solution.py:280
  78.0 9.0 %collective-permute-start.16 = (f32[4,256]{1,0:T(4,128)S(1)}, f32[4,256]{1,0:T(4,128)S(1)}, u32[]{:S(2)}, u32[]{:S(2)}) collective-permute-start(f32[4,256]{1,0:T(4,128)S(1)} %get-tuple-element.36), channel_id=1, source_target_pairs={{0,9},{1,8},{2,11},{3,10},{4,13},{5,12},{6,15},{7,14},{8,1},{9,0},... | collective-permute-start | bytes 12296 | tf_op jit(solution)/shard_map/ppermute | solution.py:280
  79.8 9.7 %collective-permute-start.17 = (f32[4,256]{1,0:T(4,128)S(1)}, f32[4,256]{1,0:T(4,128)S(1)}, u32[]{:S(2)}, u32[]{:S(2)}) collective-permute-start(f32[4,256]{1,0:T(4,128)S(1)} %get-tuple-element.37), channel_id=1, source_target_pairs={{0,10},{1,11},{2,8},{3,9},{4,14},{5,15},{6,12},{7,13},{8,2},{9,3},... | collective-permute-start | bytes 12296 | tf_op jit(solution)/shard_map/ppermute | solution.py:280
  81.1 9.6 %collective-permute-start.18 = (f32[4,256]{1,0:T(4,128)S(1)}, f32[4,256]{1,0:T(4,128)S(1)}, u32[]{:S(2)}, u32[]{:S(2)}) collective-permute-start(f32[4,256]{1,0:T(4,128)S(1)} %get-tuple-element.38), channel_id=1, source_target_pairs={{0,11},{1,10},{2,9},{3,8},{4,15},{5,14},{6,13},{7,12},{8,3},{9,2},... | collective-permute-start | bytes 12296 | tf_op jit(solution)/shard_map/ppermute | solution.py:280
  82.6 9.2 %collective-permute-start.19 = (f32[4,256]{1,0:T(4,128)S(1)}, f32[4,256]{1,0:T(4,128)S(1)}, u32[]{:S(2)}, u32[]{:S(2)}) collective-permute-start(f32[4,256]{1,0:T(4,128)S(1)} %get-tuple-element.39), channel_id=1, source_target_pairs={{0,12},{1,13},{2,14},{3,15},{4,8},{5,9},{6,10},{7,11},{8,4},{9,5},... | collective-permute-start | bytes 12296 | tf_op jit(solution)/shard_map/ppermute | solution.py:280
  84.7 11.1 %collective-permute-start.20 = (f32[4,256]{1,0:T(4,128)S(1)}, f32[4,256]{1,0:T(4,128)S(1)}, u32[]{:S(2)}, u32[]{:S(2)}) collective-permute-start(f32[4,256]{1,0:T(4,128)S(1)} %get-tuple-element.40), channel_id=1, source_target_pairs={{0,13},{1,12},{2,15},{3,14},{4,9},{5,8},{6,11},{7,10},{8,5},{9,4},... | collective-permute-start | bytes 12296 | tf_op jit(solution)/shard_map/ppermute | solution.py:280
  87.0 8.8 %collective-permute-start.21 = (f32[4,256]{1,0:T(4,128)S(1)}, f32[4,256]{1,0:T(4,128)S(1)}, u32[]{:S(2)}, u32[]{:S(2)}) collective-permute-start(f32[4,256]{1,0:T(4,128)S(1)} %get-tuple-element.41), channel_id=1, source_target_pairs={{0,14},{1,15},{2,12},{3,13},{4,10},{5,11},{6,8},{7,9},{8,6},{9,7},... | collective-permute-start | bytes 12296 | tf_op jit(solution)/shard_map/ppermute | solution.py:280
  89.4 6.4 %collective-permute-start.22 = (f32[4,256]{1,0:T(4,128)S(1)}, f32[4,256]{1,0:T(4,128)S(1)}, u32[]{:S(2)}, u32[]{:S(2)}) collective-permute-start(f32[4,256]{1,0:T(4,128)S(1)} %get-tuple-element.42), channel_id=1, source_target_pairs={{0,15},{1,14},{2,13},{3,12},{4,11},{5,10},{6,9},{7,8},{8,7},{9,6},... | collective-permute-start | bytes 12296 | tf_op jit(solution)/shard_map/ppermute | solution.py:280
  90.7 5.1 %collective-permute-start.8 = (f32[4,256]{1,0:T(4,128)S(1)}, f32[4,256]{1,0:T(4,128)S(1)}, u32[]{:S(2)}, u32[]{:S(2)}) collective-permute-start(f32[4,256]{1,0:T(4,128)S(1)} %get-tuple-element.28), channel_id=1, source_target_pairs={{0,1},{1,0},{2,3},{3,2},{4,5},{5,4},{6,7},{7,6},{8,9},{9,8},{10,11... | collective-permute-start | bytes 12296 | tf_op jit(solution)/shard_map/ppermute | solution.py:280
  91.8 4.0 %collective-permute-start.9 = (f32[4,256]{1,0:T(4,128)S(1)}, f32[4,256]{1,0:T(4,128)S(1)}, u32[]{:S(2)}, u32[]{:S(2)}) collective-permute-start(f32[4,256]{1,0:T(4,128)S(1)} %get-tuple-element.29), channel_id=1, source_target_pairs={{0,2},{1,3},{2,0},{3,1},{4,6},{5,7},{6,4},{7,5},{8,10},{9,11},{10,... | collective-permute-start | bytes 12296 | tf_op jit(solution)/shard_map/ppermute | solution.py:280
  (12 other events, 270.5 us)

commit v5 on v4

--- a/solution.py
+++ b/solution.py
@@ -73,6 +73,7 @@
 
 
 HALF = RANK // 2
+CHUNKS = HALF // ROWS_DEV
 
 
 def up_half(h, fa, fb):
@@ -123,40 +124,15 @@
     each(n, finish)
 
 
-def block_kernel(x_ref, g_ref, extra_ref, r_ref, o_ref, wa_ref, wb_ref):
-    n = r_ref.shape[0]
-    fa, fb = x_ref.shape[1] // n, g_ref.shape[1] // n
-    for d in range(n):
-        for h in range(2):
-            rank = slice(h * HALF, (h + 1) * HALF)
-            wb_ref[rank, d * fb : (d + 1) * fb] = r_ref[d, :, up_half(h, fa, fb)]
-            wa_ref[rank, d * fa : (d + 1) * fa] = r_ref[d, :, down_half(h, fa, fb)]
-    down = dot(wa_ref[...], x_ref[...], 1, 1).astype(BF16)
-    back = dot(wb_ref[...], g_ref[...], 1, 1).astype(BF16)
-    up_part = dot(down, g_ref[...], 1, 0).astype(BF16)
-    down_part = dot(back, x_ref[...], 1, 0).astype(BF16)
-    for d in range(n):
-        for h in range(2):
-            rank = slice(h * HALF, (h + 1) * HALF)
-            o_ref[d, :, up_half(h, fa, fb)] = up_part[rank, d * fb : (d + 1) * fb]
-            o_ref[d, :, down_half(h, fa, fb)] = down_part[rank, d * fa : (d + 1) * fa]
-        o_ref[d, :, o_ref.shape[2] - LANES :] = extra_ref[d]
-
-
-def sum_by_tenant(t_ref, part_ref, cut, fa, fb, grad_ref):
-    grad_ref[...] = jnp.zeros_like(grad_ref)
-
-    def body(j):
-        t = t_ref[j]
-        part = jnp.concatenate([part_ref[j, :, cut(h, fa, fb)] for h in range(2)], axis=0)
-        place = quarter_indicator(t % PER_TILE, adapter_scale)
-        grad_ref[:, tile_of(t)] += dot(part, place, 0, 0)
-
-    each(t_ref.shape[0], body)
-
-
-def updated(table_ref, grad_ref):
-    return (table_ref[...].astype(F32) - learning_rate * grad_ref[...]).astype(BF16)
+def rows_pack_kernel(list_ref, slot_ref, hidden_ref, o_ref):
+    hidden = hidden_ref[...].astype(F32)
+    size = hidden.shape[1] // CHUNKS
+    main = jnp.concatenate([hidden[:, p * size : (p + 1) * size] for p in range(CHUNKS)], axis=0)
+    row = lax.broadcasted_iota(jnp.int32, (HALF, LANES), 0) % ROWS_DEV
+    mark = jnp.zeros((HALF, LANES), jnp.int32)
+    for r in range(ROWS_DEV):
+        mark = jnp.where(row == r, list_ref[0, slot_ref[r]], mark)
+    o_ref[...] = jnp.concatenate([main, mark.astype(F32)], axis=1).astype(BF16)
 
 
 def fold_rows(product, tenant):
@@ -170,41 +146,109 @@
     return half + pltpu.roll(half, RANK, 1)
 
 
-def share_kernel(fb, t_ref, part_ref, a_ref, o_ref, u_ref, grad_ref):
-    n, fa = part_ref.shape[0], a_ref.shape[0]
-    pieces = -(-fa // LANES)
-    sum_by_tenant(t_ref, part_ref, down_half, fa, fb, grad_ref)
-    ride = [part_ref[d, :, part_ref.shape[2] - LANES :].astype(F32) for d in range(n)]
-
-    def gathered(p):
-        return jnp.concatenate([e[p * ROWS_DEV : (p + 1) * ROWS_DEV] for e in ride], axis=0)
-
-    h_cols = jnp.concatenate([gathered(p) for p in range(pieces)], axis=1)[:, :fa].astype(BF16)
-    tenant = gathered(pieces).astype(jnp.int32)
-    u_ref[...] = tenant
-    full = fold_rows(dot(h_cols, updated(a_ref, grad_ref), 1, 0), tenant)
+def rows_kernel(masks, me_ref, h0_ref, h1_ref, x_ref, a_ref, hx_ref, base_ref, u_ref, sel, sx, sb, su):
+    tiles = len(masks)
+    h = jnp.concatenate([r[k] for r in (h0_ref, h1_ref) for k in range(tiles // 2)], axis=0)
+    size = h.shape[1] - LANES
+    fa = a_ref.shape[0]
+    part = lax.broadcasted_iota(jnp.int32, (h.shape[0], LANES), 0) % HALF // ROWS_DEV
+    hx = jnp.zeros((h.shape[0], LANES), F32)
+    for p in range(CHUNKS):
+        hx = jnp.where(part == p, dot(h[:, :size], x_ref[:, p * size : (p + 1) * size], 1, 1), hx)
+    per_chunk = size // fa
+    for m in range(per_chunk):
+
+        @pl.when(me_ref[0] % per_chunk == m)
+        def _():
+            sel[...] = h[:, m * fa : (m + 1) * fa]
+
+    tenant = h[:, size:].astype(F32).astype(jnp.int32)
+    base = fold_rows(dot(sel[...], a_ref[...], 1, 0), tenant)
+    base = jnp.where(part == me_ref[0] // per_chunk, base, 0.0)
+    for k, mask in enumerate(masks):
+        d = me_ref[0] ^ mask
+        for value, dest in ((hx, sx), (base, sb)):
+            eight = value[k * HALF : k * HALF + 8] + value[k * HALF + 8 : (k + 1) * HALF]
+            dest[d] = eight[:ROWS_DEV] + eight[ROWS_DEV:]
+        su[d] = tenant[k * HALF : k * HALF + ROWS_DEV]
+    for src, dest in ((sx, hx_ref), (sb, base_ref), (su, u_ref)):
+        dest[...] = jnp.concatenate([src[d] for d in range(tiles)], axis=0)
+
+
+def plain_rows_kernel(h_ref, x_ref, a_ref, hc_ref, u_ref, hx_ref, base_ref):
+    hx_ref[...] = dot(h_ref[...], x_ref[...], 1, 1)
+    base_ref[...] = fold_rows(dot(hc_ref[...], a_ref[...], 1, 0), u_ref[...])
+
+
+def block_kernel(ride, t_ref, x_ref, g_ref, hx_ref, base_ref, u_ref, r_ref, o_ref, *refs):
+    wa_ref, wb_ref = refs[-2:]
+    n = r_ref.shape[0]
+    fa, fb = x_ref.shape[1] // n, g_ref.shape[1] // n
+    for d in range(n):
+        for h in range(2):
+            rank = slice(h * HALF, (h + 1) * HALF)
+            wb_ref[rank, d * fb : (d + 1) * fb] = r_ref[d, :, up_half(h, fa, fb)]
+            wa_ref[rank, d * fa : (d + 1) * fa] = r_ref[d, :, down_half(h, fa, fb)]
+    back = dot(wb_ref[...], g_ref[...], 1, 1).astype(BF16)
+    down = dot(wa_ref[...], x_ref[...], 1, 1).astype(BF16)
+
+    hx = hx_ref[...]
+    high = hx.astype(BF16)
+    low = (hx - high.astype(F32)).astype(BF16)
+    wide_back = jnp.concatenate([back] * PER_TILE, axis=0)
+    change = dot(high, wide_back, 1, 1) + dot(low, wide_back, 1, 1)
+    mine = u_ref[...] == t_ref[0]
+    full = base_ref[...] - jnp.where(mine, learning_rate * (adapter_scale * change), 0.0)
     quarter = full.shape[0] // PER_TILE
     spot = lax.broadcasted_iota(jnp.int32, (quarter, LANES), 1) // RANK
     packed = jnp.zeros((quarter, LANES), F32)
     for q in range(PER_TILE):
         packed = packed + jnp.where(spot == q, full[q * quarter : (q + 1) * quarter], 0.0)
-    o_ref[...] = packed
-
-
-def up_kernel(fa, t_ref, part_ref, b_ref, grad_ref, new_ref):
-    sum_by_tenant(t_ref, part_ref, up_half, fa, b_ref.shape[0], grad_ref)
-    new_ref[...] = updated(b_ref, grad_ref)
-
-
-def down_kernel(fb, t_ref, part_ref, grad_ref):
-    sum_by_tenant(t_ref, part_ref, down_half, grad_ref.shape[0], fb, grad_ref)
-
-
-def delta_kernel(shares, me_ref, u_ref, new_ref, *refs):
-    p_refs, o_refs, term = refs[:shares], refs[shares:-1], refs[-1]
-    total = p_refs[0][...]
-    for p_ref in p_refs[1:]:
-        total = total + p_ref[...]
+    if not ride:
+        refs[0][...] = packed
+
+    down_part = dot(back, x_ref[...], 1, 0).astype(BF16)
+    up_part = dot(down, g_ref[...], 1, 0).astype(BF16)
+    for d in range(n):
+        for h in range(2):
+            rank = slice(h * HALF, (h + 1) * HALF)
+            o_ref[d, :, up_half(h, fa, fb)] = up_part[rank, d * fb : (d + 1) * fb]
+            o_ref[d, :, down_half(h, fa, fb)] = down_part[rank, d * fa : (d + 1) * fa]
+        if ride:
+            o_ref[d, :, 2 * (fa + fb) :] = packed.astype(BF16)
+
+
+def sum_by_tenant(t_ref, part_ref, cut, fa, fb, grad_ref):
+    grad_ref[...] = jnp.zeros_like(grad_ref)
+
+    def body(j):
+        t = t_ref[j]
+        part = jnp.concatenate([part_ref[j, :, cut(h, fa, fb)] for h in range(2)], axis=0)
+        place = quarter_indicator(t % PER_TILE, adapter_scale)
+        grad_ref[:, tile_of(t)] += dot(part, place, 0, 0)
+
+    each(t_ref.shape[0], body)
+
+
+def updated(table_ref, grad_ref):
+    return (table_ref[...].astype(F32) - learning_rate * grad_ref[...]).astype(BF16)
+
+
+def gradient_kernel(t_ref, part_ref, down_ref, up_ref):
+    fa, fb = down_ref.shape[0], up_ref.shape[0]
+    sum_by_tenant(t_ref, part_ref, down_half, fa, fb, down_ref)
+    sum_by_tenant(t_ref, part_ref, up_half, fa, fb, up_ref)
+
+
+def delta_kernel(fa, t_ref, part_ref, b_ref, u_ref, *refs):
+    o_ref, grad_ref = refs[-2:]
+    n, fb = part_ref.shape[0], b_ref.shape[0]
+    if len(refs) == 3:
+        total = refs[0][...]
+    else:
+        total = part_ref[0, :, 2 * (fa + fb) :].astype(F32)
+        for d in range(1, n):
+            total = total + part_ref[d, :, 2 * (fa + fb) :].astype(F32)
     spot = lax.broadcasted_iota(jnp.int32, total.shape, 1) // RANK
     pieces = []
     for q in range(PER_TILE):
@@ -221,24 +265,15 @@
         ],
         axis=1,
     )
-    delta = adapter_scale * dot(spread, new_ref[...], 1, 1)
-    dest = o_refs[0] if len(o_refs) == 1 else term
-    for d in range(dest.shape[0]):
-        dest[d] = delta[d * ROWS_DEV : (d + 1) * ROWS_DEV]
-    if len(o_refs) > 1:
-        for s, o_ref in enumerate(o_refs):
-            o_ref[...] = term[me_ref[0] ^ s]
-
-
-def attention_kernel(len_ref, me_ref, base_ref, k_ref, v_ref, *refs):
-    delta_refs, o_ref, term = refs[:-2], refs[-2], refs[-1]
-    n = term.shape[0]
-    if len(delta_refs) == 1:
-        term[...] = delta_refs[0][...]
-    else:
-        for s in range(n):
-            term[me_ref[0] ^ s] = delta_refs[s][...]
-    delta = jnp.concatenate([term[d] for d in range(n)], axis=1)
+    sum_by_tenant(t_ref, part_ref, up_half, fa, fb, grad_ref)
+    delta = adapter_scale * dot(spread, updated(b_ref, grad_ref), 1, 1)
+    for d in range(n):
+        o_ref[d] = delta[d * ROWS_DEV : (d + 1) * ROWS_DEV]
+
+
+def attention_kernel(len_ref, delta_ref, base_ref, k_ref, v_ref, o_ref):
+    n = delta_ref.shape[0]
+    delta = jnp.concatenate([delta_ref[d] for d in range(n)], axis=1)
     query = (base_ref[...] + delta).astype(BF16).astype(F32)
     group = HEADS // KV_HEADS
     cache = k_ref.shape[1]
@@ -295,16 +330,16 @@
     live_cache_length,
 ):
     n = lax.axis_size("wide")
-    me = lax.axis_index("wide").astype(jnp.int32)[None]
-    direct = n == 16
+    me = lax.axis_index("wide").astype(jnp.int32)
+    small = n == 16
     fa, cols = down_factors.shape
     fb = up_factors_transposed.shape[0]
     local_rows = hidden.shape[0]
     rows = local_rows * n
+    quarter = rows // PER_TILE
     width = tokens.shape[1]
     features = query_output_gradient.shape[1]
-    pieces = -(-fa // LANES)
-    assert tokens.shape[0] == BLOCK and tenant_of_block.shape[0] == n and local_rows * (pieces + 1) <= HALF
+    assert tokens.shape[0] == BLOCK and tenant_of_block.shape[0] == n
 
     shape = (n, HALF, 2 * (fa + fb))
     chunks = 4 if fa % 64 == 0 and fb % 64 == 0 else 1
@@ -325,88 +360,96 @@
         nbytes=2 * cols * (fa + fb),
         limit=ALL_VMEM,
     )(tenant_of_block, up_factors_transposed, down_factors)
-    got = exchange(packed)
-
-    slot = row_list_entry[:, None] == jnp.arange(device_tenant_list.shape[1], dtype=jnp.int32)[None, :]
-    row_tenant = jnp.sum(jnp.where(slot, device_tenant_list, 0), axis=1)
-    slices = jnp.pad(hidden.reshape(local_rows, n, fa), ((0, 0), (0, 0), (0, pieces * LANES - fa)))
-    slices = slices.reshape(local_rows, n, pieces, LANES).transpose(1, 2, 0, 3).reshape(n, pieces * local_rows, LANES)
-    marks = jnp.broadcast_to(row_tenant.astype(BF16)[None, :, None], (n, local_rows, LANES))
-    extra = jnp.concatenate([slices, marks], axis=1)
-    extra = jnp.pad(extra, ((0, 0), (0, HALF - extra.shape[1]), (0, 0)))
-
+
+    if small:
+        held = call(
+            rows_pack_kernel,
+            jax.ShapeDtypeStruct((HALF, width // CHUNKS + LANES), BF16),
+            [smem(), smem(), vmem()],
+            vmem(),
+            nbytes=4 * local_rows * width,
+        )(device_tenant_list, row_list_entry, hidden)[None]
+        held = jnp.concatenate([held, partner(held, n // 2)], axis=0)
+        held, packed = lax.optimization_barrier((held, packed))
+        got = exchange(packed)
+        masks = [0, n // 2]
+        bit = n // 4
+        while bit > 1:
+            held = jnp.concatenate([held, partner(held, bit)], axis=0)
+            masks = masks + [m ^ bit for m in masks]
+            bit //= 2
+        masks = masks + [m ^ 1 for m in masks]
+        shapes = [(rows, BLOCK, F32), (rows, LANES, F32), (rows, LANES, jnp.int32)]
+        hx, base_low_rank, tenants = call(
+            functools.partial(rows_kernel, masks),
+            [jax.ShapeDtypeStruct((r, c), t) for r, c, t in shapes],
+            [smem()] + [vmem()] * 4,
+            [vmem()] * 3,
+            scratch=[
+                pltpu.VMEM((n * HALF, fa), BF16),
+                pltpu.VMEM((n, local_rows, LANES), F32),
+                pltpu.VMEM((n, local_rows, LANES), F32),
+                pltpu.VMEM((n, local_rows, LANES), jnp.int32),
+            ],
+            flops=8 * rows * BLOCK * width + 8 * rows * fa * cols,
+            nbytes=2 * BLOCK * width + 2 * fa * cols,
+        )(me[None], held, partner(held, 1), tokens, down_factors)
+    else:
+        got = exchange(packed)
+        slot = row_list_entry[:, None] == jnp.arange(device_tenant_list.shape[1], dtype=jnp.int32)[None, :]
+        row_tenant = jnp.sum(jnp.where(slot, device_tenant_list, 0), axis=1)
+        everyone = lax.all_gather(hidden, "wide", axis=0, tiled=True)
+        tenants = lax.all_gather(row_tenant, "wide", axis=0, tiled=True)
+        tenants = jnp.broadcast_to(tenants[:, None], (rows, LANES))
+        hx, base_low_rank = call(
+            plain_rows_kernel,
+            [jax.ShapeDtypeStruct((rows, BLOCK), F32), jax.ShapeDtypeStruct((rows, LANES), F32)],
+            [vmem()] * 5,
+            [vmem()] * 2,
+        )(everyone, tokens, down_factors, lax.dynamic_slice(everyone, (0, me * fa), (rows, fa)), tenants)
+
+    part_shape = (n, HALF, 2 * (fa + fb) + (LANES if small else 0))
+    my_tenant = lax.dynamic_slice(tenant_of_block, (me,), (1,))
     parts = call(
-        block_kernel,
-        jax.ShapeDtypeStruct((n, HALF, -(-2 * (fa + fb) // LANES) * LANES + LANES), BF16),
-        [vmem()] * 4,
-        vmem(),
+        functools.partial(block_kernel, small),
+        [jax.ShapeDtypeStruct(part_shape, BF16)]
+        + ([] if small else [jax.ShapeDtypeStruct((quarter, LANES), F32)]),
+        [smem()] + [vmem()] * 6,
+        [vmem()] * (1 if small else 2),
         scratch=[pltpu.VMEM((RANK, width), BF16), pltpu.VMEM((RANK, features), BF16)],
         flops=4 * RANK * BLOCK * n * (fa + fb),
         nbytes=2 * BLOCK * n * (fa + fb),
-    )(tokens, query_output_gradient, extra, got)
-    parts = exchange(parts)
-
-    low_rank, tenants = call(
-        functools.partial(share_kernel, fb),
-        [
-            jax.ShapeDtypeStruct((rows // PER_TILE, LANES), F32),
-            jax.ShapeDtypeStruct((rows, LANES), jnp.int32),
-        ],
-        [smem(), vmem(), vmem()],
-        [vmem()] * 2,
-        scratch=[pltpu.VMEM((fa, cols), F32)],
-        flops=2 * rows * fa * cols,
-        nbytes=2 * cols * fa,
-    )(tenant_of_block, parts, down_factors)
-    if direct:
-        low_rank = low_rank + partner(low_rank, 1)
-        low_rank = [low_rank] + [partner(low_rank, 2 * s) for s in range(1, n // 2)]
-    else:
-        low_rank = [lax.psum(low_rank, "wide")]
-
-    up_gradient, new_up = call(
-        functools.partial(up_kernel, fa),
-        [jax.ShapeDtypeStruct((fb, cols), F32), jax.ShapeDtypeStruct((fb, cols), BF16)],
-        [smem(), vmem(), vmem()],
-        [vmem()] * 2,
-        flops=2 * n * RANK * fb * LANES,
-        nbytes=8 * cols * fb,
-    )(tenant_of_block, parts, up_factors_transposed)
-    if direct:
-        shapes = [jax.ShapeDtypeStruct((local_rows, fb), F32)] * n
-    else:
-        shapes = [jax.ShapeDtypeStruct((n, local_rows, fb), F32)]
+    )(my_tenant, tokens, query_output_gradient, hx, base_low_rank, tenants, got)
+    low_rank = [lax.psum(p, "wide") for p in parts[1:]]
+    parts = exchange(parts[0])
+
     delta = call(
-        functools.partial(delta_kernel, len(low_rank)),
-        shapes,
-        [smem()] + [vmem()] * (2 + len(low_rank)),
-        [vmem()] * len(shapes),
-        scratch=[pltpu.VMEM((n, local_rows, fb), F32)],
+        functools.partial(delta_kernel, fa),
+        jax.ShapeDtypeStruct((n, local_rows, fb), F32),
+        [smem()] + [vmem()] * (3 + len(low_rank)),
+        vmem(),
+        scratch=[pltpu.VMEM((fb, cols), F32)],
         flops=2 * rows * cols * fb,
         nbytes=2 * cols * fb,
-    )(me, tenants, new_up, *low_rank)
-    if direct:
-        delta = [partner(d, s) if s else d for s, d in enumerate(delta)]
-    else:
-        delta = [exchange(delta[0])]
-
-    down_gradient = call(
-        functools.partial(down_kernel, fb),
-        jax.ShapeDtypeStruct((fa, cols), F32),
+    )(tenant_of_block, parts, up_factors_transposed, tenants, *low_rank)
+    delta = exchange(delta)
+
+    down_gradient, up_gradient = call(
+        gradient_kernel,
+        [jax.ShapeDtypeStruct((fa, cols), F32), jax.ShapeDtypeStruct((fb, cols), F32)],
         [smem(), vmem()],
-        vmem(),
-        flops=2 * n * RANK * fa * LANES,
-        nbytes=4 * cols * fa,
+        [vmem()] * 2,
+        flops=2 * n * RANK * (fa + fb) * LANES,
+        nbytes=4 * cols * (fa + fb),
     )(tenant_of_block, parts)
     attended = call(
         attention_kernel,
         jax.ShapeDtypeStruct((local_rows, HEADS * HEAD_DIM), BF16),
-        [smem(), smem()] + [vmem()] * (3 + len(delta)),
+        [smem(), vmem(), vmem(), vmem(), vmem()],
         vmem(),
-        scratch=[pltpu.VMEM((n, local_rows, fb), F32)],
         flops=4 * HEADS * local_rows * cached_key_rows.shape[1] * HEAD_DIM,
         nbytes=4 * cached_key_rows.size,
-    )(live_cache_length, me, base_query_rows.astype(F32), cached_key_rows, cached_value_rows, *delta)
+    )(live_cache_length, delta, base_query_rows.astype(F32), cached_key_rows, cached_value_rows)
     return down_gradient, up_gradient, attended
 
 

time: 99.1 us -> 78.6 us (0.79)
  starting transfers between devices: 39.7 us -> 14.8 us
  local copies, waits for them, and re-layouts: 1.51 us -> 6.9 us
  waiting for transfers between devices: 16.6 us -> 13.1 us
  Pallas kernels: 17.1 us -> 18.7 us
  blocking collectives: 22.6 us -> 23.6 us
    ppermute x23 -> x4, starting transfers between devices: 32.3 us -> 7.73 us  [partner(): lax.ppermute(x, 'wide', [(i, i ^ mask) for i in range(lax.axis_size('wide...]
    all_to_all x1 -> x2, waiting for transfers between devices: 15 us -> 2.63 us  [exchange(): return lax.all_to_all(x, 'wide', split_axis=0, concat_axis=0, tiled=True)]
    ppermute x23 -> x4, waiting for transfers between devices: 1.66 us -> 10.5 us  [partner(): lax.ppermute(x, 'wide', [(i, i ^ mask) for i in range(lax.axis_size('wide...]
    unnamed x24 -> x28, local copies, waits for them, and re-layouts: 1.27 us -> 5.62 us
    pallas_call x5, Pallas kernels: 10 us -> 11.8 us  [the longest x1 4.2 us: per_device(): call(gradient_kernel, [jax.ShapeDtypeStruct((fa, cols), F32), jax.ShapeDt...]
    all_to_all x1, blocking collectives: 22.6 us -> 23.6 us  [exchange(): return lax.all_to_all(x, 'wide', split_axis=0, concat_axis=0, tiled=True)]
    all_to_all x1 -> x2, starting transfers between devices: 7.4 us -> 7.09 us  [exchange(): return lax.all_to_all(x, 'wide', split_axis=0, concat_axis=0, tiled=True)]
  transfers between devices with their start and end apart: 24 -> 6, of which waited for: 3 -> 3; matrix products, arithmetic and copies ran while one was open for 1% -> 3% of each run, Pallas kernels for 6% -> 14%
where the time goes in v5:
time: 78.6 us; the launch traced here: 78.1 us
  blocking collectives  23.6 us (30%)
  Pallas kernels  18.7 us (24%)
  starting transfers between devices  14.8 us (19%)
  waiting for transfers between devices  13.1 us (17%)
  local copies, waits for them, and re-layouts  6.9 us (9%)
  between operations  0.82 us (1%)
    all_to_all x1, blocking collectives, exchange(): return lax.all_to_all(x, 'wide', split_axis=0, concat_axis=0, tiled=True)  23.6 us
    ppermute x4, waiting for transfers between devices, partner(): lax.ppermute(x, 'wide', [(i, i ^ mask) for i in range(lax.axis_size('wide...  10.5 us
    ppermute x4, starting transfers between devices, partner(): lax.ppermute(x, 'wide', [(i, i ^ mask) for i in range(lax.axis_size('wide...  7.73 us
    all_to_all x2, starting transfers between devices, exchange(): return lax.all_to_all(x, 'wide', split_axis=0, concat_axis=0, tiled=True)  7.09 us
    unnamed x28, local copies, waits for them, and re-layouts  5.62 us
    pallas_call x1, Pallas kernels, per_device(): call(gradient_kernel, [jax.ShapeDtypeStruct((fa, cols), F32), jax.ShapeDt...  4.2 us
    pallas_call x1, Pallas kernels, per_device(): call(pick_kernel, jax.ShapeDtypeStruct(shape, BF16), [smem(), hbm(), hbm(...  4.03 us
    pallas_call x1, Pallas kernels, per_device(): call(attention_kernel, jax.ShapeDtypeStruct((local_rows, HEADS * HEAD_DIM...  2.87 us
  transfers between devices with their start and end apart: 6, of which 3 were waited for; matrix products, arithmetic and copies ran while one was open for 3% of the time, Pallas kernels for 14%

profile of v5, /device:TPU:0, one launch (start us, length us, event | category | flops | bytes accessed | tf_op | source)
XLA Modules:
  0.0 78.1 jit_solution(10515586786073721171)
XLA Ops:
  0.6 0.8 copy-done.7
  1.4 0.7 copy-done.9
  2.1 0.7 copy-done.10
  3.3 4.1 %collective-permute-start = (bf16[1,16,1408]{2,1,0:T(8,128)(2,1)S(1)}, bf16[1,16,1408]{2,1,0:T(8,128)(2,1)S(1)}, u32[]{:S(2)}, u32[]{:S(2)}) collective-permute-start(bf16[1,16,1408]{2,1,0:T(8,128)(2,1)S(1)} %bitcast.2), channel_id=1, source_target_pairs={{0,8},{1,9},{2,10},{3,11},{4,12},{5,13},{6,14},{7,15},{8,0},{9,1},... | collective-permute-start | bytes 135176 | tf_op jit(solution)/shard_map/ppermute | solution.py:315
  7.4 4.0 %shard_map.140 = bf16[16,16,1152]{2,1,0:T(8,128)(2,1)} custom-call(s32[16]{0:T(128)} %t_ref.5, bf16[256,2048]{1,0:T(8,128)(2,1)} %b_ref.3, bf16[320,2048]{1,0:T(8,128)(2,1)} %a_ref.3), custom_call_target="tpu_custom_call" | custom-call | flops 75497472 | bytes 2359296 | tf_op jit(solution)/shard_map/pallas_call | solution.py:346
  11.5 1.6 %collective-permute-start.1 = (bf16[2,16,1408]{2,1,0:T(8,128)(2,1)S(1)}, bf16[2,16,1408]{2,1,0:T(8,128)(2,1)S(1)}, u32[]{:S(2)}, u32[]{:S(2)}) collective-permute-start(bf16[2,16,1408]{2,1,0:T(8,128)(2,1)S(1)} %pad_maximum_fusion.1), channel_id=1, source_target_pairs={{0,4},{1,5},{2,6},{3,7},{4,0},{5,1},{6,2},{7,3},{8,12},{9,13},{10,... | collective-permute-start | bytes 270344 | tf_op jit(solution)/shard_map/ppermute | solution.py:315
  13.1 0.6 constant_dynamic-update-slice_fusion.2
  13.8 3.6 %all-to-all-start = ((bf16[16,16,1152]{2,1,0:T(8,128)(2,1)}), bf16[16,16,1152]{2,1,0:T(8,128)(2,1)S(1)}, u32[]{:S(2)}, u32[]{:S(2)}) async-start(bf16[16,16,1152]{2,1,0:T(8,128)(2,1)} %shard_map.140), calls=%async_computation | async-start | bytes 1179648 | tf_op jit(solution)/shard_map/all_to_all | solution.py:311
  17.4 2.0 %collective-permute-start.2 = (bf16[4,16,1408]{2,1,0:T(8,128)(2,1)S(1)}, bf16[4,16,1408]{2,1,0:T(8,128)(2,1)S(1)}, u32[]{:S(2)}, u32[]{:S(2)}) collective-permute-start(bf16[4,16,1408]{2,1,0:T(8,128)(2,1)S(1)} %pad_maximum_fusion), channel_id=1, source_target_pairs={{0,2},{1,3},{2,0},{3,1},{4,6},{5,7},{6,4},{7,5},{8,10},{9,11},{10,... | collective-permute-start | bytes 540680 | tf_op jit(solution)/shard_map/ppermute | solution.py:315
  19.4 0.6 constant_dynamic-update-slice_fusion.1
  20.1 9.1 %collective-permute-done.2 = bf16[4,16,1408]{2,1,0:T(8,128)(2,1)S(1)} collective-permute-done((bf16[4,16,1408]{2,1,0:T(8,128)(2,1)S(1)}, bf16[4,16,1408]{2,1,0:T(8,128)(2,1)S(1)}, u32[]{:S(2)}, u32[]{:S(2)}) %collective-permute-start.2) | collective-permute-done | bytes 180256 | tf_op jit(solution)/shard_map/ppermute | solution.py:315
  29.1 0.7 constant_dynamic-update-slice_fusion.h0_ref
  29.8 0.6 dynamic_slice.3.t_ref
  30.4 1.4 %collective-permute-done.3.h1_ref = bf16[8,16,1408]{2,1,0:T(8,128)(2,1)} collective-permute-done((bf16[8,16,1408]{2,1,0:T(8,128)(2,1)}, bf16[8,16,1408]{2,1,0:T(8,128)(2,1)}, u32[]{:S(2)}, u32[]{:S(2)}) %collective-permute-start.3) | collective-permute-done | bytes 360480 | tf_op jit(solution)/shard_map/ppermute | solution.py:315
  31.8 1.0 %copy-done.6 = bf16[8,16,1408]{2,1,0:T(8,128)(2,1)S(1)} copy-done((bf16[8,16,1408]{2,1,0:T(8,128)(2,1)S(1)}, bf16[8,16,1408]{2,1,0:T(8,128)(2,1)}, u32[]{:S(2)}) %copy-start.6) | copy-done | bytes 360472
  32.8 2.8 %shard_map.141 = (f32[64,128]{1,0:T(8,128)S(1)}, f32[64,128]{1,0:T(8,128)S(1)}, s32[64,128]{1,0:T(8,128)S(1)}) custom-call(s32[1]{0:T(128)} %bitcast.me_ref, bf16[8,16,1408]{2,1,0:T(8,128)(2,1)S(1)} %copy-done.6, bf16[8,16,1408]{2,1,0:T(8,128)(2,1)} %collective-permute-done.3.h1_ref, bf16[128,5120]{1,0:T(8,128)(2,1)S(1)} %copy-done.1, ...), custom_call_target="tpu_custom_call" | custom-call | flops 671088640 | bytes 2621440 | tf_op jit(solution)/shard_map/pallas_call | solution.py:383
  35.6 1.2 %copy-done.5 = bf16[128,4096]{1,0:T(8,128)(2,1)S(1)} copy-done((bf16[128,4096]{1,0:T(8,128)(2,1)S(1)}, bf16[128,4096]{1,0:T(8,128)(2,1)}, u32[]{:S(2)}) %copy-start.5) | copy-done | bytes 1048600
  36.9 1.9 %shard_map.142 = bf16[16,16,1280]{2,1,0:T(8,128)(2,1)S(1)} custom-call(s32[1]{0:T(128)} %dynamic_slice.3.t_ref, bf16[128,5120]{1,0:T(8,128)(2,1)S(1)} %copy-done.1, bf16[128,4096]{1,0:T(8,128)(2,1)S(1)} %copy-done.5, f32[64,128]{1,0:T(8,128)S(1)} %get-tuple-element.11.hx_ref, f32[64,128]{1,0:T(8,128)S(1)} %get-tuple-element.12.base_ref, ...), custom_call_target="tpu_custom_call" | custom-call | flops 150994944 | bytes 2359296 | tf_op jit(solution)/shard_map/pallas_call | solution.py:413
  38.8 23.6 %all_to_all.15.part_ref = bf16[16,16,1280]{2,1,0:T(8,128)(2,1)S(1)} all-to-all(bf16[16,16,1280]{2,1,0:T(8,128)(2,1)S(1)} %shard_map.142), channel_id=1, replica_groups=mesh['groups'=2,'wide'=16] {'wide'}, dimensions={0} | all-to-all | bytes 1310720 | tf_op jit(solution)/shard_map/all_to_all | solution.py:311
  62.4 2.4 %shard_map.144 = f32[16,4,256]{2,1,0:T(4,128)} custom-call(s32[16]{0:T(128)S(1)} %copy-done.8, bf16[16,16,1280]{2,1,0:T(8,128)(2,1)S(1)} %all_to_all.15.part_ref, bf16[256,2048]{1,0:T(8,128)(2,1)S(1)} %copy-done.2, s32[64,128]{1,0:T(8,128)S(1)} %get-tuple-element.13.u_ref), custom_call_target="tpu_custom_call" | custom-call | flops 67108864 | bytes 1048576 | tf_op jit(solution)/shard_map/pallas_call | solution.py:426
  64.8 3.5 %all-to-all-start.2 = ((f32[16,4,256]{2,1,0:T(4,128)}), f32[16,4,256]{2,1,0:T(4,128)S(1)}, u32[]{:S(2)}, u32[]{:S(2)}) async-start(f32[16,4,256]{2,1,0:T(4,128)} %shard_map.144), calls=%async_computation.2 | async-start | bytes 131072 | tf_op jit(solution)/shard_map/all_to_all | solution.py:311
  68.3 4.2 %shard_map.143 = (f32[320,2048]{1,0:T(8,128)}, f32[256,2048]{1,0:T(8,128)}) custom-call(s32[16]{0:T(128)S(1)} %copy-done.8, bf16[16,16,1280]{2,1,0:T(8,128)(2,1)S(1)} %all_to_all.15.part_ref), custom_call_target="tpu_custom_call" | custom-call | flops 75497472 | bytes 4718592 | tf_op jit(solution)/shard_map/pallas_call | solution.py:437
  72.5 2.6 %all-to-all-done.2.delta_ref = f32[16,4,256]{2,1,0:T(4,128)S(1)} async-done(((f32[16,4,256]{2,1,0:T(4,128)}), f32[16,4,256]{2,1,0:T(4,128)S(1)}, u32[]{:S(2)}, u32[]{:S(2)}) %all-to-all-start.2) | async-done | bytes 65568 | tf_op jit(solution)/shard_map/all_to_all | solution.py:311
  75.2 2.9 %shard_map.145 = bf16[4,4096]{1,0:T(4,128)(2,1)} custom-call(s32[4]{0:T(128)S(1)} %copy-done.11, f32[16,4,256]{2,1,0:T(4,128)S(1)} %all-to-all-done.2.delta_ref, f32[4,4096]{1,0:T(4,128)S(1)} %convert_element_type.3.base_ref, bf16[4,256,512]{2,1,0:T(8,128)(2,1)S(1)} %copy-done.3, bf16[4,256,512]{2,1,0:T(8,128)(2,1)S(1)} %copy-done.4), custom_call_target="tpu_custom_call" | custom-call | flops 16777216 | bytes 2097152 | tf_op jit(solution)/shard_map/pallas_call | solution.py:445
  (29 shorter events, 0.7 us)
Async XLA Ops:
  0.6 0.8 copy-start.7
  1.4 0.7 copy-start.9
  2.1 0.7 copy-start.10
  3.3 26.5 %copy-start.8 = (s32[16]{0:T(128)S(1)}, s32[16]{0:T(128)}, u32[]{:S(2)}) copy-start(s32[16]{0:T(128)} %t_ref.5) | copy-start | bytes 196
  3.3 28.5 %copy-start = (bf16[320,2048]{1,0:T(8,128)(2,1)S(1)}, bf16[320,2048]{1,0:T(8,128)(2,1)}, u32[]{:S(2)}) copy-start(bf16[320,2048]{1,0:T(8,128)(2,1)} %a_ref.3) | copy-start | bytes 3932164
  3.3 28.5 %copy-start.1 = (bf16[128,5120]{1,0:T(8,128)(2,1)S(1)}, bf16[128,5120]{1,0:T(8,128)(2,1)}, u32[]{:S(2)}) copy-start(bf16[128,5120]{1,0:T(8,128)(2,1)} %x_ref.3) | copy-start | bytes 3932164
  3.3 8.1 %collective-permute-start = (bf16[1,16,1408]{2,1,0:T(8,128)(2,1)S(1)}, bf16[1,16,1408]{2,1,0:T(8,128)(2,1)S(1)}, u32[]{:S(2)}, u32[]{:S(2)}) collective-permute-start(bf16[1,16,1408]{2,1,0:T(8,128)(2,1)S(1)} %bitcast.2), channel_id=1, source_target_pairs={{0,8},{1,9},{2,10},{3,11},{4,12},{5,13},{6,14},{7,15},{8,0},{9,1},... | collective-permute-start | bytes 135176 | tf_op jit(solution)/shard_map/ppermute | solution.py:315
  11.5 5.9 %collective-permute-start.1 = (bf16[2,16,1408]{2,1,0:T(8,128)(2,1)S(1)}, bf16[2,16,1408]{2,1,0:T(8,128)(2,1)S(1)}, u32[]{:S(2)}, u32[]{:S(2)}) collective-permute-start(bf16[2,16,1408]{2,1,0:T(8,128)(2,1)S(1)} %pad_maximum_fusion.1), channel_id=1, source_target_pairs={{0,4},{1,5},{2,6},{3,7},{4,0},{5,1},{6,2},{7,3},{8,12},{9,13},{10,... | collective-permute-start | bytes 270344 | tf_op jit(solution)/shard_map/ppermute | solution.py:315
  13.8 21.8 %all-to-all-start = ((bf16[16,16,1152]{2,1,0:T(8,128)(2,1)}), bf16[16,16,1152]{2,1,0:T(8,128)(2,1)S(1)}, u32[]{:S(2)}, u32[]{:S(2)}) async-start(bf16[16,16,1152]{2,1,0:T(8,128)(2,1)} %shard_map.140), calls=%async_computation | async-start | bytes 1179648 | tf_op jit(solution)/shard_map/all_to_all | solution.py:311
  17.4 11.7 %collective-permute-start.2 = (bf16[4,16,1408]{2,1,0:T(8,128)(2,1)S(1)}, bf16[4,16,1408]{2,1,0:T(8,128)(2,1)S(1)}, u32[]{:S(2)}, u32[]{:S(2)}) collective-permute-start(bf16[4,16,1408]{2,1,0:T(8,128)(2,1)S(1)} %pad_maximum_fusion), channel_id=1, source_target_pairs={{0,2},{1,3},{2,0},{3,1},{4,6},{5,7},{6,4},{7,5},{8,10},{9,11},{10,... | collective-permute-start | bytes 540680 | tf_op jit(solution)/shard_map/ppermute | solution.py:315
  29.8 2.0 %collective-permute-start.3 = (bf16[8,16,1408]{2,1,0:T(8,128)(2,1)}, bf16[8,16,1408]{2,1,0:T(8,128)(2,1)}, u32[]{:S(2)}, u32[]{:S(2)}) collective-permute-start(bf16[8,16,1408]{2,1,0:T(8,128)(2,1)} %constant_dynamic-update-slice_fusion.h0_ref), channel_id=1, source_target_pairs={{0,1},{1,0},{2,3},{3,2},{4,5},{5,4},{6,7},{7,6},{8,9},{9,8},{10,11... | collective-permute-start | bytes 1081352 | tf_op jit(solution)/shard_map/ppermute | solution.py:315
  31.8 1.0 %copy-start.6 = (bf16[8,16,1408]{2,1,0:T(8,128)(2,1)S(1)}, bf16[8,16,1408]{2,1,0:T(8,128)(2,1)}, u32[]{:S(2)}) copy-start(bf16[8,16,1408]{2,1,0:T(8,128)(2,1)} %constant_dynamic-update-slice_fusion.h0_ref) | copy-start | bytes 1081348
  35.6 1.2 %copy-start.5 = (bf16[128,4096]{1,0:T(8,128)(2,1)S(1)}, bf16[128,4096]{1,0:T(8,128)(2,1)}, u32[]{:S(2)}) copy-start(bf16[128,4096]{1,0:T(8,128)(2,1)} %g_ref.1) | copy-start | bytes 3145732
  36.9 25.6 %copy-start.2 = (bf16[256,2048]{1,0:T(8,128)(2,1)S(1)}, bf16[256,2048]{1,0:T(8,128)(2,1)}, u32[]{:S(2)}) copy-start(bf16[256,2048]{1,0:T(8,128)(2,1)} %b_ref.3) | copy-start | bytes 3145732
  38.8 29.5 %copy-start.12 = (bf16[4,4096]{1,0:T(4,128)(2,1)S(1)}, bf16[4,4096]{1,0:T(4,128)(2,1)}, u32[]{:S(2)}) copy-start(bf16[4,4096]{1,0:T(4,128)(2,1)} %param.20) | copy-start | bytes 98308
  38.8 36.4 %copy-start.3 = (bf16[4,256,512]{2,1,0:T(8,128)(2,1)S(1)}, bf16[4,256,512]{2,1,0:T(8,128)(2,1)}, u32[]{:S(2)}) copy-start(bf16[4,256,512]{2,1,0:T(8,128)(2,1)} %k_ref.1) | copy-start | bytes 3145732
  38.8 36.4 %copy-start.4 = (bf16[4,256,512]{2,1,0:T(8,128)(2,1)S(1)}, bf16[4,256,512]{2,1,0:T(8,128)(2,1)}, u32[]{:S(2)}) copy-start(bf16[4,256,512]{2,1,0:T(8,128)(2,1)} %v_ref.1) | copy-start | bytes 3145732
  38.8 36.4 %copy-start.11 = (s32[4]{0:T(128)S(1)}, s32[4]{0:T(128)}, u32[]{:S(2)}) copy-start(s32[4]{0:T(128)} %len_ref.1) | copy-start | bytes 52
  64.8 10.4 %all-to-all-start.2 = ((f32[16,4,256]{2,1,0:T(4,128)}), f32[16,4,256]{2,1,0:T(4,128)S(1)}, u32[]{:S(2)}, u32[]{:S(2)}) async-start(f32[16,4,256]{2,1,0:T(4,128)} %shard_map.144), calls=%async_computation.2 | async-start | bytes 131072 | tf_op jit(solution)/shard_map/all_to_all | solution.py:311

commit v6 on v5

--- a/solution.py
+++ b/solution.py
@@ -22,7 +22,7 @@
 
 F32 = jnp.float32
 BF16 = jnp.bfloat16
-VMEM_LIMIT = 40 * 1024 * 1024
+VMEM_LIMIT = 24 * 1024 * 1024
 ALL_VMEM = 60 * 1024 * 1024
 
 
@@ -84,7 +84,7 @@
     return slice(2 * fb + h * fa, 2 * fb + (h + 1) * fa)
 
 
-def pick_kernel(t_ref, b_ref, a_ref, o_ref, b_tab, a_tab, o_buf, sem_b, sem_a, sem_o):
+def pick_kernel(tenant_ref, b_ref, a_ref, o_ref, b_tab, a_tab, o_buf, t_ref, sem_t, sem_b, sem_a, sem_o):
     n = t_ref.shape[0]
     fa, fb = a_ref.shape[0], b_ref.shape[0]
 
@@ -94,7 +94,8 @@
         return [pltpu.make_async_copy(src.at[r], dst.at[r], sem.at[c]) for c, r in enumerate(parts)]
 
     first, second = loads(b_ref, b_tab, sem_b), loads(a_ref, a_tab, sem_a)
-    for load in first + second:
+    tenants = pltpu.make_async_copy(tenant_ref, t_ref, sem_t)
+    for load in [tenants] + first + second:
         load.start()
 
     def picked(j, table):
@@ -115,7 +116,7 @@
     def finish(j):
         pltpu.make_async_copy(o_buf.at[j], o_ref.at[j], sem_o.at[j]).wait()
 
-    for load in first:
+    for load in [tenants] + first:
         load.wait()
     each(n, up_body)
     for load in second:
@@ -146,9 +147,9 @@
     return half + pltpu.roll(half, RANK, 1)
 
 
-def rows_kernel(masks, me_ref, h0_ref, h1_ref, x_ref, a_ref, hx_ref, base_ref, u_ref, sel, sx, sb, su):
-    tiles = len(masks)
-    h = jnp.concatenate([r[k] for r in (h0_ref, h1_ref) for k in range(tiles // 2)], axis=0)
+def rows_kernel(count, me_ref, *refs):
+    h_refs, (x_ref, a_ref, hx_ref, base_ref, u_ref, sel) = refs[:count], refs[count:]
+    h = jnp.concatenate([r[k] for r in h_refs for k in range(r.shape[0])], axis=0)
     size = h.shape[1] - LANES
     fa = a_ref.shape[0]
     part = lax.broadcasted_iota(jnp.int32, (h.shape[0], LANES), 0) % HALF // ROWS_DEV
@@ -165,23 +166,26 @@
     tenant = h[:, size:].astype(F32).astype(jnp.int32)
     base = fold_rows(dot(sel[...], a_ref[...], 1, 0), tenant)
     base = jnp.where(part == me_ref[0] // per_chunk, base, 0.0)
-    for k, mask in enumerate(masks):
-        d = me_ref[0] ^ mask
-        for value, dest in ((hx, sx), (base, sb)):
+    for k in range(h.shape[0] // HALF):
+        for value, dest in ((hx, hx_ref), (base, base_ref)):
             eight = value[k * HALF : k * HALF + 8] + value[k * HALF + 8 : (k + 1) * HALF]
-            dest[d] = eight[:ROWS_DEV] + eight[ROWS_DEV:]
-        su[d] = tenant[k * HALF : k * HALF + ROWS_DEV]
-    for src, dest in ((sx, hx_ref), (sb, base_ref), (su, u_ref)):
-        dest[...] = jnp.concatenate([src[d] for d in range(tiles)], axis=0)
+            dest[k] = eight[:ROWS_DEV] + eight[ROWS_DEV:]
+        u_ref[k] = tenant[k * HALF : k * HALF + ROWS_DEV]
 
 
 def plain_rows_kernel(h_ref, x_ref, a_ref, hc_ref, u_ref, hx_ref, base_ref):
-    hx_ref[...] = dot(h_ref[...], x_ref[...], 1, 1)
-    base_ref[...] = fold_rows(dot(hc_ref[...], a_ref[...], 1, 0), u_ref[...])
-
-
-def block_kernel(ride, t_ref, x_ref, g_ref, hx_ref, base_ref, u_ref, r_ref, o_ref, *refs):
-    wa_ref, wb_ref = refs[-2:]
+    hx = dot(h_ref[...], x_ref[...], 1, 1)
+    base = fold_rows(dot(hc_ref[...], a_ref[...], 1, 0), u_ref[...])
+    for d in range(hx_ref.shape[0]):
+        hx_ref[d] = hx[d * ROWS_DEV : (d + 1) * ROWS_DEV]
+        base_ref[d] = base[d * ROWS_DEV : (d + 1) * ROWS_DEV]
+
+
+def block_kernel(ride, masks, t_ref, me_ref, x_ref, g_ref, r_ref, *refs):
+    sets = (len(refs) - (7 if ride else 8)) // 3
+    hx_sets, base_sets, u_sets = (refs[i * sets : (i + 1) * sets] for i in range(3))
+    o_ref, u_ref = refs[3 * sets : 3 * sets + 2]
+    wa_ref, wb_ref, sx, sb, su = refs[-5:]
     n = r_ref.shape[0]
     fa, fb = x_ref.shape[1] // n, g_ref.shape[1] // n
     for d in range(n):
@@ -192,20 +196,27 @@
     back = dot(wb_ref[...], g_ref[...], 1, 1).astype(BF16)
     down = dot(wa_ref[...], x_ref[...], 1, 1).astype(BF16)
 
-    hx = hx_ref[...]
+    k = 0
+    for hx_ref, base_ref, tile_ref in zip(hx_sets, base_sets, u_sets):
+        for i in range(hx_ref.shape[0]):
+            d = me_ref[0] ^ masks[k] if masks else i
+            sx[d], sb[d], su[d] = hx_ref[i], base_ref[i], tile_ref[i]
+            k += 1
+    hx, base, tenant = (jnp.concatenate([v[d] for d in range(n)], axis=0) for v in (sx, sb, su))
+    u_ref[...] = tenant
     high = hx.astype(BF16)
     low = (hx - high.astype(F32)).astype(BF16)
     wide_back = jnp.concatenate([back] * PER_TILE, axis=0)
     change = dot(high, wide_back, 1, 1) + dot(low, wide_back, 1, 1)
-    mine = u_ref[...] == t_ref[0]
-    full = base_ref[...] - jnp.where(mine, learning_rate * (adapter_scale * change), 0.0)
+    mine = tenant == t_ref[0]
+    full = base - jnp.where(mine, learning_rate * (adapter_scale * change), 0.0)
     quarter = full.shape[0] // PER_TILE
     spot = lax.broadcasted_iota(jnp.int32, (quarter, LANES), 1) // RANK
     packed = jnp.zeros((quarter, LANES), F32)
     for q in range(PER_TILE):
         packed = packed + jnp.where(spot == q, full[q * quarter : (q + 1) * quarter], 0.0)
     if not ride:
-        refs[0][...] = packed
+        refs[3 * sets + 2][...] = packed
 
     down_part = dot(back, x_ref[...], 1, 0).astype(BF16)
     up_part = dot(down, g_ref[...], 1, 0).astype(BF16)
@@ -230,20 +241,24 @@
     each(t_ref.shape[0], body)
 
 
-def updated(table_ref, grad_ref):
-    return (table_ref[...].astype(F32) - learning_rate * grad_ref[...]).astype(BF16)
-
-
 def gradient_kernel(t_ref, part_ref, down_ref, up_ref):
     fa, fb = down_ref.shape[0], up_ref.shape[0]
     sum_by_tenant(t_ref, part_ref, down_half, fa, fb, down_ref)
     sum_by_tenant(t_ref, part_ref, up_half, fa, fb, up_ref)
 
 
-def delta_kernel(fa, t_ref, part_ref, b_ref, u_ref, *refs):
-    o_ref, grad_ref = refs[-2:]
+def mask_kernel(u_ref, o_ref):
+    tenant = u_ref[...]
+    lane = lax.broadcasted_iota(jnp.int32, tenant.shape, 1)
+    for c in range(TENANTS // PER_TILE):
+        mine = tenant == c * PER_TILE + lane // RANK
+        o_ref[:, c * LANES : (c + 1) * LANES] = jnp.where(mine, 1.0, 0.0).astype(BF16)
+
+
+def delta_kernel(fa, t_ref, part_ref, b_ref, u_ref, mask_ref, *refs):
+    o_ref = refs[-1]
     n, fb = part_ref.shape[0], b_ref.shape[0]
-    if len(refs) == 3:
+    if len(refs) == 2:
         total = refs[0][...]
     else:
         total = part_ref[0, :, 2 * (fa + fb) :].astype(F32)
@@ -256,17 +271,20 @@
         half = one + pltpu.roll(one, 2 * RANK, 1)
         pieces.append(half + pltpu.roll(half, RANK, 1))
     adapted = jnp.concatenate(pieces, axis=0)
-    lane = lax.broadcasted_iota(jnp.int32, adapted.shape, 1)
+    rounded = adapted.astype(BF16)
+    spread = jnp.concatenate([rounded] * (TENANTS // PER_TILE), axis=1) * mask_ref[...]
+    old = dot(spread, b_ref[...], 1, 1)
+    quarter = lax.broadcasted_iota(jnp.int32, adapted.shape, 1) // RANK
     tenant = u_ref[...]
-    spread = jnp.concatenate(
-        [
-            jnp.where(tenant == c * PER_TILE + lane // RANK, adapted, 0.0).astype(BF16)
-            for c in range(TENANTS // PER_TILE)
-        ],
-        axis=1,
-    )
-    sum_by_tenant(t_ref, part_ref, up_half, fa, fb, grad_ref)
-    delta = adapter_scale * dot(spread, updated(b_ref, grad_ref), 1, 1)
+    matched = []
+    for c in range(n // PER_TILE):
+        block = jnp.zeros(adapted.shape, jnp.int32)
+        for i in range(PER_TILE):
+            block = jnp.where(quarter == i, t_ref[c * PER_TILE + i], block)
+        matched.append(jnp.where(tenant == block, adapted, 0.0).astype(BF16))
+    up = [part_ref[j, :, up_half(h, fa, fb)] for j in range(n) for h in range(2)]
+    change = dot(jnp.concatenate(matched, axis=1), jnp.concatenate(up, axis=0), 1, 0)
+    delta = adapter_scale * (old - learning_rate * (adapter_scale * change))
     for d in range(n):
         o_ref[d] = delta[d * ROWS_DEV : (d + 1) * ROWS_DEV]
 
@@ -277,33 +295,37 @@
     query = (base_ref[...] + delta).astype(BF16).astype(F32)
     group = HEADS // KV_HEADS
     cache = k_ref.shape[1]
-    many = group * ROWS_DEV
-    row_p = lax.broadcasted_iota(jnp.int32, (many, cache), 0) % ROWS_DEV
-    row_d = lax.broadcasted_iota(jnp.int32, (many, HEAD_DIM), 0) % ROWS_DEV
-    position = lax.broadcasted_iota(jnp.int32, (many, cache), 1)
+    many = HEADS * ROWS_DEV
+    empty = jnp.zeros((group * ROWS_DEV, HEAD_DIM), F32)
+    heads = []
+    for g in range(KV_HEADS):
+        mine = [query[:, h * HEAD_DIM : (h + 1) * HEAD_DIM] for h in range(g * group, (g + 1) * group)]
+        lanes = [empty] * KV_HEADS
+        lanes[g] = jnp.concatenate(mine, axis=0)
+        heads.append(jnp.concatenate(lanes, axis=1))
+    heads = jnp.concatenate(heads, axis=0).astype(BF16)
+    row = lax.broadcasted_iota(jnp.int32, (many, cache), 0) % ROWS_DEV
     length = jnp.zeros((many, cache), jnp.int32)
+    scores = jnp.zeros((many, cache), F32)
     for r in range(ROWS_DEV):
-        length = jnp.where(row_p == r, len_ref[r], length)
-    live = position < length
+        length = jnp.where(row == r, len_ref[r], length)
+        scores = jnp.where(row == r, dot(heads, k_ref[r], 1, 1), scores)
+    live = lax.broadcasted_iota(jnp.int32, (many, cache), 1) < length
+    scores = jnp.where(live, scores / jnp.sqrt(F32(HEAD_DIM)), F32(-1e30))
+    top = jnp.max(scores, axis=-1, keepdims=True)
+    expo = jnp.where(live, jnp.exp(scores - top), 0.0)
+    weights = (expo / jnp.sum(expo, axis=-1, keepdims=True)).astype(BF16)
+    mixed = [dot(weights, v_ref[r], 1, 0) for r in range(ROWS_DEV)]
     outs = []
+    rows = group * ROWS_DEV
+    row = lax.broadcasted_iota(jnp.int32, (rows, HEAD_DIM), 0) % ROWS_DEV
     for g in range(KV_HEADS):
-        cols = slice(g * HEAD_DIM, (g + 1) * HEAD_DIM)
-        heads = jnp.concatenate(
-            [query[:, (g * group + i) * HEAD_DIM : (g * group + i + 1) * HEAD_DIM] for i in range(group)],
-            axis=0,
-        ).astype(BF16)
-        scores = jnp.zeros((many, cache), F32)
+        part = jnp.zeros((rows, HEAD_DIM), F32)
         for r in range(ROWS_DEV):
-            scores = jnp.where(row_p == r, dot(heads, k_ref[r, :, cols], 1, 1), scores)
-        scores = scores / jnp.sqrt(F32(HEAD_DIM))
-        scores = jnp.where(live, scores, F32(-1e30))
-        top = jnp.max(scores, axis=-1, keepdims=True)
-        expo = jnp.where(live, jnp.exp(scores - top), 0.0)
-        weights = (expo / jnp.sum(expo, axis=-1, keepdims=True)).astype(BF16)
-        mixed = jnp.zeros((many, HEAD_DIM), F32)
-        for r in range(ROWS_DEV):
-            mixed = jnp.where(row_d == r, dot(weights, v_ref[r, :, cols], 1, 0), mixed)
-        outs.extend(mixed[i * ROWS_DEV : (i + 1) * ROWS_DEV] for i in range(group))
+            part = jnp.where(
+                row == r, mixed[r][g * rows : (g + 1) * rows, g * HEAD_DIM : (g + 1) * HEAD_DIM], part
+            )
+        outs.extend(part[i * ROWS_DEV : (i + 1) * ROWS_DEV] for i in range(group))
     o_ref[...] = jnp.concatenate(outs, axis=1).astype(BF16)
 
 
@@ -346,12 +368,14 @@
     packed = call(
         pick_kernel,
         jax.ShapeDtypeStruct(shape, BF16),
-        [smem(), hbm(), hbm()],
+        [hbm(), hbm(), hbm()],
         hbm(),
         scratch=[
             pltpu.VMEM(up_factors_transposed.shape, BF16),
             pltpu.VMEM(down_factors.shape, BF16),
             pltpu.VMEM(shape, BF16),
+            pltpu.SMEM((n,), jnp.int32),
+            pltpu.SemaphoreType.DMA,
             pltpu.SemaphoreType.DMA((chunks,)),
             pltpu.SemaphoreType.DMA((chunks,)),
             pltpu.SemaphoreType.DMA((n,)),
@@ -368,32 +392,31 @@
             [smem(), smem(), vmem()],
             vmem(),
             nbytes=4 * local_rows * width,
+            limit=ALL_VMEM,
         )(device_tenant_list, row_list_entry, hidden)[None]
         held = jnp.concatenate([held, partner(held, n // 2)], axis=0)
         held, packed = lax.optimization_barrier((held, packed))
         got = exchange(packed)
-        masks = [0, n // 2]
-        bit = n // 4
-        while bit > 1:
-            held = jnp.concatenate([held, partner(held, bit)], axis=0)
-            masks = masks + [m ^ bit for m in masks]
-            bit //= 2
-        masks = masks + [m ^ 1 for m in masks]
-        shapes = [(rows, BLOCK, F32), (rows, LANES, F32), (rows, LANES, jnp.int32)]
-        hx, base_low_rank, tenants = call(
-            functools.partial(rows_kernel, masks),
-            [jax.ShapeDtypeStruct((r, c), t) for r, c, t in shapes],
-            [smem()] + [vmem()] * 4,
-            [vmem()] * 3,
-            scratch=[
-                pltpu.VMEM((n * HALF, fa), BF16),
-                pltpu.VMEM((n, local_rows, LANES), F32),
-                pltpu.VMEM((n, local_rows, LANES), F32),
-                pltpu.VMEM((n, local_rows, LANES), jnp.int32),
-            ],
-            flops=8 * rows * BLOCK * width + 8 * rows * fa * cols,
-            nbytes=2 * BLOCK * width + 2 * fa * cols,
-        )(me[None], held, partner(held, 1), tokens, down_factors)
+        held = jnp.concatenate([held, partner(held, n // 4)], axis=0)
+        beside = partner(held, n // 8)
+
+        def rows_call(*tiles):
+            count = sum(t.shape[0] for t in tiles)
+            shapes = [jax.ShapeDtypeStruct((count, local_rows, LANES), t) for t in (F32, F32, jnp.int32)]
+            return call(
+                functools.partial(rows_kernel, len(tiles)),
+                shapes,
+                [smem()] + [vmem()] * (2 + len(tiles)),
+                [vmem()] * 3,
+                scratch=[pltpu.VMEM((count * HALF, fa), BF16)],
+                flops=8 * count * local_rows * (BLOCK * width + fa * cols),
+                nbytes=2 * BLOCK * width + 2 * fa * cols,
+            )(me[None], *tiles, tokens, down_factors)
+
+        near = [0, n // 2, n // 4, n // 2 + n // 4]
+        masks = near + [m ^ 1 for m in near] + [m ^ n // 8 for m in near] + [m ^ n // 8 ^ 1 for m in near]
+        found = [rows_call(held, partner(held, 1)), rows_call(beside), rows_call(partner(beside, 1))]
+        hx, base_low_rank, tenants = zip(*found)
     else:
         got = exchange(packed)
         slot = row_list_entry[:, None] == jnp.arange(device_tenant_list.shape[1], dtype=jnp.int32)[None, :]
@@ -403,35 +426,46 @@
         tenants = jnp.broadcast_to(tenants[:, None], (rows, LANES))
         hx, base_low_rank = call(
             plain_rows_kernel,
-            [jax.ShapeDtypeStruct((rows, BLOCK), F32), jax.ShapeDtypeStruct((rows, LANES), F32)],
+            [jax.ShapeDtypeStruct((n, local_rows, LANES), F32)] * 2,
             [vmem()] * 5,
             [vmem()] * 2,
         )(everyone, tokens, down_factors, lax.dynamic_slice(everyone, (0, me * fa), (rows, fa)), tenants)
 
+    if not small:
+        masks, hx, base_low_rank = None, (hx,), (base_low_rank,)
+        tenants = (tenants.reshape(n, local_rows, LANES),)
     part_shape = (n, HALF, 2 * (fa + fb) + (LANES if small else 0))
     my_tenant = lax.dynamic_slice(tenant_of_block, (me,), (1,))
-    parts = call(
-        functools.partial(block_kernel, small),
-        [jax.ShapeDtypeStruct(part_shape, BF16)]
+    parts, tenants, *low_rank = call(
+        functools.partial(block_kernel, small, masks),
+        [jax.ShapeDtypeStruct(part_shape, BF16), jax.ShapeDtypeStruct((rows, LANES), jnp.int32)]
         + ([] if small else [jax.ShapeDtypeStruct((quarter, LANES), F32)]),
-        [smem()] + [vmem()] * 6,
-        [vmem()] * (1 if small else 2),
-        scratch=[pltpu.VMEM((RANK, width), BF16), pltpu.VMEM((RANK, features), BF16)],
+        [smem(), smem()] + [vmem()] * (3 + 3 * len(hx)),
+        [vmem()] * (2 if small else 3),
+        scratch=[pltpu.VMEM((RANK, width), BF16), pltpu.VMEM((RANK, features), BF16)]
+        + [pltpu.VMEM((n, local_rows, LANES), t) for t in (F32, F32, jnp.int32)],
         flops=4 * RANK * BLOCK * n * (fa + fb),
         nbytes=2 * BLOCK * n * (fa + fb),
-    )(my_tenant, tokens, query_output_gradient, hx, base_low_rank, tenants, got)
-    low_rank = [lax.psum(p, "wide") for p in parts[1:]]
-    parts = exchange(parts[0])
+    )(my_tenant, me[None], tokens, query_output_gradient, got, *hx, *base_low_rank, *tenants)
+    low_rank = [lax.psum(p, "wide") for p in low_rank]
+    parts = exchange(parts)
+    mask = call(
+        mask_kernel,
+        jax.ShapeDtypeStruct((rows, cols), BF16),
+        [vmem()],
+        vmem(),
+        flops=rows * cols,
+        nbytes=2 * rows * cols,
+    )(tenants)
 
     delta = call(
         functools.partial(delta_kernel, fa),
         jax.ShapeDtypeStruct((n, local_rows, fb), F32),
-        [smem()] + [vmem()] * (3 + len(low_rank)),
+        [smem()] + [vmem()] * (4 + len(low_rank)),
         vmem(),
-        scratch=[pltpu.VMEM((fb, cols), F32)],
         flops=2 * rows * cols * fb,
         nbytes=2 * cols * fb,
-    )(tenant_of_block, parts, up_factors_transposed, tenants, *low_rank)
+    )(tenant_of_block, parts, up_factors_transposed, tenants, mask, *low_rank)
     delta = exchange(delta)
 
     down_gradient, up_gradient = call(

time: 78.6 us -> 86 us (1.094)
  blocking collectives: 23.6 us -> 0 us
  waiting for transfers between devices: 13.1 us -> 35.7 us
  starting transfers between devices: 14.8 us -> 23.9 us
  local copies, waits for them, and re-layouts: 6.9 us -> 3.92 us
  Pallas kernels: 18.7 us -> 20.9 us
    all_to_all x1 -> x0, blocking collectives: 23.6 us -> none  [exchange(): return lax.all_to_all(x, 'wide', split_axis=0, concat_axis=0, tiled=True)]
    all_to_all x2 -> x3, waiting for transfers between devices: 2.63 us -> 19.2 us  [exchange(): return lax.all_to_all(x, 'wide', split_axis=0, concat_axis=0, tiled=True)]
    all_to_all x2 -> x3, starting transfers between devices: 7.09 us -> 16.8 us  [exchange(): return lax.all_to_all(x, 'wide', split_axis=0, concat_axis=0, tiled=True)]
    ppermute x4 -> x5, waiting for transfers between devices: 10.5 us -> 16.5 us  [partner(): lax.ppermute(x, 'wide', [(i, i ^ mask) for i in range(lax.axis_size('wide...]
    pallas_call x3 -> x6, Pallas kernels: 8.75 us -> 11.5 us  [the longest x3 6.18 us: rows_call(): call(functools.partial(rows_kernel, len(tiles)), shapes, [smem()] + [vmem...]
    unnamed x28 -> x23, local copies, waits for them, and re-layouts: 5.62 us -> 3.32 us
    pallas_call x1, Pallas kernels: 0.56 us -> 1.43 us  [per_device(): call(rows_pack_kernel, jax.ShapeDtypeStruct((HALF, width // CHUNKS + LANE...]
    ppermute x4 -> x5, starting transfers between devices: 7.73 us -> 7.19 us  [partner(): lax.ppermute(x, 'wide', [(i, i ^ mask) for i in range(lax.axis_size('wide...]
  transfers between devices with their start and end apart: 6 -> 8, of which waited for: 3 -> 4; matrix products, arithmetic and copies ran while one was open for 3% -> 1% of each run, Pallas kernels for 14% -> 16%
where the time goes in v6:
time: 86 us; the launch traced here: 85.4 us
  waiting for transfers between devices  35.7 us (42%)
  starting transfers between devices  23.9 us (28%)
  Pallas kernels  20.9 us (24%)
  local copies, waits for them, and re-layouts  3.92 us (5%)
    all_to_all x3, waiting for transfers between devices, exchange(): return lax.all_to_all(x, 'wide', split_axis=0, concat_axis=0, tiled=True)  19.2 us
    all_to_all x3, starting transfers between devices, exchange(): return lax.all_to_all(x, 'wide', split_axis=0, concat_axis=0, tiled=True)  16.8 us
    ppermute x5, waiting for transfers between devices, partner(): lax.ppermute(x, 'wide', [(i, i ^ mask) for i in range(lax.axis_size('wide...  16.5 us
    ppermute x5, starting transfers between devices, partner(): lax.ppermute(x, 'wide', [(i, i ^ mask) for i in range(lax.axis_size('wide...  7.19 us
    pallas_call x3, Pallas kernels, rows_call(): call(functools.partial(rows_kernel, len(tiles)), shapes, [smem()] + [vmem...  6.18 us
    pallas_call x1, Pallas kernels, per_device(): call(gradient_kernel, [jax.ShapeDtypeStruct((fa, cols), F32), jax.ShapeDt...  4.2 us
    pallas_call x1, Pallas kernels, per_device(): call(pick_kernel, jax.ShapeDtypeStruct(shape, BF16), [hbm(), hbm(), hbm()...  3.38 us
    unnamed x23, local copies, waits for them, and re-layouts  3.32 us
  transfers between devices with their start and end apart: 8, of which 4 were waited for; matrix products, arithmetic and copies ran while one was open for 1% of the time, Pallas kernels for 16%

profile of v6, /device:TPU:0, one launch (start us, length us, event | category | flops | bytes accessed | tf_op | source)
XLA Modules:
  0.0 85.4 jit_solution(13416697250191541944)
XLA Ops:
  0.6 1.4 %shard_map.139 = bf16[16,1408]{1,0:T(8,128)(2,1)} custom-call(s32[1,4]{1,0:T(1,128)} %list_ref.1, s32[4]{0:T(128)} %slot_ref.1, bf16[4,5120]{1,0:T(4,128)(2,1)} %hidden_ref.1), custom_call_target="tpu_custom_call" | custom-call | bytes 81920 | tf_op jit(solution)/shard_map/pallas_call | solution.py:389
  2.1 4.1 %collective-permute-start = (bf16[1,16,1408]{2,1,0:T(8,128)(2,1)}, bf16[1,16,1408]{2,1,0:T(8,128)(2,1)S(1)}, u32[]{:S(2)}, u32[]{:S(2)}) collective-permute-start(bf16[1,16,1408]{2,1,0:T(8,128)(2,1)} %bitcast.2), channel_id=1, source_target_pairs={{0,8},{1,9},{2,10},{3,11},{4,12},{5,13},{6,14},{7,15},{8,0},{9,1},... | collective-permute-start | bytes 135176 | tf_op jit(solution)/shard_map/ppermute | solution.py:337
  6.2 3.4 %shard_map.140 = bf16[16,16,1152]{2,1,0:T(8,128)(2,1)} custom-call(s32[16]{0:T(128)} %t_ref.3, bf16[256,2048]{1,0:T(8,128)(2,1)} %b_ref.3, bf16[320,2048]{1,0:T(8,128)(2,1)} %refs_2_.5), custom_call_target="tpu_custom_call" | custom-call | flops 75497472 | bytes 2359296 | tf_op jit(solution)/shard_map/pallas_call | solution.py:368
  9.6 5.5 %all-to-all-start = ((bf16[16,16,1152]{2,1,0:T(8,128)(2,1)}), bf16[16,16,1152]{2,1,0:T(8,128)(2,1)S(1)}, u32[]{:S(2)}, u32[]{:S(2)}) async-start(bf16[16,16,1152]{2,1,0:T(8,128)(2,1)} %shard_map.140), calls=%async_computation | async-start | bytes 1179648 | tf_op jit(solution)/shard_map/all_to_all | solution.py:333
  15.1 1.9 %collective-permute-start.1 = (bf16[2,16,1408]{2,1,0:T(8,128)(2,1)S(1)}, bf16[2,16,1408]{2,1,0:T(8,128)(2,1)S(1)}, u32[]{:S(2)}, u32[]{:S(2)}) collective-permute-start(bf16[2,16,1408]{2,1,0:T(8,128)(2,1)S(1)} %pad_maximum_fusion), channel_id=1, source_target_pairs={{0,4},{1,5},{2,6},{3,7},{4,0},{5,1},{6,2},{7,3},{8,12},{9,13},{10,... | collective-permute-start | bytes 270344 | tf_op jit(solution)/shard_map/ppermute | solution.py:337
  17.0 11.1 %collective-permute-done.1 = bf16[2,16,1408]{2,1,0:T(8,128)(2,1)S(1)} collective-permute-done((bf16[2,16,1408]{2,1,0:T(8,128)(2,1)S(1)}, bf16[2,16,1408]{2,1,0:T(8,128)(2,1)S(1)}, u32[]{:S(2)}, u32[]{:S(2)}) %collective-permute-start.1) | collective-permute-done | bytes 90144 | tf_op jit(solution)/shard_map/ppermute | solution.py:337
  28.1 1.2 %collective-permute-start.3 = (bf16[4,16,1408]{2,1,0:T(8,128)(2,1)S(1)}, bf16[4,16,1408]{2,1,0:T(8,128)(2,1)}, u32[]{:S(2)}, u32[]{:S(2)}) collective-permute-start(bf16[4,16,1408]{2,1,0:T(8,128)(2,1)S(1)} %constant_dynamic-update-slice_fusion.refs_0_), channel_id=1, source_target_pairs={{0,2},{1,3},{2,0},{3,1},{4,6},{5,7},{6,4},{7,5},{8,10},{9,11},{10,... | collective-permute-start | bytes 540680 | tf_op jit(solution)/shard_map/ppermute | solution.py:337
  29.3 5.4 %collective-permute-done.3.refs_0_ = bf16[4,16,1408]{2,1,0:T(8,128)(2,1)} collective-permute-done((bf16[4,16,1408]{2,1,0:T(8,128)(2,1)S(1)}, bf16[4,16,1408]{2,1,0:T(8,128)(2,1)}, u32[]{:S(2)}, u32[]{:S(2)}) %collective-permute-start.3) | collective-permute-done | bytes 180256 | tf_op jit(solution)/shard_map/ppermute | solution.py:337
  34.7 0.6 dynamic_slice.3.t_ref
  35.3 2.0 %shard_map.142 = (f32[4,4,128]{2,1,0:T(4,128)S(1)}, f32[4,4,128]{2,1,0:T(4,128)S(1)}, s32[4,4,128]{2,1,0:T(4,128)S(1)}) custom-call(s32[1]{0:T(128)} %bitcast.me_ref, bf16[4,16,1408]{2,1,0:T(8,128)(2,1)} %collective-permute-done.3.refs_0_, bf16[128,5120]{1,0:T(8,128)(2,1)S(1)} %copy-done.1, bf16[320,2048]{1,0:T(8,128)(2,1)S(1)} %copy-done), custom_call_target="tpu_custom_call" | custom-call | flops 167772160 | bytes 2621440 | tf_op jit(solution)/shard_map/pallas_call | solution.py:406
  37.4 2.1 %shard_map.141 = (f32[8,4,128]{2,1,0:T(4,128)S(1)}, f32[8,4,128]{2,1,0:T(4,128)S(1)}, s32[8,4,128]{2,1,0:T(4,128)S(1)}) custom-call(s32[1]{0:T(128)} %bitcast.me_ref, bf16[4,16,1408]{2,1,0:T(8,128)(2,1)S(1)} %constant_dynamic-update-slice_fusion.refs_0_, bf16[4,16,1408]{2,1,0:T(8,128)(2,1)} %collective-permute-done.2.refs_1_, ...), custom_call_target="tpu_custom_call" | custom-call | flops 335544320 | bytes 2621440 | tf_op jit(solution)/shard_map/pallas_call | solution.py:406
  39.5 2.1 %shard_map.143 = (f32[4,4,128]{2,1,0:T(4,128)S(1)}, f32[4,4,128]{2,1,0:T(4,128)S(1)}, s32[4,4,128]{2,1,0:T(4,128)S(1)}) custom-call(s32[1]{0:T(128)} %bitcast.me_ref, bf16[4,16,1408]{2,1,0:T(8,128)(2,1)} %collective-permute-done.4.refs_0_, bf16[128,5120]{1,0:T(8,128)(2,1)S(1)} %copy-done.1, bf16[320,2048]{1,0:T(8,128)(2,1)S(1)} %copy-done), custom_call_target="tpu_custom_call" | custom-call | flops 167772160 | bytes 2621440 | tf_op jit(solution)/shard_map/pallas_call | solution.py:406
  41.5 1.2 %copy-done.5 = bf16[128,4096]{1,0:T(8,128)(2,1)S(1)} copy-done((bf16[128,4096]{1,0:T(8,128)(2,1)S(1)}, bf16[128,4096]{1,0:T(8,128)(2,1)}, u32[]{:S(2)}) %copy-start.5) | copy-done | bytes 1048600
  42.8 1.9 %shard_map.144 = (bf16[16,16,1280]{2,1,0:T(8,128)(2,1)S(1)}, s32[64,128]{1,0:T(8,128)S(1)}) custom-call(s32[1]{0:T(128)} %dynamic_slice.3.t_ref, s32[1]{0:T(128)} %bitcast.me_ref, bf16[128,5120]{1,0:T(8,128)(2,1)S(1)} %copy-done.1, bf16[128,4096]{1,0:T(8,128)(2,1)S(1)} %copy-done.5, bf16[16,16,1152]{2,1,0:T(8,128)(2,1)S(1)} %all-to-all-done.r_ref, ...), custom_call_target="tpu_custom_call" | custom-call | flops 150994944 | bytes 2359296 | tf_op jit(solution)/shard_map/pallas_call | solution.py:439
  44.6 0.8 copy-done.6
  45.5 6.5 %all-to-all-start.1 = ((bf16[16,16,1280]{2,1,0:T(8,128)(2,1)}), bf16[16,16,1280]{2,1,0:T(8,128)(2,1)S(1)}, u32[]{:S(2)}, u32[]{:S(2)}) async-start(bf16[16,16,1280]{2,1,0:T(8,128)(2,1)} %copy-done.6), calls=%async_computation.1 | async-start | bytes 1310720 | tf_op jit(solution)/shard_map/all_to_all | solution.py:333
  52.0 0.1 shard_map.146.mask_ref
  52.1 16.5 %all-to-all-done.1.part_ref = bf16[16,16,1280]{2,1,0:T(8,128)(2,1)S(1)} async-done(((bf16[16,16,1280]{2,1,0:T(8,128)(2,1)}), bf16[16,16,1280]{2,1,0:T(8,128)(2,1)S(1)}, u32[]{:S(2)}, u32[]{:S(2)}) %all-to-all-start.1) | async-done | bytes 655392 | tf_op jit(solution)/shard_map/all_to_all | solution.py:333
  68.6 1.8 %shard_map.147 = f32[16,4,256]{2,1,0:T(4,128)} custom-call(s32[16]{0:T(128)S(1)} %copy-done.7, bf16[16,16,1280]{2,1,0:T(8,128)(2,1)S(1)} %all-to-all-done.1.part_ref, bf16[256,2048]{1,0:T(8,128)(2,1)S(1)} %copy-done.2, s32[64,128]{1,0:T(8,128)S(1)} %get-tuple-element.32.u_ref, bf16[64,2048]{1,0:T(8,128)(2,1)S(1)} %shard_map.146.mask_ref), custom_call_target="tpu_custom_call" | custom-call | flops 67108864 | bytes 1048576 | tf_op jit(solution)/shard_map/pallas_call | solution.py:461
  70.4 4.8 %all-to-all-start.2 = ((f32[16,4,256]{2,1,0:T(4,128)}), f32[16,4,256]{2,1,0:T(4,128)S(1)}, u32[]{:S(2)}, u32[]{:S(2)}) async-start(f32[16,4,256]{2,1,0:T(4,128)} %shard_map.147), calls=%async_computation.2 | async-start | bytes 131072 | tf_op jit(solution)/shard_map/all_to_all | solution.py:333
  75.2 4.2 %shard_map.145 = (f32[320,2048]{1,0:T(8,128)}, f32[256,2048]{1,0:T(8,128)}) custom-call(s32[16]{0:T(128)S(1)} %copy-done.7, bf16[16,16,1280]{2,1,0:T(8,128)(2,1)S(1)} %all-to-all-done.1.part_ref), custom_call_target="tpu_custom_call" | custom-call | flops 75497472 | bytes 4718592 | tf_op jit(solution)/shard_map/pallas_call | solution.py:471
  79.4 2.7 %all-to-all-done.2.delta_ref = f32[16,4,256]{2,1,0:T(4,128)S(1)} async-done(((f32[16,4,256]{2,1,0:T(4,128)}), f32[16,4,256]{2,1,0:T(4,128)S(1)}, u32[]{:S(2)}, u32[]{:S(2)}) %all-to-all-start.2) | async-done | bytes 65568 | tf_op jit(solution)/shard_map/all_to_all | solution.py:333
  82.1 1.2 %copy-done.4 = bf16[4,256,512]{2,1,0:T(8,128)(2,1)S(1)} copy-done((bf16[4,256,512]{2,1,0:T(8,128)(2,1)S(1)}, bf16[4,256,512]{2,1,0:T(8,128)(2,1)}, u32[]{:S(2)}) %copy-start.4) | copy-done | bytes 1048600
  83.3 2.1 %shard_map.148 = bf16[4,4096]{1,0:T(4,128)(2,1)} custom-call(s32[4]{0:T(128)S(1)} %copy-done.8, f32[16,4,256]{2,1,0:T(4,128)S(1)} %all-to-all-done.2.delta_ref, f32[4,4096]{1,0:T(4,128)S(1)} %convert_element_type.3.base_ref, bf16[4,256,512]{2,1,0:T(8,128)(2,1)S(1)} %copy-done.3, bf16[4,256,512]{2,1,0:T(8,128)(2,1)S(1)} %copy-done.4), custom_call_target="tpu_custom_call" | custom-call | flops 16777216 | bytes 2097152 | tf_op jit(solution)/shard_map/pallas_call | solution.py:479
  (29 shorter events, 0.1 us)
Async XLA Ops:
  2.1 7.5 %copy-start.9 = (bf16[16,1408]{1,0:T(8,128)(2,1)S(1)}, bf16[16,1408]{1,0:T(8,128)(2,1)}, u32[]{:S(2)}) copy-start(bf16[16,1408]{1,0:T(8,128)(2,1)} %shard_map.139) | copy-start | bytes 135172
  2.1 32.7 %copy-start.7 = (s32[16]{0:T(128)S(1)}, s32[16]{0:T(128)}, u32[]{:S(2)}) copy-start(s32[16]{0:T(128)} %t_ref.3) | copy-start | bytes 196
  2.1 33.2 %copy-start = (bf16[320,2048]{1,0:T(8,128)(2,1)S(1)}, bf16[320,2048]{1,0:T(8,128)(2,1)}, u32[]{:S(2)}) copy-start(bf16[320,2048]{1,0:T(8,128)(2,1)} %refs_2_.5) | copy-start | bytes 3932164
  2.1 33.2 %copy-start.1 = (bf16[128,5120]{1,0:T(8,128)(2,1)S(1)}, bf16[128,5120]{1,0:T(8,128)(2,1)}, u32[]{:S(2)}) copy-start(bf16[128,5120]{1,0:T(8,128)(2,1)} %x_ref.1) | copy-start | bytes 3932164
  2.1 7.5 %collective-permute-start = (bf16[1,16,1408]{2,1,0:T(8,128)(2,1)}, bf16[1,16,1408]{2,1,0:T(8,128)(2,1)S(1)}, u32[]{:S(2)}, u32[]{:S(2)}) collective-permute-start(bf16[1,16,1408]{2,1,0:T(8,128)(2,1)} %bitcast.2), channel_id=1, source_target_pairs={{0,8},{1,9},{2,10},{3,11},{4,12},{5,13},{6,14},{7,15},{8,0},{9,1},... | collective-permute-start | bytes 135176 | tf_op jit(solution)/shard_map/ppermute | solution.py:337
  9.6 31.9 %all-to-all-start = ((bf16[16,16,1152]{2,1,0:T(8,128)(2,1)}), bf16[16,16,1152]{2,1,0:T(8,128)(2,1)S(1)}, u32[]{:S(2)}, u32[]{:S(2)}) async-start(bf16[16,16,1152]{2,1,0:T(8,128)(2,1)} %shard_map.140), calls=%async_computation | async-start | bytes 1179648 | tf_op jit(solution)/shard_map/all_to_all | solution.py:333
  15.1 13.0 %collective-permute-start.1 = (bf16[2,16,1408]{2,1,0:T(8,128)(2,1)S(1)}, bf16[2,16,1408]{2,1,0:T(8,128)(2,1)S(1)}, u32[]{:S(2)}, u32[]{:S(2)}) collective-permute-start(bf16[2,16,1408]{2,1,0:T(8,128)(2,1)S(1)} %pad_maximum_fusion), channel_id=1, source_target_pairs={{0,4},{1,5},{2,6},{3,7},{4,0},{5,1},{6,2},{7,3},{8,12},{9,13},{10,... | collective-permute-start | bytes 270344 | tf_op jit(solution)/shard_map/ppermute | solution.py:337
  28.1 6.6 %collective-permute-start.3 = (bf16[4,16,1408]{2,1,0:T(8,128)(2,1)S(1)}, bf16[4,16,1408]{2,1,0:T(8,128)(2,1)}, u32[]{:S(2)}, u32[]{:S(2)}) collective-permute-start(bf16[4,16,1408]{2,1,0:T(8,128)(2,1)S(1)} %constant_dynamic-update-slice_fusion.refs_0_), channel_id=1, source_target_pairs={{0,2},{1,3},{2,0},{3,1},{4,6},{5,7},{6,4},{7,5},{8,10},{9,11},{10,... | collective-permute-start | bytes 540680 | tf_op jit(solution)/shard_map/ppermute | solution.py:337
  29.3 8.1 %collective-permute-start.2 = (bf16[4,16,1408]{2,1,0:T(8,128)(2,1)S(1)}, bf16[4,16,1408]{2,1,0:T(8,128)(2,1)}, u32[]{:S(2)}, u32[]{:S(2)}) collective-permute-start(bf16[4,16,1408]{2,1,0:T(8,128)(2,1)S(1)} %constant_dynamic-update-slice_fusion.refs_0_), channel_id=1, source_target_pairs={{0,1},{1,0},{2,3},{3,2},{4,5},{5,4},{6,7},{7,6},{8,9},{9,8},{10,11... | collective-permute-start | bytes 540680 | tf_op jit(solution)/shard_map/ppermute | solution.py:337
  34.7 4.7 %collective-permute-start.4 = (bf16[4,16,1408]{2,1,0:T(8,128)(2,1)}, bf16[4,16,1408]{2,1,0:T(8,128)(2,1)}, u32[]{:S(2)}, u32[]{:S(2)}) collective-permute-start(bf16[4,16,1408]{2,1,0:T(8,128)(2,1)} %collective-permute-done.3.refs_0_), channel_id=1, source_target_pairs={{0,1},{1,0},{2,3},{3,2},{4,5},{5,4},{6,7},{7,6},{8,9},{9,8},{10,11... | collective-permute-start | bytes 540680 | tf_op jit(solution)/shard_map/ppermute | solution.py:337
  41.5 1.2 %copy-start.5 = (bf16[128,4096]{1,0:T(8,128)(2,1)S(1)}, bf16[128,4096]{1,0:T(8,128)(2,1)}, u32[]{:S(2)}) copy-start(bf16[128,4096]{1,0:T(8,128)(2,1)} %g_ref.1) | copy-start | bytes 3145732
  44.6 0.8 copy-start.6
  45.5 23.1 %copy-start.2 = (bf16[256,2048]{1,0:T(8,128)(2,1)S(1)}, bf16[256,2048]{1,0:T(8,128)(2,1)}, u32[]{:S(2)}) copy-start(bf16[256,2048]{1,0:T(8,128)(2,1)} %b_ref.3) | copy-start | bytes 3145732
  45.5 29.7 %copy-start.10 = (bf16[4,4096]{1,0:T(4,128)(2,1)S(1)}, bf16[4,4096]{1,0:T(4,128)(2,1)}, u32[]{:S(2)}) copy-start(bf16[4,4096]{1,0:T(4,128)(2,1)} %param.20) | copy-start | bytes 98308
  45.5 36.6 %copy-start.3 = (bf16[4,256,512]{2,1,0:T(8,128)(2,1)S(1)}, bf16[4,256,512]{2,1,0:T(8,128)(2,1)}, u32[]{:S(2)}) copy-start(bf16[4,256,512]{2,1,0:T(8,128)(2,1)} %k_ref.1) | copy-start | bytes 3145732
  45.5 36.6 %copy-start.8 = (s32[4]{0:T(128)S(1)}, s32[4]{0:T(128)}, u32[]{:S(2)}) copy-start(s32[4]{0:T(128)} %len_ref.1) | copy-start | bytes 52
  45.5 23.1 %all-to-all-start.1 = ((bf16[16,16,1280]{2,1,0:T(8,128)(2,1)}), bf16[16,16,1280]{2,1,0:T(8,128)(2,1)S(1)}, u32[]{:S(2)}, u32[]{:S(2)}) async-start(bf16[16,16,1280]{2,1,0:T(8,128)(2,1)} %copy-done.6), calls=%async_computation.1 | async-start | bytes 1310720 | tf_op jit(solution)/shard_map/all_to_all | solution.py:333
  70.4 11.7 %all-to-all-start.2 = ((f32[16,4,256]{2,1,0:T(4,128)}), f32[16,4,256]{2,1,0:T(4,128)S(1)}, u32[]{:S(2)}, u32[]{:S(2)}) async-start(f32[16,4,256]{2,1,0:T(4,128)} %shard_map.147), calls=%async_computation.2 | async-start | bytes 131072 | tf_op jit(solution)/shard_map/all_to_all | solution.py:333
  82.1 1.2 %copy-start.4 = (bf16[4,256,512]{2,1,0:T(8,128)(2,1)S(1)}, bf16[4,256,512]{2,1,0:T(8,128)(2,1)}, u32[]{:S(2)}) copy-start(bf16[4,256,512]{2,1,0:T(8,128)(2,1)} %v_ref.1) | copy-start | bytes 3145732

commit v7 on v6

--- a/solution.py
+++ b/solution.py
@@ -147,9 +147,8 @@
     return half + pltpu.roll(half, RANK, 1)
 
 
-def rows_kernel(count, me_ref, *refs):
-    h_refs, (x_ref, a_ref, hx_ref, base_ref, u_ref, sel) = refs[:count], refs[count:]
-    h = jnp.concatenate([r[k] for r in h_refs for k in range(r.shape[0])], axis=0)
+def rows_kernel(me_ref, h0_ref, h1_ref, x_ref, a_ref, _, hx_ref, base_ref, u_ref, sel):
+    h = jnp.concatenate([r[k] for r in (h0_ref, h1_ref) for k in range(r.shape[0])], axis=0)
     size = h.shape[1] - LANES
     fa = a_ref.shape[0]
     part = lax.broadcasted_iota(jnp.int32, (h.shape[0], LANES), 0) % HALF // ROWS_DEV
@@ -247,15 +246,7 @@
     sum_by_tenant(t_ref, part_ref, up_half, fa, fb, up_ref)
 
 
-def mask_kernel(u_ref, o_ref):
-    tenant = u_ref[...]
-    lane = lax.broadcasted_iota(jnp.int32, tenant.shape, 1)
-    for c in range(TENANTS // PER_TILE):
-        mine = tenant == c * PER_TILE + lane // RANK
-        o_ref[:, c * LANES : (c + 1) * LANES] = jnp.where(mine, 1.0, 0.0).astype(BF16)
-
-
-def delta_kernel(fa, t_ref, part_ref, b_ref, u_ref, mask_ref, *refs):
+def delta_kernel(fa, t_ref, part_ref, b_ref, u_ref, *refs):
     o_ref = refs[-1]
     n, fb = part_ref.shape[0], b_ref.shape[0]
     if len(refs) == 2:
@@ -271,11 +262,12 @@
         half = one + pltpu.roll(one, 2 * RANK, 1)
         pieces.append(half + pltpu.roll(half, RANK, 1))
     adapted = jnp.concatenate(pieces, axis=0)
-    rounded = adapted.astype(BF16)
-    spread = jnp.concatenate([rounded] * (TENANTS // PER_TILE), axis=1) * mask_ref[...]
-    old = dot(spread, b_ref[...], 1, 1)
     quarter = lax.broadcasted_iota(jnp.int32, adapted.shape, 1) // RANK
     tenant = u_ref[...]
+    spread = [
+        jnp.where(tenant == c * PER_TILE + quarter, adapted, 0.0).astype(BF16) for c in range(TENANTS // PER_TILE)
+    ]
+    old = dot(jnp.concatenate(spread, axis=1), b_ref[...], 1, 1)
     matched = []
     for c in range(n // PER_TILE):
         block = jnp.zeros(adapted.shape, jnp.int32)
@@ -397,26 +389,23 @@
         held = jnp.concatenate([held, partner(held, n // 2)], axis=0)
         held, packed = lax.optimization_barrier((held, packed))
         got = exchange(packed)
-        held = jnp.concatenate([held, partner(held, n // 4)], axis=0)
-        beside = partner(held, n // 8)
-
-        def rows_call(*tiles):
-            count = sum(t.shape[0] for t in tiles)
-            shapes = [jax.ShapeDtypeStruct((count, local_rows, LANES), t) for t in (F32, F32, jnp.int32)]
-            return call(
-                functools.partial(rows_kernel, len(tiles)),
-                shapes,
-                [smem()] + [vmem()] * (2 + len(tiles)),
-                [vmem()] * 3,
-                scratch=[pltpu.VMEM((count * HALF, fa), BF16)],
-                flops=8 * count * local_rows * (BLOCK * width + fa * cols),
-                nbytes=2 * BLOCK * width + 2 * fa * cols,
-            )(me[None], *tiles, tokens, down_factors)
-
-        near = [0, n // 2, n // 4, n // 2 + n // 4]
-        masks = near + [m ^ 1 for m in near] + [m ^ n // 8 for m in near] + [m ^ n // 8 ^ 1 for m in near]
-        found = [rows_call(held, partner(held, 1)), rows_call(beside), rows_call(partner(beside, 1))]
-        hx, base_low_rank, tenants = zip(*found)
+        masks = [0, n // 2]
+        bit = n // 4
+        while bit > 1:
+            held = jnp.concatenate([held, partner(held, bit)], axis=0)
+            masks = masks + [m ^ bit for m in masks]
+            bit //= 2
+        masks = masks + [m ^ 1 for m in masks]
+        found = call(
+            rows_kernel,
+            [jax.ShapeDtypeStruct((n, local_rows, LANES), t) for t in (F32, F32, jnp.int32)],
+            [smem()] + [vmem()] * 5,
+            [vmem()] * 3,
+            scratch=[pltpu.VMEM((n * HALF, fa), BF16)],
+            flops=8 * rows * (BLOCK * width + fa * cols),
+            nbytes=2 * BLOCK * width + 2 * fa * cols,
+        )(me[None], held, partner(held, 1), tokens, down_factors, query_output_gradient)
+        hx, base_low_rank, tenants = ((f,) for f in found)
     else:
         got = exchange(packed)
         slot = row_list_entry[:, None] == jnp.arange(device_tenant_list.shape[1], dtype=jnp.int32)[None, :]
@@ -449,23 +438,15 @@
     )(my_tenant, me[None], tokens, query_output_gradient, got, *hx, *base_low_rank, *tenants)
     low_rank = [lax.psum(p, "wide") for p in low_rank]
     parts = exchange(parts)
-    mask = call(
-        mask_kernel,
-        jax.ShapeDtypeStruct((rows, cols), BF16),
-        [vmem()],
-        vmem(),
-        flops=rows * cols,
-        nbytes=2 * rows * cols,
-    )(tenants)
 
     delta = call(
         functools.partial(delta_kernel, fa),
         jax.ShapeDtypeStruct((n, local_rows, fb), F32),
-        [smem()] + [vmem()] * (4 + len(low_rank)),
+        [smem()] + [vmem()] * (3 + len(low_rank)),
         vmem(),
         flops=2 * rows * cols * fb,
         nbytes=2 * cols * fb,
-    )(tenant_of_block, parts, up_factors_transposed, tenants, mask, *low_rank)
+    )(tenant_of_block, parts, up_factors_transposed, tenants, *low_rank)
     delta = exchange(delta)
 
     down_gradient, up_gradient = call(

time: 86 us -> 77.4 us (0.900)
  blocking collectives: 0 us -> 23.6 us
  waiting for transfers between devices: 35.7 us -> 13.1 us
  starting transfers between devices: 23.9 us -> 15.7 us
  Pallas kernels: 20.9 us -> 17.6 us
  local copies, waits for them, and re-layouts: 3.92 us -> 6.04 us
    all_to_all x0 -> x1, blocking collectives: none -> 23.6 us  [exchange(): return lax.all_to_all(x, 'wide', split_axis=0, concat_axis=0, tiled=True)]
    all_to_all x3 -> x2, waiting for transfers between devices: 19.2 us -> 2.62 us  [exchange(): return lax.all_to_all(x, 'wide', split_axis=0, concat_axis=0, tiled=True)]
    all_to_all x3 -> x2, starting transfers between devices: 16.8 us -> 7.94 us  [exchange(): return lax.all_to_all(x, 'wide', split_axis=0, concat_axis=0, tiled=True)]
    ppermute x5 -> x4, waiting for transfers between devices: 16.5 us -> 10.5 us  [partner(): lax.ppermute(x, 'wide', [(i, i ^ mask) for i in range(lax.axis_size('wide...]
    pallas_call x4 -> x1, Pallas kernels: 6.24 us -> 2.79 us  [per_device(): call(rows_kernel, [jax.ShapeDtypeStruct((n, local_rows, LANES), t) for t...]
    unnamed x23 -> x26, local copies, waits for them, and re-layouts: 3.32 us -> 4.76 us
    ppermute x5 -> x4, starting transfers between devices: 7.19 us -> 7.73 us  [partner(): lax.ppermute(x, 'wide', [(i, i ^ mask) for i in range(lax.axis_size('wide...]
  transfers between devices with their start and end apart: 8 -> 6, of which waited for: 4 -> 3; matrix products, arithmetic and copies ran while one was open for 1% -> 3% of each run, Pallas kernels for 16% -> 14%
where the time goes in v7:
time: 77.4 us; the launch traced here: 76.8 us
  blocking collectives  23.6 us (30%)
  Pallas kernels  17.6 us (23%)
  starting transfers between devices  15.7 us (20%)
  waiting for transfers between devices  13.1 us (17%)
  local copies, waits for them, and re-layouts  6.04 us (8%)
  between operations  0.8 us (1%)
    all_to_all x1, blocking collectives, exchange(): return lax.all_to_all(x, 'wide', split_axis=0, concat_axis=0, tiled=True)  23.6 us
    ppermute x4, waiting for transfers between devices, partner(): lax.ppermute(x, 'wide', [(i, i ^ mask) for i in range(lax.axis_size('wide...  10.5 us
    all_to_all x2, starting transfers between devices, exchange(): return lax.all_to_all(x, 'wide', split_axis=0, concat_axis=0, tiled=True)  7.94 us
    ppermute x4, starting transfers between devices, partner(): lax.ppermute(x, 'wide', [(i, i ^ mask) for i in range(lax.axis_size('wide...  7.73 us
    unnamed x26, local copies, waits for them, and re-layouts  4.76 us
    pallas_call x1, Pallas kernels, per_device(): call(gradient_kernel, [jax.ShapeDtypeStruct((fa, cols), F32), jax.ShapeDt...  4.21 us
    pallas_call x1, Pallas kernels, per_device(): call(pick_kernel, jax.ShapeDtypeStruct(shape, BF16), [hbm(), hbm(), hbm()...  3.38 us
    pallas_call x1, Pallas kernels, per_device(): call(rows_kernel, [jax.ShapeDtypeStruct((n, local_rows, LANES), t) for t...  2.79 us
  transfers between devices with their start and end apart: 6, of which 3 were waited for; matrix products, arithmetic and copies ran while one was open for 3% of the time, Pallas kernels for 14%

profile of v7, /device:TPU:0, one launch (start us, length us, event | category | flops | bytes accessed | tf_op | source)
XLA Modules:
  0.0 76.8 jit_solution(14830221759761142435)
XLA Ops:
  0.6 1.4 %shard_map.139 = bf16[16,1408]{1,0:T(8,128)(2,1)} custom-call(s32[1,4]{1,0:T(1,128)} %list_ref.1, s32[4]{0:T(128)} %slot_ref.1, bf16[4,5120]{1,0:T(4,128)(2,1)} %hidden_ref.1), custom_call_target="tpu_custom_call" | custom-call | bytes 81920 | tf_op jit(solution)/shard_map/pallas_call | solution.py:381
  2.1 4.1 %collective-permute-start = (bf16[1,16,1408]{2,1,0:T(8,128)(2,1)}, bf16[1,16,1408]{2,1,0:T(8,128)(2,1)S(1)}, u32[]{:S(2)}, u32[]{:S(2)}) collective-permute-start(bf16[1,16,1408]{2,1,0:T(8,128)(2,1)} %bitcast.2), channel_id=1, source_target_pairs={{0,8},{1,9},{2,10},{3,11},{4,12},{5,13},{6,14},{7,15},{8,0},{9,1},... | collective-permute-start | bytes 135176 | tf_op jit(solution)/shard_map/ppermute | solution.py:329
  6.2 3.4 %shard_map.140 = bf16[16,16,1152]{2,1,0:T(8,128)(2,1)} custom-call(s32[16]{0:T(128)} %t_ref.3, bf16[256,2048]{1,0:T(8,128)(2,1)} %b_ref.3, bf16[320,2048]{1,0:T(8,128)(2,1)} %a_ref.3), custom_call_target="tpu_custom_call" | custom-call | flops 75497472 | bytes 2359296 | tf_op jit(solution)/shard_map/pallas_call | solution.py:360
  9.6 1.6 %collective-permute-start.1 = (bf16[2,16,1408]{2,1,0:T(8,128)(2,1)S(1)}, bf16[2,16,1408]{2,1,0:T(8,128)(2,1)S(1)}, u32[]{:S(2)}, u32[]{:S(2)}) collective-permute-start(bf16[2,16,1408]{2,1,0:T(8,128)(2,1)S(1)} %pad_maximum_fusion.1), channel_id=1, source_target_pairs={{0,4},{1,5},{2,6},{3,7},{4,0},{5,1},{6,2},{7,3},{8,12},{9,13},{10,... | collective-permute-start | bytes 270344 | tf_op jit(solution)/shard_map/ppermute | solution.py:329
  11.2 0.6 constant_dynamic-update-slice_fusion.2
  11.9 4.5 %all-to-all-start = ((bf16[16,16,1152]{2,1,0:T(8,128)(2,1)}), bf16[16,16,1152]{2,1,0:T(8,128)(2,1)S(1)}, u32[]{:S(2)}, u32[]{:S(2)}) async-start(bf16[16,16,1152]{2,1,0:T(8,128)(2,1)} %shard_map.140), calls=%async_computation | async-start | bytes 1179648 | tf_op jit(solution)/shard_map/all_to_all | solution.py:325
  16.4 2.0 %collective-permute-start.2 = (bf16[4,16,1408]{2,1,0:T(8,128)(2,1)S(1)}, bf16[4,16,1408]{2,1,0:T(8,128)(2,1)S(1)}, u32[]{:S(2)}, u32[]{:S(2)}) collective-permute-start(bf16[4,16,1408]{2,1,0:T(8,128)(2,1)S(1)} %pad_maximum_fusion), channel_id=1, source_target_pairs={{0,2},{1,3},{2,0},{3,1},{4,6},{5,7},{6,4},{7,5},{8,10},{9,11},{10,... | collective-permute-start | bytes 540680 | tf_op jit(solution)/shard_map/ppermute | solution.py:329
  18.4 0.6 constant_dynamic-update-slice_fusion.1
  19.0 9.1 %collective-permute-done.2 = bf16[4,16,1408]{2,1,0:T(8,128)(2,1)S(1)} collective-permute-done((bf16[4,16,1408]{2,1,0:T(8,128)(2,1)S(1)}, bf16[4,16,1408]{2,1,0:T(8,128)(2,1)S(1)}, u32[]{:S(2)}, u32[]{:S(2)}) %collective-permute-start.2) | collective-permute-done | bytes 180256 | tf_op jit(solution)/shard_map/ppermute | solution.py:329
  28.1 0.7 constant_dynamic-update-slice_fusion.h0_ref
  28.8 0.6 dynamic_slice.3.t_ref
  29.4 1.4 %collective-permute-done.3.h1_ref = bf16[8,16,1408]{2,1,0:T(8,128)(2,1)} collective-permute-done((bf16[8,16,1408]{2,1,0:T(8,128)(2,1)}, bf16[8,16,1408]{2,1,0:T(8,128)(2,1)}, u32[]{:S(2)}, u32[]{:S(2)}) %collective-permute-start.3) | collective-permute-done | bytes 360480 | tf_op jit(solution)/shard_map/ppermute | solution.py:329
  30.8 1.2 %copy-done.2 = bf16[128,4096]{1,0:T(8,128)(2,1)S(1)} copy-done((bf16[128,4096]{1,0:T(8,128)(2,1)S(1)}, bf16[128,4096]{1,0:T(8,128)(2,1)}, u32[]{:S(2)}) %copy-start.2) | copy-done | bytes 1048600
  32.0 1.0 %copy-done.7 = bf16[8,16,1408]{2,1,0:T(8,128)(2,1)S(1)} copy-done((bf16[8,16,1408]{2,1,0:T(8,128)(2,1)S(1)}, bf16[8,16,1408]{2,1,0:T(8,128)(2,1)}, u32[]{:S(2)}) %copy-start.7) | copy-done | bytes 360472
  33.0 2.8 %shard_map.141 = (f32[16,4,128]{2,1,0:T(4,128)S(1)}, f32[16,4,128]{2,1,0:T(4,128)S(1)}, s32[16,4,128]{2,1,0:T(4,128)S(1)}) custom-call(s32[1]{0:T(128)} %bitcast.me_ref, bf16[8,16,1408]{2,1,0:T(8,128)(2,1)S(1)} %copy-done.7, bf16[8,16,1408]{2,1,0:T(8,128)(2,1)} %collective-permute-done.3.h1_ref, bf16[128,5120]{1,0:T(8,128)(2,1)S(1)} %copy-done.1, ...), custom_call_target="tpu_custom_call" | custom-call | flops 671088640 | bytes 2621440 | tf_op jit(solution)/shard_map/pallas_call | solution.py:399
  35.8 1.2 %copy-done.3 = bf16[128,4096]{1,0:T(8,128)(2,1)S(1)} copy-done((bf16[128,4096]{1,0:T(8,128)(2,1)S(1)}, bf16[128,4096]{1,0:T(8,128)(2,1)}, u32[]{:S(2)}) %copy-start.3) | copy-done | bytes 1048600
  37.0 1.9 %shard_map.142 = (bf16[16,16,1280]{2,1,0:T(8,128)(2,1)S(1)}, s32[64,128]{1,0:T(8,128)S(1)}) custom-call(s32[1]{0:T(128)} %dynamic_slice.3.t_ref, s32[1]{0:T(128)} %bitcast.me_ref, bf16[128,5120]{1,0:T(8,128)(2,1)S(1)} %copy-done.1, bf16[128,4096]{1,0:T(8,128)(2,1)S(1)} %copy-done.3, bf16[16,16,1152]{2,1,0:T(8,128)(2,1)S(1)} %all-to-all-done.r_ref, ...), custom_call_target="tpu_custom_call" | custom-call | flops 150994944 | bytes 2359296 | tf_op jit(solution)/shard_map/pallas_call | solution.py:428
  39.0 0.0 copy-start.5
  39.0 23.6 %all_to_all.15.part_ref = bf16[16,16,1280]{2,1,0:T(8,128)(2,1)S(1)} all-to-all(bf16[16,16,1280]{2,1,0:T(8,128)(2,1)S(1)} %get-tuple-element.17), channel_id=1, replica_groups=mesh['groups'=2,'wide'=16] {'wide'}, dimensions={0} | all-to-all | bytes 1310720 | tf_op jit(solution)/shard_map/all_to_all | solution.py:325
  62.6 1.8 %shard_map.144 = f32[16,4,256]{2,1,0:T(4,128)} custom-call(s32[16]{0:T(128)S(1)} %copy-done.8, bf16[16,16,1280]{2,1,0:T(8,128)(2,1)S(1)} %all_to_all.15.part_ref, bf16[256,2048]{1,0:T(8,128)(2,1)S(1)} %copy-done.4, s32[64,128]{1,0:T(8,128)S(1)} %get-tuple-element.20.u_ref), custom_call_target="tpu_custom_call" | custom-call | flops 67108864 | bytes 1048576 | tf_op jit(solution)/shard_map/pallas_call | solution.py:442
  64.4 3.5 %all-to-all-start.2 = ((f32[16,4,256]{2,1,0:T(4,128)}), f32[16,4,256]{2,1,0:T(4,128)S(1)}, u32[]{:S(2)}, u32[]{:S(2)}) async-start(f32[16,4,256]{2,1,0:T(4,128)} %shard_map.144), calls=%async_computation.2 | async-start | bytes 131072 | tf_op jit(solution)/shard_map/all_to_all | solution.py:325
  67.9 4.2 %shard_map.143 = (f32[320,2048]{1,0:T(8,128)}, f32[256,2048]{1,0:T(8,128)}) custom-call(s32[16]{0:T(128)S(1)} %copy-done.8, bf16[16,16,1280]{2,1,0:T(8,128)(2,1)S(1)} %all_to_all.15.part_ref), custom_call_target="tpu_custom_call" | custom-call | flops 75497472 | bytes 4718592 | tf_op jit(solution)/shard_map/pallas_call | solution.py:452
  72.1 2.6 %all-to-all-done.2.delta_ref = f32[16,4,256]{2,1,0:T(4,128)S(1)} async-done(((f32[16,4,256]{2,1,0:T(4,128)}), f32[16,4,256]{2,1,0:T(4,128)S(1)}, u32[]{:S(2)}, u32[]{:S(2)}) %all-to-all-start.2) | async-done | bytes 65568 | tf_op jit(solution)/shard_map/all_to_all | solution.py:325
  74.8 2.1 %shard_map.145 = bf16[4,4096]{1,0:T(4,128)(2,1)} custom-call(s32[4]{0:T(128)S(1)} %copy-done.9, f32[16,4,256]{2,1,0:T(4,128)S(1)} %all-to-all-done.2.delta_ref, f32[4,4096]{1,0:T(4,128)S(1)} %convert_element_type.3.base_ref, bf16[4,256,512]{2,1,0:T(8,128)(2,1)S(1)} %copy-done.5, bf16[4,256,512]{2,1,0:T(8,128)(2,1)S(1)} %copy-done.6), custom_call_target="tpu_custom_call" | custom-call | flops 16777216 | bytes 2097152 | tf_op jit(solution)/shard_map/pallas_call | solution.py:460
  (27 shorter events, 0.1 us)
Async XLA Ops:
  2.1 7.5 %copy-start.10 = (bf16[16,1408]{1,0:T(8,128)(2,1)S(1)}, bf16[16,1408]{1,0:T(8,128)(2,1)}, u32[]{:S(2)}) copy-start(bf16[16,1408]{1,0:T(8,128)(2,1)} %shard_map.139) | copy-start | bytes 135172
  2.1 26.7 %copy-start.8 = (s32[16]{0:T(128)S(1)}, s32[16]{0:T(128)}, u32[]{:S(2)}) copy-start(s32[16]{0:T(128)} %t_ref.3) | copy-start | bytes 196
  2.1 28.7 %copy-start = (bf16[320,2048]{1,0:T(8,128)(2,1)S(1)}, bf16[320,2048]{1,0:T(8,128)(2,1)}, u32[]{:S(2)}) copy-start(bf16[320,2048]{1,0:T(8,128)(2,1)} %a_ref.3) | copy-start | bytes 3932164
  2.1 28.7 %copy-start.1 = (bf16[128,5120]{1,0:T(8,128)(2,1)S(1)}, bf16[128,5120]{1,0:T(8,128)(2,1)}, u32[]{:S(2)}) copy-start(bf16[128,5120]{1,0:T(8,128)(2,1)} %x_ref.3) | copy-start | bytes 3932164
  2.1 7.5 %collective-permute-start = (bf16[1,16,1408]{2,1,0:T(8,128)(2,1)}, bf16[1,16,1408]{2,1,0:T(8,128)(2,1)S(1)}, u32[]{:S(2)}, u32[]{:S(2)}) collective-permute-start(bf16[1,16,1408]{2,1,0:T(8,128)(2,1)} %bitcast.2), channel_id=1, source_target_pairs={{0,8},{1,9},{2,10},{3,11},{4,12},{5,13},{6,14},{7,15},{8,0},{9,1},... | collective-permute-start | bytes 135176 | tf_op jit(solution)/shard_map/ppermute | solution.py:329
  9.6 6.7 %collective-permute-start.1 = (bf16[2,16,1408]{2,1,0:T(8,128)(2,1)S(1)}, bf16[2,16,1408]{2,1,0:T(8,128)(2,1)S(1)}, u32[]{:S(2)}, u32[]{:S(2)}) collective-permute-start(bf16[2,16,1408]{2,1,0:T(8,128)(2,1)S(1)} %pad_maximum_fusion.1), channel_id=1, source_target_pairs={{0,4},{1,5},{2,6},{3,7},{4,0},{5,1},{6,2},{7,3},{8,12},{9,13},{10,... | collective-permute-start | bytes 270344 | tf_op jit(solution)/shard_map/ppermute | solution.py:329
  11.9 23.9 %all-to-all-start = ((bf16[16,16,1152]{2,1,0:T(8,128)(2,1)}), bf16[16,16,1152]{2,1,0:T(8,128)(2,1)S(1)}, u32[]{:S(2)}, u32[]{:S(2)}) async-start(bf16[16,16,1152]{2,1,0:T(8,128)(2,1)} %shard_map.140), calls=%async_computation | async-start | bytes 1179648 | tf_op jit(solution)/shard_map/all_to_all | solution.py:325
  16.4 11.7 %collective-permute-start.2 = (bf16[4,16,1408]{2,1,0:T(8,128)(2,1)S(1)}, bf16[4,16,1408]{2,1,0:T(8,128)(2,1)S(1)}, u32[]{:S(2)}, u32[]{:S(2)}) collective-permute-start(bf16[4,16,1408]{2,1,0:T(8,128)(2,1)S(1)} %pad_maximum_fusion), channel_id=1, source_target_pairs={{0,2},{1,3},{2,0},{3,1},{4,6},{5,7},{6,4},{7,5},{8,10},{9,11},{10,... | collective-permute-start | bytes 540680 | tf_op jit(solution)/shard_map/ppermute | solution.py:329
  28.8 2.0 %collective-permute-start.3 = (bf16[8,16,1408]{2,1,0:T(8,128)(2,1)}, bf16[8,16,1408]{2,1,0:T(8,128)(2,1)}, u32[]{:S(2)}, u32[]{:S(2)}) collective-permute-start(bf16[8,16,1408]{2,1,0:T(8,128)(2,1)} %constant_dynamic-update-slice_fusion.h0_ref), channel_id=1, source_target_pairs={{0,1},{1,0},{2,3},{3,2},{4,5},{5,4},{6,7},{7,6},{8,9},{9,8},{10,11... | collective-permute-start | bytes 1081352 | tf_op jit(solution)/shard_map/ppermute | solution.py:329
  30.8 1.2 %copy-start.2 = (bf16[128,4096]{1,0:T(8,128)(2,1)S(1)}, bf16[128,4096]{1,0:T(8,128)(2,1)}, u32[]{:S(2)}) copy-start(bf16[128,4096]{1,0:T(8,128)(2,1)} %g_ref.1) | copy-start | bytes 3145732
  32.0 1.0 %copy-start.7 = (bf16[8,16,1408]{2,1,0:T(8,128)(2,1)S(1)}, bf16[8,16,1408]{2,1,0:T(8,128)(2,1)}, u32[]{:S(2)}) copy-start(bf16[8,16,1408]{2,1,0:T(8,128)(2,1)} %constant_dynamic-update-slice_fusion.h0_ref) | copy-start | bytes 1081348
  35.8 1.2 %copy-start.3 = (bf16[128,4096]{1,0:T(8,128)(2,1)S(1)}, bf16[128,4096]{1,0:T(8,128)(2,1)}, u32[]{:S(2)}) copy-start(bf16[128,4096]{1,0:T(8,128)(2,1)} %g_ref.1) | copy-start | bytes 3145732
  37.0 25.6 %copy-start.4 = (bf16[256,2048]{1,0:T(8,128)(2,1)S(1)}, bf16[256,2048]{1,0:T(8,128)(2,1)}, u32[]{:S(2)}) copy-start(bf16[256,2048]{1,0:T(8,128)(2,1)} %b_ref.3) | copy-start | bytes 3145732
  39.0 28.9 %copy-start.11 = (bf16[4,4096]{1,0:T(4,128)(2,1)S(1)}, bf16[4,4096]{1,0:T(4,128)(2,1)}, u32[]{:S(2)}) copy-start(bf16[4,4096]{1,0:T(4,128)(2,1)} %param.20) | copy-start | bytes 98308
  39.0 35.8 %copy-start.5 = (bf16[4,256,512]{2,1,0:T(8,128)(2,1)S(1)}, bf16[4,256,512]{2,1,0:T(8,128)(2,1)}, u32[]{:S(2)}) copy-start(bf16[4,256,512]{2,1,0:T(8,128)(2,1)} %k_ref.1) | copy-start | bytes 3145732
  39.0 35.8 %copy-start.6 = (bf16[4,256,512]{2,1,0:T(8,128)(2,1)S(1)}, bf16[4,256,512]{2,1,0:T(8,128)(2,1)}, u32[]{:S(2)}) copy-start(bf16[4,256,512]{2,1,0:T(8,128)(2,1)} %v_ref.1) | copy-start | bytes 3145732
  39.0 35.8 %copy-start.9 = (s32[4]{0:T(128)S(1)}, s32[4]{0:T(128)}, u32[]{:S(2)}) copy-start(s32[4]{0:T(128)} %len_ref.1) | copy-start | bytes 52
  64.4 10.4 %all-to-all-start.2 = ((f32[16,4,256]{2,1,0:T(4,128)}), f32[16,4,256]{2,1,0:T(4,128)S(1)}, u32[]{:S(2)}, u32[]{:S(2)}) async-start(f32[16,4,256]{2,1,0:T(4,128)} %shard_map.144), calls=%async_computation.2 | async-start | bytes 131072 | tf_op jit(solution)/shard_map/all_to_all | solution.py:325

commit v8 on v7

--- a/solution.py
+++ b/solution.py
@@ -23,7 +23,7 @@
 F32 = jnp.float32
 BF16 = jnp.bfloat16
 VMEM_LIMIT = 24 * 1024 * 1024
-ALL_VMEM = 60 * 1024 * 1024
+ALL_VMEM = 58 * 1024 * 1024 + 768 * 1024
 
 
 def vmem():
@@ -147,7 +147,7 @@
     return half + pltpu.roll(half, RANK, 1)
 
 
-def rows_kernel(me_ref, h0_ref, h1_ref, x_ref, a_ref, _, hx_ref, base_ref, u_ref, sel):
+def rows_kernel(me_ref, h0_ref, h1_ref, x_ref, a_ref, hx_ref, base_ref, u_ref, sel):
     h = jnp.concatenate([r[k] for r in (h0_ref, h1_ref) for k in range(r.shape[0])], axis=0)
     size = h.shape[1] - LANES
     fa = a_ref.shape[0]
@@ -392,19 +392,19 @@
         masks = [0, n // 2]
         bit = n // 4
         while bit > 1:
-            held = jnp.concatenate([held, partner(held, bit)], axis=0)
+            held = lax.optimization_barrier(jnp.concatenate([held, partner(held, bit)], axis=0))
             masks = masks + [m ^ bit for m in masks]
             bit //= 2
         masks = masks + [m ^ 1 for m in masks]
         found = call(
             rows_kernel,
             [jax.ShapeDtypeStruct((n, local_rows, LANES), t) for t in (F32, F32, jnp.int32)],
-            [smem()] + [vmem()] * 5,
+            [smem()] + [vmem()] * 4,
             [vmem()] * 3,
             scratch=[pltpu.VMEM((n * HALF, fa), BF16)],
             flops=8 * rows * (BLOCK * width + fa * cols),
             nbytes=2 * BLOCK * width + 2 * fa * cols,
-        )(me[None], held, partner(held, 1), tokens, down_factors, query_output_gradient)
+        )(me[None], held, partner(held, 1), tokens, down_factors)
         hx, base_low_rank, tenants = ((f,) for f in found)
     else:
         got = exchange(packed)

time: 77.4 us -> 74.6 us (0.964)
  local copies, waits for them, and re-layouts: 6.04 us -> 1.85 us
    unnamed x26 -> x20, local copies, waits for them, and re-layouts: 4.76 us -> 1.26 us
  transfers between devices with their start and end apart: 6 -> 6, of which waited for: 3 -> 3; matrix products, arithmetic and copies ran while one was open for 3% -> 2% of each run, Pallas kernels for 14% -> 14%
where the time goes in v8:
time: 74.6 us; the launch traced here: 74.1 us
  blocking collectives  23.6 us (32%)
  Pallas kernels  17.6 us (24%)
  starting transfers between devices  15.7 us (21%)
  waiting for transfers between devices  13.8 us (18%)
  local copies, waits for them, and re-layouts  1.85 us (2%)
  other arithmetic  0.82 us (1%)
  between operations  0.79 us (1%)
    all_to_all x1, blocking collectives, exchange(): return lax.all_to_all(x, 'wide', split_axis=0, concat_axis=0, tiled=True)  23.6 us
    ppermute x4, waiting for transfers between devices, partner(): lax.ppermute(x, 'wide', [(i, i ^ mask) for i in range(lax.axis_size('wide...  11.1 us
    all_to_all x2, starting transfers between devices, exchange(): return lax.all_to_all(x, 'wide', split_axis=0, concat_axis=0, tiled=True)  7.94 us
    ppermute x4, starting transfers between devices, partner(): lax.ppermute(x, 'wide', [(i, i ^ mask) for i in range(lax.axis_size('wide...  7.73 us
    pallas_call x1, Pallas kernels, per_device(): call(gradient_kernel, [jax.ShapeDtypeStruct((fa, cols), F32), jax.ShapeDt...  4.2 us
    pallas_call x1, Pallas kernels, per_device(): call(pick_kernel, jax.ShapeDtypeStruct(shape, BF16), [hbm(), hbm(), hbm()...  3.38 us
    pallas_call x1, Pallas kernels, per_device(): call(rows_kernel, [jax.ShapeDtypeStruct((n, local_rows, LANES), t) for t...  2.9 us
    all_to_all x2, waiting for transfers between devices, exchange(): return lax.all_to_all(x, 'wide', split_axis=0, concat_axis=0, tiled=True)  2.63 us
  transfers between devices with their start and end apart: 6, of which 3 were waited for; matrix products, arithmetic and copies ran while one was open for 2% of the time, Pallas kernels for 14%

profile of v8, /device:TPU:0, one launch (start us, length us, event | category | flops | bytes accessed | tf_op | source)
XLA Modules:
  0.0 74.1 jit_solution(7935286145012595670)
XLA Ops:
  0.6 1.4 %shard_map.139 = bf16[16,1408]{1,0:T(8,128)(2,1)} custom-call(s32[1,4]{1,0:T(1,128)} %list_ref.1, s32[4]{0:T(128)} %slot_ref.1, bf16[4,5120]{1,0:T(4,128)(2,1)} %hidden_ref.1), custom_call_target="tpu_custom_call" | custom-call | bytes 81920 | tf_op jit(solution)/shard_map/pallas_call | solution.py:381
  2.1 4.1 %collective-permute-start = (bf16[1,16,1408]{2,1,0:T(8,128)(2,1)}, bf16[1,16,1408]{2,1,0:T(8,128)(2,1)S(1)}, u32[]{:S(2)}, u32[]{:S(2)}) collective-permute-start(bf16[1,16,1408]{2,1,0:T(8,128)(2,1)} %bitcast.2), channel_id=1, source_target_pairs={{0,8},{1,9},{2,10},{3,11},{4,12},{5,13},{6,14},{7,15},{8,0},{9,1},... | collective-permute-start | bytes 135176 | tf_op jit(solution)/shard_map/ppermute | solution.py:329
  6.2 3.4 %shard_map.140 = bf16[16,16,1152]{2,1,0:T(8,128)(2,1)} custom-call(s32[16]{0:T(128)} %t_ref.3, bf16[256,2048]{1,0:T(8,128)(2,1)} %b_ref.3, bf16[320,2048]{1,0:T(8,128)(2,1)} %a_ref.3), custom_call_target="tpu_custom_call" | custom-call | flops 75497472 | bytes 2359296 | tf_op jit(solution)/shard_map/pallas_call | solution.py:360
  9.6 1.6 %collective-permute-start.1 = (bf16[2,16,1408]{2,1,0:T(8,128)(2,1)S(1)}, bf16[2,16,1408]{2,1,0:T(8,128)(2,1)S(1)}, u32[]{:S(2)}, u32[]{:S(2)}) collective-permute-start(bf16[2,16,1408]{2,1,0:T(8,128)(2,1)S(1)} %pad_maximum_fusion.2), channel_id=1, source_target_pairs={{0,4},{1,5},{2,6},{3,7},{4,0},{5,1},{6,2},{7,3},{8,12},{9,13},{10,... | collective-permute-start | bytes 270344 | tf_op jit(solution)/shard_map/ppermute | solution.py:329
  11.2 4.5 %all-to-all-start = ((bf16[16,16,1152]{2,1,0:T(8,128)(2,1)}), bf16[16,16,1152]{2,1,0:T(8,128)(2,1)S(1)}, u32[]{:S(2)}, u32[]{:S(2)}) async-start(bf16[16,16,1152]{2,1,0:T(8,128)(2,1)} %shard_map.140), calls=%async_computation | async-start | bytes 1179648 | tf_op jit(solution)/shard_map/all_to_all | solution.py:325
  15.7 2.0 %collective-permute-start.2 = (bf16[4,16,1408]{2,1,0:T(8,128)(2,1)S(1)}, bf16[4,16,1408]{2,1,0:T(8,128)(2,1)S(1)}, u32[]{:S(2)}, u32[]{:S(2)}) collective-permute-start(bf16[4,16,1408]{2,1,0:T(8,128)(2,1)S(1)} %pad_maximum_fusion.1), channel_id=1, source_target_pairs={{0,2},{1,3},{2,0},{3,1},{4,6},{5,7},{6,4},{7,5},{8,10},{9,11},{10,... | collective-permute-start | bytes 540680 | tf_op jit(solution)/shard_map/ppermute | solution.py:329
  17.7 9.7 %collective-permute-done.2 = bf16[4,16,1408]{2,1,0:T(8,128)(2,1)S(1)} collective-permute-done((bf16[4,16,1408]{2,1,0:T(8,128)(2,1)S(1)}, bf16[4,16,1408]{2,1,0:T(8,128)(2,1)S(1)}, u32[]{:S(2)}, u32[]{:S(2)}) %collective-permute-start.2) | collective-permute-done | bytes 180256 | tf_op jit(solution)/shard_map/ppermute | solution.py:329
  27.4 0.8 %pad_maximum_fusion.h0_ref = bf16[8,16,1408]{2,1,0:T(8,128)(2,1)} fusion(bf16[4,16,1408]{2,1,0:T(8,128)(2,1)S(1)} %collective-permute-done.2, bf16[4,16,1408]{2,1,0:T(8,128)(2,1)S(1)} %pad_maximum_fusion.1), kind=kLoop, calls=%fused_computation | loop fusion | flops 180224 | bytes 720896 | tf_op jit(solution)/shard_map/concatenate | solution.py:395
  28.2 0.6 dynamic_slice.3.t_ref
  28.8 1.4 %collective-permute-done.3.h1_ref = bf16[8,16,1408]{2,1,0:T(8,128)(2,1)} collective-permute-done((bf16[8,16,1408]{2,1,0:T(8,128)(2,1)}, bf16[8,16,1408]{2,1,0:T(8,128)(2,1)}, u32[]{:S(2)}, u32[]{:S(2)}) %collective-permute-start.3) | collective-permute-done | bytes 360480 | tf_op jit(solution)/shard_map/ppermute | solution.py:329
  30.2 2.9 %shard_map.141 = (f32[16,4,128]{2,1,0:T(4,128)S(1)}, f32[16,4,128]{2,1,0:T(4,128)S(1)}, s32[16,4,128]{2,1,0:T(4,128)S(1)}) custom-call(s32[1]{0:T(128)} %bitcast.me_ref, bf16[8,16,1408]{2,1,0:T(8,128)(2,1)} %pad_maximum_fusion.h0_ref, bf16[8,16,1408]{2,1,0:T(8,128)(2,1)} %collective-permute-done.3.h1_ref, bf16[128,5120]{1,0:T(8,128)(2,1)S(1)} %copy-done.1, ...), custom_call_target="tpu_custom_call" | custom-call | flops 671088640 | bytes 2621440 | tf_op jit(solution)/shard_map/pallas_call | solution.py:399
  33.1 0.0 copy-start.5
  33.2 1.2 %copy-done.5 = bf16[128,4096]{1,0:T(8,128)(2,1)S(1)} copy-done((bf16[128,4096]{1,0:T(8,128)(2,1)S(1)}, bf16[128,4096]{1,0:T(8,128)(2,1)}, u32[]{:S(2)}) %copy-start.5) | copy-done | bytes 1048600
  34.4 1.9 %shard_map.142 = (bf16[16,16,1280]{2,1,0:T(8,128)(2,1)S(1)}, s32[64,128]{1,0:T(8,128)S(1)}) custom-call(s32[1]{0:T(128)} %dynamic_slice.3.t_ref, s32[1]{0:T(128)} %bitcast.me_ref, bf16[128,5120]{1,0:T(8,128)(2,1)S(1)} %copy-done.1, bf16[128,4096]{1,0:T(8,128)(2,1)S(1)} %copy-done.5, bf16[16,16,1152]{2,1,0:T(8,128)(2,1)S(1)} %all-to-all-done.r_ref, ...), custom_call_target="tpu_custom_call" | custom-call | flops 150994944 | bytes 2359296 | tf_op jit(solution)/shard_map/pallas_call | solution.py:428
  36.3 0.0 copy-start.9
  36.3 0.0 copy-start.3
  36.3 0.0 copy-start.4
  36.3 0.0 copy-start.7
  36.3 23.6 %all_to_all.15.part_ref = bf16[16,16,1280]{2,1,0:T(8,128)(2,1)S(1)} all-to-all(bf16[16,16,1280]{2,1,0:T(8,128)(2,1)S(1)} %get-tuple-element.17), channel_id=1, replica_groups=mesh['groups'=2,'wide'=16] {'wide'}, dimensions={0} | all-to-all | bytes 1310720 | tf_op jit(solution)/shard_map/all_to_all | solution.py:325
  59.9 1.8 %shard_map.144 = f32[16,4,256]{2,1,0:T(4,128)} custom-call(s32[16]{0:T(128)S(1)} %copy-done.6, bf16[16,16,1280]{2,1,0:T(8,128)(2,1)S(1)} %all_to_all.15.part_ref, bf16[256,2048]{1,0:T(8,128)(2,1)S(1)} %copy-done.2, s32[64,128]{1,0:T(8,128)S(1)} %get-tuple-element.20.u_ref), custom_call_target="tpu_custom_call" | custom-call | flops 67108864 | bytes 1048576 | tf_op jit(solution)/shard_map/pallas_call | solution.py:442
  61.7 3.5 %all-to-all-start.2 = ((f32[16,4,256]{2,1,0:T(4,128)}), f32[16,4,256]{2,1,0:T(4,128)S(1)}, u32[]{:S(2)}, u32[]{:S(2)}) async-start(f32[16,4,256]{2,1,0:T(4,128)} %shard_map.144), calls=%async_computation.2 | async-start | bytes 131072 | tf_op jit(solution)/shard_map/all_to_all | solution.py:325
  65.2 4.2 %shard_map.143 = (f32[320,2048]{1,0:T(8,128)}, f32[256,2048]{1,0:T(8,128)}) custom-call(s32[16]{0:T(128)S(1)} %copy-done.6, bf16[16,16,1280]{2,1,0:T(8,128)(2,1)S(1)} %all_to_all.15.part_ref), custom_call_target="tpu_custom_call" | custom-call | flops 75497472 | bytes 4718592 | tf_op jit(solution)/shard_map/pallas_call | solution.py:452
  69.4 2.6 %all-to-all-done.2.delta_ref = f32[16,4,256]{2,1,0:T(4,128)S(1)} async-done(((f32[16,4,256]{2,1,0:T(4,128)}), f32[16,4,256]{2,1,0:T(4,128)S(1)}, u32[]{:S(2)}, u32[]{:S(2)}) %all-to-all-start.2) | async-done | bytes 65568 | tf_op jit(solution)/shard_map/all_to_all | solution.py:325
  72.1 2.1 %shard_map.145 = bf16[4,4096]{1,0:T(4,128)(2,1)} custom-call(s32[4]{0:T(128)S(1)} %copy-done.7, f32[16,4,256]{2,1,0:T(4,128)S(1)} %all-to-all-done.2.delta_ref, f32[4,4096]{1,0:T(4,128)S(1)} %convert_element_type.3.base_ref, bf16[4,256,512]{2,1,0:T(8,128)(2,1)S(1)} %copy-done.3, bf16[4,256,512]{2,1,0:T(8,128)(2,1)S(1)} %copy-done.4), custom_call_target="tpu_custom_call" | custom-call | flops 16777216 | bytes 2097152 | tf_op jit(solution)/shard_map/pallas_call | solution.py:460
  (21 shorter events, 0.1 us)
Async XLA Ops:
  2.1 7.5 %copy-start.8 = (bf16[16,1408]{1,0:T(8,128)(2,1)S(1)}, bf16[16,1408]{1,0:T(8,128)(2,1)}, u32[]{:S(2)}) copy-start(bf16[16,1408]{1,0:T(8,128)(2,1)} %shard_map.139) | copy-start | bytes 135172
  2.1 26.2 %copy-start.6 = (s32[16]{0:T(128)S(1)}, s32[16]{0:T(128)}, u32[]{:S(2)}) copy-start(s32[16]{0:T(128)} %t_ref.3) | copy-start | bytes 196
  2.1 28.2 %copy-start = (bf16[320,2048]{1,0:T(8,128)(2,1)S(1)}, bf16[320,2048]{1,0:T(8,128)(2,1)}, u32[]{:S(2)}) copy-start(bf16[320,2048]{1,0:T(8,128)(2,1)} %a_ref.3) | copy-start | bytes 3932164
  2.1 28.2 %copy-start.1 = (bf16[128,5120]{1,0:T(8,128)(2,1)S(1)}, bf16[128,5120]{1,0:T(8,128)(2,1)}, u32[]{:S(2)}) copy-start(bf16[128,5120]{1,0:T(8,128)(2,1)} %x_ref.3) | copy-start | bytes 3932164
  2.1 7.5 %collective-permute-start = (bf16[1,16,1408]{2,1,0:T(8,128)(2,1)}, bf16[1,16,1408]{2,1,0:T(8,128)(2,1)S(1)}, u32[]{:S(2)}, u32[]{:S(2)}) collective-permute-start(bf16[1,16,1408]{2,1,0:T(8,128)(2,1)} %bitcast.2), channel_id=1, source_target_pairs={{0,8},{1,9},{2,10},{3,11},{4,12},{5,13},{6,14},{7,15},{8,0},{9,1},... | collective-permute-start | bytes 135176 | tf_op jit(solution)/shard_map/ppermute | solution.py:329
  9.6 6.1 %collective-permute-start.1 = (bf16[2,16,1408]{2,1,0:T(8,128)(2,1)S(1)}, bf16[2,16,1408]{2,1,0:T(8,128)(2,1)S(1)}, u32[]{:S(2)}, u32[]{:S(2)}) collective-permute-start(bf16[2,16,1408]{2,1,0:T(8,128)(2,1)S(1)} %pad_maximum_fusion.2), channel_id=1, source_target_pairs={{0,4},{1,5},{2,6},{3,7},{4,0},{5,1},{6,2},{7,3},{8,12},{9,13},{10,... | collective-permute-start | bytes 270344 | tf_op jit(solution)/shard_map/ppermute | solution.py:329
  11.2 21.9 %all-to-all-start = ((bf16[16,16,1152]{2,1,0:T(8,128)(2,1)}), bf16[16,16,1152]{2,1,0:T(8,128)(2,1)S(1)}, u32[]{:S(2)}, u32[]{:S(2)}) async-start(bf16[16,16,1152]{2,1,0:T(8,128)(2,1)} %shard_map.140), calls=%async_computation | async-start | bytes 1179648 | tf_op jit(solution)/shard_map/all_to_all | solution.py:325
  15.7 11.7 %collective-permute-start.2 = (bf16[4,16,1408]{2,1,0:T(8,128)(2,1)S(1)}, bf16[4,16,1408]{2,1,0:T(8,128)(2,1)S(1)}, u32[]{:S(2)}, u32[]{:S(2)}) collective-permute-start(bf16[4,16,1408]{2,1,0:T(8,128)(2,1)S(1)} %pad_maximum_fusion.1), channel_id=1, source_target_pairs={{0,2},{1,3},{2,0},{3,1},{4,6},{5,7},{6,4},{7,5},{8,10},{9,11},{10,... | collective-permute-start | bytes 540680 | tf_op jit(solution)/shard_map/ppermute | solution.py:329
  28.2 2.0 %collective-permute-start.3 = (bf16[8,16,1408]{2,1,0:T(8,128)(2,1)}, bf16[8,16,1408]{2,1,0:T(8,128)(2,1)}, u32[]{:S(2)}, u32[]{:S(2)}) collective-permute-start(bf16[8,16,1408]{2,1,0:T(8,128)(2,1)} %pad_maximum_fusion.h0_ref), channel_id=1, source_target_pairs={{0,1},{1,0},{2,3},{3,2},{4,5},{5,4},{6,7},{7,6},{8,9},{9,8},{10,11... | collective-permute-start | bytes 1081352 | tf_op jit(solution)/shard_map/ppermute | solution.py:329
  33.1 1.2 %copy-start.5 = (bf16[128,4096]{1,0:T(8,128)(2,1)S(1)}, bf16[128,4096]{1,0:T(8,128)(2,1)}, u32[]{:S(2)}) copy-start(bf16[128,4096]{1,0:T(8,128)(2,1)} %g_ref.1) | copy-start | bytes 3145732
  34.4 25.6 %copy-start.2 = (bf16[256,2048]{1,0:T(8,128)(2,1)S(1)}, bf16[256,2048]{1,0:T(8,128)(2,1)}, u32[]{:S(2)}) copy-start(bf16[256,2048]{1,0:T(8,128)(2,1)} %b_ref.3) | copy-start | bytes 3145732
  36.3 28.9 %copy-start.9 = (bf16[4,4096]{1,0:T(4,128)(2,1)S(1)}, bf16[4,4096]{1,0:T(4,128)(2,1)}, u32[]{:S(2)}) copy-start(bf16[4,4096]{1,0:T(4,128)(2,1)} %param.20) | copy-start | bytes 98308
  36.3 35.8 %copy-start.3 = (bf16[4,256,512]{2,1,0:T(8,128)(2,1)S(1)}, bf16[4,256,512]{2,1,0:T(8,128)(2,1)}, u32[]{:S(2)}) copy-start(bf16[4,256,512]{2,1,0:T(8,128)(2,1)} %k_ref.1) | copy-start | bytes 3145732
  36.3 35.8 %copy-start.4 = (bf16[4,256,512]{2,1,0:T(8,128)(2,1)S(1)}, bf16[4,256,512]{2,1,0:T(8,128)(2,1)}, u32[]{:S(2)}) copy-start(bf16[4,256,512]{2,1,0:T(8,128)(2,1)} %v_ref.1) | copy-start | bytes 3145732
  36.3 35.8 %copy-start.7 = (s32[4]{0:T(128)S(1)}, s32[4]{0:T(128)}, u32[]{:S(2)}) copy-start(s32[4]{0:T(128)} %len_ref.1) | copy-start | bytes 52
  61.7 10.4 %all-to-all-start.2 = ((f32[16,4,256]{2,1,0:T(4,128)}), f32[16,4,256]{2,1,0:T(4,128)S(1)}, u32[]{:S(2)}, u32[]{:S(2)}) async-start(f32[16,4,256]{2,1,0:T(4,128)} %shard_map.144), calls=%async_computation.2 | async-start | bytes 131072 | tf_op jit(solution)/shard_map/all_to_all | solution.py:325

commit v9 on v8

--- a/solution.py
+++ b/solution.py
@@ -24,6 +24,7 @@
 BF16 = jnp.bfloat16
 VMEM_LIMIT = 24 * 1024 * 1024
 ALL_VMEM = 58 * 1024 * 1024 + 768 * 1024
+ROWS_VMEM = 57 * 1024 * 1024 + 256 * 1024
 
 
 def vmem():
@@ -147,14 +148,18 @@
     return half + pltpu.roll(half, RANK, 1)
 
 
-def rows_kernel(me_ref, h0_ref, h1_ref, x_ref, a_ref, hx_ref, base_ref, u_ref, sel):
+def rows_kernel(me_ref, h0_ref, h1_ref, x_ref, a_ref, g_ref, hx_ref, base_ref, u_ref, g_out, sel, sem):
+    copy = pltpu.make_async_copy(g_ref, g_out, sem)
+    copy.start()
     h = jnp.concatenate([r[k] for r in (h0_ref, h1_ref) for k in range(r.shape[0])], axis=0)
+    tiles = h.shape[0] // HALF
     size = h.shape[1] - LANES
     fa = a_ref.shape[0]
-    part = lax.broadcasted_iota(jnp.int32, (h.shape[0], LANES), 0) % HALF // ROWS_DEV
-    hx = jnp.zeros((h.shape[0], LANES), F32)
-    for p in range(CHUNKS):
-        hx = jnp.where(part == p, dot(h[:, :size], x_ref[:, p * size : (p + 1) * size], 1, 1), hx)
+
+    def group(value, p):
+        first = [k * HALF + p * ROWS_DEV for k in range(tiles)]
+        return jnp.concatenate([value[f : f + ROWS_DEV] for f in first], axis=0)
+
     per_chunk = size // fa
     for m in range(per_chunk):
 
@@ -162,14 +167,21 @@
         def _():
             sel[...] = h[:, m * fa : (m + 1) * fa]
 
-    tenant = h[:, size:].astype(F32).astype(jnp.int32)
-    base = fold_rows(dot(sel[...], a_ref[...], 1, 0), tenant)
-    base = jnp.where(part == me_ref[0] // per_chunk, base, 0.0)
-    for k in range(h.shape[0] // HALF):
-        for value, dest in ((hx, hx_ref), (base, base_ref)):
-            eight = value[k * HALF : k * HALF + 8] + value[k * HALF + 8 : (k + 1) * HALF]
-            dest[k] = eight[:ROWS_DEV] + eight[ROWS_DEV:]
-        u_ref[k] = tenant[k * HALF : k * HALF + ROWS_DEV]
+    wide = h.astype(F32)
+    hx = jnp.zeros((tiles * ROWS_DEV, BLOCK), F32)
+    for p in range(CHUNKS):
+        chunk = group(wide[:, :size], p).astype(BF16)
+        hx = hx + dot(chunk, x_ref[:, p * size : (p + 1) * size], 1, 1)
+    tenant = group(wide[:, size:], 0).astype(jnp.int32)
+    mine = sel[...].astype(F32)
+    cols = group(mine, 0)
+    for p in range(1, CHUNKS):
+        cols = jnp.where(me_ref[0] // per_chunk == p, group(mine, p), cols)
+    base = fold_rows(dot(cols.astype(BF16), a_ref[...], 1, 0), tenant)
+    for k in range(tiles):
+        rows = slice(k * ROWS_DEV, (k + 1) * ROWS_DEV)
+        hx_ref[k], base_ref[k], u_ref[k] = hx[rows], base[rows], tenant[rows]
+    copy.wait()
 
 
 def plain_rows_kernel(h_ref, x_ref, a_ref, hc_ref, u_ref, hx_ref, base_ref):
@@ -396,15 +408,17 @@
             masks = masks + [m ^ bit for m in masks]
             bit //= 2
         masks = masks + [m ^ 1 for m in masks]
-        found = call(
+        *found, query_output_gradient = call(
             rows_kernel,
-            [jax.ShapeDtypeStruct((n, local_rows, LANES), t) for t in (F32, F32, jnp.int32)],
-            [smem()] + [vmem()] * 4,
-            [vmem()] * 3,
-            scratch=[pltpu.VMEM((n * HALF, fa), BF16)],
-            flops=8 * rows * (BLOCK * width + fa * cols),
+            [jax.ShapeDtypeStruct((n, local_rows, LANES), t) for t in (F32, F32, jnp.int32)]
+            + [jax.ShapeDtypeStruct(query_output_gradient.shape, BF16)],
+            [smem()] + [vmem()] * 4 + [hbm()],
+            [vmem()] * 4,
+            scratch=[pltpu.VMEM((n * HALF, fa), BF16), pltpu.SemaphoreType.DMA],
+            limit=ROWS_VMEM,
+            flops=2 * rows * (BLOCK * width + fa * cols),
             nbytes=2 * BLOCK * width + 2 * fa * cols,
-        )(me[None], held, partner(held, 1), tokens, down_factors)
+        )(me[None], held, partner(held, 1), tokens, down_factors, query_output_gradient)
         hx, base_low_rank, tenants = ((f,) for f in found)
     else:
         got = exchange(packed)

time: 74.6 us -> 78.2 us (1.048)
  local copies, waits for them, and re-layouts: 1.85 us -> 4.88 us
  Pallas kernels: 17.6 us -> 19 us
    unnamed x20 -> x28, local copies, waits for them, and re-layouts: 1.26 us -> 4.26 us
    pallas_call x1, Pallas kernels: 2.9 us -> 4.27 us  [per_device(): call(rows_kernel, [jax.ShapeDtypeStruct((n, local_rows, LANES), t) for t...]
  transfers between devices with their start and end apart: 6 -> 6, of which waited for: 3 -> 3; matrix products, arithmetic and copies ran while one was open for 2% -> 1% of each run, Pallas kernels for 14% -> 15%
where the time goes in v9:
time: 78.2 us; the launch traced here: 77.5 us
  blocking collectives  23.6 us (30%)
  Pallas kernels  19 us (24%)
  starting transfers between devices  15.7 us (20%)
  waiting for transfers between devices  13.4 us (17%)
  local copies, waits for them, and re-layouts  4.88 us (6%)
  between operations  0.83 us (1%)
    all_to_all x1, blocking collectives, exchange(): return lax.all_to_all(x, 'wide', split_axis=0, concat_axis=0, tiled=True)  23.6 us
    ppermute x4, waiting for transfers between devices, partner(): lax.ppermute(x, 'wide', [(i, i ^ mask) for i in range(lax.axis_size('wide...  10.7 us
    all_to_all x2, starting transfers between devices, exchange(): return lax.all_to_all(x, 'wide', split_axis=0, concat_axis=0, tiled=True)  7.94 us
    ppermute x4, starting transfers between devices, partner(): lax.ppermute(x, 'wide', [(i, i ^ mask) for i in range(lax.axis_size('wide...  7.74 us
    pallas_call x1, Pallas kernels, per_device(): call(rows_kernel, [jax.ShapeDtypeStruct((n, local_rows, LANES), t) for t...  4.27 us
    unnamed x28, local copies, waits for them, and re-layouts  4.26 us
    pallas_call x1, Pallas kernels, per_device(): call(gradient_kernel, [jax.ShapeDtypeStruct((fa, cols), F32), jax.ShapeDt...  4.19 us
    pallas_call x1, Pallas kernels, per_device(): call(pick_kernel, jax.ShapeDtypeStruct(shape, BF16), [hbm(), hbm(), hbm()...  3.38 us
  transfers between devices with their start and end apart: 6, of which 3 were waited for; matrix products, arithmetic and copies ran while one was open for 1% of the time, Pallas kernels for 15%

profile of v9, /device:TPU:0, one launch (start us, length us, event | category | flops | bytes accessed | tf_op | source)
XLA Modules:
  0.0 77.5 jit_solution(17863600342997309018)
XLA Ops:
  0.6 1.4 %shard_map.139 = bf16[16,1408]{1,0:T(8,128)(2,1)} custom-call(s32[1,4]{1,0:T(1,128)} %list_ref.1, s32[4]{0:T(128)} %slot_ref.1, bf16[4,5120]{1,0:T(4,128)(2,1)} %hidden_ref.1), custom_call_target="tpu_custom_call" | custom-call | bytes 81920 | tf_op jit(solution)/shard_map/pallas_call | solution.py:393
  2.1 4.0 %collective-permute-start = (bf16[1,16,1408]{2,1,0:T(8,128)(2,1)}, bf16[1,16,1408]{2,1,0:T(8,128)(2,1)S(1)}, u32[]{:S(2)}, u32[]{:S(2)}) collective-permute-start(bf16[1,16,1408]{2,1,0:T(8,128)(2,1)} %bitcast.2), channel_id=1, source_target_pairs={{0,8},{1,9},{2,10},{3,11},{4,12},{5,13},{6,14},{7,15},{8,0},{9,1},... | collective-permute-start | bytes 135176 | tf_op jit(solution)/shard_map/ppermute | solution.py:341
  6.1 3.4 %shard_map.140 = bf16[16,16,1152]{2,1,0:T(8,128)(2,1)} custom-call(s32[16]{0:T(128)} %t_ref.3, bf16[256,2048]{1,0:T(8,128)(2,1)} %b_ref.3, bf16[320,2048]{1,0:T(8,128)(2,1)} %a_ref.3), custom_call_target="tpu_custom_call" | custom-call | flops 75497472 | bytes 2359296 | tf_op jit(solution)/shard_map/pallas_call | solution.py:372
  9.5 1.6 %collective-permute-start.1 = (bf16[2,16,1408]{2,1,0:T(8,128)(2,1)S(1)}, bf16[2,16,1408]{2,1,0:T(8,128)(2,1)S(1)}, u32[]{:S(2)}, u32[]{:S(2)}) collective-permute-start(bf16[2,16,1408]{2,1,0:T(8,128)(2,1)S(1)} %pad_maximum_fusion.2), channel_id=1, source_target_pairs={{0,4},{1,5},{2,6},{3,7},{4,0},{5,1},{6,2},{7,3},{8,12},{9,13},{10,... | collective-permute-start | bytes 270344 | tf_op jit(solution)/shard_map/ppermute | solution.py:341
  11.2 4.5 %all-to-all-start = ((bf16[16,16,1152]{2,1,0:T(8,128)(2,1)}), bf16[16,16,1152]{2,1,0:T(8,128)(2,1)S(1)}, u32[]{:S(2)}, u32[]{:S(2)}) async-start(bf16[16,16,1152]{2,1,0:T(8,128)(2,1)} %shard_map.140), calls=%async_computation | async-start | bytes 1179648 | tf_op jit(solution)/shard_map/all_to_all | solution.py:337
  15.7 2.0 %collective-permute-start.2 = (bf16[4,16,1408]{2,1,0:T(8,128)(2,1)S(1)}, bf16[4,16,1408]{2,1,0:T(8,128)(2,1)S(1)}, u32[]{:S(2)}, u32[]{:S(2)}) collective-permute-start(bf16[4,16,1408]{2,1,0:T(8,128)(2,1)S(1)} %pad_maximum_fusion.1), channel_id=1, source_target_pairs={{0,2},{1,3},{2,0},{3,1},{4,6},{5,7},{6,4},{7,5},{8,10},{9,11},{10,... | collective-permute-start | bytes 540680 | tf_op jit(solution)/shard_map/ppermute | solution.py:341
  17.7 9.7 %collective-permute-done.2 = bf16[4,16,1408]{2,1,0:T(8,128)(2,1)S(1)} collective-permute-done((bf16[4,16,1408]{2,1,0:T(8,128)(2,1)S(1)}, bf16[4,16,1408]{2,1,0:T(8,128)(2,1)S(1)}, u32[]{:S(2)}, u32[]{:S(2)}) %collective-permute-start.2) | collective-permute-done | bytes 180256 | tf_op jit(solution)/shard_map/ppermute | solution.py:341
  27.4 0.1 collective-permute-start.3
  27.5 0.6 dynamic_slice.3.t_ref
  28.1 1.0 %collective-permute-done.3.h1_ref = bf16[8,16,1408]{2,1,0:T(8,128)(2,1)S(1)} collective-permute-done((bf16[8,16,1408]{2,1,0:T(8,128)(2,1)S(1)}, bf16[8,16,1408]{2,1,0:T(8,128)(2,1)S(1)}, u32[]{:S(2)}, u32[]{:S(2)}) %collective-permute-start.3) | collective-permute-done | bytes 360480 | tf_op jit(solution)/shard_map/ppermute | solution.py:341
  29.2 0.7 copy-done.11
  29.9 4.3 %shard_map.141 = (f32[16,4,128]{2,1,0:T(4,128)}, f32[16,4,128]{2,1,0:T(4,128)}, s32[16,4,128]{2,1,0:T(4,128)}, bf16[128,4096]{1,0:T(8,128)(2,1)}) custom-call(s32[1]{0:T(128)} %bitcast.me_ref, bf16[8,16,1408]{2,1,0:T(8,128)(2,1)} %copy-done.10, bf16[8,16,1408]{2,1,0:T(8,128)(2,1)} %copy-done.11, bf16[128,5120]{1,0:T(8,128)(2,1)} %x_ref.3, ...), custom_call_target="tpu_custom_call" | custom-call | flops 167772160 | bytes 2621440 | tf_op jit(solution)/shard_map/pallas_call | solution.py:411
  34.2 1.2 %copy-done.4 = bf16[128,4096]{1,0:T(8,128)(2,1)S(1)} copy-done((bf16[128,4096]{1,0:T(8,128)(2,1)S(1)}, bf16[128,4096]{1,0:T(8,128)(2,1)}, u32[]{:S(2)}) %copy-start.4) | copy-done | bytes 1048600
  35.4 0.8 copy-done.5
  36.2 0.8 copy-done.6
  36.9 0.8 copy-done.7
  37.7 1.9 %shard_map.142 = (bf16[16,16,1280]{2,1,0:T(8,128)(2,1)S(1)}, s32[64,128]{1,0:T(8,128)S(1)}) custom-call(s32[1]{0:T(128)} %dynamic_slice.3.t_ref, s32[1]{0:T(128)} %bitcast.me_ref, bf16[128,5120]{1,0:T(8,128)(2,1)S(1)} %copy-done, bf16[128,4096]{1,0:T(8,128)(2,1)S(1)} %copy-done.4, bf16[16,16,1152]{2,1,0:T(8,128)(2,1)S(1)} %all-to-all-done.r_ref, ...), custom_call_target="tpu_custom_call" | custom-call | flops 150994944 | bytes 2359296 | tf_op jit(solution)/shard_map/pallas_call | solution.py:442
  39.6 0.0 copy-start.2
  39.7 23.6 %all_to_all.15.part_ref = bf16[16,16,1280]{2,1,0:T(8,128)(2,1)S(1)} all-to-all(bf16[16,16,1280]{2,1,0:T(8,128)(2,1)S(1)} %get-tuple-element.19), channel_id=1, replica_groups=mesh['groups'=2,'wide'=16] {'wide'}, dimensions={0} | all-to-all | bytes 1310720 | tf_op jit(solution)/shard_map/all_to_all | solution.py:337
  63.3 1.8 %shard_map.144 = f32[16,4,256]{2,1,0:T(4,128)} custom-call(s32[16]{0:T(128)S(1)} %copy-done.8, bf16[16,16,1280]{2,1,0:T(8,128)(2,1)S(1)} %all_to_all.15.part_ref, bf16[256,2048]{1,0:T(8,128)(2,1)S(1)} %copy-done.1, s32[64,128]{1,0:T(8,128)S(1)} %get-tuple-element.22.u_ref), custom_call_target="tpu_custom_call" | custom-call | flops 67108864 | bytes 1048576 | tf_op jit(solution)/shard_map/pallas_call | solution.py:456
  65.0 3.5 %all-to-all-start.2 = ((f32[16,4,256]{2,1,0:T(4,128)}), f32[16,4,256]{2,1,0:T(4,128)S(1)}, u32[]{:S(2)}, u32[]{:S(2)}) async-start(f32[16,4,256]{2,1,0:T(4,128)} %shard_map.144), calls=%async_computation.2 | async-start | bytes 131072 | tf_op jit(solution)/shard_map/all_to_all | solution.py:337
  68.6 4.2 %shard_map.143 = (f32[320,2048]{1,0:T(8,128)}, f32[256,2048]{1,0:T(8,128)}) custom-call(s32[16]{0:T(128)S(1)} %copy-done.8, bf16[16,16,1280]{2,1,0:T(8,128)(2,1)S(1)} %all_to_all.15.part_ref), custom_call_target="tpu_custom_call" | custom-call | flops 75497472 | bytes 4718592 | tf_op jit(solution)/shard_map/pallas_call | solution.py:466
  72.8 2.6 %all-to-all-done.2.delta_ref = f32[16,4,256]{2,1,0:T(4,128)S(1)} async-done(((f32[16,4,256]{2,1,0:T(4,128)}), f32[16,4,256]{2,1,0:T(4,128)S(1)}, u32[]{:S(2)}, u32[]{:S(2)}) %all-to-all-start.2) | async-done | bytes 65568 | tf_op jit(solution)/shard_map/all_to_all | solution.py:337
  75.4 2.1 %shard_map.145 = bf16[4,4096]{1,0:T(4,128)(2,1)} custom-call(s32[4]{0:T(128)S(1)} %copy-done.9, f32[16,4,256]{2,1,0:T(4,128)S(1)} %all-to-all-done.2.delta_ref, f32[4,4096]{1,0:T(4,128)S(1)} %convert_element_type.3.base_ref, bf16[4,256,512]{2,1,0:T(8,128)(2,1)S(1)} %copy-done.2, bf16[4,256,512]{2,1,0:T(8,128)(2,1)S(1)} %copy-done.3), custom_call_target="tpu_custom_call" | custom-call | flops 16777216 | bytes 2097152 | tf_op jit(solution)/shard_map/pallas_call | solution.py:474
  (29 shorter events, 0.1 us)
Async XLA Ops:
  2.1 7.4 %copy-start.12 = (bf16[16,1408]{1,0:T(8,128)(2,1)S(1)}, bf16[16,1408]{1,0:T(8,128)(2,1)}, u32[]{:S(2)}) copy-start(bf16[16,1408]{1,0:T(8,128)(2,1)} %shard_map.139) | copy-start | bytes 135172
  2.1 25.4 %copy-start.8 = (s32[16]{0:T(128)S(1)}, s32[16]{0:T(128)}, u32[]{:S(2)}) copy-start(s32[16]{0:T(128)} %t_ref.3) | copy-start | bytes 196
  2.1 7.4 %collective-permute-start = (bf16[1,16,1408]{2,1,0:T(8,128)(2,1)}, bf16[1,16,1408]{2,1,0:T(8,128)(2,1)S(1)}, u32[]{:S(2)}, u32[]{:S(2)}) collective-permute-start(bf16[1,16,1408]{2,1,0:T(8,128)(2,1)} %bitcast.2), channel_id=1, source_target_pairs={{0,8},{1,9},{2,10},{3,11},{4,12},{5,13},{6,14},{7,15},{8,0},{9,1},... | collective-permute-start | bytes 135176 | tf_op jit(solution)/shard_map/ppermute | solution.py:341
  9.5 6.1 %collective-permute-start.1 = (bf16[2,16,1408]{2,1,0:T(8,128)(2,1)S(1)}, bf16[2,16,1408]{2,1,0:T(8,128)(2,1)S(1)}, u32[]{:S(2)}, u32[]{:S(2)}) collective-permute-start(bf16[2,16,1408]{2,1,0:T(8,128)(2,1)S(1)} %pad_maximum_fusion.2), channel_id=1, source_target_pairs={{0,4},{1,5},{2,6},{3,7},{4,0},{5,1},{6,2},{7,3},{8,12},{9,13},{10,... | collective-permute-start | bytes 270344 | tf_op jit(solution)/shard_map/ppermute | solution.py:341
  11.2 23.0 %all-to-all-start = ((bf16[16,16,1152]{2,1,0:T(8,128)(2,1)}), bf16[16,16,1152]{2,1,0:T(8,128)(2,1)S(1)}, u32[]{:S(2)}, u32[]{:S(2)}) async-start(bf16[16,16,1152]{2,1,0:T(8,128)(2,1)} %shard_map.140), calls=%async_computation | async-start | bytes 1179648 | tf_op jit(solution)/shard_map/all_to_all | solution.py:337
  15.7 11.7 %collective-permute-start.2 = (bf16[4,16,1408]{2,1,0:T(8,128)(2,1)S(1)}, bf16[4,16,1408]{2,1,0:T(8,128)(2,1)S(1)}, u32[]{:S(2)}, u32[]{:S(2)}) collective-permute-start(bf16[4,16,1408]{2,1,0:T(8,128)(2,1)S(1)} %pad_maximum_fusion.1), channel_id=1, source_target_pairs={{0,2},{1,3},{2,0},{3,1},{4,6},{5,7},{6,4},{7,5},{8,10},{9,11},{10,... | collective-permute-start | bytes 540680 | tf_op jit(solution)/shard_map/ppermute | solution.py:341
  27.4 1.8 %copy-start.10 = (bf16[8,16,1408]{2,1,0:T(8,128)(2,1)}, bf16[8,16,1408]{2,1,0:T(8,128)(2,1)S(1)}, u32[]{:S(2)}) copy-start(bf16[8,16,1408]{2,1,0:T(8,128)(2,1)S(1)} %pad_maximum_fusion.h0_ref) | copy-start | bytes 1081348
  27.4 1.7 %collective-permute-start.3 = (bf16[8,16,1408]{2,1,0:T(8,128)(2,1)S(1)}, bf16[8,16,1408]{2,1,0:T(8,128)(2,1)S(1)}, u32[]{:S(2)}, u32[]{:S(2)}) collective-permute-start(bf16[8,16,1408]{2,1,0:T(8,128)(2,1)S(1)} %pad_maximum_fusion.h0_ref), channel_id=1, source_target_pairs={{0,1},{1,0},{2,3},{3,2},{4,5},{5,4},{6,7},{7,6},{8,9},{9,8},{10,11... | collective-permute-start | bytes 1081352 | tf_op jit(solution)/shard_map/ppermute | solution.py:341
  29.2 0.7 copy-start.11
  29.9 4.3 %copy-start = (bf16[128,5120]{1,0:T(8,128)(2,1)S(1)}, bf16[128,5120]{1,0:T(8,128)(2,1)}, u32[]{:S(2)}) copy-start(bf16[128,5120]{1,0:T(8,128)(2,1)} %x_ref.3) | copy-start | bytes 3932164
  34.2 1.2 %copy-start.4 = (bf16[128,4096]{1,0:T(8,128)(2,1)S(1)}, bf16[128,4096]{1,0:T(8,128)(2,1)}, u32[]{:S(2)}) copy-start(bf16[128,4096]{1,0:T(8,128)(2,1)} %get-tuple-element.14.g_ref) | copy-start | bytes 3145732
  35.4 0.8 copy-start.5
  36.2 0.8 copy-start.6
  36.9 0.8 copy-start.7
  37.7 25.6 %copy-start.1 = (bf16[256,2048]{1,0:T(8,128)(2,1)S(1)}, bf16[256,2048]{1,0:T(8,128)(2,1)}, u32[]{:S(2)}) copy-start(bf16[256,2048]{1,0:T(8,128)(2,1)} %b_ref.3) | copy-start | bytes 3145732
  39.6 28.9 %copy-start.13 = (bf16[4,4096]{1,0:T(4,128)(2,1)S(1)}, bf16[4,4096]{1,0:T(4,128)(2,1)}, u32[]{:S(2)}) copy-start(bf16[4,4096]{1,0:T(4,128)(2,1)} %param.20) | copy-start | bytes 98308
  39.6 35.8 %copy-start.2 = (bf16[4,256,512]{2,1,0:T(8,128)(2,1)S(1)}, bf16[4,256,512]{2,1,0:T(8,128)(2,1)}, u32[]{:S(2)}) copy-start(bf16[4,256,512]{2,1,0:T(8,128)(2,1)} %k_ref.1) | copy-start | bytes 3145732
  39.6 35.8 %copy-start.3 = (bf16[4,256,512]{2,1,0:T(8,128)(2,1)S(1)}, bf16[4,256,512]{2,1,0:T(8,128)(2,1)}, u32[]{:S(2)}) copy-start(bf16[4,256,512]{2,1,0:T(8,128)(2,1)} %v_ref.1) | copy-start | bytes 3145732
  39.6 35.8 %copy-start.9 = (s32[4]{0:T(128)S(1)}, s32[4]{0:T(128)}, u32[]{:S(2)}) copy-start(s32[4]{0:T(128)} %len_ref.1) | copy-start | bytes 52
  65.0 10.4 %all-to-all-start.2 = ((f32[16,4,256]{2,1,0:T(4,128)}), f32[16,4,256]{2,1,0:T(4,128)S(1)}, u32[]{:S(2)}, u32[]{:S(2)}) async-start(f32[16,4,256]{2,1,0:T(4,128)} %shard_map.144), calls=%async_computation.2 | async-start | bytes 131072 | tf_op jit(solution)/shard_map/all_to_all | solution.py:337

commit v10 on v9

--- a/solution.py
+++ b/solution.py
@@ -24,7 +24,6 @@
 BF16 = jnp.bfloat16
 VMEM_LIMIT = 24 * 1024 * 1024
 ALL_VMEM = 58 * 1024 * 1024 + 768 * 1024
-ROWS_VMEM = 57 * 1024 * 1024 + 256 * 1024
 
 
 def vmem():
@@ -148,9 +147,7 @@
     return half + pltpu.roll(half, RANK, 1)
 
 
-def rows_kernel(me_ref, h0_ref, h1_ref, x_ref, a_ref, g_ref, hx_ref, base_ref, u_ref, g_out, sel, sem):
-    copy = pltpu.make_async_copy(g_ref, g_out, sem)
-    copy.start()
+def rows_kernel(me_ref, h0_ref, h1_ref, x_ref, a_ref, hx_ref, base_ref, u_ref, sel):
     h = jnp.concatenate([r[k] for r in (h0_ref, h1_ref) for k in range(r.shape[0])], axis=0)
     tiles = h.shape[0] // HALF
     size = h.shape[1] - LANES
@@ -181,7 +178,6 @@
     for k in range(tiles):
         rows = slice(k * ROWS_DEV, (k + 1) * ROWS_DEV)
         hx_ref[k], base_ref[k], u_ref[k] = hx[rows], base[rows], tenant[rows]
-    copy.wait()
 
 
 def plain_rows_kernel(h_ref, x_ref, a_ref, hc_ref, u_ref, hx_ref, base_ref):
@@ -408,17 +404,15 @@
             masks = masks + [m ^ bit for m in masks]
             bit //= 2
         masks = masks + [m ^ 1 for m in masks]
-        *found, query_output_gradient = call(
+        found = call(
             rows_kernel,
-            [jax.ShapeDtypeStruct((n, local_rows, LANES), t) for t in (F32, F32, jnp.int32)]
-            + [jax.ShapeDtypeStruct(query_output_gradient.shape, BF16)],
-            [smem()] + [vmem()] * 4 + [hbm()],
-            [vmem()] * 4,
-            scratch=[pltpu.VMEM((n * HALF, fa), BF16), pltpu.SemaphoreType.DMA],
-            limit=ROWS_VMEM,
+            [jax.ShapeDtypeStruct((n, local_rows, LANES), t) for t in (F32, F32, jnp.int32)],
+            [smem()] + [vmem()] * 4,
+            [vmem()] * 3,
+            scratch=[pltpu.VMEM((n * HALF, fa), BF16)],
             flops=2 * rows * (BLOCK * width + fa * cols),
             nbytes=2 * BLOCK * width + 2 * fa * cols,
-        )(me[None], held, partner(held, 1), tokens, down_factors, query_output_gradient)
+        )(me[None], held, partner(held, 1), tokens, down_factors)
         hx, base_low_rank, tenants = ((f,) for f in found)
     else:
         got = exchange(packed)

time: 78.2 us -> 73.9 us (0.945)
  local copies, waits for them, and re-layouts: 4.88 us -> 1.85 us
  Pallas kernels: 19 us -> 16.9 us
    unnamed x28 -> x20, local copies, waits for them, and re-layouts: 4.26 us -> 1.26 us
    pallas_call x1, Pallas kernels: 4.27 us -> 2.2 us  [per_device(): call(rows_kernel, [jax.ShapeDtypeStruct((n, local_rows, LANES), t) for t...]
  transfers between devices with their start and end apart: 6 -> 6, of which waited for: 3 -> 3; matrix products, arithmetic and copies ran while one was open for 1% -> 2% of each run, Pallas kernels for 15% -> 13%
where the time goes in v10:
time: 73.9 us; the launch traced here: 73.4 us
  blocking collectives  23.6 us (32%)
  Pallas kernels  16.9 us (23%)
  starting transfers between devices  15.7 us (21%)
  waiting for transfers between devices  13.8 us (19%)
  local copies, waits for them, and re-layouts  1.85 us (3%)
  other arithmetic  0.82 us (1%)
  between operations  0.79 us (1%)
    all_to_all x1, blocking collectives, exchange(): return lax.all_to_all(x, 'wide', split_axis=0, concat_axis=0, tiled=True)  23.6 us
    ppermute x4, waiting for transfers between devices, partner(): lax.ppermute(x, 'wide', [(i, i ^ mask) for i in range(lax.axis_size('wide...  11.1 us
    all_to_all x2, starting transfers between devices, exchange(): return lax.all_to_all(x, 'wide', split_axis=0, concat_axis=0, tiled=True)  7.94 us
    ppermute x4, starting transfers between devices, partner(): lax.ppermute(x, 'wide', [(i, i ^ mask) for i in range(lax.axis_size('wide...  7.73 us
    pallas_call x1, Pallas kernels, per_device(): call(gradient_kernel, [jax.ShapeDtypeStruct((fa, cols), F32), jax.ShapeDt...  4.2 us
    pallas_call x1, Pallas kernels, per_device(): call(pick_kernel, jax.ShapeDtypeStruct(shape, BF16), [hbm(), hbm(), hbm()...  3.38 us
    all_to_all x2, waiting for transfers between devices, exchange(): return lax.all_to_all(x, 'wide', split_axis=0, concat_axis=0, tiled=True)  2.64 us
    pallas_call x1, Pallas kernels, per_device(): call(rows_kernel, [jax.ShapeDtypeStruct((n, local_rows, LANES), t) for t...  2.2 us
  transfers between devices with their start and end apart: 6, of which 3 were waited for; matrix products, arithmetic and copies ran while one was open for 2% of the time, Pallas kernels for 13%

profile of v10, /device:TPU:0, one launch (start us, length us, event | category | flops | bytes accessed | tf_op | source)
XLA Modules:
  0.0 73.4 jit_solution(2211869648198739674)
XLA Ops:
  0.6 1.4 %shard_map.139 = bf16[16,1408]{1,0:T(8,128)(2,1)} custom-call(s32[1,4]{1,0:T(1,128)} %list_ref.1, s32[4]{0:T(128)} %slot_ref.1, bf16[4,5120]{1,0:T(4,128)(2,1)} %hidden_ref.1), custom_call_target="tpu_custom_call" | custom-call | bytes 81920 | tf_op jit(solution)/shard_map/pallas_call | solution.py:389
  2.1 4.1 %collective-permute-start = (bf16[1,16,1408]{2,1,0:T(8,128)(2,1)}, bf16[1,16,1408]{2,1,0:T(8,128)(2,1)S(1)}, u32[]{:S(2)}, u32[]{:S(2)}) collective-permute-start(bf16[1,16,1408]{2,1,0:T(8,128)(2,1)} %bitcast.2), channel_id=1, source_target_pairs={{0,8},{1,9},{2,10},{3,11},{4,12},{5,13},{6,14},{7,15},{8,0},{9,1},... | collective-permute-start | bytes 135176 | tf_op jit(solution)/shard_map/ppermute | solution.py:337
  6.2 3.4 %shard_map.140 = bf16[16,16,1152]{2,1,0:T(8,128)(2,1)} custom-call(s32[16]{0:T(128)} %t_ref.3, bf16[256,2048]{1,0:T(8,128)(2,1)} %b_ref.3, bf16[320,2048]{1,0:T(8,128)(2,1)} %a_ref.3), custom_call_target="tpu_custom_call" | custom-call | flops 75497472 | bytes 2359296 | tf_op jit(solution)/shard_map/pallas_call | solution.py:368
  9.6 1.6 %collective-permute-start.1 = (bf16[2,16,1408]{2,1,0:T(8,128)(2,1)S(1)}, bf16[2,16,1408]{2,1,0:T(8,128)(2,1)S(1)}, u32[]{:S(2)}, u32[]{:S(2)}) collective-permute-start(bf16[2,16,1408]{2,1,0:T(8,128)(2,1)S(1)} %pad_maximum_fusion.2), channel_id=1, source_target_pairs={{0,4},{1,5},{2,6},{3,7},{4,0},{5,1},{6,2},{7,3},{8,12},{9,13},{10,... | collective-permute-start | bytes 270344 | tf_op jit(solution)/shard_map/ppermute | solution.py:337
  11.2 4.5 %all-to-all-start = ((bf16[16,16,1152]{2,1,0:T(8,128)(2,1)}), bf16[16,16,1152]{2,1,0:T(8,128)(2,1)S(1)}, u32[]{:S(2)}, u32[]{:S(2)}) async-start(bf16[16,16,1152]{2,1,0:T(8,128)(2,1)} %shard_map.140), calls=%async_computation | async-start | bytes 1179648 | tf_op jit(solution)/shard_map/all_to_all | solution.py:333
  15.7 2.0 %collective-permute-start.2 = (bf16[4,16,1408]{2,1,0:T(8,128)(2,1)S(1)}, bf16[4,16,1408]{2,1,0:T(8,128)(2,1)S(1)}, u32[]{:S(2)}, u32[]{:S(2)}) collective-permute-start(bf16[4,16,1408]{2,1,0:T(8,128)(2,1)S(1)} %pad_maximum_fusion.1), channel_id=1, source_target_pairs={{0,2},{1,3},{2,0},{3,1},{4,6},{5,7},{6,4},{7,5},{8,10},{9,11},{10,... | collective-permute-start | bytes 540680 | tf_op jit(solution)/shard_map/ppermute | solution.py:337
  17.7 9.7 %collective-permute-done.2 = bf16[4,16,1408]{2,1,0:T(8,128)(2,1)S(1)} collective-permute-done((bf16[4,16,1408]{2,1,0:T(8,128)(2,1)S(1)}, bf16[4,16,1408]{2,1,0:T(8,128)(2,1)S(1)}, u32[]{:S(2)}, u32[]{:S(2)}) %collective-permute-start.2) | collective-permute-done | bytes 180256 | tf_op jit(solution)/shard_map/ppermute | solution.py:337
  27.4 0.8 %pad_maximum_fusion.h0_ref = bf16[8,16,1408]{2,1,0:T(8,128)(2,1)} fusion(bf16[4,16,1408]{2,1,0:T(8,128)(2,1)S(1)} %collective-permute-done.2, bf16[4,16,1408]{2,1,0:T(8,128)(2,1)S(1)} %pad_maximum_fusion.1), kind=kLoop, calls=%fused_computation | loop fusion | flops 180224 | bytes 720896 | tf_op jit(solution)/shard_map/concatenate | solution.py:403
  28.2 0.6 dynamic_slice.3.t_ref
  28.8 1.4 %collective-permute-done.3.h1_ref = bf16[8,16,1408]{2,1,0:T(8,128)(2,1)} collective-permute-done((bf16[8,16,1408]{2,1,0:T(8,128)(2,1)}, bf16[8,16,1408]{2,1,0:T(8,128)(2,1)}, u32[]{:S(2)}, u32[]{:S(2)}) %collective-permute-start.3) | collective-permute-done | bytes 360480 | tf_op jit(solution)/shard_map/ppermute | solution.py:337
  30.2 2.2 %shard_map.141 = (f32[16,4,128]{2,1,0:T(4,128)S(1)}, f32[16,4,128]{2,1,0:T(4,128)S(1)}, s32[16,4,128]{2,1,0:T(4,128)S(1)}) custom-call(s32[1]{0:T(128)} %bitcast.me_ref, bf16[8,16,1408]{2,1,0:T(8,128)(2,1)} %pad_maximum_fusion.h0_ref, bf16[8,16,1408]{2,1,0:T(8,128)(2,1)} %collective-permute-done.3.h1_ref, bf16[128,5120]{1,0:T(8,128)(2,1)S(1)} %copy-done.1, ...), custom_call_target="tpu_custom_call" | custom-call | flops 167772160 | bytes 2621440 | tf_op jit(solution)/shard_map/pallas_call | solution.py:407
  32.4 0.0 copy-start.5
  32.5 1.2 %copy-done.5 = bf16[128,4096]{1,0:T(8,128)(2,1)S(1)} copy-done((bf16[128,4096]{1,0:T(8,128)(2,1)S(1)}, bf16[128,4096]{1,0:T(8,128)(2,1)}, u32[]{:S(2)}) %copy-start.5) | copy-done | bytes 1048600
  33.7 1.9 %shard_map.142 = (bf16[16,16,1280]{2,1,0:T(8,128)(2,1)S(1)}, s32[64,128]{1,0:T(8,128)S(1)}) custom-call(s32[1]{0:T(128)} %dynamic_slice.3.t_ref, s32[1]{0:T(128)} %bitcast.me_ref, bf16[128,5120]{1,0:T(8,128)(2,1)S(1)} %copy-done.1, bf16[128,4096]{1,0:T(8,128)(2,1)S(1)} %copy-done.5, bf16[16,16,1152]{2,1,0:T(8,128)(2,1)S(1)} %all-to-all-done.r_ref, ...), custom_call_target="tpu_custom_call" | custom-call | flops 150994944 | bytes 2359296 | tf_op jit(solution)/shard_map/pallas_call | solution.py:436
  35.6 0.0 copy-start.9
  35.6 0.0 copy-start.3
  35.6 0.0 copy-start.4
  35.6 0.0 copy-start.7
  35.6 23.6 %all_to_all.15.part_ref = bf16[16,16,1280]{2,1,0:T(8,128)(2,1)S(1)} all-to-all(bf16[16,16,1280]{2,1,0:T(8,128)(2,1)S(1)} %get-tuple-element.17), channel_id=1, replica_groups=mesh['groups'=2,'wide'=16] {'wide'}, dimensions={0} | all-to-all | bytes 1310720 | tf_op jit(solution)/shard_map/all_to_all | solution.py:333
  59.2 1.8 %shard_map.144 = f32[16,4,256]{2,1,0:T(4,128)} custom-call(s32[16]{0:T(128)S(1)} %copy-done.6, bf16[16,16,1280]{2,1,0:T(8,128)(2,1)S(1)} %all_to_all.15.part_ref, bf16[256,2048]{1,0:T(8,128)(2,1)S(1)} %copy-done.2, s32[64,128]{1,0:T(8,128)S(1)} %get-tuple-element.20.u_ref), custom_call_target="tpu_custom_call" | custom-call | flops 67108864 | bytes 1048576 | tf_op jit(solution)/shard_map/pallas_call | solution.py:450
  61.0 3.5 %all-to-all-start.2 = ((f32[16,4,256]{2,1,0:T(4,128)}), f32[16,4,256]{2,1,0:T(4,128)S(1)}, u32[]{:S(2)}, u32[]{:S(2)}) async-start(f32[16,4,256]{2,1,0:T(4,128)} %shard_map.144), calls=%async_computation.2 | async-start | bytes 131072 | tf_op jit(solution)/shard_map/all_to_all | solution.py:333
  64.5 4.2 %shard_map.143 = (f32[320,2048]{1,0:T(8,128)}, f32[256,2048]{1,0:T(8,128)}) custom-call(s32[16]{0:T(128)S(1)} %copy-done.6, bf16[16,16,1280]{2,1,0:T(8,128)(2,1)S(1)} %all_to_all.15.part_ref), custom_call_target="tpu_custom_call" | custom-call | flops 75497472 | bytes 4718592 | tf_op jit(solution)/shard_map/pallas_call | solution.py:460
  68.7 2.6 %all-to-all-done.2.delta_ref = f32[16,4,256]{2,1,0:T(4,128)S(1)} async-done(((f32[16,4,256]{2,1,0:T(4,128)}), f32[16,4,256]{2,1,0:T(4,128)S(1)}, u32[]{:S(2)}, u32[]{:S(2)}) %all-to-all-start.2) | async-done | bytes 65568 | tf_op jit(solution)/shard_map/all_to_all | solution.py:333
  71.4 2.1 %shard_map.145 = bf16[4,4096]{1,0:T(4,128)(2,1)} custom-call(s32[4]{0:T(128)S(1)} %copy-done.7, f32[16,4,256]{2,1,0:T(4,128)S(1)} %all-to-all-done.2.delta_ref, f32[4,4096]{1,0:T(4,128)S(1)} %convert_element_type.3.base_ref, bf16[4,256,512]{2,1,0:T(8,128)(2,1)S(1)} %copy-done.3, bf16[4,256,512]{2,1,0:T(8,128)(2,1)S(1)} %copy-done.4), custom_call_target="tpu_custom_call" | custom-call | flops 16777216 | bytes 2097152 | tf_op jit(solution)/shard_map/pallas_call | solution.py:468
  (21 shorter events, 0.1 us)
Async XLA Ops:
  2.1 7.5 %copy-start.8 = (bf16[16,1408]{1,0:T(8,128)(2,1)S(1)}, bf16[16,1408]{1,0:T(8,128)(2,1)}, u32[]{:S(2)}) copy-start(bf16[16,1408]{1,0:T(8,128)(2,1)} %shard_map.139) | copy-start | bytes 135172
  2.1 26.2 %copy-start.6 = (s32[16]{0:T(128)S(1)}, s32[16]{0:T(128)}, u32[]{:S(2)}) copy-start(s32[16]{0:T(128)} %t_ref.3) | copy-start | bytes 196
  2.1 28.2 %copy-start = (bf16[320,2048]{1,0:T(8,128)(2,1)S(1)}, bf16[320,2048]{1,0:T(8,128)(2,1)}, u32[]{:S(2)}) copy-start(bf16[320,2048]{1,0:T(8,128)(2,1)} %a_ref.3) | copy-start | bytes 3932164
  2.1 28.2 %copy-start.1 = (bf16[128,5120]{1,0:T(8,128)(2,1)S(1)}, bf16[128,5120]{1,0:T(8,128)(2,1)}, u32[]{:S(2)}) copy-start(bf16[128,5120]{1,0:T(8,128)(2,1)} %x_ref.3) | copy-start | bytes 3932164
  2.1 7.5 %collective-permute-start = (bf16[1,16,1408]{2,1,0:T(8,128)(2,1)}, bf16[1,16,1408]{2,1,0:T(8,128)(2,1)S(1)}, u32[]{:S(2)}, u32[]{:S(2)}) collective-permute-start(bf16[1,16,1408]{2,1,0:T(8,128)(2,1)} %bitcast.2), channel_id=1, source_target_pairs={{0,8},{1,9},{2,10},{3,11},{4,12},{5,13},{6,14},{7,15},{8,0},{9,1},... | collective-permute-start | bytes 135176 | tf_op jit(solution)/shard_map/ppermute | solution.py:337
  9.6 6.1 %collective-permute-start.1 = (bf16[2,16,1408]{2,1,0:T(8,128)(2,1)S(1)}, bf16[2,16,1408]{2,1,0:T(8,128)(2,1)S(1)}, u32[]{:S(2)}, u32[]{:S(2)}) collective-permute-start(bf16[2,16,1408]{2,1,0:T(8,128)(2,1)S(1)} %pad_maximum_fusion.2), channel_id=1, source_target_pairs={{0,4},{1,5},{2,6},{3,7},{4,0},{5,1},{6,2},{7,3},{8,12},{9,13},{10,... | collective-permute-start | bytes 270344 | tf_op jit(solution)/shard_map/ppermute | solution.py:337
  11.2 21.2 %all-to-all-start = ((bf16[16,16,1152]{2,1,0:T(8,128)(2,1)}), bf16[16,16,1152]{2,1,0:T(8,128)(2,1)S(1)}, u32[]{:S(2)}, u32[]{:S(2)}) async-start(bf16[16,16,1152]{2,1,0:T(8,128)(2,1)} %shard_map.140), calls=%async_computation | async-start | bytes 1179648 | tf_op jit(solution)/shard_map/all_to_all | solution.py:333
  15.7 11.7 %collective-permute-start.2 = (bf16[4,16,1408]{2,1,0:T(8,128)(2,1)S(1)}, bf16[4,16,1408]{2,1,0:T(8,128)(2,1)S(1)}, u32[]{:S(2)}, u32[]{:S(2)}) collective-permute-start(bf16[4,16,1408]{2,1,0:T(8,128)(2,1)S(1)} %pad_maximum_fusion.1), channel_id=1, source_target_pairs={{0,2},{1,3},{2,0},{3,1},{4,6},{5,7},{6,4},{7,5},{8,10},{9,11},{10,... | collective-permute-start | bytes 540680 | tf_op jit(solution)/shard_map/ppermute | solution.py:337
  28.2 2.0 %collective-permute-start.3 = (bf16[8,16,1408]{2,1,0:T(8,128)(2,1)}, bf16[8,16,1408]{2,1,0:T(8,128)(2,1)}, u32[]{:S(2)}, u32[]{:S(2)}) collective-permute-start(bf16[8,16,1408]{2,1,0:T(8,128)(2,1)} %pad_maximum_fusion.h0_ref), channel_id=1, source_target_pairs={{0,1},{1,0},{2,3},{3,2},{4,5},{5,4},{6,7},{7,6},{8,9},{9,8},{10,11... | collective-permute-start | bytes 1081352 | tf_op jit(solution)/shard_map/ppermute | solution.py:337
  32.4 1.2 %copy-start.5 = (bf16[128,4096]{1,0:T(8,128)(2,1)S(1)}, bf16[128,4096]{1,0:T(8,128)(2,1)}, u32[]{:S(2)}) copy-start(bf16[128,4096]{1,0:T(8,128)(2,1)} %g_ref.1) | copy-start | bytes 3145732
  33.7 25.5 %copy-start.2 = (bf16[256,2048]{1,0:T(8,128)(2,1)S(1)}, bf16[256,2048]{1,0:T(8,128)(2,1)}, u32[]{:S(2)}) copy-start(bf16[256,2048]{1,0:T(8,128)(2,1)} %b_ref.3) | copy-start | bytes 3145732
  35.6 28.9 %copy-start.9 = (bf16[4,4096]{1,0:T(4,128)(2,1)S(1)}, bf16[4,4096]{1,0:T(4,128)(2,1)}, u32[]{:S(2)}) copy-start(bf16[4,4096]{1,0:T(4,128)(2,1)} %param.20) | copy-start | bytes 98308
  35.6 35.8 %copy-start.3 = (bf16[4,256,512]{2,1,0:T(8,128)(2,1)S(1)}, bf16[4,256,512]{2,1,0:T(8,128)(2,1)}, u32[]{:S(2)}) copy-start(bf16[4,256,512]{2,1,0:T(8,128)(2,1)} %k_ref.1) | copy-start | bytes 3145732
  35.6 35.8 %copy-start.4 = (bf16[4,256,512]{2,1,0:T(8,128)(2,1)S(1)}, bf16[4,256,512]{2,1,0:T(8,128)(2,1)}, u32[]{:S(2)}) copy-start(bf16[4,256,512]{2,1,0:T(8,128)(2,1)} %v_ref.1) | copy-start | bytes 3145732
  35.6 35.8 %copy-start.7 = (s32[4]{0:T(128)S(1)}, s32[4]{0:T(128)}, u32[]{:S(2)}) copy-start(s32[4]{0:T(128)} %len_ref.1) | copy-start | bytes 52
  61.0 10.4 %all-to-all-start.2 = ((f32[16,4,256]{2,1,0:T(4,128)}), f32[16,4,256]{2,1,0:T(4,128)S(1)}, u32[]{:S(2)}, u32[]{:S(2)}) async-start(f32[16,4,256]{2,1,0:T(4,128)} %shard_map.144), calls=%async_computation.2 | async-start | bytes 131072 | tf_op jit(solution)/shard_map/all_to_all | solution.py:333

commit v11 on v9

--- a/solution.py
+++ b/solution.py
@@ -24,7 +24,6 @@
 BF16 = jnp.bfloat16
 VMEM_LIMIT = 24 * 1024 * 1024
 ALL_VMEM = 58 * 1024 * 1024 + 768 * 1024
-ROWS_VMEM = 57 * 1024 * 1024 + 256 * 1024
 
 
 def vmem():
@@ -415,7 +414,6 @@
             [smem()] + [vmem()] * 4 + [hbm()],
             [vmem()] * 4,
             scratch=[pltpu.VMEM((n * HALF, fa), BF16), pltpu.SemaphoreType.DMA],
-            limit=ROWS_VMEM,
             flops=2 * rows * (BLOCK * width + fa * cols),
             nbytes=2 * BLOCK * width + 2 * fa * cols,
         )(me[None], held, partner(held, 1), tokens, down_factors, query_output_gradient)

time: 78.2 us -> 76.3 us (0.976)
  Pallas kernels: 19 us -> 17 us
  local copies, waits for them, and re-layouts: 4.88 us -> 4.05 us
    pallas_call x1, Pallas kernels: 4.27 us -> 2.29 us  [per_device(): call(rows_kernel, [jax.ShapeDtypeStruct((n, local_rows, LANES), t) for t...]
    unnamed x28 -> x24, local copies, waits for them, and re-layouts: 4.26 us -> 3.46 us
  transfers between devices with their start and end apart: 6 -> 6, of which waited for: 3 -> 3; matrix products, arithmetic and copies ran while one was open for 1% -> 2% of each run, Pallas kernels for 15% -> 13%
where the time goes in v11:
time: 76.3 us; the launch traced here: 75.7 us
  blocking collectives  23.6 us (31%)
  Pallas kernels  17 us (22%)
  starting transfers between devices  15.7 us (21%)
  waiting for transfers between devices  13.8 us (18%)
  local copies, waits for them, and re-layouts  4.05 us (5%)
  other arithmetic  0.82 us (1%)
  between operations  0.79 us (1%)
    all_to_all x1, blocking collectives, exchange(): return lax.all_to_all(x, 'wide', split_axis=0, concat_axis=0, tiled=True)  23.6 us
    ppermute x4, waiting for transfers between devices, partner(): lax.ppermute(x, 'wide', [(i, i ^ mask) for i in range(lax.axis_size('wide...  11.1 us
    all_to_all x2, starting transfers between devices, exchange(): return lax.all_to_all(x, 'wide', split_axis=0, concat_axis=0, tiled=True)  7.94 us
    ppermute x4, starting transfers between devices, partner(): lax.ppermute(x, 'wide', [(i, i ^ mask) for i in range(lax.axis_size('wide...  7.73 us
    pallas_call x1, Pallas kernels, per_device(): call(gradient_kernel, [jax.ShapeDtypeStruct((fa, cols), F32), jax.ShapeDt...  4.2 us
    unnamed x24, local copies, waits for them, and re-layouts  3.46 us
    pallas_call x1, Pallas kernels, per_device(): call(pick_kernel, jax.ShapeDtypeStruct(shape, BF16), [hbm(), hbm(), hbm()...  3.38 us
    all_to_all x2, waiting for transfers between devices, exchange(): return lax.all_to_all(x, 'wide', split_axis=0, concat_axis=0, tiled=True)  2.63 us
  transfers between devices with their start and end apart: 6, of which 3 were waited for; matrix products, arithmetic and copies ran while one was open for 2% of the time, Pallas kernels for 13%

profile of v11, /device:TPU:0, one launch (start us, length us, event | category | flops | bytes accessed | tf_op | source)
XLA Modules:
  0.0 75.7 jit_solution(5128177458197975825)
XLA Ops:
  0.6 1.4 %shard_map.139 = bf16[16,1408]{1,0:T(8,128)(2,1)} custom-call(s32[1,4]{1,0:T(1,128)} %list_ref.1, s32[4]{0:T(128)} %slot_ref.1, bf16[4,5120]{1,0:T(4,128)(2,1)} %hidden_ref.1), custom_call_target="tpu_custom_call" | custom-call | bytes 81920 | tf_op jit(solution)/shard_map/pallas_call | solution.py:392
  2.1 4.1 %collective-permute-start = (bf16[1,16,1408]{2,1,0:T(8,128)(2,1)}, bf16[1,16,1408]{2,1,0:T(8,128)(2,1)S(1)}, u32[]{:S(2)}, u32[]{:S(2)}) collective-permute-start(bf16[1,16,1408]{2,1,0:T(8,128)(2,1)} %bitcast.2), channel_id=1, source_target_pairs={{0,8},{1,9},{2,10},{3,11},{4,12},{5,13},{6,14},{7,15},{8,0},{9,1},... | collective-permute-start | bytes 135176 | tf_op jit(solution)/shard_map/ppermute | solution.py:340
  6.2 3.4 %shard_map.140 = bf16[16,16,1152]{2,1,0:T(8,128)(2,1)} custom-call(s32[16]{0:T(128)} %t_ref.3, bf16[256,2048]{1,0:T(8,128)(2,1)} %b_ref.3, bf16[320,2048]{1,0:T(8,128)(2,1)} %a_ref.3), custom_call_target="tpu_custom_call" | custom-call | flops 75497472 | bytes 2359296 | tf_op jit(solution)/shard_map/pallas_call | solution.py:371
  9.6 1.6 %collective-permute-start.1 = (bf16[2,16,1408]{2,1,0:T(8,128)(2,1)S(1)}, bf16[2,16,1408]{2,1,0:T(8,128)(2,1)S(1)}, u32[]{:S(2)}, u32[]{:S(2)}) collective-permute-start(bf16[2,16,1408]{2,1,0:T(8,128)(2,1)S(1)} %pad_maximum_fusion.2), channel_id=1, source_target_pairs={{0,4},{1,5},{2,6},{3,7},{4,0},{5,1},{6,2},{7,3},{8,12},{9,13},{10,... | collective-permute-start | bytes 270344 | tf_op jit(solution)/shard_map/ppermute | solution.py:340
  11.2 4.5 %all-to-all-start = ((bf16[16,16,1152]{2,1,0:T(8,128)(2,1)}), bf16[16,16,1152]{2,1,0:T(8,128)(2,1)S(1)}, u32[]{:S(2)}, u32[]{:S(2)}) async-start(bf16[16,16,1152]{2,1,0:T(8,128)(2,1)} %shard_map.140), calls=%async_computation | async-start | bytes 1179648 | tf_op jit(solution)/shard_map/all_to_all | solution.py:336
  15.7 2.0 %collective-permute-start.2 = (bf16[4,16,1408]{2,1,0:T(8,128)(2,1)S(1)}, bf16[4,16,1408]{2,1,0:T(8,128)(2,1)S(1)}, u32[]{:S(2)}, u32[]{:S(2)}) collective-permute-start(bf16[4,16,1408]{2,1,0:T(8,128)(2,1)S(1)} %pad_maximum_fusion.1), channel_id=1, source_target_pairs={{0,2},{1,3},{2,0},{3,1},{4,6},{5,7},{6,4},{7,5},{8,10},{9,11},{10,... | collective-permute-start | bytes 540680 | tf_op jit(solution)/shard_map/ppermute | solution.py:340
  17.7 9.7 %collective-permute-done.2 = bf16[4,16,1408]{2,1,0:T(8,128)(2,1)S(1)} collective-permute-done((bf16[4,16,1408]{2,1,0:T(8,128)(2,1)S(1)}, bf16[4,16,1408]{2,1,0:T(8,128)(2,1)S(1)}, u32[]{:S(2)}, u32[]{:S(2)}) %collective-permute-start.2) | collective-permute-done | bytes 180256 | tf_op jit(solution)/shard_map/ppermute | solution.py:340
  27.4 0.8 %pad_maximum_fusion.h0_ref = bf16[8,16,1408]{2,1,0:T(8,128)(2,1)} fusion(bf16[4,16,1408]{2,1,0:T(8,128)(2,1)S(1)} %collective-permute-done.2, bf16[4,16,1408]{2,1,0:T(8,128)(2,1)S(1)} %pad_maximum_fusion.1), kind=kLoop, calls=%fused_computation | loop fusion | flops 180224 | bytes 720896 | tf_op jit(solution)/shard_map/concatenate | solution.py:406
  28.2 0.6 dynamic_slice.3.t_ref
  28.8 1.4 %collective-permute-done.3.h1_ref = bf16[8,16,1408]{2,1,0:T(8,128)(2,1)} collective-permute-done((bf16[8,16,1408]{2,1,0:T(8,128)(2,1)}, bf16[8,16,1408]{2,1,0:T(8,128)(2,1)}, u32[]{:S(2)}, u32[]{:S(2)}) %collective-permute-start.3) | collective-permute-done | bytes 360480 | tf_op jit(solution)/shard_map/ppermute | solution.py:340
  30.2 1.2 %copy-done.3 = bf16[128,4096]{1,0:T(8,128)(2,1)S(1)} copy-done((bf16[128,4096]{1,0:T(8,128)(2,1)S(1)}, bf16[128,4096]{1,0:T(8,128)(2,1)}, u32[]{:S(2)}) %copy-start.3) | copy-done | bytes 1048600
  31.5 2.3 %shard_map.141 = (f32[16,4,128]{2,1,0:T(4,128)S(1)}, f32[16,4,128]{2,1,0:T(4,128)S(1)}, s32[16,4,128]{2,1,0:T(4,128)S(1)}, bf16[128,4096]{1,0:T(8,128)(2,1)S(1)}) custom-call(s32[1]{0:T(128)} %bitcast.me_ref, bf16[8,16,1408]{2,1,0:T(8,128)(2,1)} %pad_maximum_fusion.h0_ref, bf16[8,16,1408]{2,1,0:T(8,128)(2,1)} %collective-permute-done.3.h1_ref, ...), custom_call_target="tpu_custom_call" | custom-call | flops 167772160 | bytes 2621440 | tf_op jit(solution)/shard_map/pallas_call | solution.py:410
  33.8 0.0 copy-start.6
  33.8 1.0 %copy-done.6 = bf16[128,4096]{1,0:T(8,128)(2,1)} copy-done((bf16[128,4096]{1,0:T(8,128)(2,1)}, bf16[128,4096]{1,0:T(8,128)(2,1)S(1)}, u32[]{:S(2)}) %copy-start.6) | copy-done | bytes 1048600
  34.7 1.2 %copy-done.7 = bf16[128,4096]{1,0:T(8,128)(2,1)S(1)} copy-done((bf16[128,4096]{1,0:T(8,128)(2,1)S(1)}, bf16[128,4096]{1,0:T(8,128)(2,1)}, u32[]{:S(2)}) %copy-start.7) | copy-done | bytes 1048600
  36.0 1.9 %shard_map.142 = (bf16[16,16,1280]{2,1,0:T(8,128)(2,1)S(1)}, s32[64,128]{1,0:T(8,128)S(1)}) custom-call(s32[1]{0:T(128)} %dynamic_slice.3.t_ref, s32[1]{0:T(128)} %bitcast.me_ref, bf16[128,5120]{1,0:T(8,128)(2,1)S(1)} %copy-done.1, bf16[128,4096]{1,0:T(8,128)(2,1)S(1)} %copy-done.7, bf16[16,16,1152]{2,1,0:T(8,128)(2,1)S(1)} %all-to-all-done.r_ref, ...), custom_call_target="tpu_custom_call" | custom-call | flops 150994944 | bytes 2359296 | tf_op jit(solution)/shard_map/pallas_call | solution.py:440
  37.9 0.0 copy-start.11
  37.9 0.0 copy-start.9
  37.9 23.6 %all_to_all.15.part_ref = bf16[16,16,1280]{2,1,0:T(8,128)(2,1)S(1)} all-to-all(bf16[16,16,1280]{2,1,0:T(8,128)(2,1)S(1)} %get-tuple-element.19), channel_id=1, replica_groups=mesh['groups'=2,'wide'=16] {'wide'}, dimensions={0} | all-to-all | bytes 1310720 | tf_op jit(solution)/shard_map/all_to_all | solution.py:336
  61.5 1.8 %shard_map.144 = f32[16,4,256]{2,1,0:T(4,128)} custom-call(s32[16]{0:T(128)S(1)} %copy-done.8, bf16[16,16,1280]{2,1,0:T(8,128)(2,1)S(1)} %all_to_all.15.part_ref, bf16[256,2048]{1,0:T(8,128)(2,1)S(1)} %copy-done.2, s32[64,128]{1,0:T(8,128)S(1)} %get-tuple-element.22.u_ref), custom_call_target="tpu_custom_call" | custom-call | flops 67108864 | bytes 1048576 | tf_op jit(solution)/shard_map/pallas_call | solution.py:454
  63.3 3.5 %all-to-all-start.2 = ((f32[16,4,256]{2,1,0:T(4,128)}), f32[16,4,256]{2,1,0:T(4,128)S(1)}, u32[]{:S(2)}, u32[]{:S(2)}) async-start(f32[16,4,256]{2,1,0:T(4,128)} %shard_map.144), calls=%async_computation.2 | async-start | bytes 131072 | tf_op jit(solution)/shard_map/all_to_all | solution.py:336
  66.8 4.2 %shard_map.143 = (f32[320,2048]{1,0:T(8,128)}, f32[256,2048]{1,0:T(8,128)}) custom-call(s32[16]{0:T(128)S(1)} %copy-done.8, bf16[16,16,1280]{2,1,0:T(8,128)(2,1)S(1)} %all_to_all.15.part_ref), custom_call_target="tpu_custom_call" | custom-call | flops 75497472 | bytes 4718592 | tf_op jit(solution)/shard_map/pallas_call | solution.py:464
  71.0 2.6 %all-to-all-done.2.delta_ref = f32[16,4,256]{2,1,0:T(4,128)S(1)} async-done(((f32[16,4,256]{2,1,0:T(4,128)}), f32[16,4,256]{2,1,0:T(4,128)S(1)}, u32[]{:S(2)}, u32[]{:S(2)}) %all-to-all-start.2) | async-done | bytes 65568 | tf_op jit(solution)/shard_map/all_to_all | solution.py:336
  73.7 2.1 %shard_map.145 = bf16[4,4096]{1,0:T(4,128)(2,1)} custom-call(s32[4]{0:T(128)S(1)} %copy-done.9, f32[16,4,256]{2,1,0:T(4,128)S(1)} %all-to-all-done.2.delta_ref, f32[4,4096]{1,0:T(4,128)S(1)} %convert_element_type.3.base_ref, bf16[4,256,512]{2,1,0:T(8,128)(2,1)S(1)} %copy-done.4, bf16[4,256,512]{2,1,0:T(8,128)(2,1)S(1)} %copy-done.5), custom_call_target="tpu_custom_call" | custom-call | flops 16777216 | bytes 2097152 | tf_op jit(solution)/shard_map/pallas_call | solution.py:472
  (25 shorter events, 0.1 us)
Async XLA Ops:
  2.1 7.5 %copy-start.10 = (bf16[16,1408]{1,0:T(8,128)(2,1)S(1)}, bf16[16,1408]{1,0:T(8,128)(2,1)}, u32[]{:S(2)}) copy-start(bf16[16,1408]{1,0:T(8,128)(2,1)} %shard_map.139) | copy-start | bytes 135172
  2.1 26.2 %copy-start.8 = (s32[16]{0:T(128)S(1)}, s32[16]{0:T(128)}, u32[]{:S(2)}) copy-start(s32[16]{0:T(128)} %t_ref.3) | copy-start | bytes 196
  2.1 28.2 %copy-start = (bf16[320,2048]{1,0:T(8,128)(2,1)S(1)}, bf16[320,2048]{1,0:T(8,128)(2,1)}, u32[]{:S(2)}) copy-start(bf16[320,2048]{1,0:T(8,128)(2,1)} %a_ref.3) | copy-start | bytes 3932164
  2.1 28.2 %copy-start.1 = (bf16[128,5120]{1,0:T(8,128)(2,1)S(1)}, bf16[128,5120]{1,0:T(8,128)(2,1)}, u32[]{:S(2)}) copy-start(bf16[128,5120]{1,0:T(8,128)(2,1)} %x_ref.3) | copy-start | bytes 3932164
  2.1 7.5 %collective-permute-start = (bf16[1,16,1408]{2,1,0:T(8,128)(2,1)}, bf16[1,16,1408]{2,1,0:T(8,128)(2,1)S(1)}, u32[]{:S(2)}, u32[]{:S(2)}) collective-permute-start(bf16[1,16,1408]{2,1,0:T(8,128)(2,1)} %bitcast.2), channel_id=1, source_target_pairs={{0,8},{1,9},{2,10},{3,11},{4,12},{5,13},{6,14},{7,15},{8,0},{9,1},... | collective-permute-start | bytes 135176 | tf_op jit(solution)/shard_map/ppermute | solution.py:340
  9.6 6.1 %collective-permute-start.1 = (bf16[2,16,1408]{2,1,0:T(8,128)(2,1)S(1)}, bf16[2,16,1408]{2,1,0:T(8,128)(2,1)S(1)}, u32[]{:S(2)}, u32[]{:S(2)}) collective-permute-start(bf16[2,16,1408]{2,1,0:T(8,128)(2,1)S(1)} %pad_maximum_fusion.2), channel_id=1, source_target_pairs={{0,4},{1,5},{2,6},{3,7},{4,0},{5,1},{6,2},{7,3},{8,12},{9,13},{10,... | collective-permute-start | bytes 270344 | tf_op jit(solution)/shard_map/ppermute | solution.py:340
  11.2 23.5 %all-to-all-start = ((bf16[16,16,1152]{2,1,0:T(8,128)(2,1)}), bf16[16,16,1152]{2,1,0:T(8,128)(2,1)S(1)}, u32[]{:S(2)}, u32[]{:S(2)}) async-start(bf16[16,16,1152]{2,1,0:T(8,128)(2,1)} %shard_map.140), calls=%async_computation | async-start | bytes 1179648 | tf_op jit(solution)/shard_map/all_to_all | solution.py:336
  15.7 11.7 %collective-permute-start.2 = (bf16[4,16,1408]{2,1,0:T(8,128)(2,1)S(1)}, bf16[4,16,1408]{2,1,0:T(8,128)(2,1)S(1)}, u32[]{:S(2)}, u32[]{:S(2)}) collective-permute-start(bf16[4,16,1408]{2,1,0:T(8,128)(2,1)S(1)} %pad_maximum_fusion.1), channel_id=1, source_target_pairs={{0,2},{1,3},{2,0},{3,1},{4,6},{5,7},{6,4},{7,5},{8,10},{9,11},{10,... | collective-permute-start | bytes 540680 | tf_op jit(solution)/shard_map/ppermute | solution.py:340
  28.2 2.0 %collective-permute-start.3 = (bf16[8,16,1408]{2,1,0:T(8,128)(2,1)}, bf16[8,16,1408]{2,1,0:T(8,128)(2,1)}, u32[]{:S(2)}, u32[]{:S(2)}) collective-permute-start(bf16[8,16,1408]{2,1,0:T(8,128)(2,1)} %pad_maximum_fusion.h0_ref), channel_id=1, source_target_pairs={{0,1},{1,0},{2,3},{3,2},{4,5},{5,4},{6,7},{7,6},{8,9},{9,8},{10,11... | collective-permute-start | bytes 1081352 | tf_op jit(solution)/shard_map/ppermute | solution.py:340
  30.2 1.2 %copy-start.3 = (bf16[128,4096]{1,0:T(8,128)(2,1)S(1)}, bf16[128,4096]{1,0:T(8,128)(2,1)}, u32[]{:S(2)}) copy-start(bf16[128,4096]{1,0:T(8,128)(2,1)} %g_ref.1) | copy-start | bytes 3145732
  33.8 1.0 %copy-start.6 = (bf16[128,4096]{1,0:T(8,128)(2,1)}, bf16[128,4096]{1,0:T(8,128)(2,1)S(1)}, u32[]{:S(2)}) copy-start(bf16[128,4096]{1,0:T(8,128)(2,1)S(1)} %get-tuple-element.14.g_ref) | copy-start | bytes 3145732
  34.7 1.2 %copy-start.7 = (bf16[128,4096]{1,0:T(8,128)(2,1)S(1)}, bf16[128,4096]{1,0:T(8,128)(2,1)}, u32[]{:S(2)}) copy-start(bf16[128,4096]{1,0:T(8,128)(2,1)} %copy-done.6) | copy-start | bytes 3145732
  36.0 25.6 %copy-start.2 = (bf16[256,2048]{1,0:T(8,128)(2,1)S(1)}, bf16[256,2048]{1,0:T(8,128)(2,1)}, u32[]{:S(2)}) copy-start(bf16[256,2048]{1,0:T(8,128)(2,1)} %b_ref.3) | copy-start | bytes 3145732
  37.9 28.9 %copy-start.11 = (bf16[4,4096]{1,0:T(4,128)(2,1)S(1)}, bf16[4,4096]{1,0:T(4,128)(2,1)}, u32[]{:S(2)}) copy-start(bf16[4,4096]{1,0:T(4,128)(2,1)} %param.20) | copy-start | bytes 98308
  37.9 35.8 %copy-start.4 = (bf16[4,256,512]{2,1,0:T(8,128)(2,1)S(1)}, bf16[4,256,512]{2,1,0:T(8,128)(2,1)}, u32[]{:S(2)}) copy-start(bf16[4,256,512]{2,1,0:T(8,128)(2,1)} %k_ref.1) | copy-start | bytes 3145732
  37.9 35.8 %copy-start.5 = (bf16[4,256,512]{2,1,0:T(8,128)(2,1)S(1)}, bf16[4,256,512]{2,1,0:T(8,128)(2,1)}, u32[]{:S(2)}) copy-start(bf16[4,256,512]{2,1,0:T(8,128)(2,1)} %v_ref.1) | copy-start | bytes 3145732
  37.9 35.8 %copy-start.9 = (s32[4]{0:T(128)S(1)}, s32[4]{0:T(128)}, u32[]{:S(2)}) copy-start(s32[4]{0:T(128)} %len_ref.1) | copy-start | bytes 52
  63.3 10.4 %all-to-all-start.2 = ((f32[16,4,256]{2,1,0:T(4,128)}), f32[16,4,256]{2,1,0:T(4,128)S(1)}, u32[]{:S(2)}, u32[]{:S(2)}) async-start(f32[16,4,256]{2,1,0:T(4,128)} %shard_map.144), calls=%async_computation.2 | async-start | bytes 131072 | tf_op jit(solution)/shard_map/all_to_all | solution.py:336

commit v12 on v10

--- a/solution.py
+++ b/solution.py
@@ -24,6 +24,7 @@
 BF16 = jnp.bfloat16
 VMEM_LIMIT = 24 * 1024 * 1024
 ALL_VMEM = 58 * 1024 * 1024 + 768 * 1024
+BLOCK_VMEM = 59 * 1024 * 1024 + 512 * 1024
 
 
 def vmem():
@@ -188,11 +189,17 @@
         base_ref[d] = base[d * ROWS_DEV : (d + 1) * ROWS_DEV]
 
 
-def block_kernel(ride, masks, t_ref, me_ref, x_ref, g_ref, r_ref, *refs):
-    sets = (len(refs) - (7 if ride else 8)) // 3
+def block_kernel(ride, masks, t_ref, me_ref, x_ref, g_hbm, r_ref, *refs):
+    sets = (len(refs) - (9 if ride else 10)) // 3
     hx_sets, base_sets, u_sets = (refs[i * sets : (i + 1) * sets] for i in range(3))
     o_ref, u_ref = refs[3 * sets : 3 * sets + 2]
-    wa_ref, wb_ref, sx, sb, su = refs[-5:]
+    wa_ref, wb_ref, sx, sb, su, g_ref, sem = refs[-7:]
+    step = g_ref.shape[0] // sem.shape[0]
+    loads = []
+    for c in range(sem.shape[0]):
+        part = slice(c * step, (c + 1) * step)
+        loads.append(pltpu.make_async_copy(g_hbm.at[part], g_ref.at[part], sem.at[c]))
+        loads[-1].start()
     n = r_ref.shape[0]
     fa, fb = x_ref.shape[1] // n, g_ref.shape[1] // n
     for d in range(n):
@@ -200,8 +207,10 @@
             rank = slice(h * HALF, (h + 1) * HALF)
             wb_ref[rank, d * fb : (d + 1) * fb] = r_ref[d, :, up_half(h, fa, fb)]
             wa_ref[rank, d * fa : (d + 1) * fa] = r_ref[d, :, down_half(h, fa, fb)]
+    down = dot(wa_ref[...], x_ref[...], 1, 1).astype(BF16)
+    for load in loads:
+        load.wait()
     back = dot(wb_ref[...], g_ref[...], 1, 1).astype(BF16)
-    down = dot(wa_ref[...], x_ref[...], 1, 1).astype(BF16)
 
     k = 0
     for hx_ref, base_ref, tile_ref in zip(hx_sets, base_sets, u_sets):
@@ -437,10 +446,12 @@
         functools.partial(block_kernel, small, masks),
         [jax.ShapeDtypeStruct(part_shape, BF16), jax.ShapeDtypeStruct((rows, LANES), jnp.int32)]
         + ([] if small else [jax.ShapeDtypeStruct((quarter, LANES), F32)]),
-        [smem(), smem()] + [vmem()] * (3 + 3 * len(hx)),
+        [smem(), smem(), vmem(), hbm()] + [vmem()] * (1 + 3 * len(hx)),
         [vmem()] * (2 if small else 3),
         scratch=[pltpu.VMEM((RANK, width), BF16), pltpu.VMEM((RANK, features), BF16)]
-        + [pltpu.VMEM((n, local_rows, LANES), t) for t in (F32, F32, jnp.int32)],
+        + [pltpu.VMEM((n, local_rows, LANES), t) for t in (F32, F32, jnp.int32)]
+        + [pltpu.VMEM(query_output_gradient.shape, BF16), pltpu.SemaphoreType.DMA((4,))],
+        limit=BLOCK_VMEM,
         flops=4 * RANK * BLOCK * n * (fa + fb),
         nbytes=2 * BLOCK * n * (fa + fb),
     )(my_tenant, me[None], tokens, query_output_gradient, got, *hx, *base_low_rank, *tenants)

time: 73.9 us -> 77 us (1.042)
  Pallas kernels: 16.9 us -> 19.4 us
  local copies, waits for them, and re-layouts: 1.85 us -> 3.22 us
    pallas_call x1, Pallas kernels: 1.88 us -> 5.43 us  [per_device(): call(functools.partial(block_kernel, small, masks), [jax.ShapeDtypeStruct...]
    unnamed x20 -> x26, local copies, waits for them, and re-layouts: 1.26 us -> 2.63 us
    pallas_call x1, Pallas kernels: 2.2 us -> 1.1 us  [per_device(): call(rows_kernel, [jax.ShapeDtypeStruct((n, local_rows, LANES), t) for t...]
  transfers between devices with their start and end apart: 6 -> 6, of which waited for: 3 -> 3; matrix products, arithmetic and copies ran while one was open for 2% -> 1% of each run, Pallas kernels for 13% -> 11%
where the time goes in v12:
time: 77 us; the launch traced here: 76.4 us
  blocking collectives  23.8 us (31%)
  Pallas kernels  19.4 us (25%)
  starting transfers between devices  15.7 us (20%)
  waiting for transfers between devices  13.4 us (17%)
  local copies, waits for them, and re-layouts  3.22 us (4%)
  between operations  0.8 us (1%)
    all_to_all x1, blocking collectives, exchange(): return lax.all_to_all(x, 'wide', split_axis=0, concat_axis=0, tiled=True)  23.8 us
    ppermute x4, waiting for transfers between devices, partner(): lax.ppermute(x, 'wide', [(i, i ^ mask) for i in range(lax.axis_size('wide...  10.8 us
    all_to_all x2, starting transfers between devices, exchange(): return lax.all_to_all(x, 'wide', split_axis=0, concat_axis=0, tiled=True)  7.98 us
    ppermute x4, starting transfers between devices, partner(): lax.ppermute(x, 'wide', [(i, i ^ mask) for i in range(lax.axis_size('wide...  7.76 us
    pallas_call x1, Pallas kernels, per_device(): call(functools.partial(block_kernel, small, masks), [jax.ShapeDtypeStruct...  5.43 us
    pallas_call x1, Pallas kernels, per_device(): call(gradient_kernel, [jax.ShapeDtypeStruct((fa, cols), F32), jax.ShapeDt...  4.2 us
    pallas_call x1, Pallas kernels, per_device(): call(pick_kernel, jax.ShapeDtypeStruct(shape, BF16), [hbm(), hbm(), hbm()...  3.38 us
    all_to_all x2, waiting for transfers between devices, exchange(): return lax.all_to_all(x, 'wide', split_axis=0, concat_axis=0, tiled=True)  2.64 us
  transfers between devices with their start and end apart: 6, of which 3 were waited for; matrix products, arithmetic and copies ran while one was open for 1% of the time, Pallas kernels for 11%

profile of v12, /device:TPU:0, one launch (start us, length us, event | category | flops | bytes accessed | tf_op | source)
XLA Modules:
  0.0 76.4 jit_solution(17068876836021185980)
XLA Ops:
  0.6 1.4 %shard_map.139 = bf16[16,1408]{1,0:T(8,128)(2,1)} custom-call(s32[1,4]{1,0:T(1,128)} %list_ref.1, s32[4]{0:T(128)} %slot_ref.1, bf16[4,5120]{1,0:T(4,128)(2,1)} %hidden_ref.1), custom_call_target="tpu_custom_call" | custom-call | bytes 81920 | tf_op jit(solution)/shard_map/pallas_call | solution.py:398
  2.1 4.1 %collective-permute-start = (bf16[1,16,1408]{2,1,0:T(8,128)(2,1)}, bf16[1,16,1408]{2,1,0:T(8,128)(2,1)S(1)}, u32[]{:S(2)}, u32[]{:S(2)}) collective-permute-start(bf16[1,16,1408]{2,1,0:T(8,128)(2,1)} %bitcast.2), channel_id=1, source_target_pairs={{0,8},{1,9},{2,10},{3,11},{4,12},{5,13},{6,14},{7,15},{8,0},{9,1},... | collective-permute-start | bytes 135176 | tf_op jit(solution)/shard_map/ppermute | solution.py:346
  6.2 3.4 %shard_map.140 = bf16[16,16,1152]{2,1,0:T(8,128)(2,1)} custom-call(s32[16]{0:T(128)} %t_ref.3, bf16[256,2048]{1,0:T(8,128)(2,1)} %b_ref.3, bf16[320,2048]{1,0:T(8,128)(2,1)} %a_ref.3), custom_call_target="tpu_custom_call" | custom-call | flops 75497472 | bytes 2359296 | tf_op jit(solution)/shard_map/pallas_call | solution.py:377
  9.6 1.6 %collective-permute-start.1 = (bf16[2,16,1408]{2,1,0:T(8,128)(2,1)S(1)}, bf16[2,16,1408]{2,1,0:T(8,128)(2,1)S(1)}, u32[]{:S(2)}, u32[]{:S(2)}) collective-permute-start(bf16[2,16,1408]{2,1,0:T(8,128)(2,1)S(1)} %pad_maximum_fusion.2), channel_id=1, source_target_pairs={{0,4},{1,5},{2,6},{3,7},{4,0},{5,1},{6,2},{7,3},{8,12},{9,13},{10,... | collective-permute-start | bytes 270344 | tf_op jit(solution)/shard_map/ppermute | solution.py:346
  11.2 4.5 %all-to-all-start = ((bf16[16,16,1152]{2,1,0:T(8,128)(2,1)}), bf16[16,16,1152]{2,1,0:T(8,128)(2,1)}, u32[]{:S(2)}, u32[]{:S(2)}) async-start(bf16[16,16,1152]{2,1,0:T(8,128)(2,1)} %shard_map.140), calls=%async_computation | async-start | bytes 1179648 | tf_op jit(solution)/shard_map/all_to_all | solution.py:342
  15.8 1.9 %collective-permute-start.2 = (bf16[4,16,1408]{2,1,0:T(8,128)(2,1)S(1)}, bf16[4,16,1408]{2,1,0:T(8,128)(2,1)S(1)}, u32[]{:S(2)}, u32[]{:S(2)}) collective-permute-start(bf16[4,16,1408]{2,1,0:T(8,128)(2,1)S(1)} %pad_maximum_fusion.1), channel_id=1, source_target_pairs={{0,2},{1,3},{2,0},{3,1},{4,6},{5,7},{6,4},{7,5},{8,10},{9,11},{10,... | collective-permute-start | bytes 540680 | tf_op jit(solution)/shard_map/ppermute | solution.py:346
  17.7 9.7 %collective-permute-done.2 = bf16[4,16,1408]{2,1,0:T(8,128)(2,1)S(1)} collective-permute-done((bf16[4,16,1408]{2,1,0:T(8,128)(2,1)S(1)}, bf16[4,16,1408]{2,1,0:T(8,128)(2,1)S(1)}, u32[]{:S(2)}, u32[]{:S(2)}) %collective-permute-start.2) | collective-permute-done | bytes 180256 | tf_op jit(solution)/shard_map/ppermute | solution.py:346
  27.5 0.1 collective-permute-start.3
  27.6 0.6 dynamic_slice.3.t_ref
  28.2 1.1 %collective-permute-done.3.h1_ref = bf16[8,16,1408]{2,1,0:T(8,128)(2,1)S(1)} collective-permute-done((bf16[8,16,1408]{2,1,0:T(8,128)(2,1)S(1)}, bf16[8,16,1408]{2,1,0:T(8,128)(2,1)S(1)}, u32[]{:S(2)}, u32[]{:S(2)}) %collective-permute-start.3) | collective-permute-done | bytes 360480 | tf_op jit(solution)/shard_map/ppermute | solution.py:346
  29.2 1.1 %shard_map.141 = (f32[16,4,128]{2,1,0:T(4,128)S(1)}, f32[16,4,128]{2,1,0:T(4,128)S(1)}, s32[16,4,128]{2,1,0:T(4,128)S(1)}) custom-call(s32[1]{0:T(128)} %bitcast.me_ref, bf16[8,16,1408]{2,1,0:T(8,128)(2,1)S(1)} %pad_maximum_fusion.h0_ref, bf16[8,16,1408]{2,1,0:T(8,128)(2,1)S(1)} %collective-permute-done.3.h1_ref, bf16[128,5120]{1,0:T(8,128)(2,1)S(1)} %copy-done.1, ...), custom_call_target="tpu_custom_call" | custom-call | flops 167772160 | bytes 2621440 | tf_op jit(solution)/shard_map/pallas_call | solution.py:416
  30.3 0.0 copy-start.5
  30.3 0.6 copy-done.5
  31.0 0.6 copy-done.6
  31.6 0.6 copy-done.7
  32.2 5.4 %shard_map.142 = (bf16[16,16,1280]{2,1,0:T(8,128)(2,1)}, s32[64,128]{1,0:T(8,128)}) custom-call(s32[1]{0:T(128)} %dynamic_slice.3.t_ref, s32[1]{0:T(128)} %bitcast.me_ref, bf16[128,5120]{1,0:T(8,128)(2,1)} %x_ref.3, bf16[128,4096]{1,0:T(8,128)(2,1)} %g_hbm.1, bf16[16,16,1152]{2,1,0:T(8,128)(2,1)} %all-to-all-done.r_ref, f32[16,4,128]{2,1,0:T(4,128)} %copy-done.5, ...), custom_call_target="tpu_custom_call" | custom-call | flops 150994944 | bytes 2359296 | tf_op jit(solution)/shard_map/pallas_call | solution.py:445
  37.6 0.0 copy-start.4
  37.7 23.8 %all_to_all.15.part_ref = bf16[16,16,1280]{2,1,0:T(8,128)(2,1)S(1)} all-to-all(bf16[16,16,1280]{2,1,0:T(8,128)(2,1)} %get-tuple-element.17), channel_id=1, replica_groups=mesh['groups'=2,'wide'=16] {'wide'}, dimensions={0} | all-to-all | bytes 1310720 | tf_op jit(solution)/shard_map/all_to_all | solution.py:342
  61.5 0.8 copy-done.8
  62.2 1.8 %shard_map.144 = f32[16,4,256]{2,1,0:T(4,128)} custom-call(s32[16]{0:T(128)S(1)} %copy-done.9, bf16[16,16,1280]{2,1,0:T(8,128)(2,1)S(1)} %all_to_all.15.part_ref, bf16[256,2048]{1,0:T(8,128)(2,1)S(1)} %copy-done.2, s32[64,128]{1,0:T(8,128)S(1)} %copy-done.8), custom_call_target="tpu_custom_call" | custom-call | flops 67108864 | bytes 1048576 | tf_op jit(solution)/shard_map/pallas_call | solution.py:461
  64.0 3.5 %all-to-all-start.2 = ((f32[16,4,256]{2,1,0:T(4,128)}), f32[16,4,256]{2,1,0:T(4,128)S(1)}, u32[]{:S(2)}, u32[]{:S(2)}) async-start(f32[16,4,256]{2,1,0:T(4,128)} %shard_map.144), calls=%async_computation.2 | async-start | bytes 131072 | tf_op jit(solution)/shard_map/all_to_all | solution.py:342
  67.5 4.2 %shard_map.143 = (f32[320,2048]{1,0:T(8,128)}, f32[256,2048]{1,0:T(8,128)}) custom-call(s32[16]{0:T(128)S(1)} %copy-done.9, bf16[16,16,1280]{2,1,0:T(8,128)(2,1)S(1)} %all_to_all.15.part_ref), custom_call_target="tpu_custom_call" | custom-call | flops 75497472 | bytes 4718592 | tf_op jit(solution)/shard_map/pallas_call | solution.py:471
  71.7 2.6 %all-to-all-done.2.delta_ref = f32[16,4,256]{2,1,0:T(4,128)S(1)} async-done(((f32[16,4,256]{2,1,0:T(4,128)}), f32[16,4,256]{2,1,0:T(4,128)S(1)}, u32[]{:S(2)}, u32[]{:S(2)}) %all-to-all-start.2) | async-done | bytes 65568 | tf_op jit(solution)/shard_map/all_to_all | solution.py:342
  74.4 2.0 %shard_map.145 = bf16[4,4096]{1,0:T(4,128)(2,1)} custom-call(s32[4]{0:T(128)S(1)} %copy-done.10, f32[16,4,256]{2,1,0:T(4,128)S(1)} %all-to-all-done.2.delta_ref, f32[4,4096]{1,0:T(4,128)S(1)} %convert_element_type.3.base_ref, bf16[4,256,512]{2,1,0:T(8,128)(2,1)S(1)} %copy-done.3, bf16[4,256,512]{2,1,0:T(8,128)(2,1)S(1)} %copy-done.4), custom_call_target="tpu_custom_call" | custom-call | flops 16777216 | bytes 2097152 | tf_op jit(solution)/shard_map/pallas_call | solution.py:479
  (27 shorter events, 0.1 us)
Async XLA Ops:
  2.1 7.5 %copy-start.11 = (bf16[16,1408]{1,0:T(8,128)(2,1)S(1)}, bf16[16,1408]{1,0:T(8,128)(2,1)}, u32[]{:S(2)}) copy-start(bf16[16,1408]{1,0:T(8,128)(2,1)} %shard_map.139) | copy-start | bytes 135172
  2.1 25.5 %copy-start.9 = (s32[16]{0:T(128)S(1)}, s32[16]{0:T(128)}, u32[]{:S(2)}) copy-start(s32[16]{0:T(128)} %t_ref.3) | copy-start | bytes 196
  2.1 27.2 %copy-start = (bf16[320,2048]{1,0:T(8,128)(2,1)S(1)}, bf16[320,2048]{1,0:T(8,128)(2,1)}, u32[]{:S(2)}) copy-start(bf16[320,2048]{1,0:T(8,128)(2,1)} %a_ref.3) | copy-start | bytes 3932164
  2.1 27.2 %copy-start.1 = (bf16[128,5120]{1,0:T(8,128)(2,1)S(1)}, bf16[128,5120]{1,0:T(8,128)(2,1)}, u32[]{:S(2)}) copy-start(bf16[128,5120]{1,0:T(8,128)(2,1)} %x_ref.3) | copy-start | bytes 3932164
  2.1 7.5 %collective-permute-start = (bf16[1,16,1408]{2,1,0:T(8,128)(2,1)}, bf16[1,16,1408]{2,1,0:T(8,128)(2,1)S(1)}, u32[]{:S(2)}, u32[]{:S(2)}) collective-permute-start(bf16[1,16,1408]{2,1,0:T(8,128)(2,1)} %bitcast.2), channel_id=1, source_target_pairs={{0,8},{1,9},{2,10},{3,11},{4,12},{5,13},{6,14},{7,15},{8,0},{9,1},... | collective-permute-start | bytes 135176 | tf_op jit(solution)/shard_map/ppermute | solution.py:346
  9.6 6.1 %collective-permute-start.1 = (bf16[2,16,1408]{2,1,0:T(8,128)(2,1)S(1)}, bf16[2,16,1408]{2,1,0:T(8,128)(2,1)S(1)}, u32[]{:S(2)}, u32[]{:S(2)}) collective-permute-start(bf16[2,16,1408]{2,1,0:T(8,128)(2,1)S(1)} %pad_maximum_fusion.2), channel_id=1, source_target_pairs={{0,4},{1,5},{2,6},{3,7},{4,0},{5,1},{6,2},{7,3},{8,12},{9,13},{10,... | collective-permute-start | bytes 270344 | tf_op jit(solution)/shard_map/ppermute | solution.py:346
  11.2 20.9 %all-to-all-start = ((bf16[16,16,1152]{2,1,0:T(8,128)(2,1)}), bf16[16,16,1152]{2,1,0:T(8,128)(2,1)}, u32[]{:S(2)}, u32[]{:S(2)}) async-start(bf16[16,16,1152]{2,1,0:T(8,128)(2,1)} %shard_map.140), calls=%async_computation | async-start | bytes 1179648 | tf_op jit(solution)/shard_map/all_to_all | solution.py:342
  15.8 11.6 %collective-permute-start.2 = (bf16[4,16,1408]{2,1,0:T(8,128)(2,1)S(1)}, bf16[4,16,1408]{2,1,0:T(8,128)(2,1)S(1)}, u32[]{:S(2)}, u32[]{:S(2)}) collective-permute-start(bf16[4,16,1408]{2,1,0:T(8,128)(2,1)S(1)} %pad_maximum_fusion.1), channel_id=1, source_target_pairs={{0,2},{1,3},{2,0},{3,1},{4,6},{5,7},{6,4},{7,5},{8,10},{9,11},{10,... | collective-permute-start | bytes 540680 | tf_op jit(solution)/shard_map/ppermute | solution.py:346
  27.5 1.7 %collective-permute-start.3 = (bf16[8,16,1408]{2,1,0:T(8,128)(2,1)S(1)}, bf16[8,16,1408]{2,1,0:T(8,128)(2,1)S(1)}, u32[]{:S(2)}, u32[]{:S(2)}) collective-permute-start(bf16[8,16,1408]{2,1,0:T(8,128)(2,1)S(1)} %pad_maximum_fusion.h0_ref), channel_id=1, source_target_pairs={{0,1},{1,0},{2,3},{3,2},{4,5},{5,4},{6,7},{7,6},{8,9},{9,8},{10,11... | collective-permute-start | bytes 1081352 | tf_op jit(solution)/shard_map/ppermute | solution.py:346
  30.3 0.6 copy-start.5
  31.0 0.6 copy-start.6
  31.6 0.6 copy-start.7
  32.2 29.3 %copy-start.2 = (bf16[256,2048]{1,0:T(8,128)(2,1)S(1)}, bf16[256,2048]{1,0:T(8,128)(2,1)}, u32[]{:S(2)}) copy-start(bf16[256,2048]{1,0:T(8,128)(2,1)} %b_ref.3) | copy-start | bytes 3145732
  32.2 35.3 %copy-start.12 = (bf16[4,4096]{1,0:T(4,128)(2,1)S(1)}, bf16[4,4096]{1,0:T(4,128)(2,1)}, u32[]{:S(2)}) copy-start(bf16[4,4096]{1,0:T(4,128)(2,1)} %param.20) | copy-start | bytes 98308
  32.2 42.2 %copy-start.10 = (s32[4]{0:T(128)S(1)}, s32[4]{0:T(128)}, u32[]{:S(2)}) copy-start(s32[4]{0:T(128)} %len_ref.1) | copy-start | bytes 52
  37.6 36.7 %copy-start.3 = (bf16[4,256,512]{2,1,0:T(8,128)(2,1)S(1)}, bf16[4,256,512]{2,1,0:T(8,128)(2,1)}, u32[]{:S(2)}) copy-start(bf16[4,256,512]{2,1,0:T(8,128)(2,1)} %k_ref.1) | copy-start | bytes 3145732
  37.6 36.7 %copy-start.4 = (bf16[4,256,512]{2,1,0:T(8,128)(2,1)S(1)}, bf16[4,256,512]{2,1,0:T(8,128)(2,1)}, u32[]{:S(2)}) copy-start(bf16[4,256,512]{2,1,0:T(8,128)(2,1)} %v_ref.1) | copy-start | bytes 3145732
  61.5 0.8 copy-start.8
  64.0 10.4 %all-to-all-start.2 = ((f32[16,4,256]{2,1,0:T(4,128)}), f32[16,4,256]{2,1,0:T(4,128)S(1)}, u32[]{:S(2)}, u32[]{:S(2)}) async-start(f32[16,4,256]{2,1,0:T(4,128)} %shard_map.144), calls=%async_computation.2 | async-start | bytes 131072 | tf_op jit(solution)/shard_map/all_to_all | solution.py:342

commit v13 on v10

--- a/solution.py
+++ b/solution.py
@@ -24,6 +24,7 @@
 BF16 = jnp.bfloat16
 VMEM_LIMIT = 24 * 1024 * 1024
 ALL_VMEM = 58 * 1024 * 1024 + 768 * 1024
+PICK_VMEM = 50 * 1024 * 1024
 
 
 def vmem():
@@ -382,7 +383,7 @@
         ],
         flops=2 * RANK * LANES * n * (fa + fb),
         nbytes=2 * cols * (fa + fb),
-        limit=ALL_VMEM,
+        limit=PICK_VMEM,
     )(tenant_of_block, up_factors_transposed, down_factors)
 
     if small:

time: 73.9 us -> 75.3 us (1.019)
  local copies, waits for them, and re-layouts: 1.85 us -> 5.1 us
  starting transfers between devices: 15.7 us -> 14.6 us
  Pallas kernels: 16.9 us -> 16.1 us
    unnamed x20 -> x26, local copies, waits for them, and re-layouts: 1.26 us -> 4.46 us
    pallas_call x1, Pallas kernels: 3.38 us -> 2.45 us  [per_device(): call(pick_kernel, jax.ShapeDtypeStruct(shape, BF16), [hbm(), hbm(), hbm()...]
    all_to_all x2, starting transfers between devices: 7.94 us -> 7.07 us  [exchange(): return lax.all_to_all(x, 'wide', split_axis=0, concat_axis=0, tiled=True)]
  transfers between devices with their start and end apart: 6 -> 6, of which waited for: 3 -> 3; matrix products, arithmetic and copies ran while one was open for 2% -> 2% of each run, Pallas kernels for 13% -> 12%
where the time goes in v13:
time: 75.3 us; the launch traced here: 74.8 us
  blocking collectives  23.7 us (31%)
  Pallas kernels  16.1 us (21%)
  starting transfers between devices  14.6 us (19%)
  waiting for transfers between devices  13.7 us (18%)
  local copies, waits for them, and re-layouts  5.1 us (7%)
  other arithmetic  0.82 us (1%)
  between operations  0.79 us (1%)
    all_to_all x1, blocking collectives, exchange(): return lax.all_to_all(x, 'wide', split_axis=0, concat_axis=0, tiled=True)  23.7 us
    ppermute x4, waiting for transfers between devices, partner(): lax.ppermute(x, 'wide', [(i, i ^ mask) for i in range(lax.axis_size('wide...  11.1 us
    ppermute x4, starting transfers between devices, partner(): lax.ppermute(x, 'wide', [(i, i ^ mask) for i in range(lax.axis_size('wide...  7.55 us
    all_to_all x2, starting transfers between devices, exchange(): return lax.all_to_all(x, 'wide', split_axis=0, concat_axis=0, tiled=True)  7.07 us
    unnamed x26, local copies, waits for them, and re-layouts  4.46 us
    pallas_call x1, Pallas kernels, per_device(): call(gradient_kernel, [jax.ShapeDtypeStruct((fa, cols), F32), jax.ShapeDt...  4.22 us
    all_to_all x2, waiting for transfers between devices, exchange(): return lax.all_to_all(x, 'wide', split_axis=0, concat_axis=0, tiled=True)  2.61 us
    pallas_call x1, Pallas kernels, per_device(): call(pick_kernel, jax.ShapeDtypeStruct(shape, BF16), [hbm(), hbm(), hbm()...  2.45 us
  transfers between devices with their start and end apart: 6, of which 3 were waited for; matrix products, arithmetic and copies ran while one was open for 2% of the time, Pallas kernels for 12%

profile of v13, /device:TPU:0, one launch (start us, length us, event | category | flops | bytes accessed | tf_op | source)
XLA Modules:
  0.0 74.8 jit_solution(14419337034097877247)
XLA Ops:
  0.6 1.4 %shard_map.139 = bf16[16,1408]{1,0:T(8,128)(2,1)} custom-call(s32[1,4]{1,0:T(1,128)} %list_ref.1, s32[4]{0:T(128)} %slot_ref.1, bf16[4,5120]{1,0:T(4,128)(2,1)} %hidden_ref.1), custom_call_target="tpu_custom_call" | custom-call | bytes 81920 | tf_op jit(solution)/shard_map/pallas_call | solution.py:390
  2.1 4.0 %collective-permute-start = (bf16[1,16,1408]{2,1,0:T(8,128)(2,1)}, bf16[1,16,1408]{2,1,0:T(8,128)(2,1)S(1)}, u32[]{:S(2)}, u32[]{:S(2)}) collective-permute-start(bf16[1,16,1408]{2,1,0:T(8,128)(2,1)} %bitcast.2), channel_id=1, source_target_pairs={{0,8},{1,9},{2,10},{3,11},{4,12},{5,13},{6,14},{7,15},{8,0},{9,1},... | collective-permute-start | bytes 135176 | tf_op jit(solution)/shard_map/ppermute | solution.py:338
  6.1 1.3 %copy-done = bf16[320,2048]{1,0:T(8,128)(2,1)S(1)} copy-done((bf16[320,2048]{1,0:T(8,128)(2,1)S(1)}, bf16[320,2048]{1,0:T(8,128)(2,1)}, u32[]{:S(2)}) %copy-start) | copy-done | bytes 1310744
  7.4 1.2 %copy-done.3 = bf16[256,2048]{1,0:T(8,128)(2,1)S(1)} copy-done((bf16[256,2048]{1,0:T(8,128)(2,1)S(1)}, bf16[256,2048]{1,0:T(8,128)(2,1)}, u32[]{:S(2)}) %copy-start.3) | copy-done | bytes 1048600
  8.6 0.7 copy-done.8
  9.3 2.5 %shard_map.140 = bf16[16,16,1152]{2,1,0:T(8,128)(2,1)} custom-call(s32[16]{0:T(128)S(1)} %copy-done.8, bf16[256,2048]{1,0:T(8,128)(2,1)S(1)} %copy-done.3, bf16[320,2048]{1,0:T(8,128)(2,1)S(1)} %copy-done), custom_call_target="tpu_custom_call" | custom-call | flops 75497472 | bytes 2359296 | tf_op jit(solution)/shard_map/pallas_call | solution.py:369
  11.8 1.6 %collective-permute-start.1 = (bf16[2,16,1408]{2,1,0:T(8,128)(2,1)S(1)}, bf16[2,16,1408]{2,1,0:T(8,128)(2,1)S(1)}, u32[]{:S(2)}, u32[]{:S(2)}) collective-permute-start(bf16[2,16,1408]{2,1,0:T(8,128)(2,1)S(1)} %pad_maximum_fusion.2), channel_id=1, source_target_pairs={{0,4},{1,5},{2,6},{3,7},{4,0},{5,1},{6,2},{7,3},{8,12},{9,13},{10,... | collective-permute-start | bytes 270344 | tf_op jit(solution)/shard_map/ppermute | solution.py:338
  13.4 3.6 %all-to-all-start = ((bf16[16,16,1152]{2,1,0:T(8,128)(2,1)}), bf16[16,16,1152]{2,1,0:T(8,128)(2,1)S(1)}, u32[]{:S(2)}, u32[]{:S(2)}) async-start(bf16[16,16,1152]{2,1,0:T(8,128)(2,1)} %shard_map.140), calls=%async_computation | async-start | bytes 1179648 | tf_op jit(solution)/shard_map/all_to_all | solution.py:334
  17.1 1.9 %collective-permute-start.2 = (bf16[4,16,1408]{2,1,0:T(8,128)(2,1)S(1)}, bf16[4,16,1408]{2,1,0:T(8,128)(2,1)S(1)}, u32[]{:S(2)}, u32[]{:S(2)}) collective-permute-start(bf16[4,16,1408]{2,1,0:T(8,128)(2,1)S(1)} %pad_maximum_fusion.1), channel_id=1, source_target_pairs={{0,2},{1,3},{2,0},{3,1},{4,6},{5,7},{6,4},{7,5},{8,10},{9,11},{10,... | collective-permute-start | bytes 540680 | tf_op jit(solution)/shard_map/ppermute | solution.py:338
  19.0 9.7 %collective-permute-done.2 = bf16[4,16,1408]{2,1,0:T(8,128)(2,1)S(1)} collective-permute-done((bf16[4,16,1408]{2,1,0:T(8,128)(2,1)S(1)}, bf16[4,16,1408]{2,1,0:T(8,128)(2,1)S(1)}, u32[]{:S(2)}, u32[]{:S(2)}) %collective-permute-start.2) | collective-permute-done | bytes 180256 | tf_op jit(solution)/shard_map/ppermute | solution.py:338
  28.7 0.8 %pad_maximum_fusion.h0_ref = bf16[8,16,1408]{2,1,0:T(8,128)(2,1)} fusion(bf16[4,16,1408]{2,1,0:T(8,128)(2,1)S(1)} %collective-permute-done.2, bf16[4,16,1408]{2,1,0:T(8,128)(2,1)S(1)} %pad_maximum_fusion.1), kind=kLoop, calls=%fused_computation | loop fusion | flops 180224 | bytes 720896 | tf_op jit(solution)/shard_map/concatenate | solution.py:404
  29.4 0.6 dynamic_slice.3.t_ref
  30.1 1.4 %collective-permute-done.3.h1_ref = bf16[8,16,1408]{2,1,0:T(8,128)(2,1)} collective-permute-done((bf16[8,16,1408]{2,1,0:T(8,128)(2,1)}, bf16[8,16,1408]{2,1,0:T(8,128)(2,1)}, u32[]{:S(2)}, u32[]{:S(2)}) %collective-permute-start.3) | collective-permute-done | bytes 360480 | tf_op jit(solution)/shard_map/ppermute | solution.py:338
  31.5 2.2 %shard_map.141 = (f32[16,4,128]{2,1,0:T(4,128)S(1)}, f32[16,4,128]{2,1,0:T(4,128)S(1)}, s32[16,4,128]{2,1,0:T(4,128)S(1)}) custom-call(s32[1]{0:T(128)} %bitcast.me_ref, bf16[8,16,1408]{2,1,0:T(8,128)(2,1)} %pad_maximum_fusion.h0_ref, bf16[8,16,1408]{2,1,0:T(8,128)(2,1)} %collective-permute-done.3.h1_ref, bf16[128,5120]{1,0:T(8,128)(2,1)S(1)} %copy-done.2, ...), custom_call_target="tpu_custom_call" | custom-call | flops 167772160 | bytes 2621440 | tf_op jit(solution)/shard_map/pallas_call | solution.py:408
  33.6 0.0 copy-start.7
  33.6 1.2 %copy-done.7 = bf16[128,4096]{1,0:T(8,128)(2,1)S(1)} copy-done((bf16[128,4096]{1,0:T(8,128)(2,1)S(1)}, bf16[128,4096]{1,0:T(8,128)(2,1)}, u32[]{:S(2)}) %copy-start.7) | copy-done | bytes 1048600
  34.9 2.0 %shard_map.142 = (bf16[16,16,1280]{2,1,0:T(8,128)(2,1)S(1)}, s32[64,128]{1,0:T(8,128)S(1)}) custom-call(s32[1]{0:T(128)} %dynamic_slice.3.t_ref, s32[1]{0:T(128)} %bitcast.me_ref, bf16[128,5120]{1,0:T(8,128)(2,1)S(1)} %copy-done.2, bf16[128,4096]{1,0:T(8,128)(2,1)S(1)} %copy-done.7, bf16[16,16,1152]{2,1,0:T(8,128)(2,1)S(1)} %all-to-all-done.r_ref, ...), custom_call_target="tpu_custom_call" | custom-call | flops 150994944 | bytes 2359296 | tf_op jit(solution)/shard_map/pallas_call | solution.py:437
  36.9 0.0 copy-start.5
  36.9 23.7 %all_to_all.15.part_ref = bf16[16,16,1280]{2,1,0:T(8,128)(2,1)S(1)} all-to-all(bf16[16,16,1280]{2,1,0:T(8,128)(2,1)S(1)} %get-tuple-element.17), channel_id=1, replica_groups=mesh['groups'=2,'wide'=16] {'wide'}, dimensions={0} | all-to-all | bytes 1310720 | tf_op jit(solution)/shard_map/all_to_all | solution.py:334
  60.6 1.8 %shard_map.144 = f32[16,4,256]{2,1,0:T(4,128)} custom-call(s32[16]{0:T(128)S(1)} %copy-done.9, bf16[16,16,1280]{2,1,0:T(8,128)(2,1)S(1)} %all_to_all.15.part_ref, bf16[256,2048]{1,0:T(8,128)(2,1)S(1)} %copy-done.4, s32[64,128]{1,0:T(8,128)S(1)} %get-tuple-element.20.u_ref), custom_call_target="tpu_custom_call" | custom-call | flops 67108864 | bytes 1048576 | tf_op jit(solution)/shard_map/pallas_call | solution.py:451
  62.4 3.5 %all-to-all-start.2 = ((f32[16,4,256]{2,1,0:T(4,128)}), f32[16,4,256]{2,1,0:T(4,128)S(1)}, u32[]{:S(2)}, u32[]{:S(2)}) async-start(f32[16,4,256]{2,1,0:T(4,128)} %shard_map.144), calls=%async_computation.2 | async-start | bytes 131072 | tf_op jit(solution)/shard_map/all_to_all | solution.py:334
  65.9 4.2 %shard_map.143 = (f32[320,2048]{1,0:T(8,128)}, f32[256,2048]{1,0:T(8,128)}) custom-call(s32[16]{0:T(128)S(1)} %copy-done.9, bf16[16,16,1280]{2,1,0:T(8,128)(2,1)S(1)} %all_to_all.15.part_ref), custom_call_target="tpu_custom_call" | custom-call | flops 75497472 | bytes 4718592 | tf_op jit(solution)/shard_map/pallas_call | solution.py:461
  70.1 2.6 %all-to-all-done.2.delta_ref = f32[16,4,256]{2,1,0:T(4,128)S(1)} async-done(((f32[16,4,256]{2,1,0:T(4,128)}), f32[16,4,256]{2,1,0:T(4,128)S(1)}, u32[]{:S(2)}, u32[]{:S(2)}) %all-to-all-start.2) | async-done | bytes 65568 | tf_op jit(solution)/shard_map/all_to_all | solution.py:334
  72.7 2.1 %shard_map.145 = bf16[4,4096]{1,0:T(4,128)(2,1)} custom-call(s32[4]{0:T(128)S(1)} %copy-done.10, f32[16,4,256]{2,1,0:T(4,128)S(1)} %all-to-all-done.2.delta_ref, f32[4,4096]{1,0:T(4,128)S(1)} %convert_element_type.3.base_ref, bf16[4,256,512]{2,1,0:T(8,128)(2,1)S(1)} %copy-done.5, bf16[4,256,512]{2,1,0:T(8,128)(2,1)S(1)} %copy-done.6), custom_call_target="tpu_custom_call" | custom-call | flops 16777216 | bytes 2097152 | tf_op jit(solution)/shard_map/pallas_call | solution.py:469
  (27 shorter events, 0.1 us)
Async XLA Ops:
  2.1 9.7 %collective-permute-start = (bf16[1,16,1408]{2,1,0:T(8,128)(2,1)}, bf16[1,16,1408]{2,1,0:T(8,128)(2,1)S(1)}, u32[]{:S(2)}, u32[]{:S(2)}) collective-permute-start(bf16[1,16,1408]{2,1,0:T(8,128)(2,1)} %bitcast.2), channel_id=1, source_target_pairs={{0,8},{1,9},{2,10},{3,11},{4,12},{5,13},{6,14},{7,15},{8,0},{9,1},... | collective-permute-start | bytes 135176 | tf_op jit(solution)/shard_map/ppermute | solution.py:338
  6.1 1.3 %copy-start = (bf16[320,2048]{1,0:T(8,128)(2,1)S(1)}, bf16[320,2048]{1,0:T(8,128)(2,1)}, u32[]{:S(2)}) copy-start(bf16[320,2048]{1,0:T(8,128)(2,1)} %a_ref.3) | copy-start | bytes 3932164
  7.4 1.2 %copy-start.3 = (bf16[256,2048]{1,0:T(8,128)(2,1)S(1)}, bf16[256,2048]{1,0:T(8,128)(2,1)}, u32[]{:S(2)}) copy-start(bf16[256,2048]{1,0:T(8,128)(2,1)} %b_ref.3) | copy-start | bytes 3145732
  8.6 0.7 copy-start.8
  9.3 2.5 %copy-start.11 = (bf16[16,1408]{1,0:T(8,128)(2,1)S(1)}, bf16[16,1408]{1,0:T(8,128)(2,1)}, u32[]{:S(2)}) copy-start(bf16[16,1408]{1,0:T(8,128)(2,1)} %shard_map.139) | copy-start | bytes 135172
  9.3 20.1 %copy-start.9 = (s32[16]{0:T(128)S(1)}, s32[16]{0:T(128)}, u32[]{:S(2)}) copy-start(s32[16]{0:T(128)} %t_ref.3) | copy-start | bytes 196
  9.3 22.2 %copy-start.1 = (bf16[320,2048]{1,0:T(8,128)(2,1)S(1)}, bf16[320,2048]{1,0:T(8,128)(2,1)}, u32[]{:S(2)}) copy-start(bf16[320,2048]{1,0:T(8,128)(2,1)} %a_ref.3) | copy-start | bytes 3932164
  9.3 22.2 %copy-start.2 = (bf16[128,5120]{1,0:T(8,128)(2,1)S(1)}, bf16[128,5120]{1,0:T(8,128)(2,1)}, u32[]{:S(2)}) copy-start(bf16[128,5120]{1,0:T(8,128)(2,1)} %x_ref.3) | copy-start | bytes 3932164
  11.8 5.2 %collective-permute-start.1 = (bf16[2,16,1408]{2,1,0:T(8,128)(2,1)S(1)}, bf16[2,16,1408]{2,1,0:T(8,128)(2,1)S(1)}, u32[]{:S(2)}, u32[]{:S(2)}) collective-permute-start(bf16[2,16,1408]{2,1,0:T(8,128)(2,1)S(1)} %pad_maximum_fusion.2), channel_id=1, source_target_pairs={{0,4},{1,5},{2,6},{3,7},{4,0},{5,1},{6,2},{7,3},{8,12},{9,13},{10,... | collective-permute-start | bytes 270344 | tf_op jit(solution)/shard_map/ppermute | solution.py:338
  13.4 20.2 %all-to-all-start = ((bf16[16,16,1152]{2,1,0:T(8,128)(2,1)}), bf16[16,16,1152]{2,1,0:T(8,128)(2,1)S(1)}, u32[]{:S(2)}, u32[]{:S(2)}) async-start(bf16[16,16,1152]{2,1,0:T(8,128)(2,1)} %shard_map.140), calls=%async_computation | async-start | bytes 1179648 | tf_op jit(solution)/shard_map/all_to_all | solution.py:334
  17.1 11.6 %collective-permute-start.2 = (bf16[4,16,1408]{2,1,0:T(8,128)(2,1)S(1)}, bf16[4,16,1408]{2,1,0:T(8,128)(2,1)S(1)}, u32[]{:S(2)}, u32[]{:S(2)}) collective-permute-start(bf16[4,16,1408]{2,1,0:T(8,128)(2,1)S(1)} %pad_maximum_fusion.1), channel_id=1, source_target_pairs={{0,2},{1,3},{2,0},{3,1},{4,6},{5,7},{6,4},{7,5},{8,10},{9,11},{10,... | collective-permute-start | bytes 540680 | tf_op jit(solution)/shard_map/ppermute | solution.py:338
  29.4 2.0 %collective-permute-start.3 = (bf16[8,16,1408]{2,1,0:T(8,128)(2,1)}, bf16[8,16,1408]{2,1,0:T(8,128)(2,1)}, u32[]{:S(2)}, u32[]{:S(2)}) collective-permute-start(bf16[8,16,1408]{2,1,0:T(8,128)(2,1)} %pad_maximum_fusion.h0_ref), channel_id=1, source_target_pairs={{0,1},{1,0},{2,3},{3,2},{4,5},{5,4},{6,7},{7,6},{8,9},{9,8},{10,11... | collective-permute-start | bytes 1081352 | tf_op jit(solution)/shard_map/ppermute | solution.py:338
  33.6 1.2 %copy-start.7 = (bf16[128,4096]{1,0:T(8,128)(2,1)S(1)}, bf16[128,4096]{1,0:T(8,128)(2,1)}, u32[]{:S(2)}) copy-start(bf16[128,4096]{1,0:T(8,128)(2,1)} %g_ref.1) | copy-start | bytes 3145732
  34.9 25.7 %copy-start.4 = (bf16[256,2048]{1,0:T(8,128)(2,1)S(1)}, bf16[256,2048]{1,0:T(8,128)(2,1)}, u32[]{:S(2)}) copy-start(bf16[256,2048]{1,0:T(8,128)(2,1)} %b_ref.3) | copy-start | bytes 3145732
  36.8 29.0 %copy-start.12 = (bf16[4,4096]{1,0:T(4,128)(2,1)S(1)}, bf16[4,4096]{1,0:T(4,128)(2,1)}, u32[]{:S(2)}) copy-start(bf16[4,4096]{1,0:T(4,128)(2,1)} %param.20) | copy-start | bytes 98308
  36.9 35.9 %copy-start.5 = (bf16[4,256,512]{2,1,0:T(8,128)(2,1)S(1)}, bf16[4,256,512]{2,1,0:T(8,128)(2,1)}, u32[]{:S(2)}) copy-start(bf16[4,256,512]{2,1,0:T(8,128)(2,1)} %k_ref.1) | copy-start | bytes 3145732
  36.9 35.8 %copy-start.6 = (bf16[4,256,512]{2,1,0:T(8,128)(2,1)S(1)}, bf16[4,256,512]{2,1,0:T(8,128)(2,1)}, u32[]{:S(2)}) copy-start(bf16[4,256,512]{2,1,0:T(8,128)(2,1)} %v_ref.1) | copy-start | bytes 3145732
  36.9 35.8 %copy-start.10 = (s32[4]{0:T(128)S(1)}, s32[4]{0:T(128)}, u32[]{:S(2)}) copy-start(s32[4]{0:T(128)} %len_ref.1) | copy-start | bytes 52
  62.4 10.4 %all-to-all-start.2 = ((f32[16,4,256]{2,1,0:T(4,128)}), f32[16,4,256]{2,1,0:T(4,128)S(1)}, u32[]{:S(2)}, u32[]{:S(2)}) async-start(f32[16,4,256]{2,1,0:T(4,128)} %shard_map.144), calls=%async_computation.2 | async-start | bytes 131072 | tf_op jit(solution)/shard_map/all_to_all | solution.py:334

commit v14 on v10

--- a/solution.py
+++ b/solution.py
@@ -286,12 +286,12 @@
     change = dot(jnp.concatenate(matched, axis=1), jnp.concatenate(up, axis=0), 1, 0)
     delta = adapter_scale * (old - learning_rate * (adapter_scale * change))
     for d in range(n):
-        o_ref[d] = delta[d * ROWS_DEV : (d + 1) * ROWS_DEV]
+        o_ref[d] = delta[d * ROWS_DEV : (d + 1) * ROWS_DEV].astype(BF16)
 
 
 def attention_kernel(len_ref, delta_ref, base_ref, k_ref, v_ref, o_ref):
     n = delta_ref.shape[0]
-    delta = jnp.concatenate([delta_ref[d] for d in range(n)], axis=1)
+    delta = jnp.concatenate([delta_ref[d].astype(F32) for d in range(n)], axis=1)
     query = (base_ref[...] + delta).astype(BF16).astype(F32)
     group = HEADS // KV_HEADS
     cache = k_ref.shape[1]
@@ -449,7 +449,7 @@
 
     delta = call(
         functools.partial(delta_kernel, fa),
-        jax.ShapeDtypeStruct((n, local_rows, fb), F32),
+        jax.ShapeDtypeStruct((n, local_rows, fb), BF16),
         [smem()] + [vmem()] * (3 + len(low_rank)),
         vmem(),
         flops=2 * rows * cols * fb,

time: 73.9 us -> 73.6 us (level)
  no operation moved by 1% of the time
where the time goes in v14:
time: 73.6 us; the launch traced here: 73.2 us
  blocking collectives  23.6 us (32%)
  Pallas kernels  16.9 us (23%)
  starting transfers between devices  15.7 us (21%)
  waiting for transfers between devices  13.5 us (18%)
  local copies, waits for them, and re-layouts  1.85 us (3%)
  other arithmetic  0.82 us (1%)
  between operations  0.79 us (1%)
    all_to_all x1, blocking collectives, exchange(): return lax.all_to_all(x, 'wide', split_axis=0, concat_axis=0, tiled=True)  23.6 us
    ppermute x4, waiting for transfers between devices, partner(): lax.ppermute(x, 'wide', [(i, i ^ mask) for i in range(lax.axis_size('wide...  11.1 us
    all_to_all x2, starting transfers between devices, exchange(): return lax.all_to_all(x, 'wide', split_axis=0, concat_axis=0, tiled=True)  7.95 us
    ppermute x4, starting transfers between devices, partner(): lax.ppermute(x, 'wide', [(i, i ^ mask) for i in range(lax.axis_size('wide...  7.73 us
    pallas_call x1, Pallas kernels, per_device(): call(gradient_kernel, [jax.ShapeDtypeStruct((fa, cols), F32), jax.ShapeDt...  4.2 us
    pallas_call x1, Pallas kernels, per_device(): call(pick_kernel, jax.ShapeDtypeStruct(shape, BF16), [hbm(), hbm(), hbm()...  3.38 us
    all_to_all x2, waiting for transfers between devices, exchange(): return lax.all_to_all(x, 'wide', split_axis=0, concat_axis=0, tiled=True)  2.37 us
    pallas_call x1, Pallas kernels, per_device(): call(rows_kernel, [jax.ShapeDtypeStruct((n, local_rows, LANES), t) for t...  2.2 us
  transfers between devices with their start and end apart: 6, of which 3 were waited for; matrix products, arithmetic and copies ran while one was open for 2% of the time, Pallas kernels for 13%

profile of v14, /device:TPU:0, one launch (start us, length us, event | category | flops | bytes accessed | tf_op | source)
XLA Modules:
  0.0 73.2 jit_solution(13516107850764648163)
XLA Ops:
  0.6 1.4 %shard_map.139 = bf16[16,1408]{1,0:T(8,128)(2,1)} custom-call(s32[1,4]{1,0:T(1,128)} %list_ref.1, s32[4]{0:T(128)} %slot_ref.1, bf16[4,5120]{1,0:T(4,128)(2,1)} %hidden_ref.1), custom_call_target="tpu_custom_call" | custom-call | bytes 81920 | tf_op jit(solution)/shard_map/pallas_call | solution.py:389
  2.1 4.1 %collective-permute-start = (bf16[1,16,1408]{2,1,0:T(8,128)(2,1)}, bf16[1,16,1408]{2,1,0:T(8,128)(2,1)S(1)}, u32[]{:S(2)}, u32[]{:S(2)}) collective-permute-start(bf16[1,16,1408]{2,1,0:T(8,128)(2,1)} %bitcast.2), channel_id=1, source_target_pairs={{0,8},{1,9},{2,10},{3,11},{4,12},{5,13},{6,14},{7,15},{8,0},{9,1},... | collective-permute-start | bytes 135176 | tf_op jit(solution)/shard_map/ppermute | solution.py:337
  6.2 3.4 %shard_map.140 = bf16[16,16,1152]{2,1,0:T(8,128)(2,1)} custom-call(s32[16]{0:T(128)} %t_ref.3, bf16[256,2048]{1,0:T(8,128)(2,1)} %b_ref.3, bf16[320,2048]{1,0:T(8,128)(2,1)} %a_ref.3), custom_call_target="tpu_custom_call" | custom-call | flops 75497472 | bytes 2359296 | tf_op jit(solution)/shard_map/pallas_call | solution.py:368
  9.6 1.6 %collective-permute-start.1 = (bf16[2,16,1408]{2,1,0:T(8,128)(2,1)S(1)}, bf16[2,16,1408]{2,1,0:T(8,128)(2,1)S(1)}, u32[]{:S(2)}, u32[]{:S(2)}) collective-permute-start(bf16[2,16,1408]{2,1,0:T(8,128)(2,1)S(1)} %pad_maximum_fusion.2), channel_id=1, source_target_pairs={{0,4},{1,5},{2,6},{3,7},{4,0},{5,1},{6,2},{7,3},{8,12},{9,13},{10,... | collective-permute-start | bytes 270344 | tf_op jit(solution)/shard_map/ppermute | solution.py:337
  11.2 4.5 %all-to-all-start = ((bf16[16,16,1152]{2,1,0:T(8,128)(2,1)}), bf16[16,16,1152]{2,1,0:T(8,128)(2,1)S(1)}, u32[]{:S(2)}, u32[]{:S(2)}) async-start(bf16[16,16,1152]{2,1,0:T(8,128)(2,1)} %shard_map.140), calls=%async_computation | async-start | bytes 1179648 | tf_op jit(solution)/shard_map/all_to_all | solution.py:333
  15.7 2.0 %collective-permute-start.2 = (bf16[4,16,1408]{2,1,0:T(8,128)(2,1)S(1)}, bf16[4,16,1408]{2,1,0:T(8,128)(2,1)S(1)}, u32[]{:S(2)}, u32[]{:S(2)}) collective-permute-start(bf16[4,16,1408]{2,1,0:T(8,128)(2,1)S(1)} %pad_maximum_fusion.1), channel_id=1, source_target_pairs={{0,2},{1,3},{2,0},{3,1},{4,6},{5,7},{6,4},{7,5},{8,10},{9,11},{10,... | collective-permute-start | bytes 540680 | tf_op jit(solution)/shard_map/ppermute | solution.py:337
  17.7 9.7 %collective-permute-done.2 = bf16[4,16,1408]{2,1,0:T(8,128)(2,1)S(1)} collective-permute-done((bf16[4,16,1408]{2,1,0:T(8,128)(2,1)S(1)}, bf16[4,16,1408]{2,1,0:T(8,128)(2,1)S(1)}, u32[]{:S(2)}, u32[]{:S(2)}) %collective-permute-start.2) | collective-permute-done | bytes 180256 | tf_op jit(solution)/shard_map/ppermute | solution.py:337
  27.4 0.8 %pad_maximum_fusion.h0_ref = bf16[8,16,1408]{2,1,0:T(8,128)(2,1)} fusion(bf16[4,16,1408]{2,1,0:T(8,128)(2,1)S(1)} %collective-permute-done.2, bf16[4,16,1408]{2,1,0:T(8,128)(2,1)S(1)} %pad_maximum_fusion.1), kind=kLoop, calls=%fused_computation | loop fusion | flops 180224 | bytes 720896 | tf_op jit(solution)/shard_map/concatenate | solution.py:403
  28.2 0.6 dynamic_slice.3.t_ref
  28.8 1.4 %collective-permute-done.3.h1_ref = bf16[8,16,1408]{2,1,0:T(8,128)(2,1)} collective-permute-done((bf16[8,16,1408]{2,1,0:T(8,128)(2,1)}, bf16[8,16,1408]{2,1,0:T(8,128)(2,1)}, u32[]{:S(2)}, u32[]{:S(2)}) %collective-permute-start.3) | collective-permute-done | bytes 360480 | tf_op jit(solution)/shard_map/ppermute | solution.py:337
  30.2 2.2 %shard_map.141 = (f32[16,4,128]{2,1,0:T(4,128)S(1)}, f32[16,4,128]{2,1,0:T(4,128)S(1)}, s32[16,4,128]{2,1,0:T(4,128)S(1)}) custom-call(s32[1]{0:T(128)} %bitcast.me_ref, bf16[8,16,1408]{2,1,0:T(8,128)(2,1)} %pad_maximum_fusion.h0_ref, bf16[8,16,1408]{2,1,0:T(8,128)(2,1)} %collective-permute-done.3.h1_ref, bf16[128,5120]{1,0:T(8,128)(2,1)S(1)} %copy-done.1, ...), custom_call_target="tpu_custom_call" | custom-call | flops 167772160 | bytes 2621440 | tf_op jit(solution)/shard_map/pallas_call | solution.py:407
  32.4 0.0 copy-start.5
  32.5 1.2 %copy-done.5 = bf16[128,4096]{1,0:T(8,128)(2,1)S(1)} copy-done((bf16[128,4096]{1,0:T(8,128)(2,1)S(1)}, bf16[128,4096]{1,0:T(8,128)(2,1)}, u32[]{:S(2)}) %copy-start.5) | copy-done | bytes 1048600
  33.7 1.9 %shard_map.142 = (bf16[16,16,1280]{2,1,0:T(8,128)(2,1)S(1)}, s32[64,128]{1,0:T(8,128)S(1)}) custom-call(s32[1]{0:T(128)} %dynamic_slice.3.t_ref, s32[1]{0:T(128)} %bitcast.me_ref, bf16[128,5120]{1,0:T(8,128)(2,1)S(1)} %copy-done.1, bf16[128,4096]{1,0:T(8,128)(2,1)S(1)} %copy-done.5, bf16[16,16,1152]{2,1,0:T(8,128)(2,1)S(1)} %all-to-all-done.r_ref, ...), custom_call_target="tpu_custom_call" | custom-call | flops 150994944 | bytes 2359296 | tf_op jit(solution)/shard_map/pallas_call | solution.py:436
  35.6 0.0 copy-start.9
  35.6 0.0 copy-start.3
  35.6 0.0 copy-start.4
  35.6 0.0 copy-start.7
  35.6 23.6 %all_to_all.15.part_ref = bf16[16,16,1280]{2,1,0:T(8,128)(2,1)S(1)} all-to-all(bf16[16,16,1280]{2,1,0:T(8,128)(2,1)S(1)} %get-tuple-element.17), channel_id=1, replica_groups=mesh['groups'=2,'wide'=16] {'wide'}, dimensions={0} | all-to-all | bytes 1310720 | tf_op jit(solution)/shard_map/all_to_all | solution.py:333
  59.2 1.8 %shard_map.144 = bf16[16,4,256]{2,1,0:T(4,128)(2,1)} custom-call(s32[16]{0:T(128)S(1)} %copy-done.6, bf16[16,16,1280]{2,1,0:T(8,128)(2,1)S(1)} %all_to_all.15.part_ref, bf16[256,2048]{1,0:T(8,128)(2,1)S(1)} %copy-done.2, s32[64,128]{1,0:T(8,128)S(1)} %get-tuple-element.20.u_ref), custom_call_target="tpu_custom_call" | custom-call | flops 67108864 | bytes 1048576 | tf_op jit(solution)/shard_map/pallas_call | solution.py:450
  61.0 3.5 %all-to-all-start.2 = ((bf16[16,4,256]{2,1,0:T(4,128)(2,1)}), bf16[16,4,256]{2,1,0:T(4,128)(2,1)S(1)}, u32[]{:S(2)}, u32[]{:S(2)}) async-start(bf16[16,4,256]{2,1,0:T(4,128)(2,1)} %shard_map.144), calls=%async_computation.2 | async-start | bytes 65536 | tf_op jit(solution)/shard_map/all_to_all | solution.py:333
  64.5 4.2 %shard_map.143 = (f32[320,2048]{1,0:T(8,128)}, f32[256,2048]{1,0:T(8,128)}) custom-call(s32[16]{0:T(128)S(1)} %copy-done.6, bf16[16,16,1280]{2,1,0:T(8,128)(2,1)S(1)} %all_to_all.15.part_ref), custom_call_target="tpu_custom_call" | custom-call | flops 75497472 | bytes 4718592 | tf_op jit(solution)/shard_map/pallas_call | solution.py:460
  68.7 2.4 %all-to-all-done.2.delta_ref = bf16[16,4,256]{2,1,0:T(4,128)(2,1)S(1)} async-done(((bf16[16,4,256]{2,1,0:T(4,128)(2,1)}), bf16[16,4,256]{2,1,0:T(4,128)(2,1)S(1)}, u32[]{:S(2)}, u32[]{:S(2)}) %all-to-all-start.2) | async-done | bytes 32800 | tf_op jit(solution)/shard_map/all_to_all | solution.py:333
  71.1 2.1 %shard_map.145 = bf16[4,4096]{1,0:T(4,128)(2,1)} custom-call(s32[4]{0:T(128)S(1)} %copy-done.7, bf16[16,4,256]{2,1,0:T(4,128)(2,1)S(1)} %all-to-all-done.2.delta_ref, f32[4,4096]{1,0:T(4,128)S(1)} %convert_element_type.3.base_ref, bf16[4,256,512]{2,1,0:T(8,128)(2,1)S(1)} %copy-done.3, bf16[4,256,512]{2,1,0:T(8,128)(2,1)S(1)} %copy-done.4), custom_call_target="tpu_custom_call" | custom-call | flops 16777216 | bytes 2097152 | tf_op jit(solution)/shard_map/pallas_call | solution.py:468
  (21 shorter events, 0.1 us)
Async XLA Ops:
  2.1 7.5 %copy-start.8 = (bf16[16,1408]{1,0:T(8,128)(2,1)S(1)}, bf16[16,1408]{1,0:T(8,128)(2,1)}, u32[]{:S(2)}) copy-start(bf16[16,1408]{1,0:T(8,128)(2,1)} %shard_map.139) | copy-start | bytes 135172
  2.1 26.2 %copy-start.6 = (s32[16]{0:T(128)S(1)}, s32[16]{0:T(128)}, u32[]{:S(2)}) copy-start(s32[16]{0:T(128)} %t_ref.3) | copy-start | bytes 196
  2.1 28.2 %copy-start = (bf16[320,2048]{1,0:T(8,128)(2,1)S(1)}, bf16[320,2048]{1,0:T(8,128)(2,1)}, u32[]{:S(2)}) copy-start(bf16[320,2048]{1,0:T(8,128)(2,1)} %a_ref.3) | copy-start | bytes 3932164
  2.1 28.2 %copy-start.1 = (bf16[128,5120]{1,0:T(8,128)(2,1)S(1)}, bf16[128,5120]{1,0:T(8,128)(2,1)}, u32[]{:S(2)}) copy-start(bf16[128,5120]{1,0:T(8,128)(2,1)} %x_ref.3) | copy-start | bytes 3932164
  2.1 7.5 %collective-permute-start = (bf16[1,16,1408]{2,1,0:T(8,128)(2,1)}, bf16[1,16,1408]{2,1,0:T(8,128)(2,1)S(1)}, u32[]{:S(2)}, u32[]{:S(2)}) collective-permute-start(bf16[1,16,1408]{2,1,0:T(8,128)(2,1)} %bitcast.2), channel_id=1, source_target_pairs={{0,8},{1,9},{2,10},{3,11},{4,12},{5,13},{6,14},{7,15},{8,0},{9,1},... | collective-permute-start | bytes 135176 | tf_op jit(solution)/shard_map/ppermute | solution.py:337
  9.6 6.1 %collective-permute-start.1 = (bf16[2,16,1408]{2,1,0:T(8,128)(2,1)S(1)}, bf16[2,16,1408]{2,1,0:T(8,128)(2,1)S(1)}, u32[]{:S(2)}, u32[]{:S(2)}) collective-permute-start(bf16[2,16,1408]{2,1,0:T(8,128)(2,1)S(1)} %pad_maximum_fusion.2), channel_id=1, source_target_pairs={{0,4},{1,5},{2,6},{3,7},{4,0},{5,1},{6,2},{7,3},{8,12},{9,13},{10,... | collective-permute-start | bytes 270344 | tf_op jit(solution)/shard_map/ppermute | solution.py:337
  11.2 21.2 %all-to-all-start = ((bf16[16,16,1152]{2,1,0:T(8,128)(2,1)}), bf16[16,16,1152]{2,1,0:T(8,128)(2,1)S(1)}, u32[]{:S(2)}, u32[]{:S(2)}) async-start(bf16[16,16,1152]{2,1,0:T(8,128)(2,1)} %shard_map.140), calls=%async_computation | async-start | bytes 1179648 | tf_op jit(solution)/shard_map/all_to_all | solution.py:333
  15.7 11.7 %collective-permute-start.2 = (bf16[4,16,1408]{2,1,0:T(8,128)(2,1)S(1)}, bf16[4,16,1408]{2,1,0:T(8,128)(2,1)S(1)}, u32[]{:S(2)}, u32[]{:S(2)}) collective-permute-start(bf16[4,16,1408]{2,1,0:T(8,128)(2,1)S(1)} %pad_maximum_fusion.1), channel_id=1, source_target_pairs={{0,2},{1,3},{2,0},{3,1},{4,6},{5,7},{6,4},{7,5},{8,10},{9,11},{10,... | collective-permute-start | bytes 540680 | tf_op jit(solution)/shard_map/ppermute | solution.py:337
  28.2 2.0 %collective-permute-start.3 = (bf16[8,16,1408]{2,1,0:T(8,128)(2,1)}, bf16[8,16,1408]{2,1,0:T(8,128)(2,1)}, u32[]{:S(2)}, u32[]{:S(2)}) collective-permute-start(bf16[8,16,1408]{2,1,0:T(8,128)(2,1)} %pad_maximum_fusion.h0_ref), channel_id=1, source_target_pairs={{0,1},{1,0},{2,3},{3,2},{4,5},{5,4},{6,7},{7,6},{8,9},{9,8},{10,11... | collective-permute-start | bytes 1081352 | tf_op jit(solution)/shard_map/ppermute | solution.py:337
  32.4 1.2 %copy-start.5 = (bf16[128,4096]{1,0:T(8,128)(2,1)S(1)}, bf16[128,4096]{1,0:T(8,128)(2,1)}, u32[]{:S(2)}) copy-start(bf16[128,4096]{1,0:T(8,128)(2,1)} %g_ref.1) | copy-start | bytes 3145732
  33.7 25.5 %copy-start.2 = (bf16[256,2048]{1,0:T(8,128)(2,1)S(1)}, bf16[256,2048]{1,0:T(8,128)(2,1)}, u32[]{:S(2)}) copy-start(bf16[256,2048]{1,0:T(8,128)(2,1)} %b_ref.3) | copy-start | bytes 3145732
  35.6 28.9 %copy-start.9 = (bf16[4,4096]{1,0:T(4,128)(2,1)S(1)}, bf16[4,4096]{1,0:T(4,128)(2,1)}, u32[]{:S(2)}) copy-start(bf16[4,4096]{1,0:T(4,128)(2,1)} %param.20) | copy-start | bytes 98308
  35.6 35.5 %copy-start.3 = (bf16[4,256,512]{2,1,0:T(8,128)(2,1)S(1)}, bf16[4,256,512]{2,1,0:T(8,128)(2,1)}, u32[]{:S(2)}) copy-start(bf16[4,256,512]{2,1,0:T(8,128)(2,1)} %k_ref.1) | copy-start | bytes 3145732
  35.6 35.5 %copy-start.4 = (bf16[4,256,512]{2,1,0:T(8,128)(2,1)S(1)}, bf16[4,256,512]{2,1,0:T(8,128)(2,1)}, u32[]{:S(2)}) copy-start(bf16[4,256,512]{2,1,0:T(8,128)(2,1)} %v_ref.1) | copy-start | bytes 3145732
  35.6 35.5 %copy-start.7 = (s32[4]{0:T(128)S(1)}, s32[4]{0:T(128)}, u32[]{:S(2)}) copy-start(s32[4]{0:T(128)} %len_ref.1) | copy-start | bytes 52
  61.0 10.1 %all-to-all-start.2 = ((bf16[16,4,256]{2,1,0:T(4,128)(2,1)}), bf16[16,4,256]{2,1,0:T(4,128)(2,1)S(1)}, u32[]{:S(2)}, u32[]{:S(2)}) async-start(bf16[16,4,256]{2,1,0:T(4,128)(2,1)} %shard_map.144), calls=%async_computation.2 | async-start | bytes 65536 | tf_op jit(solution)/shard_map/all_to_all | solution.py:333
